TPU v7x, 32 devices: a whole 2x2x4 slice. The times are simulated.
32 devices in a mesh: pole: 2 (over y), prow: 4 (over z), pcol: 4 (over x, core).
Axes of the slice: x: 2, y: 2, z: 4, core: 2. Of those that a mesh axis runs over, the one named last changes fastest.
Arguments:
- inverse_top: bfloat16 [4096, 2048], P(('pole', 'prow'), 'pcol'), parts along dimension 0, as said below
- diag_inverse: float32 [8, 256, 256], P(('pole', 'pcol')), parts along dimension 0, as said below
- cross_blocks: float32 [4096, 1024], P(('pole', 'prow'), 'pcol'), parts along dimension 0, may hold values from -0.75 to 0.75
- pattern: int32 [8, 4], P('prow', 'pcol'), may hold values 0 or 1
Outputs:
- inverse_cross: float32 [4096, 1024], P(('pole', 'prow'), 'pcol'), parts along dimension 0
- inverse_diag: float32 [8, 256, 256], P(('pole', 'pcol')), parts along dimension 0
There are 2 independent parts, one for each index of `pole`. A program takes and returns all parts, laid end to end along the dimension named above; an argument that names none is the same for every part. Nothing has to cross between parts.
Inputs may be any that keep to these rules, and one draw needn't show every extreme that they name: inverse_top is symmetric. Each diag_inverse[k] is symmetric.
All inputs are finite; a program needn't handle non-finite values. No bound on the sum of `pattern` on one device may be relied on, other than what follows from the above.
Results may differ from a plain program's by a relative error of at most 0.009.
Values may be sent and summed in bfloat16 or wider, within the bound.
No kernel may reach another device: no remote copies, remote signals or barrier semaphores. Data moves between devices by JAX's collectives and lax.ppermute only.
A program may use at most 64 MiB of HBM per device.

v0:
```python
import jax
import jax.numpy as jnp
from jax import lax
from jax.sharding import PartitionSpec as P


def from_root(block, axis, holder):
    block = jnp.where(lax.axis_index(axis) == holder, block, jnp.zeros_like(block))
    return lax.psum(block, axis)


def build_panel(cross_blocks, diag_inverse, pattern):
    top_count, child_count = pattern.shape
    width = diag_inverse.shape[1]
    masked = (
        cross_blocks.reshape(top_count, width, child_count, width)
        * pattern.astype(jnp.float32)[:, None, :, None]
    )
    solved = jnp.einsum("awkv,kvu->awku", masked, diag_inverse, precision=lax.Precision.HIGHEST)
    return solved.reshape(top_count * width, child_count * width).astype(jnp.bfloat16)


def on_device(inverse_top, diag_inverse, cross_blocks, pattern):
    factor_panel = build_panel(cross_blocks, diag_inverse, pattern)
    rows_here, columns_here = factor_panel.shape
    child_count, width = (diag_inverse.shape[0], diag_inverse.shape[1])
    along_row = lax.all_gather(factor_panel, "pcol", axis=1, tiled=True)
    matched = from_root(along_row, "prow", lax.axis_index("pcol"))
    partial_value = jnp.dot(inverse_top, matched, preferred_element_type=jnp.float32)
    selected = lax.psum_scatter(
        partial_value.astype(jnp.bfloat16), "pcol", scatter_dimension=1, tiled=True
    ).astype(jnp.float32)
    local_update = jnp.einsum(
        "iku,ikv->kuv",
        factor_panel.astype(jnp.float32).reshape(rows_here, child_count, width),
        selected.reshape(rows_here, child_count, width),
        precision=lax.Precision.HIGHEST,
    )
    update = lax.psum(local_update.astype(jnp.bfloat16), "prow").astype(jnp.float32)
    return (-selected, diag_inverse + update)


def solution(mesh):
    placed = (
        P(("pole", "prow"), "pcol"),
        P(("pole", "pcol"), None, None),
        P(("pole", "prow"), "pcol"),
        P("prow", "pcol"),
    )
    return jax.shard_map(
        on_device,
        mesh=mesh,
        in_specs=placed,
        out_specs=(P(("pole", "prow"), "pcol"), P(("pole", "pcol"), None, None)),
        check_vma=False,
    )
```

profile of v0, /device:TPU:0, one launch (start us, length us, event | category | flops | bytes accessed | tf_op | source)
XLA Modules:
  0.0 157.4 jit_solution(5023975998662479105)
XLA Ops:
  7.2 0.0 copy-start
  7.2 0.0 copy-start.2
  7.2 0.0 all-gather.2.cloned.1.call-start
  7.2 0.7 convert_bitcast_fusion
  8.0 0.1 broadcast_bitcast_fusion
  8.1 1.2 broadcast_multiply_fusion
  9.2 0.0 copy-done.2
  9.2 1.3 convolution_convert_fusion.1
  10.5 0.0 all-gather.2.cloned.1.call-update
  10.5 0.0 all-reduce.3.cloned.1.call-start
  10.6 19.6 %all-gather.2.cloned.1.call-done = bf16[512,1024]{1,0:T(8,128)(2,1)} async-done(((bf16[512,256]{1,0:T(8,128)(2,1)}), bf16[512,1024]{1,0:T(8,128)(2,1)}) %all-gather.2.cloned.1.call-update) | async-done | bytes 1048592 | tf_op jit(solution)/shard_map/all_gather | solution.py:27
  30.2 2.3 %broadcast_select_fusion = bf16[512,1024]{1,0:T(8,128)(2,1)} fusion(bf16[512,1024]{1,0:T(8,128)(2,1)} %all-gather.2.cloned.1.call-done, pred[]{:T(512)S(6)} %eq.3), kind=kLoop, calls=%fused_computation.5 | loop fusion | flops 524288 | bytes 2097153 | tf_op jit(solution)/shard_map/jit(_where)/select_n | solution.py:8
  32.6 0.0 all-reduce.3.cloned.1.call-update
  32.6 0.0 reduce-scatter.2.cloned.1.call-start
  32.7 51.8 %all-reduce.3.cloned.1.call-done = bf16[512,1024]{1,0:T(8,128)(2,1)} async-done(((bf16[512,1024]{1,0:T(8,128)(2,1)}), bf16[512,1024]{1,0:T(8,128)(2,1)}) %all-reduce.3.cloned.1.call-update) | async-done | bytes 1048592 | tf_op jit(solution)/shard_map/psum | solution.py:9
  84.5 0.0 copy-done
  84.5 3.0 %fusion = bf16[512,1024]{0,1:T(8,128)(2,1)} fusion(bf16[512,1024]{1,0:T(8,128)(2,1)} %all-reduce.3.cloned.1.call-done, bf16[512,512]{1,0:T(8,128)(2,1)S(1)} %copy-done), kind=kOutput, calls=%fused_computation.1 | convolution fusion | flops 537395200 | bytes 2621440 | tf_op jit(solution)/shard_map/dot_general | solution.py:29
  87.5 0.0 copy-start.1
  87.5 0.0 reduce-scatter.2.cloned.1.call-update
  87.5 0.0 all-reduce.5.cloned.1.call-start
  87.6 24.4 %reduce-scatter.2.cloned.1.call-done = bf16[512,256]{0,1:T(8,128)(2,1)} async-done(((bf16[512,1024]{0,1:T(8,128)(2,1)}), bf16[512,256]{0,1:T(8,128)(2,1)}) %reduce-scatter.2.cloned.1.call-update) | async-done | bytes 262160 | tf_op jit(solution)/shard_map/reduce_scatter | solution.py:30
  112.0 0.0 copy-done.1
  112.0 1.9 %fusion.1 = bf16[1,256,256]{2,1,0:T(8,128)(2,1)} fusion(bf16[512,256]{1,0:T(8,128)(2,1)S(1)} %bitcast.27, bf16[512,256]{0,1:T(8,128)(2,1)} %reduce-scatter.2.cloned.1.call-done), kind=kOutput, calls=%fused_computation.4 | convolution fusion | flops 67174400 | bytes 655360 | tf_op jit(solution)/shard_map/iku,ikv->kuv/dot_general | solution.py:33
  113.8 0.0 all-reduce.5.cloned.1.call-update
  113.9 1.0 convert_negate_fusion
  114.9 1.0 copy.6
  115.9 33.3 %all-reduce.5.cloned.1.call-done = bf16[1,256,256]{2,1,0:T(8,128)(2,1)} async-done(((bf16[1,256,256]{2,1,0:T(8,128)(2,1)}), bf16[1,256,256]{2,1,0:T(8,128)(2,1)}) %all-reduce.5.cloned.1.call-update) | async-done | bytes 131088 | tf_op jit(solution)/shard_map/psum | solution.py:39
  149.2 1.6 %convert_add_fusion = f32[1,256,256]{2,1,0:T(8,128)} fusion(f32[1,256,256]{2,1,0:T(8,128)S(1)} %copy-done.2, bf16[1,256,256]{2,1,0:T(8,128)(2,1)} %all-reduce.5.cloned.1.call-done), kind=kLoop, calls=%fused_computation.8 | loop fusion | flops 131072 | bytes 655360 | tf_op jit(solution)/shard_map/add | solution.py:40
  (1 shorter events, 0.0 us)
Async XLA Ops:
  7.2 77.3 %copy-start = (bf16[512,512]{1,0:T(8,128)(2,1)S(1)}, bf16[512,512]{1,0:T(8,128)(2,1)}, u32[]{:S(2)}) copy-start(bf16[512,512]{1,0:T(8,128)(2,1)} %param.4) | copy-start | bytes 1572868
  7.2 2.1 %copy-start.2 = (f32[1,256,256]{2,1,0:T(8,128)S(1)}, f32[1,256,256]{2,1,0:T(8,128)}, u32[]{:S(2)}) copy-start(f32[1,256,256]{2,1,0:T(8,128)} %param.5) | copy-start | bytes 786436
  7.2 23.1 %all-gather.2.cloned.1.call-start = ((), (), s32[]{:S(2)}) async-start(), calls=%async_computation.1 | async-start | bytes 1310720 | tf_op jit(solution)/shard_map/all_gather | solution.py:27
  10.5 73.9 %all-reduce.3.cloned.1.call-start = ((), (), s32[]{:S(2)}) async-start(), calls=%async_computation.2 | async-start | bytes 2097152 | tf_op jit(solution)/shard_map/psum | solution.py:9
  32.6 79.3 %reduce-scatter.2.cloned.1.call-start = ((), (), s32[]{:S(2)}) async-start(), calls=%async_computation.3 | async-start | bytes 1310720 | tf_op jit(solution)/shard_map/reduce_scatter | solution.py:30
  87.5 24.4 %copy-start.1 = (bf16[2,256,256]{2,1,0:T(8,128)(2,1)S(1)}, bf16[2,256,256]{2,1,0:T(8,128)(2,1)}, u32[]{:S(2)}) copy-start(bf16[2,256,256]{2,1,0:T(8,128)(2,1)} %convolution_convert_fusion.1) | copy-start | bytes 786436
  87.5 61.7 %all-reduce.5.cloned.1.call-start = ((), (), s32[]{:S(2)}) async-start(), calls=%async_computation.4 | async-start | bytes 262144 | tf_op jit(solution)/shard_map/psum | solution.py:39
Sparse Core Ops, SparseCore 0:
  10.7 19.5 all-gather.1
  32.7 51.7 all-reduce.2
  87.7 24.2 reduce-scatter.1
  114.7 34.4 all-reduce.4
where the time goes:
time: 158 us; the launch traced here: 157 us
  waiting for transfers between devices  129 us (82%)
  between operations  13.8 us (9%)
  other arithmetic  6.87 us (4%)
  matrix products  6.19 us (4%)
    psum x1, waiting for transfers between devices, from_root(): return lax.psum(block, axis)  51.8 us
    psum x1, waiting for transfers between devices, on_device(): lax.psum(local_update.astype(jnp.bfloat16), 'prow').astype(jnp.float32)  33.3 us
    reduce_scatter x1, waiting for transfers between devices, on_device(): lax.psum_scatter(partial_value.astype(jnp.bfloat16), 'pcol', scatter_dime...  24.4 us
    all_gather x1, waiting for transfers between devices, on_device(): along_row = lax.all_gather(factor_panel, 'pcol', axis=1, tiled=True)  19.6 us
  transfers between devices with their start and end apart: 4, of which 4 were waited for; matrix products, arithmetic and copies ran while one was open for 1% of the time, Pallas kernels for 0%

commit v1 on v0

v1 whole, which is shorter than its diff:
```python
import functools
import jax
import jax.numpy as jnp
from jax import lax
from jax.experimental import pallas as pl
from jax.experimental.pallas import tpu as pltpu
from jax.sharding import PartitionSpec as P

CORES = 2
VMEM_LIMIT = 40 * 1024 * 1024


def panel_kernel(pattern_ref, cross_ref, diag_ref, panel_ref):
    width = diag_ref.shape[1]
    for a in range(pattern_ref.shape[0]):
        rows = pl.ds(a * width, width)
        masked = cross_ref[rows, :] * pattern_ref[a, 0].astype(jnp.float32)
        solved = jnp.dot(
            masked, diag_ref[0], precision=lax.Precision.HIGHEST, preferred_element_type=jnp.float32
        )
        panel_ref[rows, :] = solved.astype(jnp.bfloat16)


def build_panel(cross_blocks, diag_inverse, pattern):
    return pl.pallas_call(
        panel_kernel,
        out_shape=jax.ShapeDtypeStruct(cross_blocks.shape, jnp.bfloat16),
        in_specs=[
            pl.BlockSpec(memory_space=pltpu.SMEM),
            pl.BlockSpec(memory_space=pltpu.VMEM),
            pl.BlockSpec(memory_space=pltpu.VMEM),
        ],
        out_specs=pl.BlockSpec(memory_space=pltpu.VMEM),
        compiler_params=pltpu.CompilerParams(vmem_limit_bytes=VMEM_LIMIT),
        name="panel",
    )(pattern, cross_blocks, diag_inverse)


def product_kernel(n, slots_ref, *refs):
    tops, panels = refs[:n], refs[n:2 * n]
    cross_ref, update_ref, top_buf, panel_buf, top_sems, panel_sems = refs[2 * n:]
    copies = []
    for s in range(n):
        copy = pltpu.make_async_copy(panels[s], panel_buf.at[slots_ref[s]], panel_sems.at[s])
        copy.start()
        copies.append(copy)
    for t in range(n):
        copy = pltpu.make_async_copy(tops[t], top_buf.at[t], top_sems.at[t])
        copy.start()
        copies.append(copy)
    for copy in copies:
        copy.wait()
    total = jnp.dot(top_buf[0], panel_buf[0], preferred_element_type=jnp.float32)
    for t in range(1, n):
        total += jnp.dot(top_buf[t], panel_buf[t], preferred_element_type=jnp.float32)
    cross_ref[...] = -total
    own = panel_buf[slots_ref[0]]
    high = total.astype(jnp.bfloat16)
    low = (total - high.astype(jnp.float32)).astype(jnp.bfloat16)
    contract = (((0,), (0,)), ((), ()))
    update = lax.dot_general(own, high, contract, preferred_element_type=jnp.float32)
    update += lax.dot_general(own, low, contract, preferred_element_type=jnp.float32)
    update_ref[...] = update.astype(jnp.bfloat16)


def products(tops, panels, slots):
    n = len(tops)
    rows, width = panels[0].shape
    anywhere = pl.BlockSpec(memory_space=pl.ANY)
    vmem = pl.BlockSpec(memory_space=pltpu.VMEM)
    return pl.pallas_call(
        functools.partial(product_kernel, n),
        out_shape=(
            jax.ShapeDtypeStruct((rows, width), jnp.float32),
            jax.ShapeDtypeStruct((width, width), jnp.bfloat16),
        ),
        in_specs=[pl.BlockSpec(memory_space=pltpu.SMEM)] + [anywhere] * (2 * n),
        out_specs=(vmem, vmem),
        scratch_shapes=[
            pltpu.VMEM((n,) + tops[0].shape, jnp.bfloat16),
            pltpu.VMEM((n, rows, width), jnp.bfloat16),
            pltpu.SemaphoreType.DMA((n,)),
            pltpu.SemaphoreType.DMA((n,)),
        ],
        compiler_params=pltpu.CompilerParams(vmem_limit_bytes=VMEM_LIMIT),
        name="products",
    )(slots, *tops, *panels)


def on_device(n, inverse_top, diag_inverse, cross_blocks, pattern):
    chips = n // CORES
    row, col = lax.axis_index("prow"), lax.axis_index("pcol")

    def along_chips(block, shift):
        pairs = [(((x + shift) % chips) * CORES + c, x * CORES + c) for x in range(chips) for c in range(CORES)]
        return lax.ppermute(block, "pcol", pairs)

    def other_core(block):
        pairs = [(x * CORES + (c + 1) % CORES, x * CORES + c) for x in range(chips) for c in range(CORES)]
        return lax.ppermute(block, "pcol", pairs)

    def along_rows(block, shift):
        return lax.ppermute(block, "prow", [((i + shift) % n, i) for i in range(n)])

    near = [inverse_top] + [along_chips(inverse_top, d) for d in range(1, chips)]
    tops = [block for mine in near for block in (mine, other_core(mine))]

    factor_panel = build_panel(cross_blocks, diag_inverse, pattern)
    panels = [factor_panel] + [along_rows(factor_panel, s) for s in range(1, n)]

    wanted = (row + jnp.arange(n, dtype=jnp.int32)) % n
    across = (wanted // CORES - col // CORES) % chips
    slots = across * CORES + (wanted % CORES - col % CORES) % CORES

    inverse_cross, update = products(tops, panels, slots)
    updates = [update] + [along_rows(update, s) for s in range(1, n)]
    total = functools.reduce(jnp.add, [u.astype(jnp.float32) for u in updates])
    return inverse_cross, diag_inverse + total[None]


def solution(mesh):
    placed = (
        P(("pole", "prow"), "pcol"),
        P(("pole", "pcol"), None, None),
        P(("pole", "prow"), "pcol"),
        P("prow", "pcol"),
    )
    return jax.shard_map(
        functools.partial(on_device, mesh.shape["pcol"]),
        mesh=mesh,
        in_specs=placed,
        out_specs=(P(("pole", "prow"), "pcol"), P(("pole", "pcol"), None, None)),
        check_vma=False,
    )
```

time: 158 us -> 62.2 us (0.39)
  waiting for transfers between devices: 129 us -> 36.2 us
  starting transfers between devices: 0.16 us -> 17.4 us
  between operations: 13.8 us -> 0.68 us
  matrix products: 6.19 us -> 0 us
  other arithmetic: 6.87 us -> 0.81 us
  Pallas kernels: 0 us -> 3.67 us
  local copies, waits for them, and re-layouts: 1.09 us -> 2.74 us
    psum x2 -> x0, waiting for transfers between devices: 85.2 us -> none  [the longest x1 51.8 us: from_root(): return lax.psum(block, axis)]
    ppermute x0 -> x9, waiting for transfers between devices: none -> 36.2 us  [the longest x6 24.1 us: along_rows(): return lax.ppermute(block, 'prow', [((i + shift) % n, i) for i in range(n)])]
    reduce_scatter x1 -> x0, waiting for transfers between devices: 24.4 us -> none  [on_device(): lax.psum_scatter(partial_value.astype(jnp.bfloat16), 'pcol', scatter_dime...]
    all_gather x1 -> x0, waiting for transfers between devices: 19.6 us -> none  [on_device(): along_row = lax.all_gather(factor_panel, 'pcol', axis=1, tiled=True)]
    ppermute x0 -> x9, starting transfers between devices: none -> 17.4 us  [the longest x6 14.4 us: along_rows(): return lax.ppermute(block, 'prow', [((i + shift) % n, i) for i in range(n)])]
    dot_general x3 -> x0, matrix products: 6.19 us -> none  [the longest x1 3.02 us: on_device(): jnp.dot(inverse_top, matched, preferred_element_type=jnp.float32)]
    pallas_call x0 -> x2, Pallas kernels: none -> 3.67 us  [the longest x1 2.5 us: products(): pl.pallas_call(functools.partial(product_kernel, n), out_shape=(jax.Shape...]
    select_n x1 -> x0, other arithmetic: 2.33 us -> none  [from_root(): jnp.where(lax.axis_index(axis) == holder, block, jnp.zeros_like(block))]
  transfers between devices with their start and end apart: 4 -> 9, of which waited for: 4 -> 5; matrix products, arithmetic and copies ran while one was open for 1% -> 1% of each run, Pallas kernels for 0% -> 2%
where the time goes in v1:
time: 62.2 us; the launch traced here: 61.5 us
  waiting for transfers between devices  36.2 us (58%)
  starting transfers between devices  17.4 us (28%)
  Pallas kernels  3.67 us (6%)
  local copies, waits for them, and re-layouts  2.74 us (4%)
  other arithmetic  0.81 us (1%)
  between operations  0.68 us (1%)
    ppermute x6, waiting for transfers between devices, along_rows(): return lax.ppermute(block, 'prow', [((i + shift) % n, i) for i in range(n)])  24.1 us
    ppermute x6, starting transfers between devices, along_rows(): return lax.ppermute(block, 'prow', [((i + shift) % n, i) for i in range(n)])  14.4 us
    ppermute x1, waiting for transfers between devices, along_chips(): return lax.ppermute(block, 'pcol', pairs)  12.1 us
    ppermute x1, starting transfers between devices, along_chips(): return lax.ppermute(block, 'pcol', pairs)  3 us
    unnamed x9, local copies, waits for them, and re-layouts  2.74 us
    pallas_call x1, Pallas kernels, products(): pl.pallas_call(functools.partial(product_kernel, n), out_shape=(jax.Shape...  2.5 us
  transfers between devices with their start and end apart: 9, of which 5 were waited for; matrix products, arithmetic and copies ran while one was open for 1% of the time, Pallas kernels for 2%

profile of v1, /device:TPU:0, one launch (start us, length us, event | category | flops | bytes accessed | tf_op | source)
XLA Modules:
  0.0 61.5 jit_solution(8199740313979533448)
XLA Ops:
  0.6 3.0 %collective-permute-start.1 = (bf16[512,512]{1,0:T(8,128)(2,1)}, bf16[512,512]{1,0:T(8,128)(2,1)S(1)}, u32[]{:S(2)}, u32[]{:S(2)}) collective-permute-start(bf16[512,512]{1,0:T(8,128)(2,1)} %refs_0_.1), channel_id=1, source_target_pairs={{2,0},{3,1},{0,2},{1,3},{6,4},{7,5},{4,6},{5,7},{10,8},{11,9},{8,1... | collective-permute-start | bytes 1572872 | tf_op jit(solution)/shard_map/ppermute | solution.py:96
  3.6 0.0 collective-permute-start
  3.6 12.1 %collective-permute-done.1.refs_2_ = bf16[512,512]{1,0:T(8,128)(2,1)S(1)} collective-permute-done((bf16[512,512]{1,0:T(8,128)(2,1)}, bf16[512,512]{1,0:T(8,128)(2,1)S(1)}, u32[]{:S(2)}, u32[]{:S(2)}) %collective-permute-start.1) | collective-permute-done | bytes 524320 | tf_op jit(solution)/shard_map/ppermute | solution.py:96
  15.8 0.0 collective-permute-start.2
  15.8 0.7 %copy.6.pattern_ref = s32[2,1]{1,0:T(2,128)S(1)} copy(s32[2,1]{0,1:T(1,128)} %param.7) | data formatting | bytes 16 | tf_op args[3]
  16.5 0.0 copy-start
  16.5 0.9 %copy-done = f32[1,256,256]{2,1,0:T(8,128)S(1)} copy-done((f32[1,256,256]{2,1,0:T(8,128)S(1)}, f32[1,256,256]{2,1,0:T(8,128)}, u32[]{:S(2)}) %copy-start) | copy-done | bytes 262168
  17.5 0.0 copy-start.2
  17.5 1.0 %copy-done.2 = f32[512,256]{1,0:T(8,128)S(1)} copy-done((f32[512,256]{1,0:T(8,128)S(1)}, f32[512,256]{1,0:T(8,128)}, u32[]{:S(2)}) %copy-start.2) | copy-done | bytes 524312
  18.5 0.0 copy-start.3
  18.5 1.2 %panel.1.refs_4_ = bf16[512,256]{1,0:T(8,128)(2,1)S(1)} custom-call(s32[2,1]{1,0:T(2,128)S(1)} %copy.6.pattern_ref, f32[512,256]{1,0:T(8,128)S(1)} %copy-done.2, f32[1,256,256]{2,1,0:T(8,128)S(1)} %copy-done), custom_call_target="tpu_custom_call" | custom-call | tf_op jit(solution)/shard_map/panel/pallas_call | solution.py:25
  19.7 1.9 %collective-permute-start.5 = (bf16[512,256]{1,0:T(8,128)(2,1)S(1)}, bf16[512,256]{1,0:T(8,128)(2,1)S(1)}, u32[]{:S(2)}, u32[]{:S(2)}) collective-permute-start(bf16[512,256]{1,0:T(8,128)(2,1)S(1)} %panel.1.refs_4_), channel_id=1, source_target_pairs={{12,0},{0,4},{4,8},{8,12},{13,1},{1,5},{5,9},{9,13},{14,2},{2,6},{... | collective-permute-start | bytes 786440 | tf_op jit(solution)/shard_map/ppermute | solution.py:103
  21.6 2.6 %collective-permute-start.4 = (bf16[512,256]{1,0:T(8,128)(2,1)S(1)}, bf16[512,256]{1,0:T(8,128)(2,1)S(1)}, u32[]{:S(2)}, u32[]{:S(2)}) collective-permute-start(bf16[512,256]{1,0:T(8,128)(2,1)S(1)} %panel.1.refs_4_), channel_id=1, source_target_pairs={{8,0},{12,4},{0,8},{4,12},{9,1},{13,5},{1,9},{5,13},{10,2},{14,6},... | collective-permute-start | bytes 786440 | tf_op jit(solution)/shard_map/ppermute | solution.py:103
  24.2 1.3 %collective-permute-start.3 = (bf16[512,256]{1,0:T(8,128)(2,1)S(1)}, bf16[512,256]{1,0:T(8,128)(2,1)S(1)}, u32[]{:S(2)}, u32[]{:S(2)}) collective-permute-start(bf16[512,256]{1,0:T(8,128)(2,1)S(1)} %panel.1.refs_4_), channel_id=1, source_target_pairs={{4,0},{8,4},{12,8},{0,12},{5,1},{9,5},{13,9},{1,13},{6,2},{10,6},{... | collective-permute-start | bytes 786440 | tf_op jit(solution)/shard_map/ppermute | solution.py:103
  25.5 0.0 copy-start.1
  25.5 5.3 %collective-permute-done.5.refs_7_ = bf16[512,256]{1,0:T(8,128)(2,1)S(1)} collective-permute-done((bf16[512,256]{1,0:T(8,128)(2,1)S(1)}, bf16[512,256]{1,0:T(8,128)(2,1)S(1)}, u32[]{:S(2)}, u32[]{:S(2)}) %collective-permute-start.5) | collective-permute-done | bytes 262176 | tf_op jit(solution)/shard_map/ppermute | solution.py:103
  30.9 11.0 %collective-permute-done.4.refs_6_ = bf16[512,256]{1,0:T(8,128)(2,1)S(1)} collective-permute-done((bf16[512,256]{1,0:T(8,128)(2,1)S(1)}, bf16[512,256]{1,0:T(8,128)(2,1)S(1)}, u32[]{:S(2)}, u32[]{:S(2)}) %collective-permute-start.4) | collective-permute-done | bytes 262176 | tf_op jit(solution)/shard_map/ppermute | solution.py:103
  41.9 0.0 collective-permute-done.3.refs_5_
  41.9 0.0 collective-permute-done.refs_1_
  41.9 0.0 collective-permute-done.2.refs_3_
  41.9 0.0 copy-done.3
  41.9 2.5 %products.1 = (f32[512,256]{1,0:T(8,128)}, bf16[256,256]{1,0:T(8,128)(2,1)S(1)}) custom-call(s32[4]{0:T(128)S(1)} %fusion.slots_ref, bf16[512,512]{1,0:T(8,128)(2,1)S(1)} %copy-done.3, bf16[512,512]{1,0:T(8,128)(2,1)S(1)} %collective-permute-done.refs_1_, bf16[512,512]{1,0:T(8,128)(2,1)S(1)} %collective-permute-done.1.refs_2_, ...), custom_call_target="tpu_custom_call" | custom-call | tf_op jit(solution)/shard_map/products/pallas_call | solution.py:71
  44.4 6.2 %collective-permute-start.8 = (bf16[256,256]{1,0:T(8,128)(2,1)S(1)}, bf16[256,256]{1,0:T(8,128)(2,1)S(1)}, u32[]{:S(2)}, u32[]{:S(2)}) collective-permute-start(bf16[256,256]{1,0:T(8,128)(2,1)S(1)} %get-tuple-element.5), channel_id=1, source_target_pairs={{12,0},{0,4},{4,8},{8,12},{13,1},{1,5},{5,9},{9,13},{14,2},{2,6},{... | collective-permute-start | bytes 393224 | tf_op jit(solution)/shard_map/ppermute | solution.py:103
  50.6 1.6 %collective-permute-start.7 = (bf16[256,256]{1,0:T(8,128)(2,1)S(1)}, bf16[256,256]{1,0:T(8,128)(2,1)S(1)}, u32[]{:S(2)}, u32[]{:S(2)}) collective-permute-start(bf16[256,256]{1,0:T(8,128)(2,1)S(1)} %get-tuple-element.5), channel_id=1, source_target_pairs={{8,0},{12,4},{0,8},{4,12},{9,1},{13,5},{1,9},{5,13},{10,2},{14,6},... | collective-permute-start | bytes 393224 | tf_op jit(solution)/shard_map/ppermute | solution.py:103
  52.2 0.8 %collective-permute-start.6 = (bf16[256,256]{1,0:T(8,128)(2,1)S(1)}, bf16[256,256]{1,0:T(8,128)(2,1)S(1)}, u32[]{:S(2)}, u32[]{:S(2)}) collective-permute-start(bf16[256,256]{1,0:T(8,128)(2,1)S(1)} %get-tuple-element.5), channel_id=1, source_target_pairs={{4,0},{8,4},{12,8},{0,12},{5,1},{9,5},{13,9},{1,13},{6,2},{10,6},{... | collective-permute-start | bytes 393224 | tf_op jit(solution)/shard_map/ppermute | solution.py:103
  53.0 3.0 %collective-permute-done.8 = bf16[256,256]{1,0:T(8,128)(2,1)S(1)} collective-permute-done((bf16[256,256]{1,0:T(8,128)(2,1)S(1)}, bf16[256,256]{1,0:T(8,128)(2,1)S(1)}, u32[]{:S(2)}, u32[]{:S(2)}) %collective-permute-start.8) | collective-permute-done | bytes 131104 | tf_op jit(solution)/shard_map/ppermute | solution.py:103
  56.1 4.7 %collective-permute-done.7 = bf16[256,256]{1,0:T(8,128)(2,1)S(1)} collective-permute-done((bf16[256,256]{1,0:T(8,128)(2,1)S(1)}, bf16[256,256]{1,0:T(8,128)(2,1)S(1)}, u32[]{:S(2)}, u32[]{:S(2)}) %collective-permute-start.7) | collective-permute-done | bytes 131104 | tf_op jit(solution)/shard_map/ppermute | solution.py:103
  60.7 0.0 collective-permute-done.6
  60.7 0.0 copy-done.1
  60.7 0.8 %bitcast_add_fusion = f32[1,256,256]{2,1,0:T(8,128)} fusion(f32[1,256,256]{2,1,0:T(8,128)S(1)} %copy-done.1, bf16[256,256]{1,0:T(8,128)(2,1)S(1)} %collective-permute-done.8, bf16[256,256]{1,0:T(8,128)(2,1)S(1)} %collective-permute-done.7, bf16[256,256]{1,0:T(8,128)(2,1)S(1)} %collective-permute-done.6, bf16[256,256]{1,0:T(8,128)(2,1)S(1)} %get-tuple-element.5), kind=kLoop, calls=%fused_computation | loop fusion | flops 524288 | bytes 1048576 | tf_op jit(solution)/shard_map/add | solution.py:118
  (1 shorter events, 0.0 us)
Async XLA Ops:
  0.6 15.1 %collective-permute-start.1 = (bf16[512,512]{1,0:T(8,128)(2,1)}, bf16[512,512]{1,0:T(8,128)(2,1)S(1)}, u32[]{:S(2)}, u32[]{:S(2)}) collective-permute-start(bf16[512,512]{1,0:T(8,128)(2,1)} %refs_0_.1), channel_id=1, source_target_pairs={{2,0},{3,1},{0,2},{1,3},{6,4},{7,5},{4,6},{5,7},{10,8},{11,9},{8,1... | collective-permute-start | bytes 1572872 | tf_op jit(solution)/shard_map/ppermute | solution.py:96
  3.6 38.3 %collective-permute-start = (bf16[512,512]{1,0:T(8,128)(2,1)}, bf16[512,512]{1,0:T(8,128)(2,1)S(1)}, u32[]{:S(2)}, u32[]{:S(2)}) collective-permute-start(bf16[512,512]{1,0:T(8,128)(2,1)} %refs_0_.1), channel_id=1, source_target_pairs={{1,0},{0,1},{3,2},{2,3},{5,4},{4,5},{7,6},{6,7},{9,8},{8,9},{11,10... | collective-permute-start | bytes 1572872 | tf_op jit(solution)/shard_map/ppermute | solution.py:100
  15.8 26.2 %collective-permute-start.2 = (bf16[512,512]{1,0:T(8,128)(2,1)S(1)}, bf16[512,512]{1,0:T(8,128)(2,1)S(1)}, u32[]{:S(2)}, u32[]{:S(2)}) collective-permute-start(bf16[512,512]{1,0:T(8,128)(2,1)S(1)} %collective-permute-done.1.refs_2_), channel_id=1, source_target_pairs={{1,0},{0,1},{3,2},{2,3},{5,4},{4,5},{7,6},{6,7},{9,8},{8,9},{11,10... | collective-permute-start | bytes 1572872 | tf_op jit(solution)/shard_map/ppermute | solution.py:100
  16.5 0.9 %copy-start = (f32[1,256,256]{2,1,0:T(8,128)S(1)}, f32[1,256,256]{2,1,0:T(8,128)}, u32[]{:S(2)}) copy-start(f32[1,256,256]{2,1,0:T(8,128)} %diag_ref.1) | copy-start | bytes 786436
  17.5 1.0 %copy-start.2 = (f32[512,256]{1,0:T(8,128)S(1)}, f32[512,256]{1,0:T(8,128)}, u32[]{:S(2)}) copy-start(f32[512,256]{1,0:T(8,128)} %cross_ref.1) | copy-start | bytes 1572868
  18.5 23.4 %copy-start.3 = (bf16[512,512]{1,0:T(8,128)(2,1)S(1)}, bf16[512,512]{1,0:T(8,128)(2,1)}, u32[]{:S(2)}) copy-start(bf16[512,512]{1,0:T(8,128)(2,1)} %refs_0_.1) | copy-start | bytes 1572868
  19.7 11.2 %collective-permute-start.5 = (bf16[512,256]{1,0:T(8,128)(2,1)S(1)}, bf16[512,256]{1,0:T(8,128)(2,1)S(1)}, u32[]{:S(2)}, u32[]{:S(2)}) collective-permute-start(bf16[512,256]{1,0:T(8,128)(2,1)S(1)} %panel.1.refs_4_), channel_id=1, source_target_pairs={{12,0},{0,4},{4,8},{8,12},{13,1},{1,5},{5,9},{9,13},{14,2},{2,6},{... | collective-permute-start | bytes 786440 | tf_op jit(solution)/shard_map/ppermute | solution.py:103
  21.6 20.3 %collective-permute-start.4 = (bf16[512,256]{1,0:T(8,128)(2,1)S(1)}, bf16[512,256]{1,0:T(8,128)(2,1)S(1)}, u32[]{:S(2)}, u32[]{:S(2)}) collective-permute-start(bf16[512,256]{1,0:T(8,128)(2,1)S(1)} %panel.1.refs_4_), channel_id=1, source_target_pairs={{8,0},{12,4},{0,8},{4,12},{9,1},{13,5},{1,9},{5,13},{10,2},{14,6},... | collective-permute-start | bytes 786440 | tf_op jit(solution)/shard_map/ppermute | solution.py:103
  24.2 17.8 %collective-permute-start.3 = (bf16[512,256]{1,0:T(8,128)(2,1)S(1)}, bf16[512,256]{1,0:T(8,128)(2,1)S(1)}, u32[]{:S(2)}, u32[]{:S(2)}) collective-permute-start(bf16[512,256]{1,0:T(8,128)(2,1)S(1)} %panel.1.refs_4_), channel_id=1, source_target_pairs={{4,0},{8,4},{12,8},{0,12},{5,1},{9,5},{13,9},{1,13},{6,2},{10,6},{... | collective-permute-start | bytes 786440 | tf_op jit(solution)/shard_map/ppermute | solution.py:103
  25.5 35.2 %copy-start.1 = (f32[1,256,256]{2,1,0:T(8,128)S(1)}, f32[1,256,256]{2,1,0:T(8,128)}, u32[]{:S(2)}) copy-start(f32[1,256,256]{2,1,0:T(8,128)} %diag_ref.1) | copy-start | bytes 786436
  44.4 11.6 %collective-permute-start.8 = (bf16[256,256]{1,0:T(8,128)(2,1)S(1)}, bf16[256,256]{1,0:T(8,128)(2,1)S(1)}, u32[]{:S(2)}, u32[]{:S(2)}) collective-permute-start(bf16[256,256]{1,0:T(8,128)(2,1)S(1)} %get-tuple-element.5), channel_id=1, source_target_pairs={{12,0},{0,4},{4,8},{8,12},{13,1},{1,5},{5,9},{9,13},{14,2},{2,6},{... | collective-permute-start | bytes 393224 | tf_op jit(solution)/shard_map/ppermute | solution.py:103
  50.6 10.1 %collective-permute-start.7 = (bf16[256,256]{1,0:T(8,128)(2,1)S(1)}, bf16[256,256]{1,0:T(8,128)(2,1)S(1)}, u32[]{:S(2)}, u32[]{:S(2)}) collective-permute-start(bf16[256,256]{1,0:T(8,128)(2,1)S(1)} %get-tuple-element.5), channel_id=1, source_target_pairs={{8,0},{12,4},{0,8},{4,12},{9,1},{13,5},{1,9},{5,13},{10,2},{14,6},... | collective-permute-start | bytes 393224 | tf_op jit(solution)/shard_map/ppermute | solution.py:103
  52.2 8.5 %collective-permute-start.6 = (bf16[256,256]{1,0:T(8,128)(2,1)S(1)}, bf16[256,256]{1,0:T(8,128)(2,1)S(1)}, u32[]{:S(2)}, u32[]{:S(2)}) collective-permute-start(bf16[256,256]{1,0:T(8,128)(2,1)S(1)} %get-tuple-element.5), channel_id=1, source_target_pairs={{4,0},{8,4},{12,8},{0,12},{5,1},{9,5},{13,9},{1,13},{6,2},{10,6},{... | collective-permute-start | bytes 393224 | tf_op jit(solution)/shard_map/ppermute | solution.py:103

commit v2 on v1

v2 whole, which is shorter than its diff:
```python
import functools
import jax
import jax.numpy as jnp
from jax import lax
from jax.experimental import pallas as pl
from jax.experimental.pallas import tpu as pltpu
from jax.sharding import PartitionSpec as P

PAIR = 2
VMEM_LIMIT = 40 * 1024 * 1024
PARAMS = pltpu.CompilerParams(vmem_limit_bytes=VMEM_LIMIT)
SMEM = pl.BlockSpec(memory_space=pltpu.SMEM)
VMEM = pl.BlockSpec(memory_space=pltpu.VMEM)
ANY = pl.BlockSpec(memory_space=pl.ANY)
HBM = pl.BlockSpec(memory_space=pltpu.HBM)


def panel_kernel(pattern_ref, cross_hbm, diag_hbm, panel_ref, cross_ref, diag_ref, sems):
    width = diag_ref.shape[1]
    blocks = pattern_ref.shape[0]
    diag_copy = pltpu.make_async_copy(diag_hbm, diag_ref, sems.at[blocks])
    diag_copy.start()
    copies = []
    for a in range(blocks):
        rows = pl.ds(a * width, width)
        copies.append(pltpu.make_async_copy(cross_hbm.at[rows], cross_ref.at[rows], sems.at[a]))
        copies[a].start()
    diag_copy.wait()
    for a in range(blocks):
        copies[a].wait()
        rows = pl.ds(a * width, width)
        masked = cross_ref[rows, :] * pattern_ref[a].astype(jnp.float32)
        solved = jnp.dot(
            masked, diag_ref[0], precision=lax.Precision.HIGHEST, preferred_element_type=jnp.float32
        )
        panel_ref[rows, :] = solved.astype(jnp.bfloat16)


def build_panel(cross_blocks, diag_inverse, pattern):
    return pl.pallas_call(
        panel_kernel,
        out_shape=jax.ShapeDtypeStruct(cross_blocks.shape, jnp.bfloat16),
        in_specs=[SMEM, HBM, HBM],
        out_specs=VMEM,
        scratch_shapes=[
            pltpu.VMEM(cross_blocks.shape, jnp.float32),
            pltpu.VMEM(diag_inverse.shape, jnp.float32),
            pltpu.SemaphoreType.DMA((pattern.shape[0] + 1,)),
        ],
        compiler_params=pltpu.CompilerParams(vmem_limit_bytes=56*1024*1024),
        name="panel",
    )(pattern.reshape(-1), cross_blocks, diag_inverse)


def relay_kernel(block_ref, gate_ref, out_ref):
    del block_ref, gate_ref, out_ref


def after(block, gate):
    return pl.pallas_call(
        relay_kernel,
        out_shape=jax.ShapeDtypeStruct(block.shape, block.dtype),
        in_specs=[ANY, ANY],
        out_specs=ANY,
        input_output_aliases={0: 0},
        name="relay",
    )(block, gate)


def product_kernel(n, slots_ref, *refs):
    tops, panels = refs[:n], refs[n:2 * n]
    selected_ref, update_ref, panel_buf = refs[2 * n:]
    for s in range(n):
        panel_buf[slots_ref[s]] = panels[s][...]
    total = jnp.dot(tops[0][...], panel_buf[0], preferred_element_type=jnp.float32)
    for t in range(1, n):
        total += jnp.dot(tops[t][...], panel_buf[t], preferred_element_type=jnp.float32)
    selected_ref[...] = total
    high = total.astype(jnp.bfloat16)
    low = (total - high.astype(jnp.float32)).astype(jnp.bfloat16)
    contract = (((0,), (0,)), ((), ()))
    half = high.shape[1] // 2
    own = panels[0]
    upper = lax.dot_general(own[:, :half], high, contract, preferred_element_type=jnp.float32)
    upper += lax.dot_general(own[:, :half], low, contract, preferred_element_type=jnp.float32)
    lower = lax.dot_general(own[:, half:], high[:, half:], contract, preferred_element_type=jnp.float32)
    lower += lax.dot_general(own[:, half:], low[:, half:], contract, preferred_element_type=jnp.float32)
    update_ref[:, :2 * half] = upper.astype(jnp.bfloat16)
    update_ref[:, 2 * half:] = lower.astype(jnp.bfloat16)


def products(tops, panels, slots):
    n = len(tops)
    rows, width = panels[0].shape
    return pl.pallas_call(
        functools.partial(product_kernel, n),
        out_shape=(
            jax.ShapeDtypeStruct((rows, width), jnp.float32),
            jax.ShapeDtypeStruct((width // 2, 3 * (width // 2)), jnp.bfloat16),
        ),
        in_specs=[SMEM] + [VMEM] * (2 * n),
        out_specs=(VMEM, VMEM),
        scratch_shapes=[pltpu.VMEM((n, rows, width), jnp.bfloat16)],
        compiler_params=PARAMS,
        name="products",
    )(slots, *tops, *panels)


def finish_kernel(diag_ref, *refs):
    out_ref = refs[-1]
    total = refs[0][...].astype(jnp.float32)
    for ref in refs[1:-1]:
        total += ref[...].astype(jnp.float32)
    half = total.shape[0]
    out_ref[0, :half, :] = diag_ref[0, :half, :] + total[:, :2 * half]
    out_ref[0, half:, :half] = diag_ref[0, half:, :half] + total[:, half:2 * half].T
    out_ref[0, half:, half:] = diag_ref[0, half:, half:] + total[:, 2 * half:]


def finish(diag_inverse, updates):
    return pl.pallas_call(
        finish_kernel,
        out_shape=jax.ShapeDtypeStruct(diag_inverse.shape, jnp.float32),
        in_specs=[VMEM] * (1 + len(updates)),
        out_specs=VMEM,
        compiler_params=PARAMS,
        name="finish",
    )(diag_inverse, *updates)


def on_device(n, inverse_top, diag_inverse, cross_blocks, pattern):
    pairs = n // PAIR
    row, col = lax.axis_index("prow"), lax.axis_index("pcol")

    def from_pair(block, axis, shift, flip):
        moves = [
            (((m + shift) % pairs) * PAIR + (b ^ flip), m * PAIR + b) for m in range(pairs) for b in range(PAIR)
        ]
        return lax.ppermute(block, axis, moves)

    def mate(block, axis):
        return from_pair(block, axis, 0, 1)

    factor_panel = build_panel(cross_blocks, diag_inverse, pattern)
    crossed = [from_pair(factor_panel, "prow", d, 1) for d in range(1, pairs)]
    beside = mate(factor_panel, "prow")
    panels = [factor_panel, beside]
    for block in crossed:
        block = after(block, beside)
        panels += [mate(block, "prow"), block]

    near = [from_pair(inverse_top, "pcol", d, 0) for d in range(1, pairs)]
    tops = [inverse_top, mate(inverse_top, "pcol")]
    for block in near:
        block = after(block, panels[-1])
        tops += [block, mate(block, "pcol")]

    place = jnp.arange(n, dtype=jnp.int32)
    wanted_pair = (row // PAIR + place // PAIR) % pairs
    wanted_side = (row % PAIR) ^ (place % PAIR)
    slots = ((wanted_pair - col // PAIR) % pairs) * PAIR + (wanted_side ^ (col % PAIR))

    selected, update = products(tops, panels, slots)
    paired = (update.astype(jnp.float32) + mate(update, "prow").astype(jnp.float32)).astype(jnp.bfloat16)
    updates = [paired] + [from_pair(paired, "prow", d, 1) for d in range(1, pairs)]
    return -selected, finish(diag_inverse, updates)


def solution(mesh):
    placed = (
        P(("pole", "prow"), "pcol"),
        P(("pole", "pcol"), None, None),
        P(("pole", "prow"), "pcol"),
        P("prow", "pcol"),
    )
    return jax.shard_map(
        functools.partial(on_device, mesh.shape["pcol"]),
        mesh=mesh,
        in_specs=placed,
        out_specs=(P(("pole", "prow"), "pcol"), P(("pole", "pcol"), None, None)),
        check_vma=False,
    )
```

time: 62.2 us -> 48.4 us (0.78)
  waiting for transfers between devices: 36.2 us -> 26.9 us
  starting transfers between devices: 17.4 us -> 10.6 us
  Pallas kernels: 3.67 us -> 6.29 us
    ppermute x9 -> x8, waiting for transfers between devices: 36.2 us -> 26.9 us  [from_pair(): return lax.ppermute(block, axis, moves)]
    ppermute x9 -> x8, starting transfers between devices: 17.4 us -> 10.6 us  [from_pair(): return lax.ppermute(block, axis, moves)]
    pallas_call x1, Pallas kernels: 1.17 us -> 3.67 us  [build_panel(): pl.pallas_call(panel_kernel, out_shape=jax.ShapeDtypeStruct(cross_blocks....]
    neg x0 -> x1, other arithmetic: none -> 0.83 us  [on_device(): return (-selected, finish(diag_inverse, updates))]
    pallas_call x0 -> x3, Pallas kernels: none -> 0.81 us  [the longest x1 0.81 us: finish(): pl.pallas_call(finish_kernel, out_shape=jax.ShapeDtypeStruct(diag_inverse...]
    add x2 -> x1, other arithmetic: 0.81 us -> 0.02 us  [on_device(): (wanted_pair - col // PAIR) % pairs * PAIR + (wanted_side ^ col % PAIR)]
    pallas_call x1, Pallas kernels: 2.5 us -> 1.81 us  [products(): pl.pallas_call(functools.partial(product_kernel, n), out_shape=(jax.Shape...]
    unnamed x9 -> x18, local copies, waits for them, and re-layouts: 2.74 us -> 2.82 us
  transfers between devices with their start and end apart: 9 -> 8, of which waited for: 5 -> 5; matrix products, arithmetic and copies ran while one was open for 1% -> 2% of each run, Pallas kernels for 2% -> 8%
where the time goes in v2:
time: 48.4 us; the launch traced here: 48.2 us
  waiting for transfers between devices  26.9 us (56%)
  starting transfers between devices  10.6 us (22%)
  Pallas kernels  6.29 us (13%)
  local copies, waits for them, and re-layouts  2.82 us (6%)
  other arithmetic  0.88 us (2%)
  between operations  0.69 us (1%)
    ppermute x8, waiting for transfers between devices, from_pair(): return lax.ppermute(block, axis, moves)  26.9 us
    ppermute x8, starting transfers between devices, from_pair(): return lax.ppermute(block, axis, moves)  10.6 us
    pallas_call x1, Pallas kernels, build_panel(): pl.pallas_call(panel_kernel, out_shape=jax.ShapeDtypeStruct(cross_blocks....  3.67 us
    unnamed x18, local copies, waits for them, and re-layouts  2.82 us
    pallas_call x1, Pallas kernels, products(): pl.pallas_call(functools.partial(product_kernel, n), out_shape=(jax.Shape...  1.81 us
  transfers between devices with their start and end apart: 8, of which 5 were waited for; matrix products, arithmetic and copies ran while one was open for 2% of the time, Pallas kernels for 8%

profile of v2, /device:TPU:0, one launch (start us, length us, event | category | flops | bytes accessed | tf_op | source)
XLA Modules:
  0.0 48.2 jit_solution(17079376843924540321)
XLA Ops:
  0.6 3.0 %collective-permute-start.1 = (bf16[512,512]{1,0:T(8,128)(2,1)}, bf16[512,512]{1,0:T(8,128)(2,1)S(1)}, u32[]{:S(2)}, u32[]{:S(2)}) collective-permute-start(bf16[512,512]{1,0:T(8,128)(2,1)} %refs_0_.1), channel_id=1, source_target_pairs={{2,0},{3,1},{0,2},{1,3},{6,4},{7,5},{4,6},{5,7},{10,8},{11,9},{8,1... | collective-permute-start | bytes 1572872 | tf_op jit(solution)/shard_map/ppermute | solution.py:139
  3.6 0.0 copy-start.8
  3.6 3.7 %panel.1.refs_4_ = bf16[512,256]{1,0:T(8,128)(2,1)} custom-call(s32[2]{0:T(128)} %bitcast.1, f32[512,256]{1,0:T(8,128)} %cross_hbm.1, f32[1,256,256]{2,1,0:T(8,128)} %diag_ref.1), custom_call_target="tpu_custom_call" | custom-call | tf_op jit(solution)/shard_map/panel/pallas_call | solution.py:40
  7.3 1.6 %collective-permute-start.3 = (bf16[512,256]{1,0:T(8,128)(2,1)}, bf16[512,256]{1,0:T(8,128)(2,1)S(1)}, u32[]{:S(2)}, u32[]{:S(2)}) collective-permute-start(bf16[512,256]{1,0:T(8,128)(2,1)} %panel.1.refs_4_), channel_id=1, source_target_pairs={{4,0},{0,4},{12,8},{8,12},{5,1},{1,5},{13,9},{9,13},{6,2},{2,6},{1... | collective-permute-start | bytes 786440 | tf_op jit(solution)/shard_map/ppermute | solution.py:139
  9.0 2.5 %collective-permute-start.2 = (bf16[512,256]{1,0:T(8,128)(2,1)}, bf16[512,256]{1,0:T(8,128)(2,1)S(1)}, u32[]{:S(2)}, u32[]{:S(2)}) collective-permute-start(bf16[512,256]{1,0:T(8,128)(2,1)} %panel.1.refs_4_), channel_id=1, source_target_pairs={{12,0},{8,4},{4,8},{0,12},{13,1},{9,5},{5,9},{1,13},{14,2},{10,6},... | collective-permute-start | bytes 786440 | tf_op jit(solution)/shard_map/ppermute | solution.py:139
  11.4 0.0 copy-done.8
  11.4 0.0 collective-permute-start
  11.4 4.6 %collective-permute-done.3.gate_ref.refs_5_ = bf16[512,256]{1,0:T(8,128)(2,1)S(1)} collective-permute-done((bf16[512,256]{1,0:T(8,128)(2,1)}, bf16[512,256]{1,0:T(8,128)(2,1)S(1)}, u32[]{:S(2)}, u32[]{:S(2)}) %collective-permute-start.3) | collective-permute-done | bytes 262176 | tf_op jit(solution)/shard_map/ppermute | solution.py:139
  16.0 0.0 copy-start.5
  16.0 7.1 %collective-permute-done.2.block_ref = bf16[512,256]{1,0:T(8,128)(2,1)S(1)} collective-permute-done((bf16[512,256]{1,0:T(8,128)(2,1)}, bf16[512,256]{1,0:T(8,128)(2,1)S(1)}, u32[]{:S(2)}, u32[]{:S(2)}) %collective-permute-start.2) | collective-permute-done | bytes 262176 | tf_op jit(solution)/shard_map/ppermute | solution.py:139
  23.1 0.0 copy-done.5
  23.1 0.0 copy-start
  23.1 0.7 %copy-done = bf16[512,256]{1,0:T(8,128)(2,1)} copy-done((bf16[512,256]{1,0:T(8,128)(2,1)}, bf16[512,256]{1,0:T(8,128)(2,1)S(1)}, u32[]{:S(2)}) %copy-start) | copy-done | bytes 262168
  23.8 0.0 copy-start.1
  23.8 0.0 collective-permute-done.1.block_ref
  23.8 0.0 copy-start.2
  23.8 0.8 %copy-done.2 = bf16[512,512]{1,0:T(8,128)(2,1)} copy-done((bf16[512,512]{1,0:T(8,128)(2,1)}, bf16[512,512]{1,0:T(8,128)(2,1)S(1)}, u32[]{:S(2)}) %copy-start.2) | copy-done | bytes 524312
  24.6 0.0 copy-start.6
  24.6 0.0 copy-start.7
  24.6 0.0 collective-permute-start.4
  24.6 0.3 copy-done.1
  24.9 0.6 %collective-permute-start.5 = (bf16[512,256]{1,0:T(8,128)(2,1)S(1)}, bf16[512,256]{1,0:T(8,128)(2,1)S(1)}, u32[]{:S(2)}, u32[]{:S(2)}) collective-permute-start(bf16[512,256]{1,0:T(8,128)(2,1)S(1)} %copy-done.1), channel_id=1, source_target_pairs={{4,0},{0,4},{12,8},{8,12},{5,1},{1,5},{13,9},{9,13},{6,2},{2,6},{1... | collective-permute-start | bytes 786440 | tf_op jit(solution)/shard_map/ppermute | solution.py:139
  25.5 7.8 %collective-permute-done.5.refs_6_ = bf16[512,256]{1,0:T(8,128)(2,1)S(1)} collective-permute-done((bf16[512,256]{1,0:T(8,128)(2,1)S(1)}, bf16[512,256]{1,0:T(8,128)(2,1)S(1)}, u32[]{:S(2)}, u32[]{:S(2)}) %collective-permute-start.5) | collective-permute-done | bytes 262176 | tf_op jit(solution)/shard_map/ppermute | solution.py:139
  33.3 0.0 collective-permute-done.refs_1_
  33.3 0.0 collective-permute-done.4.refs_3_
  33.3 0.0 copy-done.6
  33.3 0.0 copy-done.7
  33.4 0.0 copy-start.3
  33.4 1.0 %copy-done.3 = bf16[512,512]{1,0:T(8,128)(2,1)S(1)} copy-done((bf16[512,512]{1,0:T(8,128)(2,1)S(1)}, bf16[512,512]{1,0:T(8,128)(2,1)}, u32[]{:S(2)}) %copy-start.3) | copy-done | bytes 524312
  34.4 1.8 %products.1 = (f32[512,256]{1,0:T(8,128)S(1)}, bf16[128,384]{1,0:T(8,128)(2,1)S(1)}) custom-call(s32[4]{0:T(128)S(1)} %fusion.2.slots_ref, bf16[512,512]{1,0:T(8,128)(2,1)S(1)} %copy-done.8, bf16[512,512]{1,0:T(8,128)(2,1)S(1)} %collective-permute-done.refs_1_, bf16[512,512]{1,0:T(8,128)(2,1)S(1)} %copy-done.3, ...), custom_call_target="tpu_custom_call" | custom-call | tf_op jit(solution)/shard_map/products/pallas_call | solution.py:95
  36.2 0.7 %collective-permute-start.6 = (bf16[128,384]{1,0:T(8,128)(2,1)S(1)}, bf16[128,384]{1,0:T(8,128)(2,1)S(1)}, u32[]{:S(2)}, u32[]{:S(2)}) collective-permute-start(bf16[128,384]{1,0:T(8,128)(2,1)S(1)} %get-tuple-element.5), channel_id=1, source_target_pairs={{4,0},{0,4},{12,8},{8,12},{5,1},{1,5},{13,9},{9,13},{6,2},{2,6},{1... | collective-permute-start | bytes 294920 | tf_op jit(solution)/shard_map/ppermute | solution.py:139
  36.9 4.0 %collective-permute-done.6 = bf16[128,384]{1,0:T(8,128)(2,1)S(1)} collective-permute-done((bf16[128,384]{1,0:T(8,128)(2,1)S(1)}, bf16[128,384]{1,0:T(8,128)(2,1)S(1)}, u32[]{:S(2)}, u32[]{:S(2)}) %collective-permute-start.6) | collective-permute-done | bytes 98336 | tf_op jit(solution)/shard_map/ppermute | solution.py:139
  40.9 2.2 %collective-permute-start.7 = (bf16[128,384]{1,0:T(8,128)(2,1)S(1)}, bf16[128,384]{1,0:T(8,128)(2,1)S(1)}, u32[]{:S(2)}, u32[]{:S(2)}) collective-permute-start(bf16[128,384]{1,0:T(8,128)(2,1)S(1)} %add_convert_fusion.refs_0_), channel_id=1, source_target_pairs={{12,0},{8,4},{4,8},{0,12},{13,1},{9,5},{5,9},{1,13},{14,2},{10,6},... | collective-permute-start | bytes 294920 | tf_op jit(solution)/shard_map/ppermute | solution.py:139
  43.2 0.0 copy-start.4
  43.2 0.8 %neg.3 = f32[512,256]{1,0:T(8,128)} negate(f32[512,256]{1,0:T(8,128)S(1)} %get-tuple-element.4) | non-fusion elementwise | flops 131072 | bytes 1048576 | tf_op jit(solution)/shard_map/neg | solution.py:166
  44.0 3.4 %collective-permute-done.7.refs_1_ = bf16[128,384]{1,0:T(8,128)(2,1)S(1)} collective-permute-done((bf16[128,384]{1,0:T(8,128)(2,1)S(1)}, bf16[128,384]{1,0:T(8,128)(2,1)S(1)}, u32[]{:S(2)}, u32[]{:S(2)}) %collective-permute-start.7) | collective-permute-done | bytes 98336 | tf_op jit(solution)/shard_map/ppermute | solution.py:139
  47.4 0.0 copy-done.4
  47.4 0.8 %finish.1 = f32[1,256,256]{2,1,0:T(8,128)} custom-call(f32[1,256,256]{2,1,0:T(8,128)S(1)} %copy-done.4, bf16[128,384]{1,0:T(8,128)(2,1)S(1)} %add_convert_fusion.refs_0_, bf16[128,384]{1,0:T(8,128)(2,1)S(1)} %collective-permute-done.7.refs_1_), custom_call_target="tpu_custom_call" | custom-call | tf_op jit(solution)/shard_map/finish/pallas_call | solution.py:121
  (4 shorter events, 0.0 us)
Async XLA Ops:
  0.6 23.2 %collective-permute-start.1 = (bf16[512,512]{1,0:T(8,128)(2,1)}, bf16[512,512]{1,0:T(8,128)(2,1)S(1)}, u32[]{:S(2)}, u32[]{:S(2)}) collective-permute-start(bf16[512,512]{1,0:T(8,128)(2,1)} %refs_0_.1), channel_id=1, source_target_pairs={{2,0},{3,1},{0,2},{1,3},{6,4},{7,5},{4,6},{5,7},{10,8},{11,9},{8,1... | collective-permute-start | bytes 1572872 | tf_op jit(solution)/shard_map/ppermute | solution.py:139
  3.6 7.8 %copy-start.8 = (bf16[512,512]{1,0:T(8,128)(2,1)S(1)}, bf16[512,512]{1,0:T(8,128)(2,1)}, u32[]{:S(2)}) copy-start(bf16[512,512]{1,0:T(8,128)(2,1)} %refs_0_.1) | copy-start | bytes 1572868
  7.3 8.7 %collective-permute-start.3 = (bf16[512,256]{1,0:T(8,128)(2,1)}, bf16[512,256]{1,0:T(8,128)(2,1)S(1)}, u32[]{:S(2)}, u32[]{:S(2)}) collective-permute-start(bf16[512,256]{1,0:T(8,128)(2,1)} %panel.1.refs_4_), channel_id=1, source_target_pairs={{4,0},{0,4},{12,8},{8,12},{5,1},{1,5},{13,9},{9,13},{6,2},{2,6},{1... | collective-permute-start | bytes 786440 | tf_op jit(solution)/shard_map/ppermute | solution.py:139
  9.0 14.1 %collective-permute-start.2 = (bf16[512,256]{1,0:T(8,128)(2,1)}, bf16[512,256]{1,0:T(8,128)(2,1)S(1)}, u32[]{:S(2)}, u32[]{:S(2)}) collective-permute-start(bf16[512,256]{1,0:T(8,128)(2,1)} %panel.1.refs_4_), channel_id=1, source_target_pairs={{12,0},{8,4},{4,8},{0,12},{13,1},{9,5},{5,9},{1,13},{14,2},{10,6},... | collective-permute-start | bytes 786440 | tf_op jit(solution)/shard_map/ppermute | solution.py:139
  11.4 21.9 %collective-permute-start = (bf16[512,512]{1,0:T(8,128)(2,1)S(1)}, bf16[512,512]{1,0:T(8,128)(2,1)S(1)}, u32[]{:S(2)}, u32[]{:S(2)}) collective-permute-start(bf16[512,512]{1,0:T(8,128)(2,1)S(1)} %copy-done.8), channel_id=1, source_target_pairs={{1,0},{0,1},{3,2},{2,3},{5,4},{4,5},{7,6},{6,7},{9,8},{8,9},{11,10... | collective-permute-start | bytes 1572872 | tf_op jit(solution)/shard_map/ppermute | solution.py:139
  16.0 7.1 %copy-start.5 = (bf16[512,256]{1,0:T(8,128)(2,1)}, bf16[512,256]{1,0:T(8,128)(2,1)S(1)}, u32[]{:S(2)}) copy-start(bf16[512,256]{1,0:T(8,128)(2,1)S(1)} %collective-permute-done.3.gate_ref.refs_5_) | copy-start | bytes 786436
  23.1 0.7 %copy-start = (bf16[512,256]{1,0:T(8,128)(2,1)}, bf16[512,256]{1,0:T(8,128)(2,1)S(1)}, u32[]{:S(2)}) copy-start(bf16[512,256]{1,0:T(8,128)(2,1)S(1)} %collective-permute-done.2.block_ref) | copy-start | bytes 786436
  23.8 1.1 %copy-start.1 = (bf16[512,256]{1,0:T(8,128)(2,1)S(1)}, bf16[512,256]{1,0:T(8,128)(2,1)}, u32[]{:S(2)}) copy-start(bf16[512,256]{1,0:T(8,128)(2,1)} %relay.2.gate_ref.refs_7_) | copy-start | bytes 786436
  23.8 0.8 %copy-start.2 = (bf16[512,512]{1,0:T(8,128)(2,1)}, bf16[512,512]{1,0:T(8,128)(2,1)S(1)}, u32[]{:S(2)}) copy-start(bf16[512,512]{1,0:T(8,128)(2,1)S(1)} %collective-permute-done.1.block_ref) | copy-start | bytes 1572868
  24.6 8.7 %copy-start.6 = (bf16[512,256]{1,0:T(8,128)(2,1)S(1)}, bf16[512,256]{1,0:T(8,128)(2,1)}, u32[]{:S(2)}) copy-start(bf16[512,256]{1,0:T(8,128)(2,1)} %copy-done.5) | copy-start | bytes 786436
  24.6 8.7 %copy-start.7 = (bf16[512,256]{1,0:T(8,128)(2,1)S(1)}, bf16[512,256]{1,0:T(8,128)(2,1)}, u32[]{:S(2)}) copy-start(bf16[512,256]{1,0:T(8,128)(2,1)} %panel.1.refs_4_) | copy-start | bytes 786436
  24.6 8.7 %collective-permute-start.4 = (bf16[512,512]{1,0:T(8,128)(2,1)}, bf16[512,512]{1,0:T(8,128)(2,1)S(1)}, u32[]{:S(2)}, u32[]{:S(2)}) collective-permute-start(bf16[512,512]{1,0:T(8,128)(2,1)} %relay.3.refs_2_), channel_id=1, source_target_pairs={{1,0},{0,1},{3,2},{2,3},{5,4},{4,5},{7,6},{6,7},{9,8},{8,9},{11,10... | collective-permute-start | bytes 1572872 | tf_op jit(solution)/shard_map/ppermute | solution.py:139
  24.9 8.4 %collective-permute-start.5 = (bf16[512,256]{1,0:T(8,128)(2,1)S(1)}, bf16[512,256]{1,0:T(8,128)(2,1)S(1)}, u32[]{:S(2)}, u32[]{:S(2)}) collective-permute-start(bf16[512,256]{1,0:T(8,128)(2,1)S(1)} %copy-done.1), channel_id=1, source_target_pairs={{4,0},{0,4},{12,8},{8,12},{5,1},{1,5},{13,9},{9,13},{6,2},{2,6},{1... | collective-permute-start | bytes 786440 | tf_op jit(solution)/shard_map/ppermute | solution.py:139
  33.4 1.0 %copy-start.3 = (bf16[512,512]{1,0:T(8,128)(2,1)S(1)}, bf16[512,512]{1,0:T(8,128)(2,1)}, u32[]{:S(2)}) copy-start(bf16[512,512]{1,0:T(8,128)(2,1)} %relay.3.refs_2_) | copy-start | bytes 1572868
  36.2 4.7 %collective-permute-start.6 = (bf16[128,384]{1,0:T(8,128)(2,1)S(1)}, bf16[128,384]{1,0:T(8,128)(2,1)S(1)}, u32[]{:S(2)}, u32[]{:S(2)}) collective-permute-start(bf16[128,384]{1,0:T(8,128)(2,1)S(1)} %get-tuple-element.5), channel_id=1, source_target_pairs={{4,0},{0,4},{12,8},{8,12},{5,1},{1,5},{13,9},{9,13},{6,2},{2,6},{1... | collective-permute-start | bytes 294920 | tf_op jit(solution)/shard_map/ppermute | solution.py:139
  40.9 6.5 %collective-permute-start.7 = (bf16[128,384]{1,0:T(8,128)(2,1)S(1)}, bf16[128,384]{1,0:T(8,128)(2,1)S(1)}, u32[]{:S(2)}, u32[]{:S(2)}) collective-permute-start(bf16[128,384]{1,0:T(8,128)(2,1)S(1)} %add_convert_fusion.refs_0_), channel_id=1, source_target_pairs={{12,0},{8,4},{4,8},{0,12},{13,1},{9,5},{5,9},{1,13},{14,2},{10,6},... | collective-permute-start | bytes 294920 | tf_op jit(solution)/shard_map/ppermute | solution.py:139
  43.2 4.3 %copy-start.4 = (f32[1,256,256]{2,1,0:T(8,128)S(1)}, f32[1,256,256]{2,1,0:T(8,128)}, u32[]{:S(2)}) copy-start(f32[1,256,256]{2,1,0:T(8,128)} %diag_ref.1) | copy-start | bytes 786436

commit v3 on v2

--- a/solution.py
+++ b/solution.py
@@ -9,31 +9,35 @@
 PAIR = 2
 VMEM_LIMIT = 40 * 1024 * 1024
 PARAMS = pltpu.CompilerParams(vmem_limit_bytes=VMEM_LIMIT)
+WHOLE = pltpu.CompilerParams(vmem_limit_bytes=56 * 1024 * 1024)
+SMALL = pltpu.CompilerParams(vmem_limit_bytes=1024 * 1024)
 SMEM = pl.BlockSpec(memory_space=pltpu.SMEM)
 VMEM = pl.BlockSpec(memory_space=pltpu.VMEM)
 ANY = pl.BlockSpec(memory_space=pl.ANY)
 HBM = pl.BlockSpec(memory_space=pltpu.HBM)
 
 
-def panel_kernel(pattern_ref, cross_hbm, diag_hbm, panel_ref, cross_ref, diag_ref, sems):
+def panel_kernel(pattern_ref, cross_hbm, diag_hbm, panel_hbm, cross_ref, diag_ref, panel_ref, in_sems, out_sems):
     width = diag_ref.shape[1]
     blocks = pattern_ref.shape[0]
-    diag_copy = pltpu.make_async_copy(diag_hbm, diag_ref, sems.at[blocks])
+    rows = [pl.ds(a * width, width) for a in range(blocks)]
+    diag_copy = pltpu.make_async_copy(diag_hbm, diag_ref, in_sems.at[blocks])
     diag_copy.start()
-    copies = []
-    for a in range(blocks):
-        rows = pl.ds(a * width, width)
-        copies.append(pltpu.make_async_copy(cross_hbm.at[rows], cross_ref.at[rows], sems.at[a]))
-        copies[a].start()
+    loads = [pltpu.make_async_copy(cross_hbm.at[r], cross_ref.at[r], in_sems.at[a]) for a, r in enumerate(rows)]
+    stores = [pltpu.make_async_copy(panel_ref.at[r], panel_hbm.at[r], out_sems.at[a]) for a, r in enumerate(rows)]
+    for load in loads:
+        load.start()
     diag_copy.wait()
     for a in range(blocks):
-        copies[a].wait()
-        rows = pl.ds(a * width, width)
-        masked = cross_ref[rows, :] * pattern_ref[a].astype(jnp.float32)
+        loads[a].wait()
+        masked = cross_ref[rows[a], :] * pattern_ref[a].astype(jnp.float32)
         solved = jnp.dot(
             masked, diag_ref[0], precision=lax.Precision.HIGHEST, preferred_element_type=jnp.float32
         )
-        panel_ref[rows, :] = solved.astype(jnp.bfloat16)
+        panel_ref[rows[a], :] = solved.astype(jnp.bfloat16)
+        stores[a].start()
+    for store in stores:
+        store.wait()
 
 
 def build_panel(cross_blocks, diag_inverse, pattern):
@@ -41,13 +45,15 @@
         panel_kernel,
         out_shape=jax.ShapeDtypeStruct(cross_blocks.shape, jnp.bfloat16),
         in_specs=[SMEM, HBM, HBM],
-        out_specs=VMEM,
+        out_specs=HBM,
         scratch_shapes=[
             pltpu.VMEM(cross_blocks.shape, jnp.float32),
             pltpu.VMEM(diag_inverse.shape, jnp.float32),
+            pltpu.VMEM(cross_blocks.shape, jnp.bfloat16),
             pltpu.SemaphoreType.DMA((pattern.shape[0] + 1,)),
+            pltpu.SemaphoreType.DMA((pattern.shape[0],)),
         ],
-        compiler_params=pltpu.CompilerParams(vmem_limit_bytes=56*1024*1024),
+        compiler_params=WHOLE,
         name="panel",
     )(pattern.reshape(-1), cross_blocks, diag_inverse)
 
@@ -63,6 +69,7 @@
         in_specs=[ANY, ANY],
         out_specs=ANY,
         input_output_aliases={0: 0},
+        compiler_params=SMALL,
         name="relay",
     )(block, gate)
 
@@ -152,7 +159,7 @@
     near = [from_pair(inverse_top, "pcol", d, 0) for d in range(1, pairs)]
     tops = [inverse_top, mate(inverse_top, "pcol")]
     for block in near:
-        block = after(block, panels[-1])
+        block = after(block, beside)
         tops += [block, mate(block, "pcol")]
 
     place = jnp.arange(n, dtype=jnp.int32)

time: 48.4 us -> 43.9 us (0.907)
  local copies, waits for them, and re-layouts: 2.82 us -> 0.01 us
  waiting for transfers between devices: 26.9 us -> 24.3 us
  starting transfers between devices: 10.6 us -> 11.6 us
    unnamed x18 -> x6, local copies, waits for them, and re-layouts: 2.82 us -> 0.01 us
    ppermute x8, waiting for transfers between devices: 26.9 us -> 24.3 us  [from_pair(): return lax.ppermute(block, axis, moves)]
    ppermute x8, starting transfers between devices: 10.6 us -> 11.6 us  [from_pair(): return lax.ppermute(block, axis, moves)]
where the time goes in v3:
time: 43.9 us; the launch traced here: 43.7 us
  waiting for transfers between devices  24.3 us (55%)
  starting transfers between devices  11.6 us (26%)
  Pallas kernels  6.27 us (14%)
  other arithmetic  0.88 us (2%)
  between operations  0.67 us (2%)
    ppermute x8, waiting for transfers between devices, from_pair(): return lax.ppermute(block, axis, moves)  24.3 us
    ppermute x8, starting transfers between devices, from_pair(): return lax.ppermute(block, axis, moves)  11.6 us
    pallas_call x1, Pallas kernels, build_panel(): pl.pallas_call(panel_kernel, out_shape=jax.ShapeDtypeStruct(cross_blocks....  3.64 us
    pallas_call x1, Pallas kernels, products(): pl.pallas_call(functools.partial(product_kernel, n), out_shape=(jax.Shape...  1.82 us
  transfers between devices with their start and end apart: 8, of which 5 were waited for; matrix products, arithmetic and copies ran while one was open for 2% of the time, Pallas kernels for 8%

profile of v3, /device:TPU:0, one launch (start us, length us, event | category | flops | bytes accessed | tf_op | source)
XLA Modules:
  0.0 43.7 jit_solution(16290784321414851857)
XLA Ops:
  0.6 3.0 %collective-permute-start.1 = (bf16[512,512]{1,0:T(8,128)(2,1)}, bf16[512,512]{1,0:T(8,128)(2,1)S(1)}, u32[]{:S(2)}, u32[]{:S(2)}) collective-permute-start(bf16[512,512]{1,0:T(8,128)(2,1)} %refs_0_.1), channel_id=1, source_target_pairs={{2,0},{3,1},{0,2},{1,3},{6,4},{7,5},{4,6},{5,7},{10,8},{11,9},{8,1... | collective-permute-start | bytes 1572872 | tf_op jit(solution)/shard_map/ppermute | solution.py:146
  3.6 0.0 copy-start.2
  3.6 3.6 %panel.1.refs_4_ = bf16[512,256]{1,0:T(8,128)(2,1)} custom-call(s32[2]{0:T(128)} %bitcast.1, f32[512,256]{1,0:T(8,128)} %cross_hbm.1, f32[1,256,256]{2,1,0:T(8,128)} %diag_ref.1), custom_call_target="tpu_custom_call" | custom-call | tf_op jit(solution)/shard_map/panel/pallas_call | solution.py:44
  7.3 1.6 %collective-permute-start.2 = (bf16[512,256]{1,0:T(8,128)(2,1)}, bf16[512,256]{1,0:T(8,128)(2,1)S(1)}, u32[]{:S(2)}, u32[]{:S(2)}) collective-permute-start(bf16[512,256]{1,0:T(8,128)(2,1)} %panel.1.refs_4_), channel_id=1, source_target_pairs={{4,0},{0,4},{12,8},{8,12},{5,1},{1,5},{13,9},{9,13},{6,2},{2,6},{1... | collective-permute-start | bytes 786440 | tf_op jit(solution)/shard_map/ppermute | solution.py:146
  8.9 2.5 %collective-permute-start.4 = (bf16[512,256]{1,0:T(8,128)(2,1)}, bf16[512,256]{1,0:T(8,128)(2,1)S(1)}, u32[]{:S(2)}, u32[]{:S(2)}) collective-permute-start(bf16[512,256]{1,0:T(8,128)(2,1)} %panel.1.refs_4_), channel_id=1, source_target_pairs={{12,0},{8,4},{4,8},{0,12},{13,1},{9,5},{5,9},{1,13},{14,2},{10,6},... | collective-permute-start | bytes 786440 | tf_op jit(solution)/shard_map/ppermute | solution.py:146
  11.4 0.0 copy-done.2
  11.4 0.0 collective-permute-start
  11.4 4.6 %collective-permute-done.2.gate_ref.refs_5_ = bf16[512,256]{1,0:T(8,128)(2,1)S(1)} collective-permute-done((bf16[512,256]{1,0:T(8,128)(2,1)}, bf16[512,256]{1,0:T(8,128)(2,1)S(1)}, u32[]{:S(2)}, u32[]{:S(2)}) %collective-permute-start.2) | collective-permute-done | bytes 262176 | tf_op jit(solution)/shard_map/ppermute | solution.py:146
  16.0 0.0 collective-permute-done.1.block_ref
  16.0 0.0 copy-start.1
  16.0 0.0 collective-permute-start.3
  16.0 7.1 %collective-permute-done.4.block_ref = bf16[512,256]{1,0:T(8,128)(2,1)S(1)} collective-permute-done((bf16[512,256]{1,0:T(8,128)(2,1)}, bf16[512,256]{1,0:T(8,128)(2,1)S(1)}, u32[]{:S(2)}, u32[]{:S(2)}) %collective-permute-start.4) | collective-permute-done | bytes 262176 | tf_op jit(solution)/shard_map/ppermute | solution.py:146
  23.1 0.6 %collective-permute-start.5 = (bf16[512,256]{1,0:T(8,128)(2,1)S(1)}, bf16[512,256]{1,0:T(8,128)(2,1)S(1)}, u32[]{:S(2)}, u32[]{:S(2)}) collective-permute-start(bf16[512,256]{1,0:T(8,128)(2,1)S(1)} %relay.3.refs_7_), channel_id=1, source_target_pairs={{4,0},{0,4},{12,8},{8,12},{5,1},{1,5},{13,9},{9,13},{6,2},{2,6},{1... | collective-permute-start | bytes 786440 | tf_op jit(solution)/shard_map/ppermute | solution.py:146
  23.7 6.2 %collective-permute-done.5.refs_6_ = bf16[512,256]{1,0:T(8,128)(2,1)S(1)} collective-permute-done((bf16[512,256]{1,0:T(8,128)(2,1)S(1)}, bf16[512,256]{1,0:T(8,128)(2,1)S(1)}, u32[]{:S(2)}, u32[]{:S(2)}) %collective-permute-start.5) | collective-permute-done | bytes 262176 | tf_op jit(solution)/shard_map/ppermute | solution.py:146
  29.9 0.0 collective-permute-done.refs_1_
  29.9 0.0 collective-permute-done.3.refs_3_
  29.9 0.0 copy-done.1
  29.9 1.8 %products.1 = (f32[512,256]{1,0:T(8,128)S(1)}, bf16[128,384]{1,0:T(8,128)(2,1)S(1)}) custom-call(s32[4]{0:T(128)S(1)} %fusion.2.slots_ref, bf16[512,512]{1,0:T(8,128)(2,1)S(1)} %copy-done.2, bf16[512,512]{1,0:T(8,128)(2,1)S(1)} %collective-permute-done.refs_1_, bf16[512,512]{1,0:T(8,128)(2,1)S(1)} %relay.2.refs_2_, ...), custom_call_target="tpu_custom_call" | custom-call | tf_op jit(solution)/shard_map/products/pallas_call | solution.py:102
  31.7 0.3 collective-permute-start.6
  32.1 4.3 %collective-permute-done.6 = bf16[128,384]{1,0:T(8,128)(2,1)S(1)} collective-permute-done((bf16[128,384]{1,0:T(8,128)(2,1)S(1)}, bf16[128,384]{1,0:T(8,128)(2,1)S(1)}, u32[]{:S(2)}, u32[]{:S(2)}) %collective-permute-start.6) | collective-permute-done | bytes 98336 | tf_op jit(solution)/shard_map/ppermute | solution.py:146
  36.4 3.5 %collective-permute-start.7 = (bf16[128,384]{1,0:T(8,128)(2,1)S(1)}, bf16[128,384]{1,0:T(8,128)(2,1)S(1)}, u32[]{:S(2)}, u32[]{:S(2)}) collective-permute-start(bf16[128,384]{1,0:T(8,128)(2,1)S(1)} %add_convert_fusion.refs_0_), channel_id=1, source_target_pairs={{12,0},{8,4},{4,8},{0,12},{13,1},{9,5},{5,9},{1,13},{14,2},{10,6},... | collective-permute-start | bytes 294920 | tf_op jit(solution)/shard_map/ppermute | solution.py:146
  39.9 0.0 copy-start
  39.9 0.8 %neg.3 = f32[512,256]{1,0:T(8,128)} negate(f32[512,256]{1,0:T(8,128)S(1)} %get-tuple-element.4) | non-fusion elementwise | flops 131072 | bytes 1048576 | tf_op jit(solution)/shard_map/neg | solution.py:173
  40.7 2.2 %collective-permute-done.7.refs_1_ = bf16[128,384]{1,0:T(8,128)(2,1)S(1)} collective-permute-done((bf16[128,384]{1,0:T(8,128)(2,1)S(1)}, bf16[128,384]{1,0:T(8,128)(2,1)S(1)}, u32[]{:S(2)}, u32[]{:S(2)}) %collective-permute-start.7) | collective-permute-done | bytes 98336 | tf_op jit(solution)/shard_map/ppermute | solution.py:146
  42.9 0.0 copy-done
  42.9 0.8 %finish.1 = f32[1,256,256]{2,1,0:T(8,128)} custom-call(f32[1,256,256]{2,1,0:T(8,128)S(1)} %copy-done, bf16[128,384]{1,0:T(8,128)(2,1)S(1)} %add_convert_fusion.refs_0_, bf16[128,384]{1,0:T(8,128)(2,1)S(1)} %collective-permute-done.7.refs_1_), custom_call_target="tpu_custom_call" | custom-call | tf_op jit(solution)/shard_map/finish/pallas_call | solution.py:128
  (4 shorter events, 0.0 us)
Async XLA Ops:
  0.6 15.4 %collective-permute-start.1 = (bf16[512,512]{1,0:T(8,128)(2,1)}, bf16[512,512]{1,0:T(8,128)(2,1)S(1)}, u32[]{:S(2)}, u32[]{:S(2)}) collective-permute-start(bf16[512,512]{1,0:T(8,128)(2,1)} %refs_0_.1), channel_id=1, source_target_pairs={{2,0},{3,1},{0,2},{1,3},{6,4},{7,5},{4,6},{5,7},{10,8},{11,9},{8,1... | collective-permute-start | bytes 1572872 | tf_op jit(solution)/shard_map/ppermute | solution.py:146
  3.6 7.8 %copy-start.2 = (bf16[512,512]{1,0:T(8,128)(2,1)S(1)}, bf16[512,512]{1,0:T(8,128)(2,1)}, u32[]{:S(2)}) copy-start(bf16[512,512]{1,0:T(8,128)(2,1)} %refs_0_.1) | copy-start | bytes 1572868
  7.3 8.7 %collective-permute-start.2 = (bf16[512,256]{1,0:T(8,128)(2,1)}, bf16[512,256]{1,0:T(8,128)(2,1)S(1)}, u32[]{:S(2)}, u32[]{:S(2)}) collective-permute-start(bf16[512,256]{1,0:T(8,128)(2,1)} %panel.1.refs_4_), channel_id=1, source_target_pairs={{4,0},{0,4},{12,8},{8,12},{5,1},{1,5},{13,9},{9,13},{6,2},{2,6},{1... | collective-permute-start | bytes 786440 | tf_op jit(solution)/shard_map/ppermute | solution.py:146
  8.9 14.1 %collective-permute-start.4 = (bf16[512,256]{1,0:T(8,128)(2,1)}, bf16[512,256]{1,0:T(8,128)(2,1)S(1)}, u32[]{:S(2)}, u32[]{:S(2)}) collective-permute-start(bf16[512,256]{1,0:T(8,128)(2,1)} %panel.1.refs_4_), channel_id=1, source_target_pairs={{12,0},{8,4},{4,8},{0,12},{13,1},{9,5},{5,9},{1,13},{14,2},{10,6},... | collective-permute-start | bytes 786440 | tf_op jit(solution)/shard_map/ppermute | solution.py:146
  11.4 18.5 %collective-permute-start = (bf16[512,512]{1,0:T(8,128)(2,1)S(1)}, bf16[512,512]{1,0:T(8,128)(2,1)S(1)}, u32[]{:S(2)}, u32[]{:S(2)}) collective-permute-start(bf16[512,512]{1,0:T(8,128)(2,1)S(1)} %copy-done.2), channel_id=1, source_target_pairs={{1,0},{0,1},{3,2},{2,3},{5,4},{4,5},{7,6},{6,7},{9,8},{8,9},{11,10... | collective-permute-start | bytes 1572872 | tf_op jit(solution)/shard_map/ppermute | solution.py:146
  16.0 13.9 %copy-start.1 = (bf16[512,256]{1,0:T(8,128)(2,1)S(1)}, bf16[512,256]{1,0:T(8,128)(2,1)}, u32[]{:S(2)}) copy-start(bf16[512,256]{1,0:T(8,128)(2,1)} %panel.1.refs_4_) | copy-start | bytes 786436
  16.0 13.9 %collective-permute-start.3 = (bf16[512,512]{1,0:T(8,128)(2,1)S(1)}, bf16[512,512]{1,0:T(8,128)(2,1)S(1)}, u32[]{:S(2)}, u32[]{:S(2)}) collective-permute-start(bf16[512,512]{1,0:T(8,128)(2,1)S(1)} %relay.2.refs_2_), channel_id=1, source_target_pairs={{1,0},{0,1},{3,2},{2,3},{5,4},{4,5},{7,6},{6,7},{9,8},{8,9},{11,10... | collective-permute-start | bytes 1572872 | tf_op jit(solution)/shard_map/ppermute | solution.py:146
  23.1 6.8 %collective-permute-start.5 = (bf16[512,256]{1,0:T(8,128)(2,1)S(1)}, bf16[512,256]{1,0:T(8,128)(2,1)S(1)}, u32[]{:S(2)}, u32[]{:S(2)}) collective-permute-start(bf16[512,256]{1,0:T(8,128)(2,1)S(1)} %relay.3.refs_7_), channel_id=1, source_target_pairs={{4,0},{0,4},{12,8},{8,12},{5,1},{1,5},{13,9},{9,13},{6,2},{2,6},{1... | collective-permute-start | bytes 786440 | tf_op jit(solution)/shard_map/ppermute | solution.py:146
  31.7 4.7 %collective-permute-start.6 = (bf16[128,384]{1,0:T(8,128)(2,1)S(1)}, bf16[128,384]{1,0:T(8,128)(2,1)S(1)}, u32[]{:S(2)}, u32[]{:S(2)}) collective-permute-start(bf16[128,384]{1,0:T(8,128)(2,1)S(1)} %get-tuple-element.5), channel_id=1, source_target_pairs={{4,0},{0,4},{12,8},{8,12},{5,1},{1,5},{13,9},{9,13},{6,2},{2,6},{1... | collective-permute-start | bytes 294920 | tf_op jit(solution)/shard_map/ppermute | solution.py:146
  36.4 6.5 %collective-permute-start.7 = (bf16[128,384]{1,0:T(8,128)(2,1)S(1)}, bf16[128,384]{1,0:T(8,128)(2,1)S(1)}, u32[]{:S(2)}, u32[]{:S(2)}) collective-permute-start(bf16[128,384]{1,0:T(8,128)(2,1)S(1)} %add_convert_fusion.refs_0_), channel_id=1, source_target_pairs={{12,0},{8,4},{4,8},{0,12},{13,1},{9,5},{5,9},{1,13},{14,2},{10,6},... | collective-permute-start | bytes 294920 | tf_op jit(solution)/shard_map/ppermute | solution.py:146
  39.9 3.0 %copy-start = (f32[1,256,256]{2,1,0:T(8,128)S(1)}, f32[1,256,256]{2,1,0:T(8,128)}, u32[]{:S(2)}) copy-start(f32[1,256,256]{2,1,0:T(8,128)} %diag_ref.1) | copy-start | bytes 786436

commit v4 on v3

--- a/solution.py
+++ b/solution.py
@@ -9,7 +9,6 @@
 PAIR = 2
 VMEM_LIMIT = 40 * 1024 * 1024
 PARAMS = pltpu.CompilerParams(vmem_limit_bytes=VMEM_LIMIT)
-WHOLE = pltpu.CompilerParams(vmem_limit_bytes=56 * 1024 * 1024)
 SMALL = pltpu.CompilerParams(vmem_limit_bytes=1024 * 1024)
 SMEM = pl.BlockSpec(memory_space=pltpu.SMEM)
 VMEM = pl.BlockSpec(memory_space=pltpu.VMEM)
@@ -17,16 +16,17 @@
 HBM = pl.BlockSpec(memory_space=pltpu.HBM)
 
 
-def panel_kernel(pattern_ref, cross_hbm, diag_hbm, panel_hbm, cross_ref, diag_ref, panel_ref, in_sems, out_sems):
+def panel_kernel(pattern_hbm, cross_hbm, diag_hbm, top_hbm, panel_ref, top_ref, pattern_ref, cross_ref, diag_ref, sems):
     width = diag_ref.shape[1]
-    blocks = pattern_ref.shape[0]
+    blocks = pattern_hbm.shape[0]
     rows = [pl.ds(a * width, width) for a in range(blocks)]
-    diag_copy = pltpu.make_async_copy(diag_hbm, diag_ref, in_sems.at[blocks])
-    diag_copy.start()
-    loads = [pltpu.make_async_copy(cross_hbm.at[r], cross_ref.at[r], in_sems.at[a]) for a, r in enumerate(rows)]
-    stores = [pltpu.make_async_copy(panel_ref.at[r], panel_hbm.at[r], out_sems.at[a]) for a, r in enumerate(rows)]
-    for load in loads:
-        load.start()
+    loads = [pltpu.make_async_copy(cross_hbm.at[r], cross_ref.at[r], sems.at[a]) for a, r in enumerate(rows)]
+    diag_copy = pltpu.make_async_copy(diag_hbm, diag_ref, sems.at[blocks])
+    pattern_copy = pltpu.make_async_copy(pattern_hbm, pattern_ref, sems.at[blocks + 1])
+    top_copy = pltpu.make_async_copy(top_hbm, top_ref, sems.at[blocks + 2])
+    for copy in [pattern_copy, diag_copy] + loads + [top_copy]:
+        copy.start()
+    pattern_copy.wait()
     diag_copy.wait()
     for a in range(blocks):
         loads[a].wait()
@@ -35,27 +35,28 @@
             masked, diag_ref[0], precision=lax.Precision.HIGHEST, preferred_element_type=jnp.float32
         )
         panel_ref[rows[a], :] = solved.astype(jnp.bfloat16)
-        stores[a].start()
-    for store in stores:
-        store.wait()
+    top_copy.wait()
 
 
-def build_panel(cross_blocks, diag_inverse, pattern):
+def build_panel(cross_blocks, diag_inverse, pattern, inverse_top):
+    inputs = [pattern.reshape(-1), cross_blocks, diag_inverse, inverse_top]
     return pl.pallas_call(
         panel_kernel,
-        out_shape=jax.ShapeDtypeStruct(cross_blocks.shape, jnp.bfloat16),
-        in_specs=[SMEM, HBM, HBM],
-        out_specs=HBM,
+        out_shape=(
+            pltpu.VMEM(cross_blocks.shape, jnp.bfloat16),
+            pltpu.VMEM(inverse_top.shape, inverse_top.dtype),
+        ),
+        in_specs=[HBM] * 4,
+        out_specs=(VMEM, VMEM),
         scratch_shapes=[
+            pltpu.SMEM((pattern.size,), jnp.int32),
             pltpu.VMEM(cross_blocks.shape, jnp.float32),
             pltpu.VMEM(diag_inverse.shape, jnp.float32),
-            pltpu.VMEM(cross_blocks.shape, jnp.bfloat16),
-            pltpu.SemaphoreType.DMA((pattern.shape[0] + 1,)),
-            pltpu.SemaphoreType.DMA((pattern.shape[0],)),
+            pltpu.SemaphoreType.DMA((pattern.size + 3,)),
         ],
-        compiler_params=WHOLE,
+        compiler_params=PARAMS,
         name="panel",
-    )(pattern.reshape(-1), cross_blocks, diag_inverse)
+    )(*[pltpu.with_memory_space_constraint(x, pltpu.HBM) for x in inputs])
 
 
 def relay_kernel(block_ref, gate_ref, out_ref):
@@ -148,7 +149,7 @@
     def mate(block, axis):
         return from_pair(block, axis, 0, 1)
 
-    factor_panel = build_panel(cross_blocks, diag_inverse, pattern)
+    factor_panel, inverse_top = build_panel(cross_blocks, diag_inverse, pattern, inverse_top)
     crossed = [from_pair(factor_panel, "prow", d, 1) for d in range(1, pairs)]
     beside = mate(factor_panel, "prow")
     panels = [factor_panel, beside]

time: 43.9 us -> 42.1 us (0.959)
  Pallas kernels: 6.27 us -> 4.82 us
    pallas_call x1, Pallas kernels: 3.64 us -> 2.2 us  [build_panel(): pl.pallas_call(panel_kernel, out_shape=(pltpu.VMEM(cross_blocks.shape, jn...]
  transfers between devices with their start and end apart: 8 -> 8, of which waited for: 5 -> 6; matrix products, arithmetic and copies ran while one was open for 2% -> 2% of each run, Pallas kernels for 8% -> 0%
where the time goes in v4:
time: 42.1 us; the launch traced here: 42 us
  waiting for transfers between devices  24.2 us (57%)
  starting transfers between devices  11.5 us (27%)
  Pallas kernels  4.82 us (11%)
  other arithmetic  0.88 us (2%)
  between operations  0.66 us (2%)
    ppermute x8, waiting for transfers between devices, from_pair(): return lax.ppermute(block, axis, moves)  24.2 us
    ppermute x8, starting transfers between devices, from_pair(): return lax.ppermute(block, axis, moves)  11.5 us
    pallas_call x1, Pallas kernels, build_panel(): pl.pallas_call(panel_kernel, out_shape=(pltpu.VMEM(cross_blocks.shape, jn...  2.2 us
    pallas_call x1, Pallas kernels, products(): pl.pallas_call(functools.partial(product_kernel, n), out_shape=(jax.Shape...  1.82 us
  transfers between devices with their start and end apart: 8, of which 6 were waited for; matrix products, arithmetic and copies ran while one was open for 2% of the time, Pallas kernels for 0%

profile of v4, /device:TPU:0, one launch (start us, length us, event | category | flops | bytes accessed | tf_op | source)
XLA Modules:
  0.0 42.0 jit_solution(8153111651020661042)
XLA Ops:
  0.6 2.2 %panel.1 = (bf16[512,256]{1,0:T(8,128)(2,1)S(1)}, bf16[512,512]{1,0:T(8,128)(2,1)S(1)}) custom-call(s32[2]{0:T(128)} %bitcast.1, f32[512,256]{1,0:T(8,128)} %cross_hbm.1, f32[1,256,256]{2,1,0:T(8,128)} %diag_ref.1, bf16[512,512]{1,0:T(8,128)(2,1)} %top_hbm.1), custom_call_target="tpu_custom_call" | custom-call | tf_op jit(solution)/shard_map/panel/pallas_call | solution.py:43
  2.8 3.0 %collective-permute-start.1 = (bf16[512,512]{1,0:T(8,128)(2,1)S(1)}, bf16[512,512]{1,0:T(8,128)(2,1)S(1)}, u32[]{:S(2)}, u32[]{:S(2)}) collective-permute-start(bf16[512,512]{1,0:T(8,128)(2,1)S(1)} %get-tuple-element.6.refs_0_), channel_id=1, source_target_pairs={{2,0},{3,1},{0,2},{1,3},{6,4},{7,5},{4,6},{5,7},{10,8},{11,9},{8,1... | collective-permute-start | bytes 1572872 | tf_op jit(solution)/shard_map/ppermute | solution.py:147
  5.8 1.6 %collective-permute-start.2 = (bf16[512,256]{1,0:T(8,128)(2,1)S(1)}, bf16[512,256]{1,0:T(8,128)(2,1)S(1)}, u32[]{:S(2)}, u32[]{:S(2)}) collective-permute-start(bf16[512,256]{1,0:T(8,128)(2,1)S(1)} %get-tuple-element.7.refs_4_), channel_id=1, source_target_pairs={{4,0},{0,4},{12,8},{8,12},{5,1},{1,5},{13,9},{9,13},{6,2},{2,6},{1... | collective-permute-start | bytes 786440 | tf_op jit(solution)/shard_map/ppermute | solution.py:147
  7.4 2.5 %collective-permute-start.4 = (bf16[512,256]{1,0:T(8,128)(2,1)S(1)}, bf16[512,256]{1,0:T(8,128)(2,1)S(1)}, u32[]{:S(2)}, u32[]{:S(2)}) collective-permute-start(bf16[512,256]{1,0:T(8,128)(2,1)S(1)} %get-tuple-element.7.refs_4_), channel_id=1, source_target_pairs={{12,0},{8,4},{4,8},{0,12},{13,1},{9,5},{5,9},{1,13},{14,2},{10,6},... | collective-permute-start | bytes 786440 | tf_op jit(solution)/shard_map/ppermute | solution.py:147
  9.9 0.0 collective-permute-start
  9.9 4.3 %collective-permute-done.2.gate_ref.refs_5_ = bf16[512,256]{1,0:T(8,128)(2,1)S(1)} collective-permute-done((bf16[512,256]{1,0:T(8,128)(2,1)S(1)}, bf16[512,256]{1,0:T(8,128)(2,1)S(1)}, u32[]{:S(2)}, u32[]{:S(2)}) %collective-permute-start.2) | collective-permute-done | bytes 262176 | tf_op jit(solution)/shard_map/ppermute | solution.py:147
  14.2 3.6 %collective-permute-done.1.block_ref = bf16[512,512]{1,0:T(8,128)(2,1)S(1)} collective-permute-done((bf16[512,512]{1,0:T(8,128)(2,1)S(1)}, bf16[512,512]{1,0:T(8,128)(2,1)S(1)}, u32[]{:S(2)}, u32[]{:S(2)}) %collective-permute-start.1) | collective-permute-done | bytes 524320 | tf_op jit(solution)/shard_map/ppermute | solution.py:147
  17.8 0.0 collective-permute-start.3
  17.8 3.6 %collective-permute-done.4.block_ref = bf16[512,256]{1,0:T(8,128)(2,1)S(1)} collective-permute-done((bf16[512,256]{1,0:T(8,128)(2,1)S(1)}, bf16[512,256]{1,0:T(8,128)(2,1)S(1)}, u32[]{:S(2)}, u32[]{:S(2)}) %collective-permute-start.4) | collective-permute-done | bytes 262176 | tf_op jit(solution)/shard_map/ppermute | solution.py:147
  21.4 0.6 %collective-permute-start.5 = (bf16[512,256]{1,0:T(8,128)(2,1)S(1)}, bf16[512,256]{1,0:T(8,128)(2,1)S(1)}, u32[]{:S(2)}, u32[]{:S(2)}) collective-permute-start(bf16[512,256]{1,0:T(8,128)(2,1)S(1)} %relay.3.refs_7_), channel_id=1, source_target_pairs={{4,0},{0,4},{12,8},{8,12},{5,1},{1,5},{13,9},{9,13},{6,2},{2,6},{1... | collective-permute-start | bytes 786440 | tf_op jit(solution)/shard_map/ppermute | solution.py:147
  22.0 6.2 %collective-permute-done.5.refs_6_ = bf16[512,256]{1,0:T(8,128)(2,1)S(1)} collective-permute-done((bf16[512,256]{1,0:T(8,128)(2,1)S(1)}, bf16[512,256]{1,0:T(8,128)(2,1)S(1)}, u32[]{:S(2)}, u32[]{:S(2)}) %collective-permute-start.5) | collective-permute-done | bytes 262176 | tf_op jit(solution)/shard_map/ppermute | solution.py:147
  28.2 0.0 collective-permute-done.refs_1_
  28.2 0.0 collective-permute-done.3.refs_3_
  28.2 1.8 %products.1 = (f32[512,256]{1,0:T(8,128)S(1)}, bf16[128,384]{1,0:T(8,128)(2,1)S(1)}) custom-call(s32[4]{0:T(128)S(1)} %fusion.2.slots_ref, bf16[512,512]{1,0:T(8,128)(2,1)S(1)} %get-tuple-element.6.refs_0_, bf16[512,512]{1,0:T(8,128)(2,1)S(1)} %collective-permute-done.refs_1_, bf16[512,512]{1,0:T(8,128)(2,1)S(1)} %relay.2.refs_2_, ...), custom_call_target="tpu_custom_call" | custom-call | tf_op jit(solution)/shard_map/products/pallas_call | solution.py:103
  30.0 0.3 collective-permute-start.6
  30.3 4.3 %collective-permute-done.6 = bf16[128,384]{1,0:T(8,128)(2,1)S(1)} collective-permute-done((bf16[128,384]{1,0:T(8,128)(2,1)S(1)}, bf16[128,384]{1,0:T(8,128)(2,1)S(1)}, u32[]{:S(2)}, u32[]{:S(2)}) %collective-permute-start.6) | collective-permute-done | bytes 98336 | tf_op jit(solution)/shard_map/ppermute | solution.py:147
  34.7 3.5 %collective-permute-start.7 = (bf16[128,384]{1,0:T(8,128)(2,1)S(1)}, bf16[128,384]{1,0:T(8,128)(2,1)S(1)}, u32[]{:S(2)}, u32[]{:S(2)}) collective-permute-start(bf16[128,384]{1,0:T(8,128)(2,1)S(1)} %add_convert_fusion.refs_0_), channel_id=1, source_target_pairs={{12,0},{8,4},{4,8},{0,12},{13,1},{9,5},{5,9},{1,13},{14,2},{10,6},... | collective-permute-start | bytes 294920 | tf_op jit(solution)/shard_map/ppermute | solution.py:147
  38.2 0.0 copy-start
  38.2 0.8 %neg.3 = f32[512,256]{1,0:T(8,128)} negate(f32[512,256]{1,0:T(8,128)S(1)} %get-tuple-element.8) | non-fusion elementwise | flops 131072 | bytes 1048576 | tf_op jit(solution)/shard_map/neg | solution.py:174
  39.0 2.2 %collective-permute-done.7.refs_1_ = bf16[128,384]{1,0:T(8,128)(2,1)S(1)} collective-permute-done((bf16[128,384]{1,0:T(8,128)(2,1)S(1)}, bf16[128,384]{1,0:T(8,128)(2,1)S(1)}, u32[]{:S(2)}, u32[]{:S(2)}) %collective-permute-start.7) | collective-permute-done | bytes 98336 | tf_op jit(solution)/shard_map/ppermute | solution.py:147
  41.2 0.0 copy-done
  41.2 0.8 %finish.1 = f32[1,256,256]{2,1,0:T(8,128)} custom-call(f32[1,256,256]{2,1,0:T(8,128)S(1)} %copy-done, bf16[128,384]{1,0:T(8,128)(2,1)S(1)} %add_convert_fusion.refs_0_, bf16[128,384]{1,0:T(8,128)(2,1)S(1)} %collective-permute-done.7.refs_1_), custom_call_target="tpu_custom_call" | custom-call | tf_op jit(solution)/shard_map/finish/pallas_call | solution.py:129
  (4 shorter events, 0.0 us)
Async XLA Ops:
  2.8 14.9 %collective-permute-start.1 = (bf16[512,512]{1,0:T(8,128)(2,1)S(1)}, bf16[512,512]{1,0:T(8,128)(2,1)S(1)}, u32[]{:S(2)}, u32[]{:S(2)}) collective-permute-start(bf16[512,512]{1,0:T(8,128)(2,1)S(1)} %get-tuple-element.6.refs_0_), channel_id=1, source_target_pairs={{2,0},{3,1},{0,2},{1,3},{6,4},{7,5},{4,6},{5,7},{10,8},{11,9},{8,1... | collective-permute-start | bytes 1572872 | tf_op jit(solution)/shard_map/ppermute | solution.py:147
  5.8 8.3 %collective-permute-start.2 = (bf16[512,256]{1,0:T(8,128)(2,1)S(1)}, bf16[512,256]{1,0:T(8,128)(2,1)S(1)}, u32[]{:S(2)}, u32[]{:S(2)}) collective-permute-start(bf16[512,256]{1,0:T(8,128)(2,1)S(1)} %get-tuple-element.7.refs_4_), channel_id=1, source_target_pairs={{4,0},{0,4},{12,8},{8,12},{5,1},{1,5},{13,9},{9,13},{6,2},{2,6},{1... | collective-permute-start | bytes 786440 | tf_op jit(solution)/shard_map/ppermute | solution.py:147
  7.4 13.9 %collective-permute-start.4 = (bf16[512,256]{1,0:T(8,128)(2,1)S(1)}, bf16[512,256]{1,0:T(8,128)(2,1)S(1)}, u32[]{:S(2)}, u32[]{:S(2)}) collective-permute-start(bf16[512,256]{1,0:T(8,128)(2,1)S(1)} %get-tuple-element.7.refs_4_), channel_id=1, source_target_pairs={{12,0},{8,4},{4,8},{0,12},{13,1},{9,5},{5,9},{1,13},{14,2},{10,6},... | collective-permute-start | bytes 786440 | tf_op jit(solution)/shard_map/ppermute | solution.py:147
  9.9 18.3 %collective-permute-start = (bf16[512,512]{1,0:T(8,128)(2,1)S(1)}, bf16[512,512]{1,0:T(8,128)(2,1)S(1)}, u32[]{:S(2)}, u32[]{:S(2)}) collective-permute-start(bf16[512,512]{1,0:T(8,128)(2,1)S(1)} %get-tuple-element.6.refs_0_), channel_id=1, source_target_pairs={{1,0},{0,1},{3,2},{2,3},{5,4},{4,5},{7,6},{6,7},{9,8},{8,9},{11,10... | collective-permute-start | bytes 1572872 | tf_op jit(solution)/shard_map/ppermute | solution.py:147
  17.8 10.4 %collective-permute-start.3 = (bf16[512,512]{1,0:T(8,128)(2,1)S(1)}, bf16[512,512]{1,0:T(8,128)(2,1)S(1)}, u32[]{:S(2)}, u32[]{:S(2)}) collective-permute-start(bf16[512,512]{1,0:T(8,128)(2,1)S(1)} %relay.2.refs_2_), channel_id=1, source_target_pairs={{1,0},{0,1},{3,2},{2,3},{5,4},{4,5},{7,6},{6,7},{9,8},{8,9},{11,10... | collective-permute-start | bytes 1572872 | tf_op jit(solution)/shard_map/ppermute | solution.py:147
  21.4 6.8 %collective-permute-start.5 = (bf16[512,256]{1,0:T(8,128)(2,1)S(1)}, bf16[512,256]{1,0:T(8,128)(2,1)S(1)}, u32[]{:S(2)}, u32[]{:S(2)}) collective-permute-start(bf16[512,256]{1,0:T(8,128)(2,1)S(1)} %relay.3.refs_7_), channel_id=1, source_target_pairs={{4,0},{0,4},{12,8},{8,12},{5,1},{1,5},{13,9},{9,13},{6,2},{2,6},{1... | collective-permute-start | bytes 786440 | tf_op jit(solution)/shard_map/ppermute | solution.py:147
  30.0 4.7 %collective-permute-start.6 = (bf16[128,384]{1,0:T(8,128)(2,1)S(1)}, bf16[128,384]{1,0:T(8,128)(2,1)S(1)}, u32[]{:S(2)}, u32[]{:S(2)}) collective-permute-start(bf16[128,384]{1,0:T(8,128)(2,1)S(1)} %get-tuple-element.9), channel_id=1, source_target_pairs={{4,0},{0,4},{12,8},{8,12},{5,1},{1,5},{13,9},{9,13},{6,2},{2,6},{1... | collective-permute-start | bytes 294920 | tf_op jit(solution)/shard_map/ppermute | solution.py:147
  34.7 6.5 %collective-permute-start.7 = (bf16[128,384]{1,0:T(8,128)(2,1)S(1)}, bf16[128,384]{1,0:T(8,128)(2,1)S(1)}, u32[]{:S(2)}, u32[]{:S(2)}) collective-permute-start(bf16[128,384]{1,0:T(8,128)(2,1)S(1)} %add_convert_fusion.refs_0_), channel_id=1, source_target_pairs={{12,0},{8,4},{4,8},{0,12},{13,1},{9,5},{5,9},{1,13},{14,2},{10,6},... | collective-permute-start | bytes 294920 | tf_op jit(solution)/shard_map/ppermute | solution.py:147
  38.2 3.0 %copy-start = (f32[1,256,256]{2,1,0:T(8,128)S(1)}, f32[1,256,256]{2,1,0:T(8,128)}, u32[]{:S(2)}) copy-start(f32[1,256,256]{2,1,0:T(8,128)} %diag_ref.1) | copy-start | bytes 786436

commit v5 on v4

v5 whole, which is shorter than its diff:
```python
import functools
import jax
import jax.numpy as jnp
from jax import lax
from jax.experimental import pallas as pl
from jax.experimental.pallas import tpu as pltpu
from jax.sharding import PartitionSpec as P

PAIR = 2
VMEM_LIMIT = 40 * 1024 * 1024
PARAMS = pltpu.CompilerParams(vmem_limit_bytes=VMEM_LIMIT)
SMALL = pltpu.CompilerParams(vmem_limit_bytes=1024 * 1024)
SMEM = pl.BlockSpec(memory_space=pltpu.SMEM)
VMEM = pl.BlockSpec(memory_space=pltpu.VMEM)
ANY = pl.BlockSpec(memory_space=pl.ANY)
HBM = pl.BlockSpec(memory_space=pltpu.HBM)


def panel_kernel(
    pattern_hbm, cross_hbm, diag_hbm, top_hbm, first_ref, second_ref, top_ref, pattern_ref, cross_ref, diag_ref, sems
):
    width = diag_ref.shape[1]
    blocks = pattern_hbm.shape[0]
    rows = [pl.ds(a * width, width) for a in range(blocks)]
    loads = [pltpu.make_async_copy(cross_hbm.at[r], cross_ref.at[r], sems.at[a]) for a, r in enumerate(rows)]
    diag_copy = pltpu.make_async_copy(diag_hbm, diag_ref, sems.at[blocks])
    pattern_copy = pltpu.make_async_copy(pattern_hbm, pattern_ref, sems.at[blocks + 1])
    top_copy = pltpu.make_async_copy(top_hbm, top_ref, sems.at[blocks + 2])
    for copy in [pattern_copy, diag_copy] + loads + [top_copy]:
        copy.start()
    pattern_copy.wait()
    diag_copy.wait()
    for a in range(blocks):
        loads[a].wait()
        masked = cross_ref[rows[a], :] * pattern_ref[a].astype(jnp.float32)
        solved = jnp.dot(
            masked, diag_ref[0], precision=lax.Precision.HIGHEST, preferred_element_type=jnp.float32
        )
        first_ref[rows[a], :] = solved[:, : width // 2].astype(jnp.bfloat16)
        second_ref[rows[a], :] = solved[:, width // 2 :].astype(jnp.bfloat16)
    top_copy.wait()


def build_panel(cross_blocks, diag_inverse, pattern, inverse_top):
    half = (cross_blocks.shape[0], cross_blocks.shape[1] // 2)
    inputs = [pattern.reshape(-1), cross_blocks, diag_inverse, inverse_top]
    return pl.pallas_call(
        panel_kernel,
        out_shape=(
            pltpu.VMEM(half, jnp.bfloat16),
            pltpu.VMEM(half, jnp.bfloat16),
            pltpu.VMEM(inverse_top.shape, inverse_top.dtype),
        ),
        in_specs=[HBM] * 4,
        out_specs=(VMEM, VMEM, VMEM),
        scratch_shapes=[
            pltpu.SMEM((pattern.size,), jnp.int32),
            pltpu.VMEM(cross_blocks.shape, jnp.float32),
            pltpu.VMEM(diag_inverse.shape, jnp.float32),
            pltpu.SemaphoreType.DMA((pattern.size + 3,)),
        ],
        compiler_params=PARAMS,
        name="panel",
    )(*[pltpu.with_memory_space_constraint(x, pltpu.HBM) for x in inputs])


def relay_kernel(*refs):
    del refs


def after(block, *gates):
    return pl.pallas_call(
        relay_kernel,
        out_shape=jax.ShapeDtypeStruct(block.shape, block.dtype),
        in_specs=[ANY] * (1 + len(gates)),
        out_specs=ANY,
        input_output_aliases={0: 0},
        compiler_params=SMALL,
        name="relay",
    )(block, *gates)


def product_kernel(n, slots_ref, *refs):
    tops, panels, lefts = refs[:n], refs[n:2 * n], refs[2 * n:-3]
    selected_ref, update_ref, panel_buf = refs[-3:]
    for s in range(n):
        panel_buf[slots_ref[s]] = panels[s][...]
    total = jnp.dot(tops[0][...], panel_buf[0], preferred_element_type=jnp.float32)
    for t in range(1, n):
        total += jnp.dot(tops[t][...], panel_buf[t], preferred_element_type=jnp.float32)
    selected_ref[...] = total
    high = total.astype(jnp.bfloat16)
    low = (total - high.astype(jnp.float32)).astype(jnp.bfloat16)
    contract = (((0,), (0,)), ((), ()))
    half = total.shape[1]
    for p, left in enumerate(lefts):
        update = lax.dot_general(left[...], high, contract, preferred_element_type=jnp.float32)
        update += lax.dot_general(left[...], low, contract, preferred_element_type=jnp.float32)
        update_ref[p * half:(p + 1) * half, :] = update.astype(jnp.bfloat16)


def products(tops, panels, lefts, slots):
    n = len(tops)
    rows, half = panels[0].shape
    return pl.pallas_call(
        functools.partial(product_kernel, n),
        out_shape=(
            jax.ShapeDtypeStruct((rows, half), jnp.float32),
            jax.ShapeDtypeStruct((len(lefts) * half, half), jnp.bfloat16),
        ),
        in_specs=[SMEM] + [VMEM] * (2 * n + len(lefts)),
        out_specs=(VMEM, VMEM),
        scratch_shapes=[pltpu.VMEM((n, rows, half), jnp.bfloat16)],
        compiler_params=PARAMS,
        name="products",
    )(slots, *tops, *panels, *lefts)


def finish_kernel(count, diag_ref, *refs):
    out_ref = refs[-1]

    def total(parts):
        value = parts[0][...].astype(jnp.float32)
        for part in parts[1:]:
            value += part[...].astype(jnp.float32)
        return value

    left, corner = total(refs[:count]), total(refs[count:2 * count])
    half = corner.shape[0]
    out_ref[0, :, :half] = diag_ref[0, :, :half] + left
    out_ref[0, :half, half:] = diag_ref[0, :half, half:] + left[half:].T
    out_ref[0, half:, half:] = diag_ref[0, half:, half:] + corner


def finish(diag_inverse, lefts, corners):
    return pl.pallas_call(
        functools.partial(finish_kernel, len(lefts)),
        out_shape=jax.ShapeDtypeStruct(diag_inverse.shape, jnp.float32),
        in_specs=[VMEM] * (1 + len(lefts) + len(corners)),
        out_specs=VMEM,
        compiler_params=PARAMS,
        name="finish",
    )(diag_inverse, *lefts, *corners)


def on_device(n, inverse_top, diag_inverse, cross_blocks, pattern):
    pairs = n // PAIR
    row, col = lax.axis_index("prow"), lax.axis_index("pcol")

    def from_pair(block, axis, shift, flip):
        moves = [
            (((m + shift) % pairs) * PAIR + (b ^ flip), m * PAIR + b) for m in range(pairs) for b in range(PAIR)
        ]
        return lax.ppermute(block, axis, moves)

    def mate(block, axis):
        return from_pair(block, axis, 0, 1)

    def exchange(update, swapped):
        paired = (update.astype(jnp.float32) + swapped.astype(jnp.float32)).astype(jnp.bfloat16)
        return [paired] + [from_pair(paired, "prow", d, 1) for d in range(1, pairs)]

    first, second, inverse_top = build_panel(cross_blocks, diag_inverse, pattern, inverse_top)

    crossed = [from_pair(first, "prow", d, 1) for d in range(1, pairs)]
    beside = mate(first, "prow")
    crossed = [after(block, beside) for block in crossed]
    swapped = [mate(block, "prow") for block in crossed]
    later = after(second, beside)
    crossed_later = [from_pair(later, "prow", d, 1) for d in range(1, pairs)]
    beside_later = mate(later, "prow")
    crossed_later = [after(block, beside_later) for block in crossed_later]
    swapped_later = [mate(block, "prow") for block in crossed_later]

    near = [from_pair(inverse_top, "pcol", d, 0) for d in range(1, pairs)]
    tops = [inverse_top, mate(inverse_top, "pcol")]
    for block in near:
        block = after(block, swapped[0], *crossed_later)
        tops += [block, mate(block, "pcol")]

    def in_order(own, mates, blocks, others):
        return [own, mates] + [block for pair in zip(others, blocks) for block in pair]

    place = jnp.arange(n, dtype=jnp.int32)
    wanted_pair = (row // PAIR + place // PAIR) % pairs
    wanted_side = (row % PAIR) ^ (place % PAIR)
    slots = ((wanted_pair - col // PAIR) % pairs) * PAIR + (wanted_side ^ (col % PAIR))

    selected_left, update_left = products(tops, in_order(first, beside, crossed, swapped), [first, later], slots)
    swapped_left = mate(update_left, "prow")
    swapped_later = [after(block, swapped_left) for block in swapped_later]
    selected_right, corner = products(
        tops, in_order(later, beside_later, crossed_later, swapped_later), [later], slots
    )
    inverse_cross = -jnp.concatenate([selected_left, selected_right], axis=1)
    left_parts = exchange(update_left, swapped_left)
    corner_parts = exchange(corner, mate(corner, "prow"))
    return inverse_cross, finish(diag_inverse, left_parts, corner_parts)


def solution(mesh):
    placed = (
        P(("pole", "prow"), "pcol"),
        P(("pole", "pcol"), None, None),
        P(("pole", "prow"), "pcol"),
        P("prow", "pcol"),
    )
    return jax.shard_map(
        functools.partial(on_device, mesh.shape["pcol"]),
        mesh=mesh,
        in_specs=placed,
        out_specs=(P(("pole", "prow"), "pcol"), P(("pole", "pcol"), None, None)),
        check_vma=False,
    )
```

time: 42.1 us -> 44.6 us (1.059)
  starting transfers between devices: 11.5 us -> 17.8 us
  waiting for transfers between devices: 24.2 us -> 18.7 us
  Pallas kernels: 4.82 us -> 6.37 us
    ppermute x8 -> x13, starting transfers between devices: 11.5 us -> 17.8 us  [from_pair(): return lax.ppermute(block, axis, moves)]
    ppermute x8 -> x13, waiting for transfers between devices: 24.2 us -> 18.7 us  [from_pair(): return lax.ppermute(block, axis, moves)]
    pallas_call x1 -> x2, Pallas kernels: 1.82 us -> 3.36 us  [products(): pl.pallas_call(functools.partial(product_kernel, n), out_shape=(jax.Shape...]
  transfers between devices with their start and end apart: 8 -> 13, of which waited for: 6 -> 10; matrix products, arithmetic and copies ran while one was open for 2% -> 2% of each run, Pallas kernels for 0% -> 4%
where the time goes in v5:
time: 44.6 us; the launch traced here: 44.5 us
  waiting for transfers between devices  18.7 us (42%)
  starting transfers between devices  17.8 us (40%)
  Pallas kernels  6.37 us (14%)
  other arithmetic  0.88 us (2%)
  between operations  0.68 us (2%)
    ppermute x13, waiting for transfers between devices, from_pair(): return lax.ppermute(block, axis, moves)  18.7 us
    ppermute x13, starting transfers between devices, from_pair(): return lax.ppermute(block, axis, moves)  17.8 us
    pallas_call x2, Pallas kernels, products(): pl.pallas_call(functools.partial(product_kernel, n), out_shape=(jax.Shape...  3.36 us
    pallas_call x1, Pallas kernels, build_panel(): pl.pallas_call(panel_kernel, out_shape=(pltpu.VMEM(half, jnp.bfloat16), p...  2.2 us
  transfers between devices with their start and end apart: 13, of which 10 were waited for; matrix products, arithmetic and copies ran while one was open for 2% of the time, Pallas kernels for 4%

profile of v5, /device:TPU:0, one launch (start us, length us, event | category | flops | bytes accessed | tf_op | source)
XLA Modules:
  0.0 44.5 jit_solution(7457206098557048788)
XLA Ops:
  0.6 2.2 %panel.1 = (bf16[512,128]{1,0:T(8,128)(2,1)S(1)}, bf16[512,128]{1,0:T(8,128)(2,1)S(1)}, bf16[512,512]{1,0:T(8,128)(2,1)S(1)}) custom-call(s32[2]{0:T(128)} %bitcast.1, f32[512,256]{1,0:T(8,128)} %cross_hbm.1, f32[1,256,256]{2,1,0:T(8,128)} %diag_ref.1, bf16[512,512]{1,0:T(8,128)(2,1)} %top_hbm.1), custom_call_target="tpu_custom_call" | custom-call | tf_op jit(solution)/shard_map/panel/pallas_call | solution.py:47
  2.8 3.0 %collective-permute-start.1 = (bf16[512,512]{1,0:T(8,128)(2,1)S(1)}, bf16[512,512]{1,0:T(8,128)(2,1)S(1)}, u32[]{:S(2)}, u32[]{:S(2)}) collective-permute-start(bf16[512,512]{1,0:T(8,128)(2,1)S(1)} %get-tuple-element.9.refs_0_), channel_id=1, source_target_pairs={{2,0},{3,1},{0,2},{1,3},{6,4},{7,5},{4,6},{5,7},{10,8},{11,9},{8,1... | collective-permute-start | bytes 1572872 | tf_op jit(solution)/shard_map/ppermute | solution.py:154
  5.8 1.6 %collective-permute-start.3 = (bf16[512,128]{1,0:T(8,128)(2,1)S(1)}, bf16[512,128]{1,0:T(8,128)(2,1)S(1)}, u32[]{:S(2)}, u32[]{:S(2)}) collective-permute-start(bf16[512,128]{1,0:T(8,128)(2,1)S(1)} %get-tuple-element.10.refs_4_.refs_8_), channel_id=1, source_target_pairs={{4,0},{0,4},{12,8},{8,12},{5,1},{1,5},{13,9},{9,13},{6,2},{2,6},{1... | collective-permute-start | bytes 393224 | tf_op jit(solution)/shard_map/ppermute | solution.py:154
  7.4 2.5 %collective-permute-start.2 = (bf16[512,128]{1,0:T(8,128)(2,1)S(1)}, bf16[512,128]{1,0:T(8,128)(2,1)S(1)}, u32[]{:S(2)}, u32[]{:S(2)}) collective-permute-start(bf16[512,128]{1,0:T(8,128)(2,1)S(1)} %get-tuple-element.10.refs_4_.refs_8_), channel_id=1, source_target_pairs={{12,0},{8,4},{4,8},{0,12},{13,1},{9,5},{5,9},{1,13},{14,2},{10,6},... | collective-permute-start | bytes 393224 | tf_op jit(solution)/shard_map/ppermute | solution.py:154
  9.9 0.9 %collective-permute-done.3.refs_1_.refs_5_ = bf16[512,128]{1,0:T(8,128)(2,1)S(1)} collective-permute-done((bf16[512,128]{1,0:T(8,128)(2,1)S(1)}, bf16[512,128]{1,0:T(8,128)(2,1)S(1)}, u32[]{:S(2)}, u32[]{:S(2)}) %collective-permute-start.3) | collective-permute-done | bytes 131104 | tf_op jit(solution)/shard_map/ppermute | solution.py:154
  10.8 2.2 %collective-permute-start.6 = (bf16[512,128]{1,0:T(8,128)(2,1)S(1)}, bf16[512,128]{1,0:T(8,128)(2,1)S(1)}, u32[]{:S(2)}, u32[]{:S(2)}) collective-permute-start(bf16[512,128]{1,0:T(8,128)(2,1)S(1)} %relay.6.refs_9_.refs_4_.refs_8_), channel_id=1, source_target_pairs={{4,0},{0,4},{12,8},{8,12},{5,1},{1,5},{13,9},{9,13},{6,2},{2,6},{1... | collective-permute-start | bytes 393224 | tf_op jit(solution)/shard_map/ppermute | solution.py:154
  13.0 3.4 %collective-permute-start.5 = (bf16[512,128]{1,0:T(8,128)(2,1)S(1)}, bf16[512,128]{1,0:T(8,128)(2,1)S(1)}, u32[]{:S(2)}, u32[]{:S(2)}) collective-permute-start(bf16[512,128]{1,0:T(8,128)(2,1)S(1)} %relay.6.refs_9_.refs_4_.refs_8_), channel_id=1, source_target_pairs={{12,0},{8,4},{4,8},{0,12},{13,1},{9,5},{5,9},{1,13},{14,2},{10,6},... | collective-permute-start | bytes 393224 | tf_op jit(solution)/shard_map/ppermute | solution.py:154
  16.5 0.7 %collective-permute-done.2.refs_0_ = bf16[512,128]{1,0:T(8,128)(2,1)S(1)} collective-permute-done((bf16[512,128]{1,0:T(8,128)(2,1)S(1)}, bf16[512,128]{1,0:T(8,128)(2,1)S(1)}, u32[]{:S(2)}, u32[]{:S(2)}) %collective-permute-start.2) | collective-permute-done | bytes 131104 | tf_op jit(solution)/shard_map/ppermute | solution.py:154
  17.2 0.4 collective-permute-start.4
  17.6 0.0 collective-permute-start
  17.6 1.6 %collective-permute-done.6.refs_1_.refs_5_ = bf16[512,128]{1,0:T(8,128)(2,1)S(1)} collective-permute-done((bf16[512,128]{1,0:T(8,128)(2,1)S(1)}, bf16[512,128]{1,0:T(8,128)(2,1)S(1)}, u32[]{:S(2)}, u32[]{:S(2)}) %collective-permute-start.6) | collective-permute-done | bytes 131104 | tf_op jit(solution)/shard_map/ppermute | solution.py:154
  19.2 3.6 %collective-permute-done.5.refs_0_ = bf16[512,128]{1,0:T(8,128)(2,1)S(1)} collective-permute-done((bf16[512,128]{1,0:T(8,128)(2,1)S(1)}, bf16[512,128]{1,0:T(8,128)(2,1)S(1)}, u32[]{:S(2)}, u32[]{:S(2)}) %collective-permute-start.5) | collective-permute-done | bytes 131104 | tf_op jit(solution)/shard_map/ppermute | solution.py:154
  22.8 0.8 %collective-permute-done.4.refs_1_.refs_6_ = bf16[512,128]{1,0:T(8,128)(2,1)S(1)} collective-permute-done((bf16[512,128]{1,0:T(8,128)(2,1)S(1)}, bf16[512,128]{1,0:T(8,128)(2,1)S(1)}, u32[]{:S(2)}, u32[]{:S(2)}) %collective-permute-start.4) | collective-permute-done | bytes 131104 | tf_op jit(solution)/shard_map/ppermute | solution.py:154
  23.6 0.0 collective-permute-done.1.refs_0_
  23.6 0.0 collective-permute-start.7
  23.6 0.1 collective-permute-start.8
  23.7 0.0 collective-permute-done.refs_1_
  23.7 1.8 %collective-permute-done.7.refs_3_ = bf16[512,512]{1,0:T(8,128)(2,1)S(1)} collective-permute-done((bf16[512,512]{1,0:T(8,128)(2,1)S(1)}, bf16[512,512]{1,0:T(8,128)(2,1)S(1)}, u32[]{:S(2)}, u32[]{:S(2)}) %collective-permute-start.7) | collective-permute-done | bytes 524320 | tf_op jit(solution)/shard_map/ppermute | solution.py:154
  25.5 1.8 %products.2 = (f32[512,128]{1,0:T(8,128)S(1)}, bf16[256,128]{1,0:T(8,128)(2,1)S(1)}) custom-call(s32[4]{0:T(128)S(1)} %fusion.2.slots_ref, bf16[512,512]{1,0:T(8,128)(2,1)S(1)} %get-tuple-element.9.refs_0_, bf16[512,512]{1,0:T(8,128)(2,1)S(1)} %collective-permute-done.refs_1_, bf16[512,512]{1,0:T(8,128)(2,1)S(1)} %relay.8.refs_2_, ...), custom_call_target="tpu_custom_call" | custom-call | tf_op jit(solution)/shard_map/products/pallas_call | solution.py:105
  27.3 0.3 collective-permute-start.9
  27.6 1.9 %collective-permute-done.8.refs_0_ = bf16[512,128]{1,0:T(8,128)(2,1)S(1)} collective-permute-done((bf16[512,128]{1,0:T(8,128)(2,1)S(1)}, bf16[512,128]{1,0:T(8,128)(2,1)S(1)}, u32[]{:S(2)}, u32[]{:S(2)}) %collective-permute-start.8) | collective-permute-done | bytes 131104 | tf_op jit(solution)/shard_map/ppermute | solution.py:154
  29.5 2.1 %collective-permute-done.9.refs_1_ = bf16[256,128]{1,0:T(8,128)(2,1)S(1)} collective-permute-done((bf16[256,128]{1,0:T(8,128)(2,1)S(1)}, bf16[256,128]{1,0:T(8,128)(2,1)S(1)}, u32[]{:S(2)}, u32[]{:S(2)}) %collective-permute-start.9) | collective-permute-done | bytes 65568 | tf_op jit(solution)/shard_map/ppermute | solution.py:154
  31.6 1.6 %products.3 = (f32[512,128]{1,0:T(8,128)S(1)}, bf16[128,128]{1,0:T(8,128)(2,1)S(1)}) custom-call(s32[4]{0:T(128)S(1)} %fusion.2.slots_ref, bf16[512,512]{1,0:T(8,128)(2,1)S(1)} %get-tuple-element.9.refs_0_, bf16[512,512]{1,0:T(8,128)(2,1)S(1)} %collective-permute-done.refs_1_, bf16[512,512]{1,0:T(8,128)(2,1)S(1)} %relay.8.refs_2_, ...), custom_call_target="tpu_custom_call" | custom-call | tf_op jit(solution)/shard_map/products/pallas_call | solution.py:105
  33.2 0.3 collective-permute-start.11
  33.5 2.4 %collective-permute-start.10 = (bf16[256,128]{1,0:T(8,128)(2,1)S(1)}, bf16[256,128]{1,0:T(8,128)(2,1)S(1)}, u32[]{:S(2)}, u32[]{:S(2)}) collective-permute-start(bf16[256,128]{1,0:T(8,128)(2,1)S(1)} %add_convert_fusion.refs_0_), channel_id=1, source_target_pairs={{12,0},{8,4},{4,8},{0,12},{13,1},{9,5},{5,9},{1,13},{14,2},{10,6},... | collective-permute-start | bytes 196616 | tf_op jit(solution)/shard_map/ppermute | solution.py:154
  35.9 2.0 %collective-permute-done.11 = bf16[128,128]{1,0:T(8,128)(2,1)S(1)} collective-permute-done((bf16[128,128]{1,0:T(8,128)(2,1)S(1)}, bf16[128,128]{1,0:T(8,128)(2,1)S(1)}, u32[]{:S(2)}, u32[]{:S(2)}) %collective-permute-start.11) | collective-permute-done | bytes 32800 | tf_op jit(solution)/shard_map/ppermute | solution.py:154
  37.9 1.7 %collective-permute-start.12 = (bf16[128,128]{1,0:T(8,128)(2,1)S(1)}, bf16[128,128]{1,0:T(8,128)(2,1)S(1)}, u32[]{:S(2)}, u32[]{:S(2)}) collective-permute-start(bf16[128,128]{1,0:T(8,128)(2,1)S(1)} %add_convert_fusion.1.refs_2_), channel_id=1, source_target_pairs={{12,0},{8,4},{4,8},{0,12},{13,1},{9,5},{5,9},{1,13},{14,2},{10,6},... | collective-permute-start | bytes 98312 | tf_op jit(solution)/shard_map/ppermute | solution.py:154
  39.6 0.0 copy-start
  39.6 0.8 %maximum_negate_fusion = f32[512,256]{1,0:T(8,128)} fusion(f32[512,128]{1,0:T(8,128)S(1)} %get-tuple-element.14, f32[512,128]{1,0:T(8,128)S(1)} %get-tuple-element.12), kind=kLoop, calls=%fused_computation | loop fusion | flops 262144 | bytes 1048576 | tf_op jit(solution)/shard_map/neg | solution.py:195
  40.4 3.3 %collective-permute-done.12.refs_3_ = bf16[128,128]{1,0:T(8,128)(2,1)S(1)} collective-permute-done((bf16[128,128]{1,0:T(8,128)(2,1)S(1)}, bf16[128,128]{1,0:T(8,128)(2,1)S(1)}, u32[]{:S(2)}, u32[]{:S(2)}) %collective-permute-start.12) | collective-permute-done | bytes 32800 | tf_op jit(solution)/shard_map/ppermute | solution.py:154
  43.7 0.0 collective-permute-done.10.refs_1_
  43.7 0.0 copy-done
  43.7 0.8 %finish.1 = f32[1,256,256]{2,1,0:T(8,128)} custom-call(f32[1,256,256]{2,1,0:T(8,128)S(1)} %copy-done, bf16[256,128]{1,0:T(8,128)(2,1)S(1)} %add_convert_fusion.refs_0_, bf16[256,128]{1,0:T(8,128)(2,1)S(1)} %collective-permute-done.10.refs_1_, bf16[128,128]{1,0:T(8,128)(2,1)S(1)} %add_convert_fusion.1.refs_2_, ...), custom_call_target="tpu_custom_call" | custom-call | tf_op jit(solution)/shard_map/finish/pallas_call | solution.py:136
  (8 shorter events, 0.1 us)
Async XLA Ops:
  2.8 20.7 %collective-permute-start.1 = (bf16[512,512]{1,0:T(8,128)(2,1)S(1)}, bf16[512,512]{1,0:T(8,128)(2,1)S(1)}, u32[]{:S(2)}, u32[]{:S(2)}) collective-permute-start(bf16[512,512]{1,0:T(8,128)(2,1)S(1)} %get-tuple-element.9.refs_0_), channel_id=1, source_target_pairs={{2,0},{3,1},{0,2},{1,3},{6,4},{7,5},{4,6},{5,7},{10,8},{11,9},{8,1... | collective-permute-start | bytes 1572872 | tf_op jit(solution)/shard_map/ppermute | solution.py:154
  5.8 5.0 %collective-permute-start.3 = (bf16[512,128]{1,0:T(8,128)(2,1)S(1)}, bf16[512,128]{1,0:T(8,128)(2,1)S(1)}, u32[]{:S(2)}, u32[]{:S(2)}) collective-permute-start(bf16[512,128]{1,0:T(8,128)(2,1)S(1)} %get-tuple-element.10.refs_4_.refs_8_), channel_id=1, source_target_pairs={{4,0},{0,4},{12,8},{8,12},{5,1},{1,5},{13,9},{9,13},{6,2},{2,6},{1... | collective-permute-start | bytes 393224 | tf_op jit(solution)/shard_map/ppermute | solution.py:154
  7.4 9.8 %collective-permute-start.2 = (bf16[512,128]{1,0:T(8,128)(2,1)S(1)}, bf16[512,128]{1,0:T(8,128)(2,1)S(1)}, u32[]{:S(2)}, u32[]{:S(2)}) collective-permute-start(bf16[512,128]{1,0:T(8,128)(2,1)S(1)} %get-tuple-element.10.refs_4_.refs_8_), channel_id=1, source_target_pairs={{12,0},{8,4},{4,8},{0,12},{13,1},{9,5},{5,9},{1,13},{14,2},{10,6},... | collective-permute-start | bytes 393224 | tf_op jit(solution)/shard_map/ppermute | solution.py:154
  10.8 8.4 %collective-permute-start.6 = (bf16[512,128]{1,0:T(8,128)(2,1)S(1)}, bf16[512,128]{1,0:T(8,128)(2,1)S(1)}, u32[]{:S(2)}, u32[]{:S(2)}) collective-permute-start(bf16[512,128]{1,0:T(8,128)(2,1)S(1)} %relay.6.refs_9_.refs_4_.refs_8_), channel_id=1, source_target_pairs={{4,0},{0,4},{12,8},{8,12},{5,1},{1,5},{13,9},{9,13},{6,2},{2,6},{1... | collective-permute-start | bytes 393224 | tf_op jit(solution)/shard_map/ppermute | solution.py:154
  13.0 9.7 %collective-permute-start.5 = (bf16[512,128]{1,0:T(8,128)(2,1)S(1)}, bf16[512,128]{1,0:T(8,128)(2,1)S(1)}, u32[]{:S(2)}, u32[]{:S(2)}) collective-permute-start(bf16[512,128]{1,0:T(8,128)(2,1)S(1)} %relay.6.refs_9_.refs_4_.refs_8_), channel_id=1, source_target_pairs={{12,0},{8,4},{4,8},{0,12},{13,1},{9,5},{5,9},{1,13},{14,2},{10,6},... | collective-permute-start | bytes 393224 | tf_op jit(solution)/shard_map/ppermute | solution.py:154
  17.2 6.4 %collective-permute-start.4 = (bf16[512,128]{1,0:T(8,128)(2,1)S(1)}, bf16[512,128]{1,0:T(8,128)(2,1)S(1)}, u32[]{:S(2)}, u32[]{:S(2)}) collective-permute-start(bf16[512,128]{1,0:T(8,128)(2,1)S(1)} %relay.5.refs_7_), channel_id=1, source_target_pairs={{4,0},{0,4},{12,8},{8,12},{5,1},{1,5},{13,9},{9,13},{6,2},{2,6},{1... | collective-permute-start | bytes 393224 | tf_op jit(solution)/shard_map/ppermute | solution.py:154
  17.6 6.1 %collective-permute-start = (bf16[512,512]{1,0:T(8,128)(2,1)S(1)}, bf16[512,512]{1,0:T(8,128)(2,1)S(1)}, u32[]{:S(2)}, u32[]{:S(2)}) collective-permute-start(bf16[512,512]{1,0:T(8,128)(2,1)S(1)} %get-tuple-element.9.refs_0_), channel_id=1, source_target_pairs={{1,0},{0,1},{3,2},{2,3},{5,4},{4,5},{7,6},{6,7},{9,8},{8,9},{11,10... | collective-permute-start | bytes 1572872 | tf_op jit(solution)/shard_map/ppermute | solution.py:154
  23.6 1.9 %collective-permute-start.7 = (bf16[512,512]{1,0:T(8,128)(2,1)S(1)}, bf16[512,512]{1,0:T(8,128)(2,1)S(1)}, u32[]{:S(2)}, u32[]{:S(2)}) collective-permute-start(bf16[512,512]{1,0:T(8,128)(2,1)S(1)} %relay.8.refs_2_), channel_id=1, source_target_pairs={{1,0},{0,1},{3,2},{2,3},{5,4},{4,5},{7,6},{6,7},{9,8},{8,9},{11,10... | collective-permute-start | bytes 1572872 | tf_op jit(solution)/shard_map/ppermute | solution.py:154
  23.6 5.9 %collective-permute-start.8 = (bf16[512,128]{1,0:T(8,128)(2,1)S(1)}, bf16[512,128]{1,0:T(8,128)(2,1)S(1)}, u32[]{:S(2)}, u32[]{:S(2)}) collective-permute-start(bf16[512,128]{1,0:T(8,128)(2,1)S(1)} %relay.7.refs_2_.refs_7_), channel_id=1, source_target_pairs={{4,0},{0,4},{12,8},{8,12},{5,1},{1,5},{13,9},{9,13},{6,2},{2,6},{1... | collective-permute-start | bytes 393224 | tf_op jit(solution)/shard_map/ppermute | solution.py:154
  27.3 4.3 %collective-permute-start.9 = (bf16[256,128]{1,0:T(8,128)(2,1)S(1)}, bf16[256,128]{1,0:T(8,128)(2,1)S(1)}, u32[]{:S(2)}, u32[]{:S(2)}) collective-permute-start(bf16[256,128]{1,0:T(8,128)(2,1)S(1)} %get-tuple-element.13), channel_id=1, source_target_pairs={{4,0},{0,4},{12,8},{8,12},{5,1},{1,5},{13,9},{9,13},{6,2},{2,6},{1... | collective-permute-start | bytes 196616 | tf_op jit(solution)/shard_map/ppermute | solution.py:154
  33.2 4.7 %collective-permute-start.11 = (bf16[128,128]{1,0:T(8,128)(2,1)S(1)}, bf16[128,128]{1,0:T(8,128)(2,1)S(1)}, u32[]{:S(2)}, u32[]{:S(2)}) collective-permute-start(bf16[128,128]{1,0:T(8,128)(2,1)S(1)} %get-tuple-element.15), channel_id=1, source_target_pairs={{4,0},{0,4},{12,8},{8,12},{5,1},{1,5},{13,9},{9,13},{6,2},{2,6},{1... | collective-permute-start | bytes 98312 | tf_op jit(solution)/shard_map/ppermute | solution.py:154
  33.5 10.2 %collective-permute-start.10 = (bf16[256,128]{1,0:T(8,128)(2,1)S(1)}, bf16[256,128]{1,0:T(8,128)(2,1)S(1)}, u32[]{:S(2)}, u32[]{:S(2)}) collective-permute-start(bf16[256,128]{1,0:T(8,128)(2,1)S(1)} %add_convert_fusion.refs_0_), channel_id=1, source_target_pairs={{12,0},{8,4},{4,8},{0,12},{13,1},{9,5},{5,9},{1,13},{14,2},{10,6},... | collective-permute-start | bytes 196616 | tf_op jit(solution)/shard_map/ppermute | solution.py:154
  37.9 5.8 %collective-permute-start.12 = (bf16[128,128]{1,0:T(8,128)(2,1)S(1)}, bf16[128,128]{1,0:T(8,128)(2,1)S(1)}, u32[]{:S(2)}, u32[]{:S(2)}) collective-permute-start(bf16[128,128]{1,0:T(8,128)(2,1)S(1)} %add_convert_fusion.1.refs_2_), channel_id=1, source_target_pairs={{12,0},{8,4},{4,8},{0,12},{13,1},{9,5},{5,9},{1,13},{14,2},{10,6},... | collective-permute-start | bytes 98312 | tf_op jit(solution)/shard_map/ppermute | solution.py:154
  39.6 4.1 %copy-start = (f32[1,256,256]{2,1,0:T(8,128)S(1)}, f32[1,256,256]{2,1,0:T(8,128)}, u32[]{:S(2)}) copy-start(f32[1,256,256]{2,1,0:T(8,128)} %diag_ref.1) | copy-start | bytes 786436

commit v6 on v4

--- a/solution.py
+++ b/solution.py
@@ -7,6 +7,7 @@
 from jax.sharding import PartitionSpec as P
 
 PAIR = 2
+HOP_COST = 10**10
 VMEM_LIMIT = 40 * 1024 * 1024
 PARAMS = pltpu.CompilerParams(vmem_limit_bytes=VMEM_LIMIT)
 SMALL = pltpu.CompilerParams(vmem_limit_bytes=1024 * 1024)
@@ -14,6 +15,15 @@
 VMEM = pl.BlockSpec(memory_space=pltpu.VMEM)
 ANY = pl.BlockSpec(memory_space=pl.ANY)
 HBM = pl.BlockSpec(memory_space=pltpu.HBM)
+
+
+def split(value):
+    high = value.astype(jnp.bfloat16)
+    return high, (value - high.astype(jnp.float32)).astype(jnp.bfloat16)
+
+
+def dot(left, right):
+    return jnp.dot(left, right, preferred_element_type=jnp.float32)
 
 
 def panel_kernel(pattern_hbm, cross_hbm, diag_hbm, top_hbm, panel_ref, top_ref, pattern_ref, cross_ref, diag_ref, sems):
@@ -28,12 +38,11 @@
         copy.start()
     pattern_copy.wait()
     diag_copy.wait()
+    diag_high, diag_low = split(diag_ref[0])
     for a in range(blocks):
         loads[a].wait()
-        masked = cross_ref[rows[a], :] * pattern_ref[a].astype(jnp.float32)
-        solved = jnp.dot(
-            masked, diag_ref[0], precision=lax.Precision.HIGHEST, preferred_element_type=jnp.float32
-        )
+        high, low = split(cross_ref[rows[a], :] * pattern_ref[a].astype(jnp.float32))
+        solved = dot(high, diag_high) + (dot(high, diag_low) + dot(low, diag_high))
         panel_ref[rows[a], :] = solved.astype(jnp.bfloat16)
     top_copy.wait()
 
@@ -63,7 +72,7 @@
     del block_ref, gate_ref, out_ref
 
 
-def after(block, gate):
+def after(block, gate, cost=0):
     return pl.pallas_call(
         relay_kernel,
         out_shape=jax.ShapeDtypeStruct(block.shape, block.dtype),
@@ -71,47 +80,77 @@
         out_specs=ANY,
         input_output_aliases={0: 0},
         compiler_params=SMALL,
+        cost_estimate=pl.CostEstimate(flops=cost, bytes_accessed=cost // 256, transcendentals=0),
         name="relay",
     )(block, gate)
 
 
-def product_kernel(n, slots_ref, *refs):
-    tops, panels = refs[:n], refs[n:2 * n]
-    selected_ref, update_ref, panel_buf = refs[2 * n:]
-    for s in range(n):
-        panel_buf[slots_ref[s]] = panels[s][...]
-    total = jnp.dot(tops[0][...], panel_buf[0], preferred_element_type=jnp.float32)
+def partial_kernel(n, slots_ref, *refs):
+    tops, panels = refs[:n], refs[n:n + n // 2 + 1]
+    partial_ref, chosen_ref, turned_ref, panel_buf = refs[n + n // 2 + 1:]
+    places = [0] + list(range(1, n, 2))
+    for place, panel in zip(places, panels):
+        panel_buf[slots_ref[place]] = panel[...]
+    for d, place in enumerate(range(2, n, 2)):
+        slot = slots_ref[place]
+        panel_buf[slot] = jnp.zeros(panel_buf.shape[1:], panel_buf.dtype)
+        for t in range(n):
+            @pl.when(slot == t)
+            def _():
+                chosen_ref[d] = tops[t][...]
+    total = dot(tops[0][...], panel_buf[0])
     for t in range(1, n):
-        total += jnp.dot(tops[t][...], panel_buf[t], preferred_element_type=jnp.float32)
-    selected_ref[...] = total
-    high = total.astype(jnp.bfloat16)
-    low = (total - high.astype(jnp.float32)).astype(jnp.bfloat16)
-    contract = (((0,), (0,)), ((), ()))
-    half = high.shape[1] // 2
-    own = panels[0]
-    upper = lax.dot_general(own[:, :half], high, contract, preferred_element_type=jnp.float32)
-    upper += lax.dot_general(own[:, :half], low, contract, preferred_element_type=jnp.float32)
-    lower = lax.dot_general(own[:, half:], high[:, half:], contract, preferred_element_type=jnp.float32)
-    lower += lax.dot_general(own[:, half:], low[:, half:], contract, preferred_element_type=jnp.float32)
-    update_ref[:, :2 * half] = upper.astype(jnp.bfloat16)
-    update_ref[:, 2 * half:] = lower.astype(jnp.bfloat16)
-
-
-def products(tops, panels, slots):
+        total += dot(tops[t][...], panel_buf[t])
+    partial_ref[...] = total
+    turned_ref[...] = panels[0][...].astype(jnp.float32).T.astype(jnp.bfloat16)
+
+
+def partial_product(tops, panels, slots):
     n = len(tops)
     rows, width = panels[0].shape
     return pl.pallas_call(
-        functools.partial(product_kernel, n),
+        functools.partial(partial_kernel, n),
+        out_shape=(
+            jax.ShapeDtypeStruct((rows, width), jnp.float32),
+            jax.ShapeDtypeStruct((n // 2 - 1,) + tops[0].shape, jnp.bfloat16),
+            jax.ShapeDtypeStruct((width, rows), jnp.bfloat16),
+        ),
+        in_specs=[SMEM] + [VMEM] * (n + len(panels)),
+        out_specs=(VMEM, VMEM, VMEM),
+        scratch_shapes=[pltpu.VMEM((n, rows, width), jnp.bfloat16)],
+        compiler_params=PARAMS,
+        cost_estimate=pl.CostEstimate(
+            flops=2 * n * rows * rows * width, bytes_accessed=2 * n * rows * (rows + width), transcendentals=0
+        ),
+        name="partial",
+    )(slots, *tops, *panels)
+
+
+def product_kernel(partial_ref, chosen_ref, turned_ref, *refs):
+    panels, (selected_ref, update_ref) = refs[:-2], refs[-2:]
+    total = partial_ref[...]
+    for d, panel in enumerate(panels):
+        total += dot(chosen_ref[d], panel[...])
+    selected_ref[...] = total
+    rounded = total.astype(jnp.bfloat16)
+    half = rounded.shape[1] // 2
+    update_ref[:, :2 * half] = dot(turned_ref[:half], rounded).astype(jnp.bfloat16)
+    update_ref[:, 2 * half:] = dot(turned_ref[half:], rounded[:, half:]).astype(jnp.bfloat16)
+
+
+def products(partial, chosen, turned, panels):
+    rows, width = panels[0].shape
+    return pl.pallas_call(
+        product_kernel,
         out_shape=(
             jax.ShapeDtypeStruct((rows, width), jnp.float32),
             jax.ShapeDtypeStruct((width // 2, 3 * (width // 2)), jnp.bfloat16),
         ),
-        in_specs=[SMEM] + [VMEM] * (2 * n),
+        in_specs=[VMEM] * (3 + len(panels)),
         out_specs=(VMEM, VMEM),
-        scratch_shapes=[pltpu.VMEM((n, rows, width), jnp.bfloat16)],
         compiler_params=PARAMS,
         name="products",
-    )(slots, *tops, *panels)
+    )(partial, chosen, turned, *panels)
 
 
 def finish_kernel(diag_ref, *refs):
@@ -150,17 +189,15 @@
         return from_pair(block, axis, 0, 1)
 
     factor_panel, inverse_top = build_panel(cross_blocks, diag_inverse, pattern, inverse_top)
+    beside = mate(factor_panel, "prow")
     crossed = [from_pair(factor_panel, "prow", d, 1) for d in range(1, pairs)]
-    beside = mate(factor_panel, "prow")
-    panels = [factor_panel, beside]
-    for block in crossed:
-        block = after(block, beside)
-        panels += [mate(block, "prow"), block]
+    crossed = [after(block, beside, HOP_COST) for block in crossed]
+    swapped = [mate(block, "prow") for block in crossed]
 
     near = [from_pair(inverse_top, "pcol", d, 0) for d in range(1, pairs)]
     tops = [inverse_top, mate(inverse_top, "pcol")]
     for block in near:
-        block = after(block, beside)
+        block = after(block, crossed[-1])
         tops += [block, mate(block, "pcol")]
 
     place = jnp.arange(n, dtype=jnp.int32)
@@ -168,7 +205,8 @@
     wanted_side = (row % PAIR) ^ (place % PAIR)
     slots = ((wanted_pair - col // PAIR) % pairs) * PAIR + (wanted_side ^ (col % PAIR))
 
-    selected, update = products(tops, panels, slots)
+    parts = partial_product(tops, [factor_panel, beside] + crossed, slots)
+    selected, update = products(*parts, swapped)
     paired = (update.astype(jnp.float32) + mate(update, "prow").astype(jnp.float32)).astype(jnp.bfloat16)
     updates = [paired] + [from_pair(paired, "prow", d, 1) for d in range(1, pairs)]
     return -selected, finish(diag_inverse, updates)

time: 42.1 us -> 42.6 us (1.012)
  waiting for transfers between devices: 24.2 us -> 26.4 us
  starting transfers between devices: 11.5 us -> 9.9 us
    ppermute x8, waiting for transfers between devices: 24.2 us -> 26.4 us  [from_pair(): return lax.ppermute(block, axis, moves)]
    ppermute x8, starting transfers between devices: 11.5 us -> 9.9 us  [from_pair(): return lax.ppermute(block, axis, moves)]
    pallas_call x1 -> x2, Pallas kernels: 1.82 us -> 1.95 us  [the longest x1 1.36 us: partial_product(): pl.pallas_call(functools.partial(partial_kernel, n), out_shape=(jax.Shape...]
  transfers between devices with their start and end apart: 8 -> 8, of which waited for: 6 -> 7; matrix products, arithmetic and copies ran while one was open for 2% -> 2% of each run, Pallas kernels for 0% -> 3%
where the time goes in v6:
time: 42.6 us; the launch traced here: 42.4 us
  waiting for transfers between devices  26.4 us (62%)
  starting transfers between devices  9.9 us (23%)
  Pallas kernels  4.53 us (11%)
  other arithmetic  0.88 us (2%)
  between operations  0.67 us (2%)
    ppermute x8, waiting for transfers between devices, from_pair(): return lax.ppermute(block, axis, moves)  26.4 us
    ppermute x8, starting transfers between devices, from_pair(): return lax.ppermute(block, axis, moves)  9.9 us
    pallas_call x1, Pallas kernels, build_panel(): pl.pallas_call(panel_kernel, out_shape=(pltpu.VMEM(cross_blocks.shape, jn...  1.78 us
    pallas_call x1, Pallas kernels, partial_product(): pl.pallas_call(functools.partial(partial_kernel, n), out_shape=(jax.Shape...  1.36 us
  transfers between devices with their start and end apart: 8, of which 7 were waited for; matrix products, arithmetic and copies ran while one was open for 2% of the time, Pallas kernels for 3%

profile of v6, /device:TPU:0, one launch (start us, length us, event | category | flops | bytes accessed | tf_op | source)
XLA Modules:
  0.0 42.4 jit_solution(11265694497428299291)
XLA Ops:
  0.6 1.8 %panel.1 = (bf16[512,256]{1,0:T(8,128)(2,1)S(1)}, bf16[512,512]{1,0:T(8,128)(2,1)S(1)}) custom-call(s32[2]{0:T(128)} %bitcast.1, f32[512,256]{1,0:T(8,128)} %cross_hbm.1, f32[1,256,256]{2,1,0:T(8,128)} %diag_ref.1, bf16[512,512]{1,0:T(8,128)(2,1)} %top_hbm.1), custom_call_target="tpu_custom_call" | custom-call | tf_op jit(solution)/shard_map/panel/pallas_call | solution.py:52
  2.4 3.1 %collective-permute-start.3 = (bf16[512,256]{1,0:T(8,128)(2,1)S(1)}, bf16[512,256]{1,0:T(8,128)(2,1)S(1)}, u32[]{:S(2)}, u32[]{:S(2)}) collective-permute-start(bf16[512,256]{1,0:T(8,128)(2,1)S(1)} %get-tuple-element.10.refs_4_), channel_id=1, source_target_pairs={{4,0},{0,4},{12,8},{8,12},{5,1},{1,5},{13,9},{9,13},{6,2},{2,6},{1... | collective-permute-start | bytes 786440 | tf_op jit(solution)/shard_map/ppermute | solution.py:186
  5.5 2.5 %collective-permute-start.2 = (bf16[512,256]{1,0:T(8,128)(2,1)S(1)}, bf16[512,256]{1,0:T(8,128)(2,1)S(1)}, u32[]{:S(2)}, u32[]{:S(2)}) collective-permute-start(bf16[512,256]{1,0:T(8,128)(2,1)S(1)} %get-tuple-element.10.refs_4_), channel_id=1, source_target_pairs={{12,0},{8,4},{4,8},{0,12},{13,1},{9,5},{5,9},{1,13},{14,2},{10,6},... | collective-permute-start | bytes 786440 | tf_op jit(solution)/shard_map/ppermute | solution.py:186
  8.0 1.5 %collective-permute-start.1 = (bf16[512,512]{1,0:T(8,128)(2,1)S(1)}, bf16[512,512]{1,0:T(8,128)(2,1)S(1)}, u32[]{:S(2)}, u32[]{:S(2)}) collective-permute-start(bf16[512,512]{1,0:T(8,128)(2,1)S(1)} %get-tuple-element.9.refs_0_), channel_id=1, source_target_pairs={{2,0},{3,1},{0,2},{1,3},{6,4},{7,5},{4,6},{5,7},{10,8},{11,9},{8,1... | collective-permute-start | bytes 1572872 | tf_op jit(solution)/shard_map/ppermute | solution.py:186
  9.5 0.0 collective-permute-start
  9.5 2.7 %collective-permute-done.3.gate_ref.refs_5_ = bf16[512,256]{1,0:T(8,128)(2,1)S(1)} collective-permute-done((bf16[512,256]{1,0:T(8,128)(2,1)S(1)}, bf16[512,256]{1,0:T(8,128)(2,1)S(1)}, u32[]{:S(2)}, u32[]{:S(2)}) %collective-permute-start.3) | collective-permute-done | bytes 262176 | tf_op jit(solution)/shard_map/ppermute | solution.py:186
  12.2 7.5 %collective-permute-done.2.block_ref = bf16[512,256]{1,0:T(8,128)(2,1)S(1)} collective-permute-done((bf16[512,256]{1,0:T(8,128)(2,1)S(1)}, bf16[512,256]{1,0:T(8,128)(2,1)S(1)}, u32[]{:S(2)}, u32[]{:S(2)}) %collective-permute-start.2) | collective-permute-done | bytes 262176 | tf_op jit(solution)/shard_map/ppermute | solution.py:186
  19.7 1.4 %collective-permute-done.1.block_ref = bf16[512,512]{1,0:T(8,128)(2,1)S(1)} collective-permute-done((bf16[512,512]{1,0:T(8,128)(2,1)S(1)}, bf16[512,512]{1,0:T(8,128)(2,1)S(1)}, u32[]{:S(2)}, u32[]{:S(2)}) %collective-permute-start.1) | collective-permute-done | bytes 524320 | tf_op jit(solution)/shard_map/ppermute | solution.py:186
  21.1 0.0 collective-permute-start.4
  21.1 0.7 %collective-permute-start.5 = (bf16[512,256]{1,0:T(8,128)(2,1)S(1)}, bf16[512,256]{1,0:T(8,128)(2,1)S(1)}, u32[]{:S(2)}, u32[]{:S(2)}) collective-permute-start(bf16[512,256]{1,0:T(8,128)(2,1)S(1)} %relay.2.gate_ref.refs_6_), channel_id=1, source_target_pairs={{4,0},{0,4},{12,8},{8,12},{5,1},{1,5},{13,9},{9,13},{6,2},{2,6},{1... | collective-permute-start | bytes 786440 | tf_op jit(solution)/shard_map/ppermute | solution.py:186
  21.8 0.0 collective-permute-done.refs_1_
  21.8 1.2 %collective-permute-done.4.refs_3_ = bf16[512,512]{1,0:T(8,128)(2,1)S(1)} collective-permute-done((bf16[512,512]{1,0:T(8,128)(2,1)S(1)}, bf16[512,512]{1,0:T(8,128)(2,1)S(1)}, u32[]{:S(2)}, u32[]{:S(2)}) %collective-permute-start.4) | collective-permute-done | bytes 524320 | tf_op jit(solution)/shard_map/ppermute | solution.py:186
  23.0 1.4 %partial.1 = (f32[512,256]{1,0:T(8,128)S(1)}, bf16[1,512,512]{2,1,0:T(8,128)(2,1)S(1)}, bf16[256,512]{1,0:T(8,128)(2,1)S(1)}) custom-call(s32[4]{0:T(128)S(1)} %fusion.2.slots_ref, bf16[512,512]{1,0:T(8,128)(2,1)S(1)} %get-tuple-element.9.refs_0_, bf16[512,512]{1,0:T(8,128)(2,1)S(1)} %collective-permute-done.refs_1_, bf16[512,512]{1,0:T(8,128)(2,1)S(1)} %relay.3.refs_2_, ...), custom_call_target="tpu_custom_call" | custom-call | flops 536870912 | bytes 3145728 | tf_op jit(solution)/shard_map/partial/pallas_call | solution.py:111
  24.4 5.4 %collective-permute-done.5.refs_0_ = bf16[512,256]{1,0:T(8,128)(2,1)S(1)} collective-permute-done((bf16[512,256]{1,0:T(8,128)(2,1)S(1)}, bf16[512,256]{1,0:T(8,128)(2,1)S(1)}, u32[]{:S(2)}, u32[]{:S(2)}) %collective-permute-start.5) | collective-permute-done | bytes 262176 | tf_op jit(solution)/shard_map/ppermute | solution.py:186
  29.8 0.6 %products.1 = (f32[512,256]{1,0:T(8,128)S(1)}, bf16[128,384]{1,0:T(8,128)(2,1)S(1)}) custom-call(f32[512,256]{1,0:T(8,128)S(1)} %get-tuple-element.11.partial_ref, bf16[1,512,512]{2,1,0:T(8,128)(2,1)S(1)} %get-tuple-element.12.chosen_ref, bf16[256,512]{1,0:T(8,128)(2,1)S(1)} %get-tuple-element.13.turned_ref, bf16[512,256]{1,0:T(8,128)(2,1)S(1)} %collective-permute-done.5.refs_0_), custom_call_target="tpu_custom_call" | custom-call | tf_op jit(solution)/shard_map/products/pallas_call | solution.py:143
  30.4 0.7 %collective-permute-start.6 = (bf16[128,384]{1,0:T(8,128)(2,1)S(1)}, bf16[128,384]{1,0:T(8,128)(2,1)S(1)}, u32[]{:S(2)}, u32[]{:S(2)}) collective-permute-start(bf16[128,384]{1,0:T(8,128)(2,1)S(1)} %get-tuple-element.15), channel_id=1, source_target_pairs={{4,0},{0,4},{12,8},{8,12},{5,1},{1,5},{13,9},{9,13},{6,2},{2,6},{1... | collective-permute-start | bytes 294920 | tf_op jit(solution)/shard_map/ppermute | solution.py:186
  31.1 3.9 %collective-permute-done.6 = bf16[128,384]{1,0:T(8,128)(2,1)S(1)} collective-permute-done((bf16[128,384]{1,0:T(8,128)(2,1)S(1)}, bf16[128,384]{1,0:T(8,128)(2,1)S(1)}, u32[]{:S(2)}, u32[]{:S(2)}) %collective-permute-start.6) | collective-permute-done | bytes 98336 | tf_op jit(solution)/shard_map/ppermute | solution.py:186
  35.1 1.4 %collective-permute-start.7 = (bf16[128,384]{1,0:T(8,128)(2,1)S(1)}, bf16[128,384]{1,0:T(8,128)(2,1)S(1)}, u32[]{:S(2)}, u32[]{:S(2)}) collective-permute-start(bf16[128,384]{1,0:T(8,128)(2,1)S(1)} %add_convert_fusion.refs_0_), channel_id=1, source_target_pairs={{12,0},{8,4},{4,8},{0,12},{13,1},{9,5},{5,9},{1,13},{14,2},{10,6},... | collective-permute-start | bytes 294920 | tf_op jit(solution)/shard_map/ppermute | solution.py:186
  36.5 0.0 copy-start
  36.5 0.8 %neg.3 = f32[512,256]{1,0:T(8,128)} negate(f32[512,256]{1,0:T(8,128)S(1)} %get-tuple-element.14) | non-fusion elementwise | flops 131072 | bytes 1048576 | tf_op jit(solution)/shard_map/neg | solution.py:212
  37.4 4.2 %collective-permute-done.7.refs_1_ = bf16[128,384]{1,0:T(8,128)(2,1)S(1)} collective-permute-done((bf16[128,384]{1,0:T(8,128)(2,1)S(1)}, bf16[128,384]{1,0:T(8,128)(2,1)S(1)}, u32[]{:S(2)}, u32[]{:S(2)}) %collective-permute-start.7) | collective-permute-done | bytes 98336 | tf_op jit(solution)/shard_map/ppermute | solution.py:186
  41.6 0.0 copy-done
  41.6 0.8 %finish.1 = f32[1,256,256]{2,1,0:T(8,128)} custom-call(f32[1,256,256]{2,1,0:T(8,128)S(1)} %copy-done, bf16[128,384]{1,0:T(8,128)(2,1)S(1)} %add_convert_fusion.refs_0_, bf16[128,384]{1,0:T(8,128)(2,1)S(1)} %collective-permute-done.7.refs_1_), custom_call_target="tpu_custom_call" | custom-call | tf_op jit(solution)/shard_map/finish/pallas_call | solution.py:168
  (4 shorter events, 0.0 us)
Async XLA Ops:
  2.4 9.8 %collective-permute-start.3 = (bf16[512,256]{1,0:T(8,128)(2,1)S(1)}, bf16[512,256]{1,0:T(8,128)(2,1)S(1)}, u32[]{:S(2)}, u32[]{:S(2)}) collective-permute-start(bf16[512,256]{1,0:T(8,128)(2,1)S(1)} %get-tuple-element.10.refs_4_), channel_id=1, source_target_pairs={{4,0},{0,4},{12,8},{8,12},{5,1},{1,5},{13,9},{9,13},{6,2},{2,6},{1... | collective-permute-start | bytes 786440 | tf_op jit(solution)/shard_map/ppermute | solution.py:186
  5.5 14.2 %collective-permute-start.2 = (bf16[512,256]{1,0:T(8,128)(2,1)S(1)}, bf16[512,256]{1,0:T(8,128)(2,1)S(1)}, u32[]{:S(2)}, u32[]{:S(2)}) collective-permute-start(bf16[512,256]{1,0:T(8,128)(2,1)S(1)} %get-tuple-element.10.refs_4_), channel_id=1, source_target_pairs={{12,0},{8,4},{4,8},{0,12},{13,1},{9,5},{5,9},{1,13},{14,2},{10,6},... | collective-permute-start | bytes 786440 | tf_op jit(solution)/shard_map/ppermute | solution.py:186
  8.0 13.1 %collective-permute-start.1 = (bf16[512,512]{1,0:T(8,128)(2,1)S(1)}, bf16[512,512]{1,0:T(8,128)(2,1)S(1)}, u32[]{:S(2)}, u32[]{:S(2)}) collective-permute-start(bf16[512,512]{1,0:T(8,128)(2,1)S(1)} %get-tuple-element.9.refs_0_), channel_id=1, source_target_pairs={{2,0},{3,1},{0,2},{1,3},{6,4},{7,5},{4,6},{5,7},{10,8},{11,9},{8,1... | collective-permute-start | bytes 1572872 | tf_op jit(solution)/shard_map/ppermute | solution.py:186
  9.5 12.3 %collective-permute-start = (bf16[512,512]{1,0:T(8,128)(2,1)S(1)}, bf16[512,512]{1,0:T(8,128)(2,1)S(1)}, u32[]{:S(2)}, u32[]{:S(2)}) collective-permute-start(bf16[512,512]{1,0:T(8,128)(2,1)S(1)} %get-tuple-element.9.refs_0_), channel_id=1, source_target_pairs={{1,0},{0,1},{3,2},{2,3},{5,4},{4,5},{7,6},{6,7},{9,8},{8,9},{11,10... | collective-permute-start | bytes 1572872 | tf_op jit(solution)/shard_map/ppermute | solution.py:186
  21.1 1.9 %collective-permute-start.4 = (bf16[512,512]{1,0:T(8,128)(2,1)S(1)}, bf16[512,512]{1,0:T(8,128)(2,1)S(1)}, u32[]{:S(2)}, u32[]{:S(2)}) collective-permute-start(bf16[512,512]{1,0:T(8,128)(2,1)S(1)} %relay.3.refs_2_), channel_id=1, source_target_pairs={{1,0},{0,1},{3,2},{2,3},{5,4},{4,5},{7,6},{6,7},{9,8},{8,9},{11,10... | collective-permute-start | bytes 1572872 | tf_op jit(solution)/shard_map/ppermute | solution.py:186
  21.1 8.7 %collective-permute-start.5 = (bf16[512,256]{1,0:T(8,128)(2,1)S(1)}, bf16[512,256]{1,0:T(8,128)(2,1)S(1)}, u32[]{:S(2)}, u32[]{:S(2)}) collective-permute-start(bf16[512,256]{1,0:T(8,128)(2,1)S(1)} %relay.2.gate_ref.refs_6_), channel_id=1, source_target_pairs={{4,0},{0,4},{12,8},{8,12},{5,1},{1,5},{13,9},{9,13},{6,2},{2,6},{1... | collective-permute-start | bytes 786440 | tf_op jit(solution)/shard_map/ppermute | solution.py:186
  30.4 4.7 %collective-permute-start.6 = (bf16[128,384]{1,0:T(8,128)(2,1)S(1)}, bf16[128,384]{1,0:T(8,128)(2,1)S(1)}, u32[]{:S(2)}, u32[]{:S(2)}) collective-permute-start(bf16[128,384]{1,0:T(8,128)(2,1)S(1)} %get-tuple-element.15), channel_id=1, source_target_pairs={{4,0},{0,4},{12,8},{8,12},{5,1},{1,5},{13,9},{9,13},{6,2},{2,6},{1... | collective-permute-start | bytes 294920 | tf_op jit(solution)/shard_map/ppermute | solution.py:186
  35.1 6.5 %collective-permute-start.7 = (bf16[128,384]{1,0:T(8,128)(2,1)S(1)}, bf16[128,384]{1,0:T(8,128)(2,1)S(1)}, u32[]{:S(2)}, u32[]{:S(2)}) collective-permute-start(bf16[128,384]{1,0:T(8,128)(2,1)S(1)} %add_convert_fusion.refs_0_), channel_id=1, source_target_pairs={{12,0},{8,4},{4,8},{0,12},{13,1},{9,5},{5,9},{1,13},{14,2},{10,6},... | collective-permute-start | bytes 294920 | tf_op jit(solution)/shard_map/ppermute | solution.py:186
  36.5 5.1 %copy-start = (f32[1,256,256]{2,1,0:T(8,128)S(1)}, f32[1,256,256]{2,1,0:T(8,128)}, u32[]{:S(2)}) copy-start(f32[1,256,256]{2,1,0:T(8,128)} %diag_ref.1) | copy-start | bytes 786436

commit v7 on v6

--- a/solution.py
+++ b/solution.py
@@ -85,9 +85,15 @@
     )(block, gate)
 
 
+def store_upper(out_ref, update):
+    half = update.shape[0] // 2
+    out_ref[:, :2 * half] = update[:half].astype(jnp.bfloat16)
+    out_ref[:, 2 * half:] = update[half:, half:].astype(jnp.bfloat16)
+
+
 def partial_kernel(n, slots_ref, *refs):
     tops, panels = refs[:n], refs[n:n + n // 2 + 1]
-    partial_ref, chosen_ref, turned_ref, panel_buf = refs[n + n // 2 + 1:]
+    partial_ref, chosen_ref, turned_ref, update_ref, panel_buf = refs[n + n // 2 + 1:]
     places = [0] + list(range(1, n, 2))
     for place, panel in zip(places, panels):
         panel_buf[slots_ref[place]] = panel[...]
@@ -102,7 +108,9 @@
     for t in range(1, n):
         total += dot(tops[t][...], panel_buf[t])
     partial_ref[...] = total
-    turned_ref[...] = panels[0][...].astype(jnp.float32).T.astype(jnp.bfloat16)
+    turned = panels[0][...].astype(jnp.float32).T.astype(jnp.bfloat16)
+    turned_ref[...] = turned
+    store_upper(update_ref, dot(turned, total.astype(jnp.bfloat16)))
 
 
 def partial_product(tops, panels, slots):
@@ -114,9 +122,10 @@
             jax.ShapeDtypeStruct((rows, width), jnp.float32),
             jax.ShapeDtypeStruct((n // 2 - 1,) + tops[0].shape, jnp.bfloat16),
             jax.ShapeDtypeStruct((width, rows), jnp.bfloat16),
+            jax.ShapeDtypeStruct((width // 2, 3 * (width // 2)), jnp.bfloat16),
         ),
         in_specs=[SMEM] + [VMEM] * (n + len(panels)),
-        out_specs=(VMEM, VMEM, VMEM),
+        out_specs=(VMEM, VMEM, VMEM, VMEM),
         scratch_shapes=[pltpu.VMEM((n, rows, width), jnp.bfloat16)],
         compiler_params=PARAMS,
         cost_estimate=pl.CostEstimate(
@@ -126,22 +135,22 @@
     )(slots, *tops, *panels)
 
 
-def product_kernel(partial_ref, chosen_ref, turned_ref, *refs):
+def product_kernel(alone, partial_ref, chosen_ref, turned_ref, *refs):
     panels, (selected_ref, update_ref) = refs[:-2], refs[-2:]
-    total = partial_ref[...]
-    for d, panel in enumerate(panels):
-        total += dot(chosen_ref[d], panel[...])
-    selected_ref[...] = total
-    rounded = total.astype(jnp.bfloat16)
-    half = rounded.shape[1] // 2
-    update_ref[:, :2 * half] = dot(turned_ref[:half], rounded).astype(jnp.bfloat16)
-    update_ref[:, 2 * half:] = dot(turned_ref[half:], rounded[:, half:]).astype(jnp.bfloat16)
+    rest = dot(chosen_ref[0], panels[0][...])
+    for d, panel in enumerate(panels[1:], 1):
+        rest += dot(chosen_ref[d], panel[...])
+    selected_ref[...] = partial_ref[...] + rest
+    update = dot(turned_ref[...], rest.astype(jnp.bfloat16))
+    if alone:
+        update += update.T
+    store_upper(update_ref, update)
 
 
 def products(partial, chosen, turned, panels):
     rows, width = panels[0].shape
     return pl.pallas_call(
-        product_kernel,
+        functools.partial(product_kernel, len(panels) == 1),
         out_shape=(
             jax.ShapeDtypeStruct((rows, width), jnp.float32),
             jax.ShapeDtypeStruct((width // 2, 3 * (width // 2)), jnp.bfloat16),
@@ -205,10 +214,17 @@
     wanted_side = (row % PAIR) ^ (place % PAIR)
     slots = ((wanted_pair - col // PAIR) % pairs) * PAIR + (wanted_side ^ (col % PAIR))
 
-    parts = partial_product(tops, [factor_panel, beside] + crossed, slots)
-    selected, update = products(*parts, swapped)
-    paired = (update.astype(jnp.float32) + mate(update, "prow").astype(jnp.float32)).astype(jnp.bfloat16)
-    updates = [paired] + [from_pair(paired, "prow", d, 1) for d in range(1, pairs)]
+    partial, chosen, turned, early = partial_product(tops, [factor_panel, beside] + crossed, slots)
+    arrived = after(mate(early, "prow"), swapped[-1])
+    early = (early.astype(jnp.float32) + arrived.astype(jnp.float32)).astype(jnp.bfloat16)
+    updates = [early] + [after(from_pair(early, "prow", d, 1), early, HOP_COST) for d in range(1, pairs)]
+
+    swapped = [after(block, early) for block in swapped]
+    selected, late = products(partial, chosen, turned, swapped)
+    if pairs > 2:
+        parts = [late] + [from_pair(late, "prow", d, 0) for d in range(1, pairs)]
+        late = functools.reduce(jnp.add, [part.astype(jnp.float32) for part in parts]).astype(jnp.bfloat16)
+    updates += [late, mate(late, "prow")]
     return -selected, finish(diag_inverse, updates)
 
 

time: 42.6 us -> 41.3 us (0.969)
  waiting for transfers between devices: 26.4 us -> 24.8 us
    ppermute x8 -> x9, waiting for transfers between devices: 26.4 us -> 24.8 us  [from_pair(): return lax.ppermute(block, axis, moves)]
    ppermute x8 -> x9, starting transfers between devices: 9.9 us -> 9.97 us  [from_pair(): return lax.ppermute(block, axis, moves)]
  transfers between devices with their start and end apart: 8 -> 9, of which waited for: 7 -> 8; matrix products, arithmetic and copies ran while one was open for 2% -> 2% of each run, Pallas kernels for 3% -> 5%
where the time goes in v7:
time: 41.3 us; the launch traced here: 41.1 us
  waiting for transfers between devices  24.8 us (60%)
  starting transfers between devices  9.97 us (24%)
  Pallas kernels  4.83 us (12%)
  other arithmetic  0.88 us (2%)
  between operations  0.68 us (2%)
    ppermute x9, waiting for transfers between devices, from_pair(): return lax.ppermute(block, axis, moves)  24.8 us
    ppermute x9, starting transfers between devices, from_pair(): return lax.ppermute(block, axis, moves)  9.97 us
    pallas_call x1, Pallas kernels, build_panel(): pl.pallas_call(panel_kernel, out_shape=(pltpu.VMEM(cross_blocks.shape, jn...  1.78 us
    pallas_call x1, Pallas kernels, partial_product(): pl.pallas_call(functools.partial(partial_kernel, n), out_shape=(jax.Shape...  1.61 us
    neg x1, other arithmetic, on_device(): return (-selected, finish(diag_inverse, updates))  0.83 us
  transfers between devices with their start and end apart: 9, of which 8 were waited for; matrix products, arithmetic and copies ran while one was open for 2% of the time, Pallas kernels for 5%

profile of v7, /device:TPU:0, one launch (start us, length us, event | category | flops | bytes accessed | tf_op | source)
XLA Modules:
  0.0 41.1 jit_solution(8456728317879845827)
XLA Ops:
  0.6 1.8 %panel.1 = (bf16[512,256]{1,0:T(8,128)(2,1)S(1)}, bf16[512,512]{1,0:T(8,128)(2,1)S(1)}) custom-call(s32[2]{0:T(128)} %bitcast.1, f32[512,256]{1,0:T(8,128)} %cross_hbm.1, f32[1,256,256]{2,1,0:T(8,128)} %diag_ref.1, bf16[512,512]{1,0:T(8,128)(2,1)} %top_hbm.1), custom_call_target="tpu_custom_call" | custom-call | tf_op jit(solution)/shard_map/panel/pallas_call | solution.py:52
  2.4 3.1 %collective-permute-start.3 = (bf16[512,256]{1,0:T(8,128)(2,1)S(1)}, bf16[512,256]{1,0:T(8,128)(2,1)S(1)}, u32[]{:S(2)}, u32[]{:S(2)}) collective-permute-start(bf16[512,256]{1,0:T(8,128)(2,1)S(1)} %get-tuple-element.11.refs_4_), channel_id=1, source_target_pairs={{4,0},{0,4},{12,8},{8,12},{5,1},{1,5},{13,9},{9,13},{6,2},{2,6},{1... | collective-permute-start | bytes 786440 | tf_op jit(solution)/shard_map/ppermute | solution.py:195
  5.5 2.5 %collective-permute-start.2 = (bf16[512,256]{1,0:T(8,128)(2,1)S(1)}, bf16[512,256]{1,0:T(8,128)(2,1)S(1)}, u32[]{:S(2)}, u32[]{:S(2)}) collective-permute-start(bf16[512,256]{1,0:T(8,128)(2,1)S(1)} %get-tuple-element.11.refs_4_), channel_id=1, source_target_pairs={{12,0},{8,4},{4,8},{0,12},{13,1},{9,5},{5,9},{1,13},{14,2},{10,6},... | collective-permute-start | bytes 786440 | tf_op jit(solution)/shard_map/ppermute | solution.py:195
  8.0 1.5 %collective-permute-start.1 = (bf16[512,512]{1,0:T(8,128)(2,1)S(1)}, bf16[512,512]{1,0:T(8,128)(2,1)S(1)}, u32[]{:S(2)}, u32[]{:S(2)}) collective-permute-start(bf16[512,512]{1,0:T(8,128)(2,1)S(1)} %get-tuple-element.10.refs_0_), channel_id=1, source_target_pairs={{2,0},{3,1},{0,2},{1,3},{6,4},{7,5},{4,6},{5,7},{10,8},{11,9},{8,1... | collective-permute-start | bytes 1572872 | tf_op jit(solution)/shard_map/ppermute | solution.py:195
  9.5 0.0 collective-permute-start
  9.5 2.7 %collective-permute-done.3.gate_ref.refs_5_ = bf16[512,256]{1,0:T(8,128)(2,1)S(1)} collective-permute-done((bf16[512,256]{1,0:T(8,128)(2,1)S(1)}, bf16[512,256]{1,0:T(8,128)(2,1)S(1)}, u32[]{:S(2)}, u32[]{:S(2)}) %collective-permute-start.3) | collective-permute-done | bytes 262176 | tf_op jit(solution)/shard_map/ppermute | solution.py:195
  12.2 7.5 %collective-permute-done.2.block_ref = bf16[512,256]{1,0:T(8,128)(2,1)S(1)} collective-permute-done((bf16[512,256]{1,0:T(8,128)(2,1)S(1)}, bf16[512,256]{1,0:T(8,128)(2,1)S(1)}, u32[]{:S(2)}, u32[]{:S(2)}) %collective-permute-start.2) | collective-permute-done | bytes 262176 | tf_op jit(solution)/shard_map/ppermute | solution.py:195
  19.7 1.4 %collective-permute-done.1.block_ref = bf16[512,512]{1,0:T(8,128)(2,1)S(1)} collective-permute-done((bf16[512,512]{1,0:T(8,128)(2,1)S(1)}, bf16[512,512]{1,0:T(8,128)(2,1)S(1)}, u32[]{:S(2)}, u32[]{:S(2)}) %collective-permute-start.1) | collective-permute-done | bytes 524320 | tf_op jit(solution)/shard_map/ppermute | solution.py:195
  21.1 0.0 collective-permute-start.4
  21.1 0.7 %collective-permute-start.5 = (bf16[512,256]{1,0:T(8,128)(2,1)S(1)}, bf16[512,256]{1,0:T(8,128)(2,1)S(1)}, u32[]{:S(2)}, u32[]{:S(2)}) collective-permute-start(bf16[512,256]{1,0:T(8,128)(2,1)S(1)} %relay.5.gate_ref.refs_6_), channel_id=1, source_target_pairs={{4,0},{0,4},{12,8},{8,12},{5,1},{1,5},{13,9},{9,13},{6,2},{2,6},{1... | collective-permute-start | bytes 786440 | tf_op jit(solution)/shard_map/ppermute | solution.py:195
  21.8 0.0 collective-permute-done.refs_1_
  21.8 1.2 %collective-permute-done.4.refs_3_ = bf16[512,512]{1,0:T(8,128)(2,1)S(1)} collective-permute-done((bf16[512,512]{1,0:T(8,128)(2,1)S(1)}, bf16[512,512]{1,0:T(8,128)(2,1)S(1)}, u32[]{:S(2)}, u32[]{:S(2)}) %collective-permute-start.4) | collective-permute-done | bytes 524320 | tf_op jit(solution)/shard_map/ppermute | solution.py:195
  23.0 1.6 %partial.1 = (f32[512,256]{1,0:T(8,128)S(1)}, bf16[1,512,512]{2,1,0:T(8,128)(2,1)S(1)}, bf16[256,512]{1,0:T(8,128)(2,1)S(1)}, bf16[128,384]{1,0:T(8,128)(2,1)S(1)}) custom-call(s32[4]{0:T(128)S(1)} %fusion.2.slots_ref, bf16[512,512]{1,0:T(8,128)(2,1)S(1)} %get-tuple-element.10.refs_0_, bf16[512,512]{1,0:T(8,128)(2,1)S(1)} %collective-permute-done.refs_1_, ...), custom_call_target="tpu_custom_call" | custom-call | flops 536870912 | bytes 3145728 | tf_op jit(solution)/shard_map/partial/pallas_call | solution.py:119
  24.6 0.7 %collective-permute-start.6 = (bf16[128,384]{1,0:T(8,128)(2,1)S(1)}, bf16[128,384]{1,0:T(8,128)(2,1)S(1)}, u32[]{:S(2)}, u32[]{:S(2)}) collective-permute-start(bf16[128,384]{1,0:T(8,128)(2,1)S(1)} %get-tuple-element.15), channel_id=1, source_target_pairs={{4,0},{0,4},{12,8},{8,12},{5,1},{1,5},{13,9},{9,13},{6,2},{2,6},{1... | collective-permute-start | bytes 294920 | tf_op jit(solution)/shard_map/ppermute | solution.py:195
  25.4 4.8 %collective-permute-done.5.gate_ref.block_ref = bf16[512,256]{1,0:T(8,128)(2,1)S(1)} collective-permute-done((bf16[512,256]{1,0:T(8,128)(2,1)S(1)}, bf16[512,256]{1,0:T(8,128)(2,1)S(1)}, u32[]{:S(2)}, u32[]{:S(2)}) %collective-permute-start.5) | collective-permute-done | bytes 262176 | tf_op jit(solution)/shard_map/ppermute | solution.py:195
  30.2 1.7 %collective-permute-done.6.block_ref = bf16[128,384]{1,0:T(8,128)(2,1)S(1)} collective-permute-done((bf16[128,384]{1,0:T(8,128)(2,1)S(1)}, bf16[128,384]{1,0:T(8,128)(2,1)S(1)}, u32[]{:S(2)}, u32[]{:S(2)}) %collective-permute-start.6) | collective-permute-done | bytes 98336 | tf_op jit(solution)/shard_map/ppermute | solution.py:195
  31.9 1.4 %collective-permute-start.7 = (bf16[128,384]{1,0:T(8,128)(2,1)S(1)}, bf16[128,384]{1,0:T(8,128)(2,1)S(1)}, u32[]{:S(2)}, u32[]{:S(2)}) collective-permute-start(bf16[128,384]{1,0:T(8,128)(2,1)S(1)} %add_convert_fusion.gate_ref.refs_0_), channel_id=1, source_target_pairs={{12,0},{8,4},{4,8},{0,12},{13,1},{9,5},{5,9},{1,13},{14,2},{10,6},... | collective-permute-start | bytes 294920 | tf_op jit(solution)/shard_map/ppermute | solution.py:195
  33.4 0.6 %products.1 = (f32[512,256]{1,0:T(8,128)S(1)}, bf16[128,384]{1,0:T(8,128)(2,1)S(1)}) custom-call(f32[512,256]{1,0:T(8,128)S(1)} %get-tuple-element.12.partial_ref, bf16[1,512,512]{2,1,0:T(8,128)(2,1)S(1)} %get-tuple-element.13.chosen_ref, bf16[256,512]{1,0:T(8,128)(2,1)S(1)} %get-tuple-element.14.turned_ref, bf16[512,256]{1,0:T(8,128)(2,1)S(1)} %relay.8.refs_0_), custom_call_target="tpu_custom_call" | custom-call | tf_op jit(solution)/shard_map/products/pallas_call | solution.py:152
  34.0 0.1 collective-permute-start.8
  34.1 0.8 %neg.3 = f32[512,256]{1,0:T(8,128)} negate(f32[512,256]{1,0:T(8,128)S(1)} %get-tuple-element.16) | non-fusion elementwise | flops 131072 | bytes 1048576 | tf_op jit(solution)/shard_map/neg | solution.py:228
  34.9 0.0 copy-start
  34.9 4.5 %collective-permute-done.7.block_ref = bf16[128,384]{1,0:T(8,128)(2,1)S(1)} collective-permute-done((bf16[128,384]{1,0:T(8,128)(2,1)S(1)}, bf16[128,384]{1,0:T(8,128)(2,1)S(1)}, u32[]{:S(2)}, u32[]{:S(2)}) %collective-permute-start.7) | collective-permute-done | bytes 98336 | tf_op jit(solution)/shard_map/ppermute | solution.py:195
  39.4 1.0 %collective-permute-done.8.refs_3_ = bf16[128,384]{1,0:T(8,128)(2,1)S(1)} collective-permute-done((bf16[128,384]{1,0:T(8,128)(2,1)S(1)}, bf16[128,384]{1,0:T(8,128)(2,1)S(1)}, u32[]{:S(2)}, u32[]{:S(2)}) %collective-permute-start.8) | collective-permute-done | bytes 98336 | tf_op jit(solution)/shard_map/ppermute | solution.py:195
  40.3 0.0 copy-done
  40.3 0.8 %finish.1 = f32[1,256,256]{2,1,0:T(8,128)} custom-call(f32[1,256,256]{2,1,0:T(8,128)S(1)} %copy-done, bf16[128,384]{1,0:T(8,128)(2,1)S(1)} %add_convert_fusion.gate_ref.refs_0_, bf16[128,384]{1,0:T(8,128)(2,1)S(1)} %relay.9.refs_1_, bf16[128,384]{1,0:T(8,128)(2,1)S(1)} %get-tuple-element.17.refs_2_, bf16[128,384]{1,0:T(8,128)(2,1)S(1)} %collective-permute-done.8.refs_3_), custom_call_target="tpu_custom_call" | custom-call | tf_op jit(solution)/shard_map/finish/pallas_call | solution.py:177
  (7 shorter events, 0.1 us)
Async XLA Ops:
  2.4 9.8 %collective-permute-start.3 = (bf16[512,256]{1,0:T(8,128)(2,1)S(1)}, bf16[512,256]{1,0:T(8,128)(2,1)S(1)}, u32[]{:S(2)}, u32[]{:S(2)}) collective-permute-start(bf16[512,256]{1,0:T(8,128)(2,1)S(1)} %get-tuple-element.11.refs_4_), channel_id=1, source_target_pairs={{4,0},{0,4},{12,8},{8,12},{5,1},{1,5},{13,9},{9,13},{6,2},{2,6},{1... | collective-permute-start | bytes 786440 | tf_op jit(solution)/shard_map/ppermute | solution.py:195
  5.5 14.2 %collective-permute-start.2 = (bf16[512,256]{1,0:T(8,128)(2,1)S(1)}, bf16[512,256]{1,0:T(8,128)(2,1)S(1)}, u32[]{:S(2)}, u32[]{:S(2)}) collective-permute-start(bf16[512,256]{1,0:T(8,128)(2,1)S(1)} %get-tuple-element.11.refs_4_), channel_id=1, source_target_pairs={{12,0},{8,4},{4,8},{0,12},{13,1},{9,5},{5,9},{1,13},{14,2},{10,6},... | collective-permute-start | bytes 786440 | tf_op jit(solution)/shard_map/ppermute | solution.py:195
  8.0 13.1 %collective-permute-start.1 = (bf16[512,512]{1,0:T(8,128)(2,1)S(1)}, bf16[512,512]{1,0:T(8,128)(2,1)S(1)}, u32[]{:S(2)}, u32[]{:S(2)}) collective-permute-start(bf16[512,512]{1,0:T(8,128)(2,1)S(1)} %get-tuple-element.10.refs_0_), channel_id=1, source_target_pairs={{2,0},{3,1},{0,2},{1,3},{6,4},{7,5},{4,6},{5,7},{10,8},{11,9},{8,1... | collective-permute-start | bytes 1572872 | tf_op jit(solution)/shard_map/ppermute | solution.py:195
  9.5 12.3 %collective-permute-start = (bf16[512,512]{1,0:T(8,128)(2,1)S(1)}, bf16[512,512]{1,0:T(8,128)(2,1)S(1)}, u32[]{:S(2)}, u32[]{:S(2)}) collective-permute-start(bf16[512,512]{1,0:T(8,128)(2,1)S(1)} %get-tuple-element.10.refs_0_), channel_id=1, source_target_pairs={{1,0},{0,1},{3,2},{2,3},{5,4},{4,5},{7,6},{6,7},{9,8},{8,9},{11,10... | collective-permute-start | bytes 1572872 | tf_op jit(solution)/shard_map/ppermute | solution.py:195
  21.1 1.9 %collective-permute-start.4 = (bf16[512,512]{1,0:T(8,128)(2,1)S(1)}, bf16[512,512]{1,0:T(8,128)(2,1)S(1)}, u32[]{:S(2)}, u32[]{:S(2)}) collective-permute-start(bf16[512,512]{1,0:T(8,128)(2,1)S(1)} %relay.6.refs_2_), channel_id=1, source_target_pairs={{1,0},{0,1},{3,2},{2,3},{5,4},{4,5},{7,6},{6,7},{9,8},{8,9},{11,10... | collective-permute-start | bytes 1572872 | tf_op jit(solution)/shard_map/ppermute | solution.py:195
  21.1 9.1 %collective-permute-start.5 = (bf16[512,256]{1,0:T(8,128)(2,1)S(1)}, bf16[512,256]{1,0:T(8,128)(2,1)S(1)}, u32[]{:S(2)}, u32[]{:S(2)}) collective-permute-start(bf16[512,256]{1,0:T(8,128)(2,1)S(1)} %relay.5.gate_ref.refs_6_), channel_id=1, source_target_pairs={{4,0},{0,4},{12,8},{8,12},{5,1},{1,5},{13,9},{9,13},{6,2},{2,6},{1... | collective-permute-start | bytes 786440 | tf_op jit(solution)/shard_map/ppermute | solution.py:195
  24.6 7.3 %collective-permute-start.6 = (bf16[128,384]{1,0:T(8,128)(2,1)S(1)}, bf16[128,384]{1,0:T(8,128)(2,1)S(1)}, u32[]{:S(2)}, u32[]{:S(2)}) collective-permute-start(bf16[128,384]{1,0:T(8,128)(2,1)S(1)} %get-tuple-element.15), channel_id=1, source_target_pairs={{4,0},{0,4},{12,8},{8,12},{5,1},{1,5},{13,9},{9,13},{6,2},{2,6},{1... | collective-permute-start | bytes 294920 | tf_op jit(solution)/shard_map/ppermute | solution.py:195
  31.9 7.4 %collective-permute-start.7 = (bf16[128,384]{1,0:T(8,128)(2,1)S(1)}, bf16[128,384]{1,0:T(8,128)(2,1)S(1)}, u32[]{:S(2)}, u32[]{:S(2)}) collective-permute-start(bf16[128,384]{1,0:T(8,128)(2,1)S(1)} %add_convert_fusion.gate_ref.refs_0_), channel_id=1, source_target_pairs={{12,0},{8,4},{4,8},{0,12},{13,1},{9,5},{5,9},{1,13},{14,2},{10,6},... | collective-permute-start | bytes 294920 | tf_op jit(solution)/shard_map/ppermute | solution.py:195
  34.0 6.3 %collective-permute-start.8 = (bf16[128,384]{1,0:T(8,128)(2,1)S(1)}, bf16[128,384]{1,0:T(8,128)(2,1)S(1)}, u32[]{:S(2)}, u32[]{:S(2)}) collective-permute-start(bf16[128,384]{1,0:T(8,128)(2,1)S(1)} %get-tuple-element.17.refs_2_), channel_id=1, source_target_pairs={{4,0},{0,4},{12,8},{8,12},{5,1},{1,5},{13,9},{9,13},{6,2},{2,6},{1... | collective-permute-start | bytes 294920 | tf_op jit(solution)/shard_map/ppermute | solution.py:195
  34.9 5.4 %copy-start = (f32[1,256,256]{2,1,0:T(8,128)S(1)}, f32[1,256,256]{2,1,0:T(8,128)}, u32[]{:S(2)}) copy-start(f32[1,256,256]{2,1,0:T(8,128)} %diag_ref.1) | copy-start | bytes 786436

commit v8 on v7

--- a/solution.py
+++ b/solution.py
@@ -85,10 +85,12 @@
     )(block, gate)
 
 
-def store_upper(out_ref, update):
+def store_upper(out_ref, update, *others):
     half = update.shape[0] // 2
-    out_ref[:, :2 * half] = update[:half].astype(jnp.bfloat16)
-    out_ref[:, 2 * half:] = update[half:, half:].astype(jnp.bfloat16)
+    for columns, value in ((pl.ds(0, 2 * half), update[:half]), (pl.ds(2 * half, half), update[half:, half:])):
+        for other in others:
+            value += other[:, columns].astype(jnp.float32)
+        out_ref[:, columns] = value.astype(jnp.bfloat16)
 
 
 def partial_kernel(n, slots_ref, *refs):
@@ -135,8 +137,8 @@
     )(slots, *tops, *panels)
 
 
-def product_kernel(alone, partial_ref, chosen_ref, turned_ref, *refs):
-    panels, (selected_ref, update_ref) = refs[:-2], refs[-2:]
+def product_kernel(count, alone, partial_ref, chosen_ref, turned_ref, *refs):
+    panels, early, (selected_ref, update_ref) = refs[:count], refs[count:-2], refs[-2:]
     rest = dot(chosen_ref[0], panels[0][...])
     for d, panel in enumerate(panels[1:], 1):
         rest += dot(chosen_ref[d], panel[...])
@@ -144,22 +146,23 @@
     update = dot(turned_ref[...], rest.astype(jnp.bfloat16))
     if alone:
         update += update.T
-    store_upper(update_ref, update)
-
-
-def products(partial, chosen, turned, panels):
+    store_upper(update_ref, update, *early)
+
+
+def products(partial, chosen, turned, panels, early):
     rows, width = panels[0].shape
-    return pl.pallas_call(
-        functools.partial(product_kernel, len(panels) == 1),
+    alone = len(panels) == 1
+    return pl.pallas_call(
+        functools.partial(product_kernel, len(panels), alone),
         out_shape=(
             jax.ShapeDtypeStruct((rows, width), jnp.float32),
             jax.ShapeDtypeStruct((width // 2, 3 * (width // 2)), jnp.bfloat16),
         ),
-        in_specs=[VMEM] * (3 + len(panels)),
+        in_specs=[VMEM] * (3 + len(panels) + len(early)),
         out_specs=(VMEM, VMEM),
         compiler_params=PARAMS,
         name="products",
-    )(partial, chosen, turned, *panels)
+    )(partial, chosen, turned, *panels, *early)
 
 
 def finish_kernel(diag_ref, *refs):
@@ -215,17 +218,14 @@
     slots = ((wanted_pair - col // PAIR) % pairs) * PAIR + (wanted_side ^ (col % PAIR))
 
     partial, chosen, turned, early = partial_product(tops, [factor_panel, beside] + crossed, slots)
-    arrived = after(mate(early, "prow"), swapped[-1])
-    early = (early.astype(jnp.float32) + arrived.astype(jnp.float32)).astype(jnp.bfloat16)
-    updates = [early] + [after(from_pair(early, "prow", d, 1), early, HOP_COST) for d in range(1, pairs)]
-
-    swapped = [after(block, early) for block in swapped]
-    selected, late = products(partial, chosen, turned, swapped)
+    early = [early] + [after(from_pair(early, "prow", d, 1), swapped[-1]) for d in range(1, pairs)]
     if pairs > 2:
-        parts = [late] + [from_pair(late, "prow", d, 0) for d in range(1, pairs)]
-        late = functools.reduce(jnp.add, [part.astype(jnp.float32) for part in parts]).astype(jnp.bfloat16)
-    updates += [late, mate(late, "prow")]
-    return -selected, finish(diag_inverse, updates)
+        selected, late = products(partial, chosen, turned, swapped, [])
+        parts = early + [late] + [from_pair(late, "prow", d, 0) for d in range(1, pairs)]
+        update = functools.reduce(jnp.add, [part.astype(jnp.float32) for part in parts]).astype(jnp.bfloat16)
+    else:
+        selected, update = products(partial, chosen, turned, swapped, early)
+    return -selected, finish(diag_inverse, [update, mate(update, "prow")])
 
 
 def solution(mesh):

time: 41.3 us -> 38.2 us (0.925)
  waiting for transfers between devices: 24.8 us -> 22.5 us
  starting transfers between devices: 9.97 us -> 9.22 us
    ppermute x9 -> x8, waiting for transfers between devices: 24.8 us -> 22.5 us  [from_pair(): return lax.ppermute(block, axis, moves)]
    ppermute x9 -> x8, starting transfers between devices: 9.97 us -> 9.22 us  [from_pair(): return lax.ppermute(block, axis, moves)]
  transfers between devices with their start and end apart: 9 -> 8, of which waited for: 8 -> 6; matrix products, arithmetic and copies ran while one was open for 2% -> 2% of each run, Pallas kernels for 5% -> 4%
where the time goes in v8:
time: 38.2 us; the launch traced here: 38 us
  waiting for transfers between devices  22.5 us (59%)
  starting transfers between devices  9.22 us (24%)
  Pallas kernels  4.83 us (13%)
  other arithmetic  0.85 us (2%)
  between operations  0.68 us (2%)
    ppermute x8, waiting for transfers between devices, from_pair(): return lax.ppermute(block, axis, moves)  22.5 us
    ppermute x8, starting transfers between devices, from_pair(): return lax.ppermute(block, axis, moves)  9.22 us
    pallas_call x1, Pallas kernels, build_panel(): pl.pallas_call(panel_kernel, out_shape=(pltpu.VMEM(cross_blocks.shape, jn...  1.78 us
    pallas_call x1, Pallas kernels, partial_product(): pl.pallas_call(functools.partial(partial_kernel, n), out_shape=(jax.Shape...  1.61 us
    neg x1, other arithmetic, on_device(): return (-selected, finish(diag_inverse, [update, mate(update, 'prow')]))  0.83 us
    pallas_call x1, Pallas kernels, finish(): pl.pallas_call(finish_kernel, out_shape=jax.ShapeDtypeStruct(diag_inverse...  0.81 us
  transfers between devices with their start and end apart: 8, of which 6 were waited for; matrix products, arithmetic and copies ran while one was open for 2% of the time, Pallas kernels for 4%

profile of v8, /device:TPU:0, one launch (start us, length us, event | category | flops | bytes accessed | tf_op | source)
XLA Modules:
  0.0 38.0 jit_solution(9111542929781615053)
XLA Ops:
  0.6 1.8 %panel.1 = (bf16[512,256]{1,0:T(8,128)(2,1)S(1)}, bf16[512,512]{1,0:T(8,128)(2,1)S(1)}) custom-call(s32[2]{0:T(128)} %bitcast.1, f32[512,256]{1,0:T(8,128)} %cross_hbm.1, f32[1,256,256]{2,1,0:T(8,128)} %diag_ref.1, bf16[512,512]{1,0:T(8,128)(2,1)} %top_hbm.1), custom_call_target="tpu_custom_call" | custom-call | tf_op jit(solution)/shard_map/panel/pallas_call | solution.py:52
  2.4 3.1 %collective-permute-start.3 = (bf16[512,256]{1,0:T(8,128)(2,1)S(1)}, bf16[512,256]{1,0:T(8,128)(2,1)S(1)}, u32[]{:S(2)}, u32[]{:S(2)}) collective-permute-start(bf16[512,256]{1,0:T(8,128)(2,1)S(1)} %get-tuple-element.11.refs_4_), channel_id=1, source_target_pairs={{4,0},{0,4},{12,8},{8,12},{5,1},{1,5},{13,9},{9,13},{6,2},{2,6},{1... | collective-permute-start | bytes 786440 | tf_op jit(solution)/shard_map/ppermute | solution.py:198
  5.5 2.5 %collective-permute-start.2 = (bf16[512,256]{1,0:T(8,128)(2,1)S(1)}, bf16[512,256]{1,0:T(8,128)(2,1)S(1)}, u32[]{:S(2)}, u32[]{:S(2)}) collective-permute-start(bf16[512,256]{1,0:T(8,128)(2,1)S(1)} %get-tuple-element.11.refs_4_), channel_id=1, source_target_pairs={{12,0},{8,4},{4,8},{0,12},{13,1},{9,5},{5,9},{1,13},{14,2},{10,6},... | collective-permute-start | bytes 786440 | tf_op jit(solution)/shard_map/ppermute | solution.py:198
  8.0 1.5 %collective-permute-start.1 = (bf16[512,512]{1,0:T(8,128)(2,1)S(1)}, bf16[512,512]{1,0:T(8,128)(2,1)S(1)}, u32[]{:S(2)}, u32[]{:S(2)}) collective-permute-start(bf16[512,512]{1,0:T(8,128)(2,1)S(1)} %get-tuple-element.10.refs_0_), channel_id=1, source_target_pairs={{2,0},{3,1},{0,2},{1,3},{6,4},{7,5},{4,6},{5,7},{10,8},{11,9},{8,1... | collective-permute-start | bytes 1572872 | tf_op jit(solution)/shard_map/ppermute | solution.py:198
  9.5 0.0 collective-permute-start
  9.5 2.7 %collective-permute-done.3.gate_ref.refs_5_ = bf16[512,256]{1,0:T(8,128)(2,1)S(1)} collective-permute-done((bf16[512,256]{1,0:T(8,128)(2,1)S(1)}, bf16[512,256]{1,0:T(8,128)(2,1)S(1)}, u32[]{:S(2)}, u32[]{:S(2)}) %collective-permute-start.3) | collective-permute-done | bytes 262176 | tf_op jit(solution)/shard_map/ppermute | solution.py:198
  12.2 7.5 %collective-permute-done.2.block_ref = bf16[512,256]{1,0:T(8,128)(2,1)S(1)} collective-permute-done((bf16[512,256]{1,0:T(8,128)(2,1)S(1)}, bf16[512,256]{1,0:T(8,128)(2,1)S(1)}, u32[]{:S(2)}, u32[]{:S(2)}) %collective-permute-start.2) | collective-permute-done | bytes 262176 | tf_op jit(solution)/shard_map/ppermute | solution.py:198
  19.7 1.4 %collective-permute-done.1.block_ref = bf16[512,512]{1,0:T(8,128)(2,1)S(1)} collective-permute-done((bf16[512,512]{1,0:T(8,128)(2,1)S(1)}, bf16[512,512]{1,0:T(8,128)(2,1)S(1)}, u32[]{:S(2)}, u32[]{:S(2)}) %collective-permute-start.1) | collective-permute-done | bytes 524320 | tf_op jit(solution)/shard_map/ppermute | solution.py:198
  21.1 0.0 collective-permute-start.4
  21.1 0.7 %collective-permute-start.5 = (bf16[512,256]{1,0:T(8,128)(2,1)S(1)}, bf16[512,256]{1,0:T(8,128)(2,1)S(1)}, u32[]{:S(2)}, u32[]{:S(2)}) collective-permute-start(bf16[512,256]{1,0:T(8,128)(2,1)S(1)} %relay.3.gate_ref.refs_6_), channel_id=1, source_target_pairs={{4,0},{0,4},{12,8},{8,12},{5,1},{1,5},{13,9},{9,13},{6,2},{2,6},{1... | collective-permute-start | bytes 786440 | tf_op jit(solution)/shard_map/ppermute | solution.py:198
  21.8 0.0 collective-permute-done.refs_1_
  21.8 1.2 %collective-permute-done.4.refs_3_ = bf16[512,512]{1,0:T(8,128)(2,1)S(1)} collective-permute-done((bf16[512,512]{1,0:T(8,128)(2,1)S(1)}, bf16[512,512]{1,0:T(8,128)(2,1)S(1)}, u32[]{:S(2)}, u32[]{:S(2)}) %collective-permute-start.4) | collective-permute-done | bytes 524320 | tf_op jit(solution)/shard_map/ppermute | solution.py:198
  23.0 1.6 %partial.1 = (f32[512,256]{1,0:T(8,128)S(1)}, bf16[1,512,512]{2,1,0:T(8,128)(2,1)S(1)}, bf16[256,512]{1,0:T(8,128)(2,1)S(1)}, bf16[128,384]{1,0:T(8,128)(2,1)S(1)}) custom-call(s32[4]{0:T(128)S(1)} %fusion.2.slots_ref, bf16[512,512]{1,0:T(8,128)(2,1)S(1)} %get-tuple-element.10.refs_0_, bf16[512,512]{1,0:T(8,128)(2,1)S(1)} %collective-permute-done.refs_1_, ...), custom_call_target="tpu_custom_call" | custom-call | flops 536870912 | bytes 3145728 | tf_op jit(solution)/shard_map/partial/pallas_call | solution.py:121
  24.6 1.4 %collective-permute-start.6 = (bf16[128,384]{1,0:T(8,128)(2,1)S(1)}, bf16[128,384]{1,0:T(8,128)(2,1)S(1)}, u32[]{:S(2)}, u32[]{:S(2)}) collective-permute-start(bf16[128,384]{1,0:T(8,128)(2,1)S(1)} %get-tuple-element.15.refs_1_), channel_id=1, source_target_pairs={{12,0},{8,4},{4,8},{0,12},{13,1},{9,5},{5,9},{1,13},{14,2},{10,6},... | collective-permute-start | bytes 294920 | tf_op jit(solution)/shard_map/ppermute | solution.py:198
  26.0 5.9 %collective-permute-done.5.gate_ref.refs_0_ = bf16[512,256]{1,0:T(8,128)(2,1)S(1)} collective-permute-done((bf16[512,256]{1,0:T(8,128)(2,1)S(1)}, bf16[512,256]{1,0:T(8,128)(2,1)S(1)}, u32[]{:S(2)}, u32[]{:S(2)}) %collective-permute-start.5) | collective-permute-done | bytes 262176 | tf_op jit(solution)/shard_map/ppermute | solution.py:198
  31.9 0.0 collective-permute-done.6.block_ref
  31.9 0.6 %products.1 = (f32[512,256]{1,0:T(8,128)S(1)}, bf16[128,384]{1,0:T(8,128)(2,1)S(1)}) custom-call(f32[512,256]{1,0:T(8,128)S(1)} %get-tuple-element.12.partial_ref, bf16[1,512,512]{2,1,0:T(8,128)(2,1)S(1)} %get-tuple-element.13.chosen_ref, bf16[256,512]{1,0:T(8,128)(2,1)S(1)} %get-tuple-element.14.turned_ref, ...), custom_call_target="tpu_custom_call" | custom-call | tf_op jit(solution)/shard_map/products/pallas_call | solution.py:155
  32.6 0.1 collective-permute-start.7
  32.6 0.0 copy-start
  32.6 0.8 %neg.3 = f32[512,256]{1,0:T(8,128)} negate(f32[512,256]{1,0:T(8,128)S(1)} %get-tuple-element.16) | non-fusion elementwise | flops 131072 | bytes 1048576 | tf_op jit(solution)/shard_map/neg | solution.py:228
  33.5 3.8 %collective-permute-done.7.refs_1_ = bf16[128,384]{1,0:T(8,128)(2,1)S(1)} collective-permute-done((bf16[128,384]{1,0:T(8,128)(2,1)S(1)}, bf16[128,384]{1,0:T(8,128)(2,1)S(1)}, u32[]{:S(2)}, u32[]{:S(2)}) %collective-permute-start.7) | collective-permute-done | bytes 98336 | tf_op jit(solution)/shard_map/ppermute | solution.py:198
  37.2 0.0 copy-done
  37.2 0.8 %finish.1 = f32[1,256,256]{2,1,0:T(8,128)} custom-call(f32[1,256,256]{2,1,0:T(8,128)S(1)} %copy-done, bf16[128,384]{1,0:T(8,128)(2,1)S(1)} %get-tuple-element.17.refs_0_, bf16[128,384]{1,0:T(8,128)(2,1)S(1)} %collective-permute-done.7.refs_1_), custom_call_target="tpu_custom_call" | custom-call | tf_op jit(solution)/shard_map/finish/pallas_call | solution.py:180
  (4 shorter events, 0.0 us)
Async XLA Ops:
  2.4 9.8 %collective-permute-start.3 = (bf16[512,256]{1,0:T(8,128)(2,1)S(1)}, bf16[512,256]{1,0:T(8,128)(2,1)S(1)}, u32[]{:S(2)}, u32[]{:S(2)}) collective-permute-start(bf16[512,256]{1,0:T(8,128)(2,1)S(1)} %get-tuple-element.11.refs_4_), channel_id=1, source_target_pairs={{4,0},{0,4},{12,8},{8,12},{5,1},{1,5},{13,9},{9,13},{6,2},{2,6},{1... | collective-permute-start | bytes 786440 | tf_op jit(solution)/shard_map/ppermute | solution.py:198
  5.5 14.2 %collective-permute-start.2 = (bf16[512,256]{1,0:T(8,128)(2,1)S(1)}, bf16[512,256]{1,0:T(8,128)(2,1)S(1)}, u32[]{:S(2)}, u32[]{:S(2)}) collective-permute-start(bf16[512,256]{1,0:T(8,128)(2,1)S(1)} %get-tuple-element.11.refs_4_), channel_id=1, source_target_pairs={{12,0},{8,4},{4,8},{0,12},{13,1},{9,5},{5,9},{1,13},{14,2},{10,6},... | collective-permute-start | bytes 786440 | tf_op jit(solution)/shard_map/ppermute | solution.py:198
  8.0 13.1 %collective-permute-start.1 = (bf16[512,512]{1,0:T(8,128)(2,1)S(1)}, bf16[512,512]{1,0:T(8,128)(2,1)S(1)}, u32[]{:S(2)}, u32[]{:S(2)}) collective-permute-start(bf16[512,512]{1,0:T(8,128)(2,1)S(1)} %get-tuple-element.10.refs_0_), channel_id=1, source_target_pairs={{2,0},{3,1},{0,2},{1,3},{6,4},{7,5},{4,6},{5,7},{10,8},{11,9},{8,1... | collective-permute-start | bytes 1572872 | tf_op jit(solution)/shard_map/ppermute | solution.py:198
  9.5 12.3 %collective-permute-start = (bf16[512,512]{1,0:T(8,128)(2,1)S(1)}, bf16[512,512]{1,0:T(8,128)(2,1)S(1)}, u32[]{:S(2)}, u32[]{:S(2)}) collective-permute-start(bf16[512,512]{1,0:T(8,128)(2,1)S(1)} %get-tuple-element.10.refs_0_), channel_id=1, source_target_pairs={{1,0},{0,1},{3,2},{2,3},{5,4},{4,5},{7,6},{6,7},{9,8},{8,9},{11,10... | collective-permute-start | bytes 1572872 | tf_op jit(solution)/shard_map/ppermute | solution.py:198
  21.1 1.9 %collective-permute-start.4 = (bf16[512,512]{1,0:T(8,128)(2,1)S(1)}, bf16[512,512]{1,0:T(8,128)(2,1)S(1)}, u32[]{:S(2)}, u32[]{:S(2)}) collective-permute-start(bf16[512,512]{1,0:T(8,128)(2,1)S(1)} %relay.4.refs_2_), channel_id=1, source_target_pairs={{1,0},{0,1},{3,2},{2,3},{5,4},{4,5},{7,6},{6,7},{9,8},{8,9},{11,10... | collective-permute-start | bytes 1572872 | tf_op jit(solution)/shard_map/ppermute | solution.py:198
  21.1 10.8 %collective-permute-start.5 = (bf16[512,256]{1,0:T(8,128)(2,1)S(1)}, bf16[512,256]{1,0:T(8,128)(2,1)S(1)}, u32[]{:S(2)}, u32[]{:S(2)}) collective-permute-start(bf16[512,256]{1,0:T(8,128)(2,1)S(1)} %relay.3.gate_ref.refs_6_), channel_id=1, source_target_pairs={{4,0},{0,4},{12,8},{8,12},{5,1},{1,5},{13,9},{9,13},{6,2},{2,6},{1... | collective-permute-start | bytes 786440 | tf_op jit(solution)/shard_map/ppermute | solution.py:198
  24.6 7.3 %collective-permute-start.6 = (bf16[128,384]{1,0:T(8,128)(2,1)S(1)}, bf16[128,384]{1,0:T(8,128)(2,1)S(1)}, u32[]{:S(2)}, u32[]{:S(2)}) collective-permute-start(bf16[128,384]{1,0:T(8,128)(2,1)S(1)} %get-tuple-element.15.refs_1_), channel_id=1, source_target_pairs={{12,0},{8,4},{4,8},{0,12},{13,1},{9,5},{5,9},{1,13},{14,2},{10,6},... | collective-permute-start | bytes 294920 | tf_op jit(solution)/shard_map/ppermute | solution.py:198
  32.6 4.7 %collective-permute-start.7 = (bf16[128,384]{1,0:T(8,128)(2,1)S(1)}, bf16[128,384]{1,0:T(8,128)(2,1)S(1)}, u32[]{:S(2)}, u32[]{:S(2)}) collective-permute-start(bf16[128,384]{1,0:T(8,128)(2,1)S(1)} %get-tuple-element.17.refs_0_), channel_id=1, source_target_pairs={{4,0},{0,4},{12,8},{8,12},{5,1},{1,5},{13,9},{9,13},{6,2},{2,6},{1... | collective-permute-start | bytes 294920 | tf_op jit(solution)/shard_map/ppermute | solution.py:198
  32.6 4.6 %copy-start = (f32[1,256,256]{2,1,0:T(8,128)S(1)}, f32[1,256,256]{2,1,0:T(8,128)}, u32[]{:S(2)}) copy-start(f32[1,256,256]{2,1,0:T(8,128)} %diag_ref.1) | copy-start | bytes 786436

commit v9 on v8

--- a/solution.py
+++ b/solution.py
@@ -68,21 +68,21 @@
     )(*[pltpu.with_memory_space_constraint(x, pltpu.HBM) for x in inputs])
 
 
-def relay_kernel(block_ref, gate_ref, out_ref):
-    del block_ref, gate_ref, out_ref
-
-
-def after(block, gate, cost=0):
+def relay_kernel(*refs):
+    del refs
+
+
+def after(block, *gates, cost=0):
     return pl.pallas_call(
         relay_kernel,
         out_shape=jax.ShapeDtypeStruct(block.shape, block.dtype),
-        in_specs=[ANY, ANY],
+        in_specs=[ANY] * (1 + len(gates)),
         out_specs=ANY,
         input_output_aliases={0: 0},
         compiler_params=SMALL,
         cost_estimate=pl.CostEstimate(flops=cost, bytes_accessed=cost // 256, transcendentals=0),
         name="relay",
-    )(block, gate)
+    )(block, *gates)
 
 
 def store_upper(out_ref, update, *others):
@@ -203,7 +203,8 @@
     factor_panel, inverse_top = build_panel(cross_blocks, diag_inverse, pattern, inverse_top)
     beside = mate(factor_panel, "prow")
     crossed = [from_pair(factor_panel, "prow", d, 1) for d in range(1, pairs)]
-    crossed = [after(block, beside, HOP_COST) for block in crossed]
+    crossed = [after(block, factor_panel, cost=HOP_COST) for block in crossed]
+    beside = after(beside, *crossed, cost=HOP_COST)
     swapped = [mate(block, "prow") for block in crossed]
 
     near = [from_pair(inverse_top, "pcol", d, 0) for d in range(1, pairs)]

time: 38.2 us -> 37.5 us (0.982)
  waiting for transfers between devices: 22.5 us -> 17.2 us
  starting transfers between devices: 9.22 us -> 13.8 us
    ppermute x8, waiting for transfers between devices: 22.5 us -> 17.2 us  [from_pair(): return lax.ppermute(block, axis, moves)]
    ppermute x8, starting transfers between devices: 9.22 us -> 13.8 us  [from_pair(): return lax.ppermute(block, axis, moves)]
  transfers between devices with their start and end apart: 8 -> 8, of which waited for: 6 -> 5; matrix products, arithmetic and copies ran while one was open for 2% -> 2% of each run, Pallas kernels for 4% -> 4%
where the time goes in v9:
time: 37.5 us; the launch traced here: 37.4 us
  waiting for transfers between devices  17.2 us (46%)
  starting transfers between devices  13.8 us (37%)
  Pallas kernels  4.83 us (13%)
  other arithmetic  0.85 us (2%)
  between operations  0.68 us (2%)
    ppermute x8, waiting for transfers between devices, from_pair(): return lax.ppermute(block, axis, moves)  17.2 us
    ppermute x8, starting transfers between devices, from_pair(): return lax.ppermute(block, axis, moves)  13.8 us
    pallas_call x1, Pallas kernels, build_panel(): pl.pallas_call(panel_kernel, out_shape=(pltpu.VMEM(cross_blocks.shape, jn...  1.78 us
    pallas_call x1, Pallas kernels, partial_product(): pl.pallas_call(functools.partial(partial_kernel, n), out_shape=(jax.Shape...  1.61 us
    neg x1, other arithmetic, on_device(): return (-selected, finish(diag_inverse, [update, mate(update, 'prow')]))  0.83 us
    pallas_call x1, Pallas kernels, finish(): pl.pallas_call(finish_kernel, out_shape=jax.ShapeDtypeStruct(diag_inverse...  0.81 us
  transfers between devices with their start and end apart: 8, of which 5 were waited for; matrix products, arithmetic and copies ran while one was open for 2% of the time, Pallas kernels for 4%

profile of v9, /device:TPU:0, one launch (start us, length us, event | category | flops | bytes accessed | tf_op | source)
XLA Modules:
  0.0 37.4 jit_solution(5869504836650060495)
XLA Ops:
  0.6 1.8 %panel.1 = (bf16[512,256]{1,0:T(8,128)(2,1)S(1)}, bf16[512,512]{1,0:T(8,128)(2,1)S(1)}) custom-call(s32[2]{0:T(128)} %bitcast.1, f32[512,256]{1,0:T(8,128)} %cross_hbm.1, f32[1,256,256]{2,1,0:T(8,128)} %diag_ref.1, bf16[512,512]{1,0:T(8,128)(2,1)} %top_hbm.1), custom_call_target="tpu_custom_call" | custom-call | tf_op jit(solution)/shard_map/panel/pallas_call | solution.py:52
  2.4 5.1 %collective-permute-start.2 = (bf16[512,256]{1,0:T(8,128)(2,1)S(1)}, bf16[512,256]{1,0:T(8,128)(2,1)S(1)}, u32[]{:S(2)}, u32[]{:S(2)}) collective-permute-start(bf16[512,256]{1,0:T(8,128)(2,1)S(1)} %get-tuple-element.11.refs_1_.refs_4_), channel_id=1, source_target_pairs={{12,0},{8,4},{4,8},{0,12},{13,1},{9,5},{5,9},{1,13},{14,2},{10,6},... | collective-permute-start | bytes 786440 | tf_op jit(solution)/shard_map/ppermute | solution.py:198
  7.5 0.0 collective-permute-start.4
  7.5 1.5 %collective-permute-start.1 = (bf16[512,512]{1,0:T(8,128)(2,1)S(1)}, bf16[512,512]{1,0:T(8,128)(2,1)S(1)}, u32[]{:S(2)}, u32[]{:S(2)}) collective-permute-start(bf16[512,512]{1,0:T(8,128)(2,1)S(1)} %get-tuple-element.10.refs_0_), channel_id=1, source_target_pairs={{2,0},{3,1},{0,2},{1,3},{6,4},{7,5},{4,6},{5,7},{10,8},{11,9},{8,1... | collective-permute-start | bytes 1572872 | tf_op jit(solution)/shard_map/ppermute | solution.py:198
  9.0 0.0 collective-permute-start
  9.1 5.7 %collective-permute-done.2.refs_0_ = bf16[512,256]{1,0:T(8,128)(2,1)S(1)} collective-permute-done((bf16[512,256]{1,0:T(8,128)(2,1)S(1)}, bf16[512,256]{1,0:T(8,128)(2,1)S(1)}, u32[]{:S(2)}, u32[]{:S(2)}) %collective-permute-start.2) | collective-permute-done | bytes 262176 | tf_op jit(solution)/shard_map/ppermute | solution.py:198
  14.8 4.4 %collective-permute-start.5 = (bf16[512,256]{1,0:T(8,128)(2,1)S(1)}, bf16[512,256]{1,0:T(8,128)(2,1)S(1)}, u32[]{:S(2)}, u32[]{:S(2)}) collective-permute-start(bf16[512,256]{1,0:T(8,128)(2,1)S(1)} %relay.4.refs_1_.refs_6_), channel_id=1, source_target_pairs={{4,0},{0,4},{12,8},{8,12},{5,1},{1,5},{13,9},{9,13},{6,2},{2,6},{1... | collective-permute-start | bytes 786440 | tf_op jit(solution)/shard_map/ppermute | solution.py:198
  19.2 1.7 %collective-permute-done.1.refs_0_ = bf16[512,512]{1,0:T(8,128)(2,1)S(1)} collective-permute-done((bf16[512,512]{1,0:T(8,128)(2,1)S(1)}, bf16[512,512]{1,0:T(8,128)(2,1)S(1)}, u32[]{:S(2)}, u32[]{:S(2)}) %collective-permute-start.1) | collective-permute-done | bytes 524320 | tf_op jit(solution)/shard_map/ppermute | solution.py:198
  20.9 0.0 collective-permute-start.3
  20.9 0.0 collective-permute-done.4.refs_0_
  20.9 0.0 collective-permute-done.refs_1_
  20.9 1.9 %collective-permute-done.3.refs_3_ = bf16[512,512]{1,0:T(8,128)(2,1)S(1)} collective-permute-done((bf16[512,512]{1,0:T(8,128)(2,1)S(1)}, bf16[512,512]{1,0:T(8,128)(2,1)S(1)}, u32[]{:S(2)}, u32[]{:S(2)}) %collective-permute-start.3) | collective-permute-done | bytes 524320 | tf_op jit(solution)/shard_map/ppermute | solution.py:198
  22.8 1.6 %partial.1 = (f32[512,256]{1,0:T(8,128)S(1)}, bf16[1,512,512]{2,1,0:T(8,128)(2,1)S(1)}, bf16[256,512]{1,0:T(8,128)(2,1)S(1)}, bf16[128,384]{1,0:T(8,128)(2,1)S(1)}) custom-call(s32[4]{0:T(128)S(1)} %fusion.2.slots_ref, bf16[512,512]{1,0:T(8,128)(2,1)S(1)} %get-tuple-element.10.refs_0_, bf16[512,512]{1,0:T(8,128)(2,1)S(1)} %collective-permute-done.refs_1_, ...), custom_call_target="tpu_custom_call" | custom-call | flops 536870912 | bytes 3145728 | tf_op jit(solution)/shard_map/partial/pallas_call | solution.py:121
  24.5 0.8 %collective-permute-start.6 = (bf16[128,384]{1,0:T(8,128)(2,1)S(1)}, bf16[128,384]{1,0:T(8,128)(2,1)S(1)}, u32[]{:S(2)}, u32[]{:S(2)}) collective-permute-start(bf16[128,384]{1,0:T(8,128)(2,1)S(1)} %get-tuple-element.15.refs_1_), channel_id=1, source_target_pairs={{12,0},{8,4},{4,8},{0,12},{13,1},{9,5},{5,9},{1,13},{14,2},{10,6},... | collective-permute-start | bytes 294920 | tf_op jit(solution)/shard_map/ppermute | solution.py:198
  25.3 0.0 collective-permute-done.5.refs_1_.refs_0_
  25.3 6.0 %collective-permute-done.6.refs_0_ = bf16[128,384]{1,0:T(8,128)(2,1)S(1)} collective-permute-done((bf16[128,384]{1,0:T(8,128)(2,1)S(1)}, bf16[128,384]{1,0:T(8,128)(2,1)S(1)}, u32[]{:S(2)}, u32[]{:S(2)}) %collective-permute-start.6) | collective-permute-done | bytes 98336 | tf_op jit(solution)/shard_map/ppermute | solution.py:198
  31.3 0.6 %products.1 = (f32[512,256]{1,0:T(8,128)S(1)}, bf16[128,384]{1,0:T(8,128)(2,1)S(1)}) custom-call(f32[512,256]{1,0:T(8,128)S(1)} %get-tuple-element.12.partial_ref, bf16[1,512,512]{2,1,0:T(8,128)(2,1)S(1)} %get-tuple-element.13.chosen_ref, bf16[256,512]{1,0:T(8,128)(2,1)S(1)} %get-tuple-element.14.turned_ref, ...), custom_call_target="tpu_custom_call" | custom-call | tf_op jit(solution)/shard_map/products/pallas_call | solution.py:155
  31.9 2.0 %collective-permute-start.7 = (bf16[128,384]{1,0:T(8,128)(2,1)S(1)}, bf16[128,384]{1,0:T(8,128)(2,1)S(1)}, u32[]{:S(2)}, u32[]{:S(2)}) collective-permute-start(bf16[128,384]{1,0:T(8,128)(2,1)S(1)} %get-tuple-element.17.refs_0_), channel_id=1, source_target_pairs={{4,0},{0,4},{12,8},{8,12},{5,1},{1,5},{13,9},{9,13},{6,2},{2,6},{1... | collective-permute-start | bytes 294920 | tf_op jit(solution)/shard_map/ppermute | solution.py:198
  33.9 0.0 copy-start
  33.9 0.8 %neg.3 = f32[512,256]{1,0:T(8,128)} negate(f32[512,256]{1,0:T(8,128)S(1)} %get-tuple-element.16) | non-fusion elementwise | flops 131072 | bytes 1048576 | tf_op jit(solution)/shard_map/neg | solution.py:229
  34.7 1.8 %collective-permute-done.7.refs_1_ = bf16[128,384]{1,0:T(8,128)(2,1)S(1)} collective-permute-done((bf16[128,384]{1,0:T(8,128)(2,1)S(1)}, bf16[128,384]{1,0:T(8,128)(2,1)S(1)}, u32[]{:S(2)}, u32[]{:S(2)}) %collective-permute-start.7) | collective-permute-done | bytes 98336 | tf_op jit(solution)/shard_map/ppermute | solution.py:198
  36.6 0.0 copy-done
  36.6 0.8 %finish.1 = f32[1,256,256]{2,1,0:T(8,128)} custom-call(f32[1,256,256]{2,1,0:T(8,128)S(1)} %copy-done, bf16[128,384]{1,0:T(8,128)(2,1)S(1)} %get-tuple-element.17.refs_0_, bf16[128,384]{1,0:T(8,128)(2,1)S(1)} %collective-permute-done.7.refs_1_), custom_call_target="tpu_custom_call" | custom-call | tf_op jit(solution)/shard_map/finish/pallas_call | solution.py:180
  (5 shorter events, 0.0 us)
Async XLA Ops:
  2.4 12.3 %collective-permute-start.2 = (bf16[512,256]{1,0:T(8,128)(2,1)S(1)}, bf16[512,256]{1,0:T(8,128)(2,1)S(1)}, u32[]{:S(2)}, u32[]{:S(2)}) collective-permute-start(bf16[512,256]{1,0:T(8,128)(2,1)S(1)} %get-tuple-element.11.refs_1_.refs_4_), channel_id=1, source_target_pairs={{12,0},{8,4},{4,8},{0,12},{13,1},{9,5},{5,9},{1,13},{14,2},{10,6},... | collective-permute-start | bytes 786440 | tf_op jit(solution)/shard_map/ppermute | solution.py:198
  7.5 13.4 %collective-permute-start.4 = (bf16[512,256]{1,0:T(8,128)(2,1)S(1)}, bf16[512,256]{1,0:T(8,128)(2,1)S(1)}, u32[]{:S(2)}, u32[]{:S(2)}) collective-permute-start(bf16[512,256]{1,0:T(8,128)(2,1)S(1)} %get-tuple-element.11.refs_1_.refs_4_), channel_id=1, source_target_pairs={{4,0},{0,4},{12,8},{8,12},{5,1},{1,5},{13,9},{9,13},{6,2},{2,6},{1... | collective-permute-start | bytes 786440 | tf_op jit(solution)/shard_map/ppermute | solution.py:198
  7.5 13.4 %collective-permute-start.1 = (bf16[512,512]{1,0:T(8,128)(2,1)S(1)}, bf16[512,512]{1,0:T(8,128)(2,1)S(1)}, u32[]{:S(2)}, u32[]{:S(2)}) collective-permute-start(bf16[512,512]{1,0:T(8,128)(2,1)S(1)} %get-tuple-element.10.refs_0_), channel_id=1, source_target_pairs={{2,0},{3,1},{0,2},{1,3},{6,4},{7,5},{4,6},{5,7},{10,8},{11,9},{8,1... | collective-permute-start | bytes 1572872 | tf_op jit(solution)/shard_map/ppermute | solution.py:198
  9.0 11.9 %collective-permute-start = (bf16[512,512]{1,0:T(8,128)(2,1)S(1)}, bf16[512,512]{1,0:T(8,128)(2,1)S(1)}, u32[]{:S(2)}, u32[]{:S(2)}) collective-permute-start(bf16[512,512]{1,0:T(8,128)(2,1)S(1)} %get-tuple-element.10.refs_0_), channel_id=1, source_target_pairs={{1,0},{0,1},{3,2},{2,3},{5,4},{4,5},{7,6},{6,7},{9,8},{8,9},{11,10... | collective-permute-start | bytes 1572872 | tf_op jit(solution)/shard_map/ppermute | solution.py:198
  14.8 10.5 %collective-permute-start.5 = (bf16[512,256]{1,0:T(8,128)(2,1)S(1)}, bf16[512,256]{1,0:T(8,128)(2,1)S(1)}, u32[]{:S(2)}, u32[]{:S(2)}) collective-permute-start(bf16[512,256]{1,0:T(8,128)(2,1)S(1)} %relay.4.refs_1_.refs_6_), channel_id=1, source_target_pairs={{4,0},{0,4},{12,8},{8,12},{5,1},{1,5},{13,9},{9,13},{6,2},{2,6},{1... | collective-permute-start | bytes 786440 | tf_op jit(solution)/shard_map/ppermute | solution.py:198
  20.9 1.9 %collective-permute-start.3 = (bf16[512,512]{1,0:T(8,128)(2,1)S(1)}, bf16[512,512]{1,0:T(8,128)(2,1)S(1)}, u32[]{:S(2)}, u32[]{:S(2)}) collective-permute-start(bf16[512,512]{1,0:T(8,128)(2,1)S(1)} %relay.5.refs_2_), channel_id=1, source_target_pairs={{1,0},{0,1},{3,2},{2,3},{5,4},{4,5},{7,6},{6,7},{9,8},{8,9},{11,10... | collective-permute-start | bytes 1572872 | tf_op jit(solution)/shard_map/ppermute | solution.py:198
  24.5 6.8 %collective-permute-start.6 = (bf16[128,384]{1,0:T(8,128)(2,1)S(1)}, bf16[128,384]{1,0:T(8,128)(2,1)S(1)}, u32[]{:S(2)}, u32[]{:S(2)}) collective-permute-start(bf16[128,384]{1,0:T(8,128)(2,1)S(1)} %get-tuple-element.15.refs_1_), channel_id=1, source_target_pairs={{12,0},{8,4},{4,8},{0,12},{13,1},{9,5},{5,9},{1,13},{14,2},{10,6},... | collective-permute-start | bytes 294920 | tf_op jit(solution)/shard_map/ppermute | solution.py:198
  31.9 4.7 %collective-permute-start.7 = (bf16[128,384]{1,0:T(8,128)(2,1)S(1)}, bf16[128,384]{1,0:T(8,128)(2,1)S(1)}, u32[]{:S(2)}, u32[]{:S(2)}) collective-permute-start(bf16[128,384]{1,0:T(8,128)(2,1)S(1)} %get-tuple-element.17.refs_0_), channel_id=1, source_target_pairs={{4,0},{0,4},{12,8},{8,12},{5,1},{1,5},{13,9},{9,13},{6,2},{2,6},{1... | collective-permute-start | bytes 294920 | tf_op jit(solution)/shard_map/ppermute | solution.py:198
  33.9 2.7 %copy-start = (f32[1,256,256]{2,1,0:T(8,128)S(1)}, f32[1,256,256]{2,1,0:T(8,128)}, u32[]{:S(2)}) copy-start(f32[1,256,256]{2,1,0:T(8,128)} %diag_ref.1) | copy-start | bytes 786436

commit v10 on v9

--- a/solution.py
+++ b/solution.py
@@ -200,17 +200,17 @@
     def mate(block, axis):
         return from_pair(block, axis, 0, 1)
 
+    near = [from_pair(inverse_top, "pcol", d, 0) for d in range(1, pairs)]
     factor_panel, inverse_top = build_panel(cross_blocks, diag_inverse, pattern, inverse_top)
     beside = mate(factor_panel, "prow")
     crossed = [from_pair(factor_panel, "prow", d, 1) for d in range(1, pairs)]
-    crossed = [after(block, factor_panel, cost=HOP_COST) for block in crossed]
-    beside = after(beside, *crossed, cost=HOP_COST)
+    near = [after(block, factor_panel) for block in near]
+    crossed = [after(block, near[0], cost=HOP_COST) for block in crossed]
+    beside = after(beside, *crossed, cost=2 * HOP_COST)
     swapped = [mate(block, "prow") for block in crossed]
 
-    near = [from_pair(inverse_top, "pcol", d, 0) for d in range(1, pairs)]
     tops = [inverse_top, mate(inverse_top, "pcol")]
     for block in near:
-        block = after(block, crossed[-1])
         tops += [block, mate(block, "pcol")]
 
     place = jnp.arange(n, dtype=jnp.int32)

time: 37.5 us -> 36.2 us (0.965)
  waiting for transfers between devices: 17.2 us -> 16 us
    ppermute x8, waiting for transfers between devices: 17.2 us -> 16 us  [from_pair(): return lax.ppermute(block, axis, moves)]
  transfers between devices with their start and end apart: 8 -> 8, of which waited for: 5 -> 6; matrix products, arithmetic and copies ran while one was open for 2% -> 2% of each run, Pallas kernels for 4% -> 9%
where the time goes in v10:
time: 36.2 us; the launch traced here: 36.1 us
  waiting for transfers between devices  16 us (44%)
  starting transfers between devices  13.7 us (38%)
  Pallas kernels  4.83 us (13%)
  other arithmetic  0.85 us (2%)
  between operations  0.67 us (2%)
    ppermute x8, waiting for transfers between devices, from_pair(): return lax.ppermute(block, axis, moves)  16 us
    ppermute x8, starting transfers between devices, from_pair(): return lax.ppermute(block, axis, moves)  13.7 us
    pallas_call x1, Pallas kernels, build_panel(): pl.pallas_call(panel_kernel, out_shape=(pltpu.VMEM(cross_blocks.shape, jn...  1.78 us
    pallas_call x1, Pallas kernels, partial_product(): pl.pallas_call(functools.partial(partial_kernel, n), out_shape=(jax.Shape...  1.62 us
    neg x1, other arithmetic, on_device(): return (-selected, finish(diag_inverse, [update, mate(update, 'prow')]))  0.83 us
    pallas_call x1, Pallas kernels, finish(): pl.pallas_call(finish_kernel, out_shape=jax.ShapeDtypeStruct(diag_inverse...  0.81 us
  transfers between devices with their start and end apart: 8, of which 6 were waited for; matrix products, arithmetic and copies ran while one was open for 2% of the time, Pallas kernels for 9%

profile of v10, /device:TPU:0, one launch (start us, length us, event | category | flops | bytes accessed | tf_op | source)
XLA Modules:
  0.0 36.1 jit_solution(18077116809286176210)
XLA Ops:
  0.6 3.0 %collective-permute-start.1 = (bf16[512,512]{1,0:T(8,128)(2,1)}, bf16[512,512]{1,0:T(8,128)(2,1)S(1)}, u32[]{:S(2)}, u32[]{:S(2)}) collective-permute-start(bf16[512,512]{1,0:T(8,128)(2,1)} %top_hbm.1), channel_id=1, source_target_pairs={{2,0},{3,1},{0,2},{1,3},{6,4},{7,5},{4,6},{5,7},{10,8},{11,9},{8,1... | collective-permute-start | bytes 1572872 | tf_op jit(solution)/shard_map/ppermute | solution.py:198
  3.6 1.8 %panel.1 = (bf16[512,256]{1,0:T(8,128)(2,1)S(1)}, bf16[512,512]{1,0:T(8,128)(2,1)S(1)}) custom-call(s32[2]{0:T(128)} %bitcast.1, f32[512,256]{1,0:T(8,128)} %cross_hbm.1, f32[1,256,256]{2,1,0:T(8,128)} %diag_ref.1, bf16[512,512]{1,0:T(8,128)(2,1)} %top_hbm.1), custom_call_target="tpu_custom_call" | custom-call | tf_op jit(solution)/shard_map/panel/pallas_call | solution.py:52
  5.4 3.7 %collective-permute-start.4 = (bf16[512,256]{1,0:T(8,128)(2,1)S(1)}, bf16[512,256]{1,0:T(8,128)(2,1)S(1)}, u32[]{:S(2)}, u32[]{:S(2)}) collective-permute-start(bf16[512,256]{1,0:T(8,128)(2,1)S(1)} %get-tuple-element.11.refs_1_.refs_4_), channel_id=1, source_target_pairs={{12,0},{8,4},{4,8},{0,12},{13,1},{9,5},{5,9},{1,13},{14,2},{10,6},... | collective-permute-start | bytes 786440 | tf_op jit(solution)/shard_map/ppermute | solution.py:198
  9.1 0.0 collective-permute-start.3
  9.1 0.0 collective-permute-start
  9.1 6.7 %collective-permute-done.1.refs_0_ = bf16[512,512]{1,0:T(8,128)(2,1)S(1)} collective-permute-done((bf16[512,512]{1,0:T(8,128)(2,1)}, bf16[512,512]{1,0:T(8,128)(2,1)S(1)}, u32[]{:S(2)}, u32[]{:S(2)}) %collective-permute-start.1) | collective-permute-done | bytes 524320 | tf_op jit(solution)/shard_map/ppermute | solution.py:198
  15.8 0.0 collective-permute-start.2
  15.8 0.8 %collective-permute-done.4.refs_0_ = bf16[512,256]{1,0:T(8,128)(2,1)S(1)} collective-permute-done((bf16[512,256]{1,0:T(8,128)(2,1)S(1)}, bf16[512,256]{1,0:T(8,128)(2,1)S(1)}, u32[]{:S(2)}, u32[]{:S(2)}) %collective-permute-start.4) | collective-permute-done | bytes 262176 | tf_op jit(solution)/shard_map/ppermute | solution.py:198
  16.6 3.9 %collective-permute-start.5 = (bf16[512,256]{1,0:T(8,128)(2,1)S(1)}, bf16[512,256]{1,0:T(8,128)(2,1)S(1)}, u32[]{:S(2)}, u32[]{:S(2)}) collective-permute-start(bf16[512,256]{1,0:T(8,128)(2,1)S(1)} %relay.5.refs_1_.refs_6_), channel_id=1, source_target_pairs={{4,0},{0,4},{12,8},{8,12},{5,1},{1,5},{13,9},{9,13},{6,2},{2,6},{1... | collective-permute-start | bytes 786440 | tf_op jit(solution)/shard_map/ppermute | solution.py:198
  20.4 0.5 %collective-permute-done.3.refs_0_ = bf16[512,256]{1,0:T(8,128)(2,1)S(1)} collective-permute-done((bf16[512,256]{1,0:T(8,128)(2,1)S(1)}, bf16[512,256]{1,0:T(8,128)(2,1)S(1)}, u32[]{:S(2)}, u32[]{:S(2)}) %collective-permute-start.3) | collective-permute-done | bytes 262176 | tf_op jit(solution)/shard_map/ppermute | solution.py:198
  20.9 0.0 collective-permute-done.refs_1_
  20.9 0.0 collective-permute-done.2.refs_3_
  20.9 1.6 %partial.1 = (f32[512,256]{1,0:T(8,128)S(1)}, bf16[1,512,512]{2,1,0:T(8,128)(2,1)S(1)}, bf16[256,512]{1,0:T(8,128)(2,1)S(1)}, bf16[128,384]{1,0:T(8,128)(2,1)S(1)}) custom-call(s32[4]{0:T(128)S(1)} %fusion.2.slots_ref, bf16[512,512]{1,0:T(8,128)(2,1)S(1)} %get-tuple-element.10.refs_0_, bf16[512,512]{1,0:T(8,128)(2,1)S(1)} %collective-permute-done.refs_1_, ...), custom_call_target="tpu_custom_call" | custom-call | flops 536870912 | bytes 3145728 | tf_op jit(solution)/shard_map/partial/pallas_call | solution.py:121
  22.6 2.1 %collective-permute-start.6 = (bf16[128,384]{1,0:T(8,128)(2,1)S(1)}, bf16[128,384]{1,0:T(8,128)(2,1)S(1)}, u32[]{:S(2)}, u32[]{:S(2)}) collective-permute-start(bf16[128,384]{1,0:T(8,128)(2,1)S(1)} %get-tuple-element.15.refs_1_), channel_id=1, source_target_pairs={{12,0},{8,4},{4,8},{0,12},{13,1},{9,5},{5,9},{1,13},{14,2},{10,6},... | collective-permute-start | bytes 294920 | tf_op jit(solution)/shard_map/ppermute | solution.py:198
  24.6 2.1 %collective-permute-done.5.refs_1_.refs_0_ = bf16[512,256]{1,0:T(8,128)(2,1)S(1)} collective-permute-done((bf16[512,256]{1,0:T(8,128)(2,1)S(1)}, bf16[512,256]{1,0:T(8,128)(2,1)S(1)}, u32[]{:S(2)}, u32[]{:S(2)}) %collective-permute-start.5) | collective-permute-done | bytes 262176 | tf_op jit(solution)/shard_map/ppermute | solution.py:198
  26.7 3.3 %collective-permute-done.6.refs_0_ = bf16[128,384]{1,0:T(8,128)(2,1)S(1)} collective-permute-done((bf16[128,384]{1,0:T(8,128)(2,1)S(1)}, bf16[128,384]{1,0:T(8,128)(2,1)S(1)}, u32[]{:S(2)}, u32[]{:S(2)}) %collective-permute-start.6) | collective-permute-done | bytes 98336 | tf_op jit(solution)/shard_map/ppermute | solution.py:198
  30.0 0.6 %products.1 = (f32[512,256]{1,0:T(8,128)S(1)}, bf16[128,384]{1,0:T(8,128)(2,1)S(1)}) custom-call(f32[512,256]{1,0:T(8,128)S(1)} %get-tuple-element.12.partial_ref, bf16[1,512,512]{2,1,0:T(8,128)(2,1)S(1)} %get-tuple-element.13.chosen_ref, bf16[256,512]{1,0:T(8,128)(2,1)S(1)} %get-tuple-element.14.turned_ref, ...), custom_call_target="tpu_custom_call" | custom-call | tf_op jit(solution)/shard_map/products/pallas_call | solution.py:155
  30.6 1.1 %collective-permute-start.7 = (bf16[128,384]{1,0:T(8,128)(2,1)S(1)}, bf16[128,384]{1,0:T(8,128)(2,1)S(1)}, u32[]{:S(2)}, u32[]{:S(2)}) collective-permute-start(bf16[128,384]{1,0:T(8,128)(2,1)S(1)} %get-tuple-element.17.refs_0_), channel_id=1, source_target_pairs={{4,0},{0,4},{12,8},{8,12},{5,1},{1,5},{13,9},{9,13},{6,2},{2,6},{1... | collective-permute-start | bytes 294920 | tf_op jit(solution)/shard_map/ppermute | solution.py:198
  31.7 0.0 copy-start
  31.7 0.8 %neg.3 = f32[512,256]{1,0:T(8,128)} negate(f32[512,256]{1,0:T(8,128)S(1)} %get-tuple-element.16) | non-fusion elementwise | flops 131072 | bytes 1048576 | tf_op jit(solution)/shard_map/neg | solution.py:229
  32.5 2.8 %collective-permute-done.7.refs_1_ = bf16[128,384]{1,0:T(8,128)(2,1)S(1)} collective-permute-done((bf16[128,384]{1,0:T(8,128)(2,1)S(1)}, bf16[128,384]{1,0:T(8,128)(2,1)S(1)}, u32[]{:S(2)}, u32[]{:S(2)}) %collective-permute-start.7) | collective-permute-done | bytes 98336 | tf_op jit(solution)/shard_map/ppermute | solution.py:198
  35.3 0.0 copy-done
  35.3 0.8 %finish.1 = f32[1,256,256]{2,1,0:T(8,128)} custom-call(f32[1,256,256]{2,1,0:T(8,128)S(1)} %copy-done, bf16[128,384]{1,0:T(8,128)(2,1)S(1)} %get-tuple-element.17.refs_0_, bf16[128,384]{1,0:T(8,128)(2,1)S(1)} %collective-permute-done.7.refs_1_), custom_call_target="tpu_custom_call" | custom-call | tf_op jit(solution)/shard_map/finish/pallas_call | solution.py:180
  (5 shorter events, 0.0 us)
Async XLA Ops:
  0.6 15.1 %collective-permute-start.1 = (bf16[512,512]{1,0:T(8,128)(2,1)}, bf16[512,512]{1,0:T(8,128)(2,1)S(1)}, u32[]{:S(2)}, u32[]{:S(2)}) collective-permute-start(bf16[512,512]{1,0:T(8,128)(2,1)} %top_hbm.1), channel_id=1, source_target_pairs={{2,0},{3,1},{0,2},{1,3},{6,4},{7,5},{4,6},{5,7},{10,8},{11,9},{8,1... | collective-permute-start | bytes 1572872 | tf_op jit(solution)/shard_map/ppermute | solution.py:198
  5.4 11.1 %collective-permute-start.4 = (bf16[512,256]{1,0:T(8,128)(2,1)S(1)}, bf16[512,256]{1,0:T(8,128)(2,1)S(1)}, u32[]{:S(2)}, u32[]{:S(2)}) collective-permute-start(bf16[512,256]{1,0:T(8,128)(2,1)S(1)} %get-tuple-element.11.refs_1_.refs_4_), channel_id=1, source_target_pairs={{12,0},{8,4},{4,8},{0,12},{13,1},{9,5},{5,9},{1,13},{14,2},{10,6},... | collective-permute-start | bytes 786440 | tf_op jit(solution)/shard_map/ppermute | solution.py:198
  9.1 11.8 %collective-permute-start.3 = (bf16[512,256]{1,0:T(8,128)(2,1)S(1)}, bf16[512,256]{1,0:T(8,128)(2,1)S(1)}, u32[]{:S(2)}, u32[]{:S(2)}) collective-permute-start(bf16[512,256]{1,0:T(8,128)(2,1)S(1)} %get-tuple-element.11.refs_1_.refs_4_), channel_id=1, source_target_pairs={{4,0},{0,4},{12,8},{8,12},{5,1},{1,5},{13,9},{9,13},{6,2},{2,6},{1... | collective-permute-start | bytes 786440 | tf_op jit(solution)/shard_map/ppermute | solution.py:198
  9.1 11.8 %collective-permute-start = (bf16[512,512]{1,0:T(8,128)(2,1)S(1)}, bf16[512,512]{1,0:T(8,128)(2,1)S(1)}, u32[]{:S(2)}, u32[]{:S(2)}) collective-permute-start(bf16[512,512]{1,0:T(8,128)(2,1)S(1)} %get-tuple-element.10.refs_0_), channel_id=1, source_target_pairs={{1,0},{0,1},{3,2},{2,3},{5,4},{4,5},{7,6},{6,7},{9,8},{8,9},{11,10... | collective-permute-start | bytes 1572872 | tf_op jit(solution)/shard_map/ppermute | solution.py:198
  15.8 5.2 %collective-permute-start.2 = (bf16[512,512]{1,0:T(8,128)(2,1)S(1)}, bf16[512,512]{1,0:T(8,128)(2,1)S(1)}, u32[]{:S(2)}, u32[]{:S(2)}) collective-permute-start(bf16[512,512]{1,0:T(8,128)(2,1)S(1)} %relay.4.refs_1_.refs_2_), channel_id=1, source_target_pairs={{1,0},{0,1},{3,2},{2,3},{5,4},{4,5},{7,6},{6,7},{9,8},{8,9},{11,10... | collective-permute-start | bytes 1572872 | tf_op jit(solution)/shard_map/ppermute | solution.py:198
  16.6 10.1 %collective-permute-start.5 = (bf16[512,256]{1,0:T(8,128)(2,1)S(1)}, bf16[512,256]{1,0:T(8,128)(2,1)S(1)}, u32[]{:S(2)}, u32[]{:S(2)}) collective-permute-start(bf16[512,256]{1,0:T(8,128)(2,1)S(1)} %relay.5.refs_1_.refs_6_), channel_id=1, source_target_pairs={{4,0},{0,4},{12,8},{8,12},{5,1},{1,5},{13,9},{9,13},{6,2},{2,6},{1... | collective-permute-start | bytes 786440 | tf_op jit(solution)/shard_map/ppermute | solution.py:198
  22.6 7.4 %collective-permute-start.6 = (bf16[128,384]{1,0:T(8,128)(2,1)S(1)}, bf16[128,384]{1,0:T(8,128)(2,1)S(1)}, u32[]{:S(2)}, u32[]{:S(2)}) collective-permute-start(bf16[128,384]{1,0:T(8,128)(2,1)S(1)} %get-tuple-element.15.refs_1_), channel_id=1, source_target_pairs={{12,0},{8,4},{4,8},{0,12},{13,1},{9,5},{5,9},{1,13},{14,2},{10,6},... | collective-permute-start | bytes 294920 | tf_op jit(solution)/shard_map/ppermute | solution.py:198
  30.6 4.7 %collective-permute-start.7 = (bf16[128,384]{1,0:T(8,128)(2,1)S(1)}, bf16[128,384]{1,0:T(8,128)(2,1)S(1)}, u32[]{:S(2)}, u32[]{:S(2)}) collective-permute-start(bf16[128,384]{1,0:T(8,128)(2,1)S(1)} %get-tuple-element.17.refs_0_), channel_id=1, source_target_pairs={{4,0},{0,4},{12,8},{8,12},{5,1},{1,5},{13,9},{9,13},{6,2},{2,6},{1... | collective-permute-start | bytes 294920 | tf_op jit(solution)/shard_map/ppermute | solution.py:198
  31.7 3.6 %copy-start = (f32[1,256,256]{2,1,0:T(8,128)S(1)}, f32[1,256,256]{2,1,0:T(8,128)}, u32[]{:S(2)}) copy-start(f32[1,256,256]{2,1,0:T(8,128)} %diag_ref.1) | copy-start | bytes 786436

commit v11 on v10

--- a/solution.py
+++ b/solution.py
@@ -96,10 +96,10 @@
 def partial_kernel(n, slots_ref, *refs):
     tops, panels = refs[:n], refs[n:n + n // 2 + 1]
     partial_ref, chosen_ref, turned_ref, update_ref, panel_buf = refs[n + n // 2 + 1:]
-    places = [0] + list(range(1, n, 2))
+    places = [0, 1] + list(range(2, n, 2))
     for place, panel in zip(places, panels):
         panel_buf[slots_ref[place]] = panel[...]
-    for d, place in enumerate(range(2, n, 2)):
+    for d, place in enumerate(range(3, n, 2)):
         slot = slots_ref[place]
         panel_buf[slot] = jnp.zeros(panel_buf.shape[1:], panel_buf.dtype)
         for t in range(n):
@@ -203,7 +203,7 @@
     near = [from_pair(inverse_top, "pcol", d, 0) for d in range(1, pairs)]
     factor_panel, inverse_top = build_panel(cross_blocks, diag_inverse, pattern, inverse_top)
     beside = mate(factor_panel, "prow")
-    crossed = [from_pair(factor_panel, "prow", d, 1) for d in range(1, pairs)]
+    crossed = [from_pair(factor_panel, "prow", d, 0) for d in range(1, pairs)]
     near = [after(block, factor_panel) for block in near]
     crossed = [after(block, near[0], cost=HOP_COST) for block in crossed]
     beside = after(beside, *crossed, cost=2 * HOP_COST)
@@ -219,7 +219,7 @@
     slots = ((wanted_pair - col // PAIR) % pairs) * PAIR + (wanted_side ^ (col % PAIR))
 
     partial, chosen, turned, early = partial_product(tops, [factor_panel, beside] + crossed, slots)
-    early = [early] + [after(from_pair(early, "prow", d, 1), swapped[-1]) for d in range(1, pairs)]
+    early = [early] + [after(from_pair(early, "prow", d, 0), swapped[-1]) for d in range(1, pairs)]
     if pairs > 2:
         selected, late = products(partial, chosen, turned, swapped, [])
         parts = early + [late] + [from_pair(late, "prow", d, 0) for d in range(1, pairs)]

time: 36.2 us -> 36.7 us (1.014)
  starting transfers between devices: 13.7 us -> 14.6 us
  waiting for transfers between devices: 16 us -> 15.5 us
    ppermute x8, starting transfers between devices: 13.7 us -> 14.6 us  [from_pair(): return lax.ppermute(block, axis, moves)]
    ppermute x8, waiting for transfers between devices: 16 us -> 15.5 us  [from_pair(): return lax.ppermute(block, axis, moves)]
  transfers between devices with their start and end apart: 8 -> 8, of which waited for: 6 -> 4; matrix products, arithmetic and copies ran while one was open for 2% -> 2% of each run, Pallas kernels for 9% -> 9%
where the time goes in v11:
time: 36.7 us; the launch traced here: 36.5 us
  waiting for transfers between devices  15.5 us (42%)
  starting transfers between devices  14.6 us (40%)
  Pallas kernels  4.83 us (13%)
  other arithmetic  0.85 us (2%)
  between operations  0.67 us (2%)
    ppermute x8, waiting for transfers between devices, from_pair(): return lax.ppermute(block, axis, moves)  15.5 us
    ppermute x8, starting transfers between devices, from_pair(): return lax.ppermute(block, axis, moves)  14.6 us
    pallas_call x1, Pallas kernels, build_panel(): pl.pallas_call(panel_kernel, out_shape=(pltpu.VMEM(cross_blocks.shape, jn...  1.78 us
    pallas_call x1, Pallas kernels, partial_product(): pl.pallas_call(functools.partial(partial_kernel, n), out_shape=(jax.Shape...  1.62 us
    neg x1, other arithmetic, on_device(): return (-selected, finish(diag_inverse, [update, mate(update, 'prow')]))  0.83 us
    pallas_call x1, Pallas kernels, finish(): pl.pallas_call(finish_kernel, out_shape=jax.ShapeDtypeStruct(diag_inverse...  0.81 us
  transfers between devices with their start and end apart: 8, of which 4 were waited for; matrix products, arithmetic and copies ran while one was open for 2% of the time, Pallas kernels for 9%

profile of v11, /device:TPU:0, one launch (start us, length us, event | category | flops | bytes accessed | tf_op | source)
XLA Modules:
  0.0 36.5 jit_solution(15054350788986354253)
XLA Ops:
  0.6 3.0 %collective-permute-start.1 = (bf16[512,512]{1,0:T(8,128)(2,1)}, bf16[512,512]{1,0:T(8,128)(2,1)S(1)}, u32[]{:S(2)}, u32[]{:S(2)}) collective-permute-start(bf16[512,512]{1,0:T(8,128)(2,1)} %top_hbm.1), channel_id=1, source_target_pairs={{2,0},{3,1},{0,2},{1,3},{6,4},{7,5},{4,6},{5,7},{10,8},{11,9},{8,1... | collective-permute-start | bytes 1572872 | tf_op jit(solution)/shard_map/ppermute | solution.py:198
  3.6 1.8 %panel.1 = (bf16[512,256]{1,0:T(8,128)(2,1)S(1)}, bf16[512,512]{1,0:T(8,128)(2,1)S(1)}) custom-call(s32[2]{0:T(128)} %bitcast.1, f32[512,256]{1,0:T(8,128)} %cross_hbm.1, f32[1,256,256]{2,1,0:T(8,128)} %diag_ref.1, bf16[512,512]{1,0:T(8,128)(2,1)} %top_hbm.1), custom_call_target="tpu_custom_call" | custom-call | tf_op jit(solution)/shard_map/panel/pallas_call | solution.py:52
  5.4 2.7 %collective-permute-start.4 = (bf16[512,256]{1,0:T(8,128)(2,1)S(1)}, bf16[512,256]{1,0:T(8,128)(2,1)S(1)}, u32[]{:S(2)}, u32[]{:S(2)}) collective-permute-start(bf16[512,256]{1,0:T(8,128)(2,1)S(1)} %get-tuple-element.11.refs_1_.refs_4_), channel_id=1, source_target_pairs={{8,0},{12,4},{0,8},{4,12},{9,1},{13,5},{1,9},{5,13},{10,2},{14,6},... | collective-permute-start | bytes 786440 | tf_op jit(solution)/shard_map/ppermute | solution.py:198
  8.1 1.6 %collective-permute-start.3 = (bf16[512,256]{1,0:T(8,128)(2,1)S(1)}, bf16[512,256]{1,0:T(8,128)(2,1)S(1)}, u32[]{:S(2)}, u32[]{:S(2)}) collective-permute-start(bf16[512,256]{1,0:T(8,128)(2,1)S(1)} %get-tuple-element.11.refs_1_.refs_4_), channel_id=1, source_target_pairs={{4,0},{0,4},{12,8},{8,12},{5,1},{1,5},{13,9},{9,13},{6,2},{2,6},{1... | collective-permute-start | bytes 786440 | tf_op jit(solution)/shard_map/ppermute | solution.py:198
  9.7 0.0 collective-permute-start
  9.7 6.1 %collective-permute-done.1.refs_0_ = bf16[512,512]{1,0:T(8,128)(2,1)S(1)} collective-permute-done((bf16[512,512]{1,0:T(8,128)(2,1)}, bf16[512,512]{1,0:T(8,128)(2,1)S(1)}, u32[]{:S(2)}, u32[]{:S(2)}) %collective-permute-start.1) | collective-permute-done | bytes 524320 | tf_op jit(solution)/shard_map/ppermute | solution.py:198
  15.8 0.0 collective-permute-start.2
  15.8 4.1 %collective-permute-done.4.refs_0_ = bf16[512,256]{1,0:T(8,128)(2,1)S(1)} collective-permute-done((bf16[512,256]{1,0:T(8,128)(2,1)S(1)}, bf16[512,256]{1,0:T(8,128)(2,1)S(1)}, u32[]{:S(2)}, u32[]{:S(2)}) %collective-permute-start.4) | collective-permute-done | bytes 262176 | tf_op jit(solution)/shard_map/ppermute | solution.py:198
  19.9 0.6 %collective-permute-start.5 = (bf16[512,256]{1,0:T(8,128)(2,1)S(1)}, bf16[512,256]{1,0:T(8,128)(2,1)S(1)}, u32[]{:S(2)}, u32[]{:S(2)}) collective-permute-start(bf16[512,256]{1,0:T(8,128)(2,1)S(1)} %relay.5.refs_1_.refs_6_), channel_id=1, source_target_pairs={{4,0},{0,4},{12,8},{8,12},{5,1},{1,5},{13,9},{9,13},{6,2},{2,6},{1... | collective-permute-start | bytes 786440 | tf_op jit(solution)/shard_map/ppermute | solution.py:198
  20.4 0.0 collective-permute-done.3.refs_0_
  20.4 0.0 collective-permute-done.refs_1_
  20.4 0.0 collective-permute-done.2.refs_3_
  20.5 1.6 %partial.1 = (f32[512,256]{1,0:T(8,128)S(1)}, bf16[1,512,512]{2,1,0:T(8,128)(2,1)S(1)}, bf16[256,512]{1,0:T(8,128)(2,1)S(1)}, bf16[128,384]{1,0:T(8,128)(2,1)S(1)}) custom-call(s32[4]{0:T(128)S(1)} %fusion.2.slots_ref, bf16[512,512]{1,0:T(8,128)(2,1)S(1)} %get-tuple-element.10.refs_0_, bf16[512,512]{1,0:T(8,128)(2,1)S(1)} %collective-permute-done.refs_1_, ...), custom_call_target="tpu_custom_call" | custom-call | flops 536870912 | bytes 3145728 | tf_op jit(solution)/shard_map/partial/pallas_call | solution.py:121
  22.1 3.4 %collective-permute-start.6 = (bf16[128,384]{1,0:T(8,128)(2,1)S(1)}, bf16[128,384]{1,0:T(8,128)(2,1)S(1)}, u32[]{:S(2)}, u32[]{:S(2)}) collective-permute-start(bf16[128,384]{1,0:T(8,128)(2,1)S(1)} %get-tuple-element.15.refs_1_), channel_id=1, source_target_pairs={{8,0},{12,4},{0,8},{4,12},{9,1},{13,5},{1,9},{5,13},{10,2},{14,6},... | collective-permute-start | bytes 294920 | tf_op jit(solution)/shard_map/ppermute | solution.py:198
  25.5 3.6 %collective-permute-done.5.refs_1_.refs_0_ = bf16[512,256]{1,0:T(8,128)(2,1)S(1)} collective-permute-done((bf16[512,256]{1,0:T(8,128)(2,1)S(1)}, bf16[512,256]{1,0:T(8,128)(2,1)S(1)}, u32[]{:S(2)}, u32[]{:S(2)}) %collective-permute-start.5) | collective-permute-done | bytes 262176 | tf_op jit(solution)/shard_map/ppermute | solution.py:198
  29.1 0.0 collective-permute-done.6.refs_0_
  29.1 0.6 %products.1 = (f32[512,256]{1,0:T(8,128)S(1)}, bf16[128,384]{1,0:T(8,128)(2,1)S(1)}) custom-call(f32[512,256]{1,0:T(8,128)S(1)} %get-tuple-element.12.partial_ref, bf16[1,512,512]{2,1,0:T(8,128)(2,1)S(1)} %get-tuple-element.13.chosen_ref, bf16[256,512]{1,0:T(8,128)(2,1)S(1)} %get-tuple-element.14.turned_ref, ...), custom_call_target="tpu_custom_call" | custom-call | tf_op jit(solution)/shard_map/products/pallas_call | solution.py:155
  29.7 3.4 %collective-permute-start.7 = (bf16[128,384]{1,0:T(8,128)(2,1)S(1)}, bf16[128,384]{1,0:T(8,128)(2,1)S(1)}, u32[]{:S(2)}, u32[]{:S(2)}) collective-permute-start(bf16[128,384]{1,0:T(8,128)(2,1)S(1)} %get-tuple-element.17.refs_0_), channel_id=1, source_target_pairs={{4,0},{0,4},{12,8},{8,12},{5,1},{1,5},{13,9},{9,13},{6,2},{2,6},{1... | collective-permute-start | bytes 294920 | tf_op jit(solution)/shard_map/ppermute | solution.py:198
  33.1 0.0 copy-start
  33.1 0.8 %neg.3 = f32[512,256]{1,0:T(8,128)} negate(f32[512,256]{1,0:T(8,128)S(1)} %get-tuple-element.16) | non-fusion elementwise | flops 131072 | bytes 1048576 | tf_op jit(solution)/shard_map/neg | solution.py:229
  33.9 1.8 %collective-permute-done.7.refs_1_ = bf16[128,384]{1,0:T(8,128)(2,1)S(1)} collective-permute-done((bf16[128,384]{1,0:T(8,128)(2,1)S(1)}, bf16[128,384]{1,0:T(8,128)(2,1)S(1)}, u32[]{:S(2)}, u32[]{:S(2)}) %collective-permute-start.7) | collective-permute-done | bytes 98336 | tf_op jit(solution)/shard_map/ppermute | solution.py:198
  35.7 0.0 copy-done
  35.7 0.8 %finish.1 = f32[1,256,256]{2,1,0:T(8,128)} custom-call(f32[1,256,256]{2,1,0:T(8,128)S(1)} %copy-done, bf16[128,384]{1,0:T(8,128)(2,1)S(1)} %get-tuple-element.17.refs_0_, bf16[128,384]{1,0:T(8,128)(2,1)S(1)} %collective-permute-done.7.refs_1_), custom_call_target="tpu_custom_call" | custom-call | tf_op jit(solution)/shard_map/finish/pallas_call | solution.py:180
  (5 shorter events, 0.0 us)
Async XLA Ops:
  0.6 15.1 %collective-permute-start.1 = (bf16[512,512]{1,0:T(8,128)(2,1)}, bf16[512,512]{1,0:T(8,128)(2,1)S(1)}, u32[]{:S(2)}, u32[]{:S(2)}) collective-permute-start(bf16[512,512]{1,0:T(8,128)(2,1)} %top_hbm.1), channel_id=1, source_target_pairs={{2,0},{3,1},{0,2},{1,3},{6,4},{7,5},{4,6},{5,7},{10,8},{11,9},{8,1... | collective-permute-start | bytes 1572872 | tf_op jit(solution)/shard_map/ppermute | solution.py:198
  5.4 14.5 %collective-permute-start.4 = (bf16[512,256]{1,0:T(8,128)(2,1)S(1)}, bf16[512,256]{1,0:T(8,128)(2,1)S(1)}, u32[]{:S(2)}, u32[]{:S(2)}) collective-permute-start(bf16[512,256]{1,0:T(8,128)(2,1)S(1)} %get-tuple-element.11.refs_1_.refs_4_), channel_id=1, source_target_pairs={{8,0},{12,4},{0,8},{4,12},{9,1},{13,5},{1,9},{5,13},{10,2},{14,6},... | collective-permute-start | bytes 786440 | tf_op jit(solution)/shard_map/ppermute | solution.py:198
  8.1 12.4 %collective-permute-start.3 = (bf16[512,256]{1,0:T(8,128)(2,1)S(1)}, bf16[512,256]{1,0:T(8,128)(2,1)S(1)}, u32[]{:S(2)}, u32[]{:S(2)}) collective-permute-start(bf16[512,256]{1,0:T(8,128)(2,1)S(1)} %get-tuple-element.11.refs_1_.refs_4_), channel_id=1, source_target_pairs={{4,0},{0,4},{12,8},{8,12},{5,1},{1,5},{13,9},{9,13},{6,2},{2,6},{1... | collective-permute-start | bytes 786440 | tf_op jit(solution)/shard_map/ppermute | solution.py:198
  9.7 10.8 %collective-permute-start = (bf16[512,512]{1,0:T(8,128)(2,1)S(1)}, bf16[512,512]{1,0:T(8,128)(2,1)S(1)}, u32[]{:S(2)}, u32[]{:S(2)}) collective-permute-start(bf16[512,512]{1,0:T(8,128)(2,1)S(1)} %get-tuple-element.10.refs_0_), channel_id=1, source_target_pairs={{1,0},{0,1},{3,2},{2,3},{5,4},{4,5},{7,6},{6,7},{9,8},{8,9},{11,10... | collective-permute-start | bytes 1572872 | tf_op jit(solution)/shard_map/ppermute | solution.py:198
  15.8 4.7 %collective-permute-start.2 = (bf16[512,512]{1,0:T(8,128)(2,1)S(1)}, bf16[512,512]{1,0:T(8,128)(2,1)S(1)}, u32[]{:S(2)}, u32[]{:S(2)}) collective-permute-start(bf16[512,512]{1,0:T(8,128)(2,1)S(1)} %relay.4.refs_1_.refs_2_), channel_id=1, source_target_pairs={{1,0},{0,1},{3,2},{2,3},{5,4},{4,5},{7,6},{6,7},{9,8},{8,9},{11,10... | collective-permute-start | bytes 1572872 | tf_op jit(solution)/shard_map/ppermute | solution.py:198
  19.9 9.2 %collective-permute-start.5 = (bf16[512,256]{1,0:T(8,128)(2,1)S(1)}, bf16[512,256]{1,0:T(8,128)(2,1)S(1)}, u32[]{:S(2)}, u32[]{:S(2)}) collective-permute-start(bf16[512,256]{1,0:T(8,128)(2,1)S(1)} %relay.5.refs_1_.refs_6_), channel_id=1, source_target_pairs={{4,0},{0,4},{12,8},{8,12},{5,1},{1,5},{13,9},{9,13},{6,2},{2,6},{1... | collective-permute-start | bytes 786440 | tf_op jit(solution)/shard_map/ppermute | solution.py:198
  22.1 7.0 %collective-permute-start.6 = (bf16[128,384]{1,0:T(8,128)(2,1)S(1)}, bf16[128,384]{1,0:T(8,128)(2,1)S(1)}, u32[]{:S(2)}, u32[]{:S(2)}) collective-permute-start(bf16[128,384]{1,0:T(8,128)(2,1)S(1)} %get-tuple-element.15.refs_1_), channel_id=1, source_target_pairs={{8,0},{12,4},{0,8},{4,12},{9,1},{13,5},{1,9},{5,13},{10,2},{14,6},... | collective-permute-start | bytes 294920 | tf_op jit(solution)/shard_map/ppermute | solution.py:198
  29.7 6.0 %collective-permute-start.7 = (bf16[128,384]{1,0:T(8,128)(2,1)S(1)}, bf16[128,384]{1,0:T(8,128)(2,1)S(1)}, u32[]{:S(2)}, u32[]{:S(2)}) collective-permute-start(bf16[128,384]{1,0:T(8,128)(2,1)S(1)} %get-tuple-element.17.refs_0_), channel_id=1, source_target_pairs={{4,0},{0,4},{12,8},{8,12},{5,1},{1,5},{13,9},{9,13},{6,2},{2,6},{1... | collective-permute-start | bytes 294920 | tf_op jit(solution)/shard_map/ppermute | solution.py:198
  33.1 2.6 %copy-start = (f32[1,256,256]{2,1,0:T(8,128)S(1)}, f32[1,256,256]{2,1,0:T(8,128)}, u32[]{:S(2)}) copy-start(f32[1,256,256]{2,1,0:T(8,128)} %diag_ref.1) | copy-start | bytes 786436

commit v12 on v10

--- a/solution.py
+++ b/solution.py
@@ -219,7 +219,7 @@
     slots = ((wanted_pair - col // PAIR) % pairs) * PAIR + (wanted_side ^ (col % PAIR))
 
     partial, chosen, turned, early = partial_product(tops, [factor_panel, beside] + crossed, slots)
-    early = [early] + [after(from_pair(early, "prow", d, 1), swapped[-1]) for d in range(1, pairs)]
+    early = [early] + [after(from_pair(early, "prow", d, 0), swapped[-1]) for d in range(1, pairs)]
     if pairs > 2:
         selected, late = products(partial, chosen, turned, swapped, [])
         parts = early + [late] + [from_pair(late, "prow", d, 0) for d in range(1, pairs)]

time: 36.2 us -> 36.4 us (level)
  waiting for transfers between devices: 16 us -> 18.3 us
  starting transfers between devices: 13.7 us -> 11.6 us
    ppermute x8, waiting for transfers between devices: 16 us -> 18.3 us  [from_pair(): return lax.ppermute(block, axis, moves)]
    ppermute x8, starting transfers between devices: 13.7 us -> 11.6 us  [from_pair(): return lax.ppermute(block, axis, moves)]
where the time goes in v12:
time: 36.4 us; the launch traced here: 36.3 us
  waiting for transfers between devices  18.3 us (50%)
  starting transfers between devices  11.6 us (32%)
  Pallas kernels  4.83 us (13%)
  other arithmetic  0.85 us (2%)
  between operations  0.67 us (2%)
    ppermute x8, waiting for transfers between devices, from_pair(): return lax.ppermute(block, axis, moves)  18.3 us
    ppermute x8, starting transfers between devices, from_pair(): return lax.ppermute(block, axis, moves)  11.6 us
    pallas_call x1, Pallas kernels, build_panel(): pl.pallas_call(panel_kernel, out_shape=(pltpu.VMEM(cross_blocks.shape, jn...  1.78 us
    pallas_call x1, Pallas kernels, partial_product(): pl.pallas_call(functools.partial(partial_kernel, n), out_shape=(jax.Shape...  1.62 us
    neg x1, other arithmetic, on_device(): return (-selected, finish(diag_inverse, [update, mate(update, 'prow')]))  0.83 us
    pallas_call x1, Pallas kernels, finish(): pl.pallas_call(finish_kernel, out_shape=jax.ShapeDtypeStruct(diag_inverse...  0.81 us
  transfers between devices with their start and end apart: 8, of which 6 were waited for; matrix products, arithmetic and copies ran while one was open for 2% of the time, Pallas kernels for 9%

profile of v12, /device:TPU:0, one launch (start us, length us, event | category | flops | bytes accessed | tf_op | source)
XLA Modules:
  0.0 36.3 jit_solution(12258734603558651985)
XLA Ops:
  0.6 3.0 %collective-permute-start.1 = (bf16[512,512]{1,0:T(8,128)(2,1)}, bf16[512,512]{1,0:T(8,128)(2,1)S(1)}, u32[]{:S(2)}, u32[]{:S(2)}) collective-permute-start(bf16[512,512]{1,0:T(8,128)(2,1)} %top_hbm.1), channel_id=1, source_target_pairs={{2,0},{3,1},{0,2},{1,3},{6,4},{7,5},{4,6},{5,7},{10,8},{11,9},{8,1... | collective-permute-start | bytes 1572872 | tf_op jit(solution)/shard_map/ppermute | solution.py:198
  3.6 1.8 %panel.1 = (bf16[512,256]{1,0:T(8,128)(2,1)S(1)}, bf16[512,512]{1,0:T(8,128)(2,1)S(1)}) custom-call(s32[2]{0:T(128)} %bitcast.1, f32[512,256]{1,0:T(8,128)} %cross_hbm.1, f32[1,256,256]{2,1,0:T(8,128)} %diag_ref.1, bf16[512,512]{1,0:T(8,128)(2,1)} %top_hbm.1), custom_call_target="tpu_custom_call" | custom-call | tf_op jit(solution)/shard_map/panel/pallas_call | solution.py:52
  5.4 3.7 %collective-permute-start.4 = (bf16[512,256]{1,0:T(8,128)(2,1)S(1)}, bf16[512,256]{1,0:T(8,128)(2,1)S(1)}, u32[]{:S(2)}, u32[]{:S(2)}) collective-permute-start(bf16[512,256]{1,0:T(8,128)(2,1)S(1)} %get-tuple-element.11.refs_1_.refs_4_), channel_id=1, source_target_pairs={{12,0},{8,4},{4,8},{0,12},{13,1},{9,5},{5,9},{1,13},{14,2},{10,6},... | collective-permute-start | bytes 786440 | tf_op jit(solution)/shard_map/ppermute | solution.py:198
  9.1 0.0 collective-permute-start.3
  9.1 0.0 collective-permute-start
  9.1 6.7 %collective-permute-done.1.refs_0_ = bf16[512,512]{1,0:T(8,128)(2,1)S(1)} collective-permute-done((bf16[512,512]{1,0:T(8,128)(2,1)}, bf16[512,512]{1,0:T(8,128)(2,1)S(1)}, u32[]{:S(2)}, u32[]{:S(2)}) %collective-permute-start.1) | collective-permute-done | bytes 524320 | tf_op jit(solution)/shard_map/ppermute | solution.py:198
  15.8 0.0 collective-permute-start.2
  15.8 0.8 %collective-permute-done.4.refs_0_ = bf16[512,256]{1,0:T(8,128)(2,1)S(1)} collective-permute-done((bf16[512,256]{1,0:T(8,128)(2,1)S(1)}, bf16[512,256]{1,0:T(8,128)(2,1)S(1)}, u32[]{:S(2)}, u32[]{:S(2)}) %collective-permute-start.4) | collective-permute-done | bytes 262176 | tf_op jit(solution)/shard_map/ppermute | solution.py:198
  16.6 3.9 %collective-permute-start.5 = (bf16[512,256]{1,0:T(8,128)(2,1)S(1)}, bf16[512,256]{1,0:T(8,128)(2,1)S(1)}, u32[]{:S(2)}, u32[]{:S(2)}) collective-permute-start(bf16[512,256]{1,0:T(8,128)(2,1)S(1)} %relay.5.refs_1_.refs_6_), channel_id=1, source_target_pairs={{4,0},{0,4},{12,8},{8,12},{5,1},{1,5},{13,9},{9,13},{6,2},{2,6},{1... | collective-permute-start | bytes 786440 | tf_op jit(solution)/shard_map/ppermute | solution.py:198
  20.4 0.5 %collective-permute-done.3.refs_0_ = bf16[512,256]{1,0:T(8,128)(2,1)S(1)} collective-permute-done((bf16[512,256]{1,0:T(8,128)(2,1)S(1)}, bf16[512,256]{1,0:T(8,128)(2,1)S(1)}, u32[]{:S(2)}, u32[]{:S(2)}) %collective-permute-start.3) | collective-permute-done | bytes 262176 | tf_op jit(solution)/shard_map/ppermute | solution.py:198
  20.9 0.0 collective-permute-done.refs_1_
  20.9 0.0 collective-permute-done.2.refs_3_
  20.9 1.6 %partial.1 = (f32[512,256]{1,0:T(8,128)S(1)}, bf16[1,512,512]{2,1,0:T(8,128)(2,1)S(1)}, bf16[256,512]{1,0:T(8,128)(2,1)S(1)}, bf16[128,384]{1,0:T(8,128)(2,1)S(1)}) custom-call(s32[4]{0:T(128)S(1)} %fusion.2.slots_ref, bf16[512,512]{1,0:T(8,128)(2,1)S(1)} %get-tuple-element.10.refs_0_, bf16[512,512]{1,0:T(8,128)(2,1)S(1)} %collective-permute-done.refs_1_, ...), custom_call_target="tpu_custom_call" | custom-call | flops 536870912 | bytes 3145728 | tf_op jit(solution)/shard_map/partial/pallas_call | solution.py:121
  22.6 0.6 %collective-permute-start.6 = (bf16[128,384]{1,0:T(8,128)(2,1)S(1)}, bf16[128,384]{1,0:T(8,128)(2,1)S(1)}, u32[]{:S(2)}, u32[]{:S(2)}) collective-permute-start(bf16[128,384]{1,0:T(8,128)(2,1)S(1)} %get-tuple-element.15.refs_1_), channel_id=1, source_target_pairs={{8,0},{12,4},{0,8},{4,12},{9,1},{13,5},{1,9},{5,13},{10,2},{14,6},... | collective-permute-start | bytes 294920 | tf_op jit(solution)/shard_map/ppermute | solution.py:198
  23.2 3.7 %collective-permute-done.5.refs_1_.refs_0_ = bf16[512,256]{1,0:T(8,128)(2,1)S(1)} collective-permute-done((bf16[512,256]{1,0:T(8,128)(2,1)S(1)}, bf16[512,256]{1,0:T(8,128)(2,1)S(1)}, u32[]{:S(2)}, u32[]{:S(2)}) %collective-permute-start.5) | collective-permute-done | bytes 262176 | tf_op jit(solution)/shard_map/ppermute | solution.py:198
  26.9 3.3 %collective-permute-done.6.refs_0_ = bf16[128,384]{1,0:T(8,128)(2,1)S(1)} collective-permute-done((bf16[128,384]{1,0:T(8,128)(2,1)S(1)}, bf16[128,384]{1,0:T(8,128)(2,1)S(1)}, u32[]{:S(2)}, u32[]{:S(2)}) %collective-permute-start.6) | collective-permute-done | bytes 98336 | tf_op jit(solution)/shard_map/ppermute | solution.py:198
  30.2 0.6 %products.1 = (f32[512,256]{1,0:T(8,128)S(1)}, bf16[128,384]{1,0:T(8,128)(2,1)S(1)}) custom-call(f32[512,256]{1,0:T(8,128)S(1)} %get-tuple-element.12.partial_ref, bf16[1,512,512]{2,1,0:T(8,128)(2,1)S(1)} %get-tuple-element.13.chosen_ref, bf16[256,512]{1,0:T(8,128)(2,1)S(1)} %get-tuple-element.14.turned_ref, ...), custom_call_target="tpu_custom_call" | custom-call | tf_op jit(solution)/shard_map/products/pallas_call | solution.py:155
  30.8 0.4 %collective-permute-start.7 = (bf16[128,384]{1,0:T(8,128)(2,1)S(1)}, bf16[128,384]{1,0:T(8,128)(2,1)S(1)}, u32[]{:S(2)}, u32[]{:S(2)}) collective-permute-start(bf16[128,384]{1,0:T(8,128)(2,1)S(1)} %get-tuple-element.17.refs_0_), channel_id=1, source_target_pairs={{4,0},{0,4},{12,8},{8,12},{5,1},{1,5},{13,9},{9,13},{6,2},{2,6},{1... | collective-permute-start | bytes 294920 | tf_op jit(solution)/shard_map/ppermute | solution.py:198
  31.2 0.0 copy-start
  31.2 0.8 %neg.3 = f32[512,256]{1,0:T(8,128)} negate(f32[512,256]{1,0:T(8,128)S(1)} %get-tuple-element.16) | non-fusion elementwise | flops 131072 | bytes 1048576 | tf_op jit(solution)/shard_map/neg | solution.py:229
  32.0 3.4 %collective-permute-done.7.refs_1_ = bf16[128,384]{1,0:T(8,128)(2,1)S(1)} collective-permute-done((bf16[128,384]{1,0:T(8,128)(2,1)S(1)}, bf16[128,384]{1,0:T(8,128)(2,1)S(1)}, u32[]{:S(2)}, u32[]{:S(2)}) %collective-permute-start.7) | collective-permute-done | bytes 98336 | tf_op jit(solution)/shard_map/ppermute | solution.py:198
  35.5 0.0 copy-done
  35.5 0.8 %finish.1 = f32[1,256,256]{2,1,0:T(8,128)} custom-call(f32[1,256,256]{2,1,0:T(8,128)S(1)} %copy-done, bf16[128,384]{1,0:T(8,128)(2,1)S(1)} %get-tuple-element.17.refs_0_, bf16[128,384]{1,0:T(8,128)(2,1)S(1)} %collective-permute-done.7.refs_1_), custom_call_target="tpu_custom_call" | custom-call | tf_op jit(solution)/shard_map/finish/pallas_call | solution.py:180
  (5 shorter events, 0.0 us)
Async XLA Ops:
  0.6 15.1 %collective-permute-start.1 = (bf16[512,512]{1,0:T(8,128)(2,1)}, bf16[512,512]{1,0:T(8,128)(2,1)S(1)}, u32[]{:S(2)}, u32[]{:S(2)}) collective-permute-start(bf16[512,512]{1,0:T(8,128)(2,1)} %top_hbm.1), channel_id=1, source_target_pairs={{2,0},{3,1},{0,2},{1,3},{6,4},{7,5},{4,6},{5,7},{10,8},{11,9},{8,1... | collective-permute-start | bytes 1572872 | tf_op jit(solution)/shard_map/ppermute | solution.py:198
  5.4 11.1 %collective-permute-start.4 = (bf16[512,256]{1,0:T(8,128)(2,1)S(1)}, bf16[512,256]{1,0:T(8,128)(2,1)S(1)}, u32[]{:S(2)}, u32[]{:S(2)}) collective-permute-start(bf16[512,256]{1,0:T(8,128)(2,1)S(1)} %get-tuple-element.11.refs_1_.refs_4_), channel_id=1, source_target_pairs={{12,0},{8,4},{4,8},{0,12},{13,1},{9,5},{5,9},{1,13},{14,2},{10,6},... | collective-permute-start | bytes 786440 | tf_op jit(solution)/shard_map/ppermute | solution.py:198
  9.1 11.8 %collective-permute-start.3 = (bf16[512,256]{1,0:T(8,128)(2,1)S(1)}, bf16[512,256]{1,0:T(8,128)(2,1)S(1)}, u32[]{:S(2)}, u32[]{:S(2)}) collective-permute-start(bf16[512,256]{1,0:T(8,128)(2,1)S(1)} %get-tuple-element.11.refs_1_.refs_4_), channel_id=1, source_target_pairs={{4,0},{0,4},{12,8},{8,12},{5,1},{1,5},{13,9},{9,13},{6,2},{2,6},{1... | collective-permute-start | bytes 786440 | tf_op jit(solution)/shard_map/ppermute | solution.py:198
  9.1 11.8 %collective-permute-start = (bf16[512,512]{1,0:T(8,128)(2,1)S(1)}, bf16[512,512]{1,0:T(8,128)(2,1)S(1)}, u32[]{:S(2)}, u32[]{:S(2)}) collective-permute-start(bf16[512,512]{1,0:T(8,128)(2,1)S(1)} %get-tuple-element.10.refs_0_), channel_id=1, source_target_pairs={{1,0},{0,1},{3,2},{2,3},{5,4},{4,5},{7,6},{6,7},{9,8},{8,9},{11,10... | collective-permute-start | bytes 1572872 | tf_op jit(solution)/shard_map/ppermute | solution.py:198
  15.8 5.2 %collective-permute-start.2 = (bf16[512,512]{1,0:T(8,128)(2,1)S(1)}, bf16[512,512]{1,0:T(8,128)(2,1)S(1)}, u32[]{:S(2)}, u32[]{:S(2)}) collective-permute-start(bf16[512,512]{1,0:T(8,128)(2,1)S(1)} %relay.4.refs_1_.refs_2_), channel_id=1, source_target_pairs={{1,0},{0,1},{3,2},{2,3},{5,4},{4,5},{7,6},{6,7},{9,8},{8,9},{11,10... | collective-permute-start | bytes 1572872 | tf_op jit(solution)/shard_map/ppermute | solution.py:198
  16.6 10.3 %collective-permute-start.5 = (bf16[512,256]{1,0:T(8,128)(2,1)S(1)}, bf16[512,256]{1,0:T(8,128)(2,1)S(1)}, u32[]{:S(2)}, u32[]{:S(2)}) collective-permute-start(bf16[512,256]{1,0:T(8,128)(2,1)S(1)} %relay.5.refs_1_.refs_6_), channel_id=1, source_target_pairs={{4,0},{0,4},{12,8},{8,12},{5,1},{1,5},{13,9},{9,13},{6,2},{2,6},{1... | collective-permute-start | bytes 786440 | tf_op jit(solution)/shard_map/ppermute | solution.py:198
  22.6 7.6 %collective-permute-start.6 = (bf16[128,384]{1,0:T(8,128)(2,1)S(1)}, bf16[128,384]{1,0:T(8,128)(2,1)S(1)}, u32[]{:S(2)}, u32[]{:S(2)}) collective-permute-start(bf16[128,384]{1,0:T(8,128)(2,1)S(1)} %get-tuple-element.15.refs_1_), channel_id=1, source_target_pairs={{8,0},{12,4},{0,8},{4,12},{9,1},{13,5},{1,9},{5,13},{10,2},{14,6},... | collective-permute-start | bytes 294920 | tf_op jit(solution)/shard_map/ppermute | solution.py:198
  30.8 4.7 %collective-permute-start.7 = (bf16[128,384]{1,0:T(8,128)(2,1)S(1)}, bf16[128,384]{1,0:T(8,128)(2,1)S(1)}, u32[]{:S(2)}, u32[]{:S(2)}) collective-permute-start(bf16[128,384]{1,0:T(8,128)(2,1)S(1)} %get-tuple-element.17.refs_0_), channel_id=1, source_target_pairs={{4,0},{0,4},{12,8},{8,12},{5,1},{1,5},{13,9},{9,13},{6,2},{2,6},{1... | collective-permute-start | bytes 294920 | tf_op jit(solution)/shard_map/ppermute | solution.py:198
  31.2 4.3 %copy-start = (f32[1,256,256]{2,1,0:T(8,128)S(1)}, f32[1,256,256]{2,1,0:T(8,128)}, u32[]{:S(2)}) copy-start(f32[1,256,256]{2,1,0:T(8,128)} %diag_ref.1) | copy-start | bytes 786436

commit v13 on v10

--- a/solution.py
+++ b/solution.py
@@ -87,10 +87,16 @@
 
 def store_upper(out_ref, update, *others):
     half = update.shape[0] // 2
-    for columns, value in ((pl.ds(0, 2 * half), update[:half]), (pl.ds(2 * half, half), update[half:, half:])):
+    quarter = half // 2
+    left, right = update[:, :half], update[:, half:]
+    lanes = lax.broadcasted_iota(jnp.int32, (quarter, half), 1)
+    last = jnp.where(lanes < quarter, pltpu.roll(right[3 * quarter:], quarter, 1), left[quarter:half])
+    tiles = [left[:quarter], right[:quarter], right[quarter:half], right[half:3 * quarter], last]
+    for t, tile in enumerate(tiles):
+        columns = pl.ds(t * half, half)
         for other in others:
-            value += other[:, columns].astype(jnp.float32)
-        out_ref[:, columns] = value.astype(jnp.bfloat16)
+            tile += other[:, columns].astype(jnp.float32)
+        out_ref[:, columns] = tile.astype(jnp.bfloat16)
 
 
 def partial_kernel(n, slots_ref, *refs):
@@ -124,7 +130,7 @@
             jax.ShapeDtypeStruct((rows, width), jnp.float32),
             jax.ShapeDtypeStruct((n // 2 - 1,) + tops[0].shape, jnp.bfloat16),
             jax.ShapeDtypeStruct((width, rows), jnp.bfloat16),
-            jax.ShapeDtypeStruct((width // 2, 3 * (width // 2)), jnp.bfloat16),
+            jax.ShapeDtypeStruct((width // 4, 5 * (width // 2)), jnp.bfloat16),
         ),
         in_specs=[SMEM] + [VMEM] * (n + len(panels)),
         out_specs=(VMEM, VMEM, VMEM, VMEM),
@@ -156,7 +162,7 @@
         functools.partial(product_kernel, len(panels), alone),
         out_shape=(
             jax.ShapeDtypeStruct((rows, width), jnp.float32),
-            jax.ShapeDtypeStruct((width // 2, 3 * (width // 2)), jnp.bfloat16),
+            jax.ShapeDtypeStruct((width // 4, 5 * (width // 2)), jnp.bfloat16),
         ),
         in_specs=[VMEM] * (3 + len(panels) + len(early)),
         out_specs=(VMEM, VMEM),
@@ -170,10 +176,22 @@
     total = refs[0][...].astype(jnp.float32)
     for ref in refs[1:-1]:
         total += ref[...].astype(jnp.float32)
-    half = total.shape[0]
-    out_ref[0, :half, :] = diag_ref[0, :half, :] + total[:, :2 * half]
-    out_ref[0, half:, :half] = diag_ref[0, half:, :half] + total[:, half:2 * half].T
-    out_ref[0, half:, half:] = diag_ref[0, half:, half:] + total[:, 2 * half:]
+    quarter = total.shape[0]
+    half = 2 * quarter
+    tiles = [total[:, t * half:(t + 1) * half] for t in range(5)]
+    rows = lax.broadcasted_iota(jnp.int32, (half, half), 0)
+    columns = lax.broadcasted_iota(jnp.int32, (half, half), 1)
+    mirrored = (rows >= quarter) & (columns < quarter)
+
+    def corner(top, bottom):
+        block = jnp.concatenate([top, bottom], axis=0)
+        return jnp.where(mirrored, block.T, block)
+
+    side = jnp.concatenate([tiles[1], tiles[2]], axis=0)
+    out_ref[0, :half, :half] = diag_ref[0, :half, :half] + corner(tiles[0], tiles[4])
+    out_ref[0, :half, half:] = diag_ref[0, :half, half:] + side
+    out_ref[0, half:, :half] = diag_ref[0, half:, :half] + side.T
+    out_ref[0, half:, half:] = diag_ref[0, half:, half:] + corner(tiles[3], pltpu.roll(tiles[4], quarter, 1))
 
 
 def finish(diag_inverse, updates):

time: 36.2 us -> 35.8 us (0.989)
  waiting for transfers between devices: 16 us -> 15.5 us
    ppermute x8, waiting for transfers between devices: 16 us -> 15.5 us  [from_pair(): return lax.ppermute(block, axis, moves)]
  transfers between devices with their start and end apart: 8 -> 8, of which waited for: 6 -> 6; matrix products, arithmetic and copies ran while one was open for 2% -> 2% of each run, Pallas kernels for 9% -> 10%
where the time goes in v13:
time: 35.8 us; the launch traced here: 35.7 us
  waiting for transfers between devices  15.5 us (43%)
  starting transfers between devices  13.6 us (38%)
  Pallas kernels  5.02 us (14%)
  other arithmetic  0.85 us (2%)
  between operations  0.66 us (2%)
    ppermute x8, waiting for transfers between devices, from_pair(): return lax.ppermute(block, axis, moves)  15.5 us
    ppermute x8, starting transfers between devices, from_pair(): return lax.ppermute(block, axis, moves)  13.6 us
    pallas_call x1, Pallas kernels, build_panel(): pl.pallas_call(panel_kernel, out_shape=(pltpu.VMEM(cross_blocks.shape, jn...  1.78 us
    pallas_call x1, Pallas kernels, partial_product(): pl.pallas_call(functools.partial(partial_kernel, n), out_shape=(jax.Shape...  1.69 us
    pallas_call x1, Pallas kernels, finish(): pl.pallas_call(finish_kernel, out_shape=jax.ShapeDtypeStruct(diag_inverse...  0.87 us
    neg x1, other arithmetic, on_device(): return (-selected, finish(diag_inverse, [update, mate(update, 'prow')]))  0.83 us
  transfers between devices with their start and end apart: 8, of which 6 were waited for; matrix products, arithmetic and copies ran while one was open for 2% of the time, Pallas kernels for 10%

profile of v13, /device:TPU:0, one launch (start us, length us, event | category | flops | bytes accessed | tf_op | source)
XLA Modules:
  0.0 35.7 jit_solution(9893620006203335944)
XLA Ops:
  0.6 3.0 %collective-permute-start.1 = (bf16[512,512]{1,0:T(8,128)(2,1)}, bf16[512,512]{1,0:T(8,128)(2,1)S(1)}, u32[]{:S(2)}, u32[]{:S(2)}) collective-permute-start(bf16[512,512]{1,0:T(8,128)(2,1)} %top_hbm.1), channel_id=1, source_target_pairs={{2,0},{3,1},{0,2},{1,3},{6,4},{7,5},{4,6},{5,7},{10,8},{11,9},{8,1... | collective-permute-start | bytes 1572872 | tf_op jit(solution)/shard_map/ppermute | solution.py:216
  3.6 1.8 %panel.1 = (bf16[512,256]{1,0:T(8,128)(2,1)S(1)}, bf16[512,512]{1,0:T(8,128)(2,1)S(1)}) custom-call(s32[2]{0:T(128)} %bitcast.1, f32[512,256]{1,0:T(8,128)} %cross_hbm.1, f32[1,256,256]{2,1,0:T(8,128)} %diag_ref.1, bf16[512,512]{1,0:T(8,128)(2,1)} %top_hbm.1), custom_call_target="tpu_custom_call" | custom-call | tf_op jit(solution)/shard_map/panel/pallas_call | solution.py:52
  5.4 3.7 %collective-permute-start.4 = (bf16[512,256]{1,0:T(8,128)(2,1)S(1)}, bf16[512,256]{1,0:T(8,128)(2,1)S(1)}, u32[]{:S(2)}, u32[]{:S(2)}) collective-permute-start(bf16[512,256]{1,0:T(8,128)(2,1)S(1)} %get-tuple-element.11.refs_1_.refs_4_), channel_id=1, source_target_pairs={{12,0},{8,4},{4,8},{0,12},{13,1},{9,5},{5,9},{1,13},{14,2},{10,6},... | collective-permute-start | bytes 786440 | tf_op jit(solution)/shard_map/ppermute | solution.py:216
  9.1 0.0 collective-permute-start.3
  9.1 0.0 collective-permute-start
  9.1 6.7 %collective-permute-done.1.refs_0_ = bf16[512,512]{1,0:T(8,128)(2,1)S(1)} collective-permute-done((bf16[512,512]{1,0:T(8,128)(2,1)}, bf16[512,512]{1,0:T(8,128)(2,1)S(1)}, u32[]{:S(2)}, u32[]{:S(2)}) %collective-permute-start.1) | collective-permute-done | bytes 524320 | tf_op jit(solution)/shard_map/ppermute | solution.py:216
  15.8 0.0 collective-permute-start.2
  15.8 0.8 %collective-permute-done.4.refs_0_ = bf16[512,256]{1,0:T(8,128)(2,1)S(1)} collective-permute-done((bf16[512,256]{1,0:T(8,128)(2,1)S(1)}, bf16[512,256]{1,0:T(8,128)(2,1)S(1)}, u32[]{:S(2)}, u32[]{:S(2)}) %collective-permute-start.4) | collective-permute-done | bytes 262176 | tf_op jit(solution)/shard_map/ppermute | solution.py:216
  16.6 3.9 %collective-permute-start.5 = (bf16[512,256]{1,0:T(8,128)(2,1)S(1)}, bf16[512,256]{1,0:T(8,128)(2,1)S(1)}, u32[]{:S(2)}, u32[]{:S(2)}) collective-permute-start(bf16[512,256]{1,0:T(8,128)(2,1)S(1)} %relay.5.refs_1_.refs_6_), channel_id=1, source_target_pairs={{4,0},{0,4},{12,8},{8,12},{5,1},{1,5},{13,9},{9,13},{6,2},{2,6},{1... | collective-permute-start | bytes 786440 | tf_op jit(solution)/shard_map/ppermute | solution.py:216
  20.4 0.5 %collective-permute-done.3.refs_0_ = bf16[512,256]{1,0:T(8,128)(2,1)S(1)} collective-permute-done((bf16[512,256]{1,0:T(8,128)(2,1)S(1)}, bf16[512,256]{1,0:T(8,128)(2,1)S(1)}, u32[]{:S(2)}, u32[]{:S(2)}) %collective-permute-start.3) | collective-permute-done | bytes 262176 | tf_op jit(solution)/shard_map/ppermute | solution.py:216
  20.9 0.0 collective-permute-done.refs_1_
  20.9 0.0 collective-permute-done.2.refs_3_
  20.9 1.7 %partial.1 = (f32[512,256]{1,0:T(8,128)S(1)}, bf16[1,512,512]{2,1,0:T(8,128)(2,1)S(1)}, bf16[256,512]{1,0:T(8,128)(2,1)S(1)}, bf16[64,640]{1,0:T(8,128)(2,1)S(1)}) custom-call(s32[4]{0:T(128)S(1)} %fusion.2.slots_ref, bf16[512,512]{1,0:T(8,128)(2,1)S(1)} %get-tuple-element.10.refs_0_, bf16[512,512]{1,0:T(8,128)(2,1)S(1)} %collective-permute-done.refs_1_, ...), custom_call_target="tpu_custom_call" | custom-call | flops 536870912 | bytes 3145728 | tf_op jit(solution)/shard_map/partial/pallas_call | solution.py:127
  22.6 2.1 %collective-permute-start.6 = (bf16[64,640]{1,0:T(8,128)(2,1)S(1)}, bf16[64,640]{1,0:T(8,128)(2,1)S(1)}, u32[]{:S(2)}, u32[]{:S(2)}) collective-permute-start(bf16[64,640]{1,0:T(8,128)(2,1)S(1)} %get-tuple-element.15.refs_1_), channel_id=1, source_target_pairs={{12,0},{8,4},{4,8},{0,12},{13,1},{9,5},{5,9},{1,13},{14,2},{10,6},... | collective-permute-start | bytes 245768 | tf_op jit(solution)/shard_map/ppermute | solution.py:216
  24.7 1.8 %collective-permute-done.5.refs_1_.refs_0_ = bf16[512,256]{1,0:T(8,128)(2,1)S(1)} collective-permute-done((bf16[512,256]{1,0:T(8,128)(2,1)S(1)}, bf16[512,256]{1,0:T(8,128)(2,1)S(1)}, u32[]{:S(2)}, u32[]{:S(2)}) %collective-permute-start.5) | collective-permute-done | bytes 262176 | tf_op jit(solution)/shard_map/ppermute | solution.py:216
  26.5 3.1 %collective-permute-done.6.refs_0_ = bf16[64,640]{1,0:T(8,128)(2,1)S(1)} collective-permute-done((bf16[64,640]{1,0:T(8,128)(2,1)S(1)}, bf16[64,640]{1,0:T(8,128)(2,1)S(1)}, u32[]{:S(2)}, u32[]{:S(2)}) %collective-permute-start.6) | collective-permute-done | bytes 81952 | tf_op jit(solution)/shard_map/ppermute | solution.py:216
  29.6 0.7 %products.1 = (f32[512,256]{1,0:T(8,128)S(1)}, bf16[64,640]{1,0:T(8,128)(2,1)S(1)}) custom-call(f32[512,256]{1,0:T(8,128)S(1)} %get-tuple-element.12.partial_ref, bf16[1,512,512]{2,1,0:T(8,128)(2,1)S(1)} %get-tuple-element.13.chosen_ref, bf16[256,512]{1,0:T(8,128)(2,1)S(1)} %get-tuple-element.14.turned_ref, ...), custom_call_target="tpu_custom_call" | custom-call | tf_op jit(solution)/shard_map/products/pallas_call | solution.py:161
  30.3 1.0 %collective-permute-start.7 = (bf16[64,640]{1,0:T(8,128)(2,1)S(1)}, bf16[64,640]{1,0:T(8,128)(2,1)S(1)}, u32[]{:S(2)}, u32[]{:S(2)}) collective-permute-start(bf16[64,640]{1,0:T(8,128)(2,1)S(1)} %get-tuple-element.17.refs_0_), channel_id=1, source_target_pairs={{4,0},{0,4},{12,8},{8,12},{5,1},{1,5},{13,9},{9,13},{6,2},{2,6},{1... | collective-permute-start | bytes 245768 | tf_op jit(solution)/shard_map/ppermute | solution.py:216
  31.3 0.0 copy-start
  31.3 0.8 %neg.3 = f32[512,256]{1,0:T(8,128)} negate(f32[512,256]{1,0:T(8,128)S(1)} %get-tuple-element.16) | non-fusion elementwise | flops 131072 | bytes 1048576 | tf_op jit(solution)/shard_map/neg | solution.py:247
  32.1 2.7 %collective-permute-done.7.refs_1_ = bf16[64,640]{1,0:T(8,128)(2,1)S(1)} collective-permute-done((bf16[64,640]{1,0:T(8,128)(2,1)S(1)}, bf16[64,640]{1,0:T(8,128)(2,1)S(1)}, u32[]{:S(2)}, u32[]{:S(2)}) %collective-permute-start.7) | collective-permute-done | bytes 81952 | tf_op jit(solution)/shard_map/ppermute | solution.py:216
  34.8 0.0 copy-done
  34.8 0.9 %finish.1 = f32[1,256,256]{2,1,0:T(8,128)} custom-call(f32[1,256,256]{2,1,0:T(8,128)S(1)} %copy-done, bf16[64,640]{1,0:T(8,128)(2,1)S(1)} %get-tuple-element.17.refs_0_, bf16[64,640]{1,0:T(8,128)(2,1)S(1)} %collective-permute-done.7.refs_1_), custom_call_target="tpu_custom_call" | custom-call | tf_op jit(solution)/shard_map/finish/pallas_call | solution.py:198
  (5 shorter events, 0.0 us)
Async XLA Ops:
  0.6 15.1 %collective-permute-start.1 = (bf16[512,512]{1,0:T(8,128)(2,1)}, bf16[512,512]{1,0:T(8,128)(2,1)S(1)}, u32[]{:S(2)}, u32[]{:S(2)}) collective-permute-start(bf16[512,512]{1,0:T(8,128)(2,1)} %top_hbm.1), channel_id=1, source_target_pairs={{2,0},{3,1},{0,2},{1,3},{6,4},{7,5},{4,6},{5,7},{10,8},{11,9},{8,1... | collective-permute-start | bytes 1572872 | tf_op jit(solution)/shard_map/ppermute | solution.py:216
  5.4 11.1 %collective-permute-start.4 = (bf16[512,256]{1,0:T(8,128)(2,1)S(1)}, bf16[512,256]{1,0:T(8,128)(2,1)S(1)}, u32[]{:S(2)}, u32[]{:S(2)}) collective-permute-start(bf16[512,256]{1,0:T(8,128)(2,1)S(1)} %get-tuple-element.11.refs_1_.refs_4_), channel_id=1, source_target_pairs={{12,0},{8,4},{4,8},{0,12},{13,1},{9,5},{5,9},{1,13},{14,2},{10,6},... | collective-permute-start | bytes 786440 | tf_op jit(solution)/shard_map/ppermute | solution.py:216
  9.1 11.8 %collective-permute-start.3 = (bf16[512,256]{1,0:T(8,128)(2,1)S(1)}, bf16[512,256]{1,0:T(8,128)(2,1)S(1)}, u32[]{:S(2)}, u32[]{:S(2)}) collective-permute-start(bf16[512,256]{1,0:T(8,128)(2,1)S(1)} %get-tuple-element.11.refs_1_.refs_4_), channel_id=1, source_target_pairs={{4,0},{0,4},{12,8},{8,12},{5,1},{1,5},{13,9},{9,13},{6,2},{2,6},{1... | collective-permute-start | bytes 786440 | tf_op jit(solution)/shard_map/ppermute | solution.py:216
  9.1 11.8 %collective-permute-start = (bf16[512,512]{1,0:T(8,128)(2,1)S(1)}, bf16[512,512]{1,0:T(8,128)(2,1)S(1)}, u32[]{:S(2)}, u32[]{:S(2)}) collective-permute-start(bf16[512,512]{1,0:T(8,128)(2,1)S(1)} %get-tuple-element.10.refs_0_), channel_id=1, source_target_pairs={{1,0},{0,1},{3,2},{2,3},{5,4},{4,5},{7,6},{6,7},{9,8},{8,9},{11,10... | collective-permute-start | bytes 1572872 | tf_op jit(solution)/shard_map/ppermute | solution.py:216
  15.8 5.2 %collective-permute-start.2 = (bf16[512,512]{1,0:T(8,128)(2,1)S(1)}, bf16[512,512]{1,0:T(8,128)(2,1)S(1)}, u32[]{:S(2)}, u32[]{:S(2)}) collective-permute-start(bf16[512,512]{1,0:T(8,128)(2,1)S(1)} %relay.4.refs_1_.refs_2_), channel_id=1, source_target_pairs={{1,0},{0,1},{3,2},{2,3},{5,4},{4,5},{7,6},{6,7},{9,8},{8,9},{11,10... | collective-permute-start | bytes 1572872 | tf_op jit(solution)/shard_map/ppermute | solution.py:216
  16.6 10.0 %collective-permute-start.5 = (bf16[512,256]{1,0:T(8,128)(2,1)S(1)}, bf16[512,256]{1,0:T(8,128)(2,1)S(1)}, u32[]{:S(2)}, u32[]{:S(2)}) collective-permute-start(bf16[512,256]{1,0:T(8,128)(2,1)S(1)} %relay.5.refs_1_.refs_6_), channel_id=1, source_target_pairs={{4,0},{0,4},{12,8},{8,12},{5,1},{1,5},{13,9},{9,13},{6,2},{2,6},{1... | collective-permute-start | bytes 786440 | tf_op jit(solution)/shard_map/ppermute | solution.py:216
  22.6 7.0 %collective-permute-start.6 = (bf16[64,640]{1,0:T(8,128)(2,1)S(1)}, bf16[64,640]{1,0:T(8,128)(2,1)S(1)}, u32[]{:S(2)}, u32[]{:S(2)}) collective-permute-start(bf16[64,640]{1,0:T(8,128)(2,1)S(1)} %get-tuple-element.15.refs_1_), channel_id=1, source_target_pairs={{12,0},{8,4},{4,8},{0,12},{13,1},{9,5},{5,9},{1,13},{14,2},{10,6},... | collective-permute-start | bytes 245768 | tf_op jit(solution)/shard_map/ppermute | solution.py:216
  30.3 4.5 %collective-permute-start.7 = (bf16[64,640]{1,0:T(8,128)(2,1)S(1)}, bf16[64,640]{1,0:T(8,128)(2,1)S(1)}, u32[]{:S(2)}, u32[]{:S(2)}) collective-permute-start(bf16[64,640]{1,0:T(8,128)(2,1)S(1)} %get-tuple-element.17.refs_0_), channel_id=1, source_target_pairs={{4,0},{0,4},{12,8},{8,12},{5,1},{1,5},{13,9},{9,13},{6,2},{2,6},{1... | collective-permute-start | bytes 245768 | tf_op jit(solution)/shard_map/ppermute | solution.py:216
  31.3 3.5 %copy-start = (f32[1,256,256]{2,1,0:T(8,128)S(1)}, f32[1,256,256]{2,1,0:T(8,128)}, u32[]{:S(2)}) copy-start(f32[1,256,256]{2,1,0:T(8,128)} %diag_ref.1) | copy-start | bytes 786436

commit v14 on v13

--- a/solution.py
+++ b/solution.py
@@ -26,46 +26,48 @@
     return jnp.dot(left, right, preferred_element_type=jnp.float32)
 
 
-def panel_kernel(pattern_hbm, cross_hbm, diag_hbm, top_hbm, panel_ref, top_ref, pattern_ref, cross_ref, diag_ref, sems):
+def token_kernel(out_ref):
+    out_ref[...] = jnp.zeros_like(out_ref)
+
+
+def token():
+    return pl.pallas_call(
+        token_kernel,
+        out_shape=jax.ShapeDtypeStruct((8, 128), jnp.float32),
+        out_specs=VMEM,
+        compiler_params=SMALL,
+        cost_estimate=pl.CostEstimate(flops=HOP_COST, bytes_accessed=0, transcendentals=0),
+        name="token",
+    )()
+
+
+def panel_kernel(pattern_ref, cross_ref, diag_ref, top_hbm, token_ref, panel_ref, top_ref, sem):
+    del token_ref
     width = diag_ref.shape[1]
-    blocks = pattern_hbm.shape[0]
-    rows = [pl.ds(a * width, width) for a in range(blocks)]
-    loads = [pltpu.make_async_copy(cross_hbm.at[r], cross_ref.at[r], sems.at[a]) for a, r in enumerate(rows)]
-    diag_copy = pltpu.make_async_copy(diag_hbm, diag_ref, sems.at[blocks])
-    pattern_copy = pltpu.make_async_copy(pattern_hbm, pattern_ref, sems.at[blocks + 1])
-    top_copy = pltpu.make_async_copy(top_hbm, top_ref, sems.at[blocks + 2])
-    for copy in [pattern_copy, diag_copy] + loads + [top_copy]:
-        copy.start()
-    pattern_copy.wait()
-    diag_copy.wait()
+    top_copy = pltpu.make_async_copy(top_hbm, top_ref, sem)
+    top_copy.start()
     diag_high, diag_low = split(diag_ref[0])
-    for a in range(blocks):
-        loads[a].wait()
-        high, low = split(cross_ref[rows[a], :] * pattern_ref[a].astype(jnp.float32))
+    for a in range(pattern_ref.shape[1]):
+        rows = pl.ds(a * width, width)
+        high, low = split(cross_ref[rows, :] * pattern_ref[:, a:a + 1].astype(jnp.float32))
         solved = dot(high, diag_high) + (dot(high, diag_low) + dot(low, diag_high))
-        panel_ref[rows[a], :] = solved.astype(jnp.bfloat16)
+        panel_ref[rows, :] = solved.astype(jnp.bfloat16)
     top_copy.wait()
 
 
 def build_panel(cross_blocks, diag_inverse, pattern, inverse_top):
-    inputs = [pattern.reshape(-1), cross_blocks, diag_inverse, inverse_top]
     return pl.pallas_call(
         panel_kernel,
         out_shape=(
             pltpu.VMEM(cross_blocks.shape, jnp.bfloat16),
             pltpu.VMEM(inverse_top.shape, inverse_top.dtype),
         ),
-        in_specs=[HBM] * 4,
+        in_specs=[VMEM, VMEM, VMEM, HBM, ANY],
         out_specs=(VMEM, VMEM),
-        scratch_shapes=[
-            pltpu.SMEM((pattern.size,), jnp.int32),
-            pltpu.VMEM(cross_blocks.shape, jnp.float32),
-            pltpu.VMEM(diag_inverse.shape, jnp.float32),
-            pltpu.SemaphoreType.DMA((pattern.size + 3,)),
-        ],
+        scratch_shapes=[pltpu.SemaphoreType.DMA],
         compiler_params=PARAMS,
         name="panel",
-    )(*[pltpu.with_memory_space_constraint(x, pltpu.HBM) for x in inputs])
+    )(pattern.T, cross_blocks, diag_inverse, pltpu.with_memory_space_constraint(inverse_top, pltpu.HBM), token())
 
 
 def relay_kernel(*refs):

time: 35.8 us -> 35.8 us (level)
  Pallas kernels: 5.02 us -> 4.29 us
  local copies, waits for them, and re-layouts: 0.01 us -> 0.66 us
    pallas_call x1, Pallas kernels: 1.78 us -> 1.05 us  [build_panel(): pl.pallas_call(panel_kernel, out_shape=(pltpu.VMEM(cross_blocks.shape, jn...]
    unnamed x2 -> x6, local copies, waits for them, and re-layouts: 0.01 us -> 0.66 us
  transfers between devices with their start and end apart: 8 -> 8, of which waited for: 6 -> 6; matrix products, arithmetic and copies ran while one was open for 2% -> 2% of each run, Pallas kernels for 10% -> 8%
where the time goes in v14:
time: 35.8 us; the launch traced here: 35.6 us
  waiting for transfers between devices  15.5 us (43%)
  starting transfers between devices  13.6 us (38%)
  Pallas kernels  4.29 us (12%)
  other arithmetic  0.85 us (2%)
  between operations  0.68 us (2%)
  local copies, waits for them, and re-layouts  0.66 us (2%)
    ppermute x8, waiting for transfers between devices, from_pair(): return lax.ppermute(block, axis, moves)  15.5 us
    ppermute x8, starting transfers between devices, from_pair(): return lax.ppermute(block, axis, moves)  13.6 us
    pallas_call x1, Pallas kernels, partial_product(): pl.pallas_call(functools.partial(partial_kernel, n), out_shape=(jax.Shape...  1.69 us
    pallas_call x1, Pallas kernels, build_panel(): pl.pallas_call(panel_kernel, out_shape=(pltpu.VMEM(cross_blocks.shape, jn...  1.05 us
    pallas_call x1, Pallas kernels, finish(): pl.pallas_call(finish_kernel, out_shape=jax.ShapeDtypeStruct(diag_inverse...  0.86 us
    neg x1, other arithmetic, on_device(): return (-selected, finish(diag_inverse, [update, mate(update, 'prow')]))  0.83 us
  transfers between devices with their start and end apart: 8, of which 6 were waited for; matrix products, arithmetic and copies ran while one was open for 2% of the time, Pallas kernels for 8%

profile of v14, /device:TPU:0, one launch (start us, length us, event | category | flops | bytes accessed | tf_op | source)
XLA Modules:
  0.0 35.6 jit_solution(11611895679983292177)
XLA Ops:
  0.6 0.0 copy-start
  0.6 0.0 copy-start.1
  0.6 3.0 %collective-permute-start.1 = (bf16[512,512]{1,0:T(8,128)(2,1)}, bf16[512,512]{1,0:T(8,128)(2,1)S(1)}, u32[]{:S(2)}, u32[]{:S(2)}) collective-permute-start(bf16[512,512]{1,0:T(8,128)(2,1)} %top_hbm.1), channel_id=1, source_target_pairs={{2,0},{3,1},{0,2},{1,3},{6,4},{7,5},{4,6},{5,7},{10,8},{11,9},{8,1... | collective-permute-start | bytes 1572872 | tf_op jit(solution)/shard_map/ppermute | solution.py:218
  3.7 0.0 copy-start.2
  3.7 0.0 copy-done
  3.7 0.0 copy-done.1
  3.7 0.6 %copy-done.2 = s32[2,1]{0,1:T(1,128)S(1)} copy-done((s32[2,1]{0,1:T(1,128)S(1)}, s32[2,1]{0,1:T(1,128)}, u32[]{:S(2)}) %copy-start.2) | copy-done | bytes 32
  4.3 1.1 %panel.1 = (bf16[512,256]{1,0:T(8,128)(2,1)S(1)}, bf16[512,512]{1,0:T(8,128)(2,1)S(1)}) custom-call(s32[1,2]{1,0:T(1,128)S(1)} %bitcast.1, f32[512,256]{1,0:T(8,128)S(1)} %copy-done.1, f32[1,256,256]{2,1,0:T(8,128)S(1)} %copy-done, bf16[512,512]{1,0:T(8,128)(2,1)} %top_hbm.1, f32[8,128]{1,0:T(8,128)S(1)} %token_.1.token_ref), custom_call_target="tpu_custom_call" | custom-call | tf_op jit(solution)/shard_map/panel/pallas_call | solution.py:59
  5.4 3.7 %collective-permute-start.4 = (bf16[512,256]{1,0:T(8,128)(2,1)S(1)}, bf16[512,256]{1,0:T(8,128)(2,1)S(1)}, u32[]{:S(2)}, u32[]{:S(2)}) collective-permute-start(bf16[512,256]{1,0:T(8,128)(2,1)S(1)} %get-tuple-element.11.refs_1_.refs_4_), channel_id=1, source_target_pairs={{12,0},{8,4},{4,8},{0,12},{13,1},{9,5},{5,9},{1,13},{14,2},{10,6},... | collective-permute-start | bytes 786440 | tf_op jit(solution)/shard_map/ppermute | solution.py:218
  9.0 0.0 collective-permute-start.3
  9.0 0.0 collective-permute-start
  9.1 6.7 %collective-permute-done.1.refs_0_ = bf16[512,512]{1,0:T(8,128)(2,1)S(1)} collective-permute-done((bf16[512,512]{1,0:T(8,128)(2,1)}, bf16[512,512]{1,0:T(8,128)(2,1)S(1)}, u32[]{:S(2)}, u32[]{:S(2)}) %collective-permute-start.1) | collective-permute-done | bytes 524320 | tf_op jit(solution)/shard_map/ppermute | solution.py:218
  15.8 0.0 collective-permute-start.2
  15.8 0.7 %collective-permute-done.4.refs_0_ = bf16[512,256]{1,0:T(8,128)(2,1)S(1)} collective-permute-done((bf16[512,256]{1,0:T(8,128)(2,1)S(1)}, bf16[512,256]{1,0:T(8,128)(2,1)S(1)}, u32[]{:S(2)}, u32[]{:S(2)}) %collective-permute-start.4) | collective-permute-done | bytes 262176 | tf_op jit(solution)/shard_map/ppermute | solution.py:218
  16.5 3.9 %collective-permute-start.5 = (bf16[512,256]{1,0:T(8,128)(2,1)S(1)}, bf16[512,256]{1,0:T(8,128)(2,1)S(1)}, u32[]{:S(2)}, u32[]{:S(2)}) collective-permute-start(bf16[512,256]{1,0:T(8,128)(2,1)S(1)} %relay.5.refs_1_.refs_6_), channel_id=1, source_target_pairs={{4,0},{0,4},{12,8},{8,12},{5,1},{1,5},{13,9},{9,13},{6,2},{2,6},{1... | collective-permute-start | bytes 786440 | tf_op jit(solution)/shard_map/ppermute | solution.py:218
  20.4 0.5 %collective-permute-done.3.refs_0_ = bf16[512,256]{1,0:T(8,128)(2,1)S(1)} collective-permute-done((bf16[512,256]{1,0:T(8,128)(2,1)S(1)}, bf16[512,256]{1,0:T(8,128)(2,1)S(1)}, u32[]{:S(2)}, u32[]{:S(2)}) %collective-permute-start.3) | collective-permute-done | bytes 262176 | tf_op jit(solution)/shard_map/ppermute | solution.py:218
  20.9 0.0 collective-permute-done.refs_1_
  20.9 0.0 collective-permute-done.2.refs_3_
  20.9 1.7 %partial.1 = (f32[512,256]{1,0:T(8,128)S(1)}, bf16[1,512,512]{2,1,0:T(8,128)(2,1)S(1)}, bf16[256,512]{1,0:T(8,128)(2,1)S(1)}, bf16[64,640]{1,0:T(8,128)(2,1)S(1)}) custom-call(s32[4]{0:T(128)S(1)} %fusion.2.slots_ref, bf16[512,512]{1,0:T(8,128)(2,1)S(1)} %get-tuple-element.10.refs_0_, bf16[512,512]{1,0:T(8,128)(2,1)S(1)} %collective-permute-done.refs_1_, ...), custom_call_target="tpu_custom_call" | custom-call | flops 536870912 | bytes 3145728 | tf_op jit(solution)/shard_map/partial/pallas_call | solution.py:129
  22.6 2.1 %collective-permute-start.6 = (bf16[64,640]{1,0:T(8,128)(2,1)S(1)}, bf16[64,640]{1,0:T(8,128)(2,1)S(1)}, u32[]{:S(2)}, u32[]{:S(2)}) collective-permute-start(bf16[64,640]{1,0:T(8,128)(2,1)S(1)} %get-tuple-element.15.refs_1_), channel_id=1, source_target_pairs={{12,0},{8,4},{4,8},{0,12},{13,1},{9,5},{5,9},{1,13},{14,2},{10,6},... | collective-permute-start | bytes 245768 | tf_op jit(solution)/shard_map/ppermute | solution.py:218
  24.6 1.8 %collective-permute-done.5.refs_1_.refs_0_ = bf16[512,256]{1,0:T(8,128)(2,1)S(1)} collective-permute-done((bf16[512,256]{1,0:T(8,128)(2,1)S(1)}, bf16[512,256]{1,0:T(8,128)(2,1)S(1)}, u32[]{:S(2)}, u32[]{:S(2)}) %collective-permute-start.5) | collective-permute-done | bytes 262176 | tf_op jit(solution)/shard_map/ppermute | solution.py:218
  26.5 3.1 %collective-permute-done.6.refs_0_ = bf16[64,640]{1,0:T(8,128)(2,1)S(1)} collective-permute-done((bf16[64,640]{1,0:T(8,128)(2,1)S(1)}, bf16[64,640]{1,0:T(8,128)(2,1)S(1)}, u32[]{:S(2)}, u32[]{:S(2)}) %collective-permute-start.6) | collective-permute-done | bytes 81952 | tf_op jit(solution)/shard_map/ppermute | solution.py:218
  29.6 0.7 %products.1 = (f32[512,256]{1,0:T(8,128)S(1)}, bf16[64,640]{1,0:T(8,128)(2,1)S(1)}) custom-call(f32[512,256]{1,0:T(8,128)S(1)} %get-tuple-element.12.partial_ref, bf16[1,512,512]{2,1,0:T(8,128)(2,1)S(1)} %get-tuple-element.13.chosen_ref, bf16[256,512]{1,0:T(8,128)(2,1)S(1)} %get-tuple-element.14.turned_ref, ...), custom_call_target="tpu_custom_call" | custom-call | tf_op jit(solution)/shard_map/products/pallas_call | solution.py:163
  30.3 1.0 %collective-permute-start.7 = (bf16[64,640]{1,0:T(8,128)(2,1)S(1)}, bf16[64,640]{1,0:T(8,128)(2,1)S(1)}, u32[]{:S(2)}, u32[]{:S(2)}) collective-permute-start(bf16[64,640]{1,0:T(8,128)(2,1)S(1)} %get-tuple-element.17.refs_0_), channel_id=1, source_target_pairs={{4,0},{0,4},{12,8},{8,12},{5,1},{1,5},{13,9},{9,13},{6,2},{2,6},{1... | collective-permute-start | bytes 245768 | tf_op jit(solution)/shard_map/ppermute | solution.py:218
  31.2 0.8 %neg.3 = f32[512,256]{1,0:T(8,128)} negate(f32[512,256]{1,0:T(8,128)S(1)} %get-tuple-element.16) | non-fusion elementwise | flops 131072 | bytes 1048576 | tf_op jit(solution)/shard_map/neg | solution.py:249
  32.1 2.7 %collective-permute-done.7.refs_1_ = bf16[64,640]{1,0:T(8,128)(2,1)S(1)} collective-permute-done((bf16[64,640]{1,0:T(8,128)(2,1)S(1)}, bf16[64,640]{1,0:T(8,128)(2,1)S(1)}, u32[]{:S(2)}, u32[]{:S(2)}) %collective-permute-start.7) | collective-permute-done | bytes 81952 | tf_op jit(solution)/shard_map/ppermute | solution.py:218
  34.8 0.9 %finish.1 = f32[1,256,256]{2,1,0:T(8,128)} custom-call(f32[1,256,256]{2,1,0:T(8,128)S(1)} %copy-done, bf16[64,640]{1,0:T(8,128)(2,1)S(1)} %get-tuple-element.17.refs_0_, bf16[64,640]{1,0:T(8,128)(2,1)S(1)} %collective-permute-done.7.refs_1_), custom_call_target="tpu_custom_call" | custom-call | tf_op jit(solution)/shard_map/finish/pallas_call | solution.py:200
  (6 shorter events, 0.0 us)
Async XLA Ops:
  0.6 3.0 %copy-start = (f32[1,256,256]{2,1,0:T(8,128)S(1)}, f32[1,256,256]{2,1,0:T(8,128)}, u32[]{:S(2)}) copy-start(f32[1,256,256]{2,1,0:T(8,128)} %diag_ref.3) | copy-start | bytes 786436
  0.6 3.0 %copy-start.1 = (f32[512,256]{1,0:T(8,128)S(1)}, f32[512,256]{1,0:T(8,128)}, u32[]{:S(2)}) copy-start(f32[512,256]{1,0:T(8,128)} %cross_ref.1) | copy-start | bytes 1572868
  0.6 15.1 %collective-permute-start.1 = (bf16[512,512]{1,0:T(8,128)(2,1)}, bf16[512,512]{1,0:T(8,128)(2,1)S(1)}, u32[]{:S(2)}, u32[]{:S(2)}) collective-permute-start(bf16[512,512]{1,0:T(8,128)(2,1)} %top_hbm.1), channel_id=1, source_target_pairs={{2,0},{3,1},{0,2},{1,3},{6,4},{7,5},{4,6},{5,7},{10,8},{11,9},{8,1... | collective-permute-start | bytes 1572872 | tf_op jit(solution)/shard_map/ppermute | solution.py:218
  3.7 0.7 %copy-start.2 = (s32[2,1]{0,1:T(1,128)S(1)}, s32[2,1]{0,1:T(1,128)}, u32[]{:S(2)}) copy-start(s32[2,1]{0,1:T(1,128)} %param.7) | copy-start | bytes 28
  5.4 11.1 %collective-permute-start.4 = (bf16[512,256]{1,0:T(8,128)(2,1)S(1)}, bf16[512,256]{1,0:T(8,128)(2,1)S(1)}, u32[]{:S(2)}, u32[]{:S(2)}) collective-permute-start(bf16[512,256]{1,0:T(8,128)(2,1)S(1)} %get-tuple-element.11.refs_1_.refs_4_), channel_id=1, source_target_pairs={{12,0},{8,4},{4,8},{0,12},{13,1},{9,5},{5,9},{1,13},{14,2},{10,6},... | collective-permute-start | bytes 786440 | tf_op jit(solution)/shard_map/ppermute | solution.py:218
  9.0 11.8 %collective-permute-start.3 = (bf16[512,256]{1,0:T(8,128)(2,1)S(1)}, bf16[512,256]{1,0:T(8,128)(2,1)S(1)}, u32[]{:S(2)}, u32[]{:S(2)}) collective-permute-start(bf16[512,256]{1,0:T(8,128)(2,1)S(1)} %get-tuple-element.11.refs_1_.refs_4_), channel_id=1, source_target_pairs={{4,0},{0,4},{12,8},{8,12},{5,1},{1,5},{13,9},{9,13},{6,2},{2,6},{1... | collective-permute-start | bytes 786440 | tf_op jit(solution)/shard_map/ppermute | solution.py:218
  9.0 11.8 %collective-permute-start = (bf16[512,512]{1,0:T(8,128)(2,1)S(1)}, bf16[512,512]{1,0:T(8,128)(2,1)S(1)}, u32[]{:S(2)}, u32[]{:S(2)}) collective-permute-start(bf16[512,512]{1,0:T(8,128)(2,1)S(1)} %get-tuple-element.10.refs_0_), channel_id=1, source_target_pairs={{1,0},{0,1},{3,2},{2,3},{5,4},{4,5},{7,6},{6,7},{9,8},{8,9},{11,10... | collective-permute-start | bytes 1572872 | tf_op jit(solution)/shard_map/ppermute | solution.py:218
  15.8 5.1 %collective-permute-start.2 = (bf16[512,512]{1,0:T(8,128)(2,1)S(1)}, bf16[512,512]{1,0:T(8,128)(2,1)S(1)}, u32[]{:S(2)}, u32[]{:S(2)}) collective-permute-start(bf16[512,512]{1,0:T(8,128)(2,1)S(1)} %relay.4.refs_1_.refs_2_), channel_id=1, source_target_pairs={{1,0},{0,1},{3,2},{2,3},{5,4},{4,5},{7,6},{6,7},{9,8},{8,9},{11,10... | collective-permute-start | bytes 1572872 | tf_op jit(solution)/shard_map/ppermute | solution.py:218
  16.5 10.0 %collective-permute-start.5 = (bf16[512,256]{1,0:T(8,128)(2,1)S(1)}, bf16[512,256]{1,0:T(8,128)(2,1)S(1)}, u32[]{:S(2)}, u32[]{:S(2)}) collective-permute-start(bf16[512,256]{1,0:T(8,128)(2,1)S(1)} %relay.5.refs_1_.refs_6_), channel_id=1, source_target_pairs={{4,0},{0,4},{12,8},{8,12},{5,1},{1,5},{13,9},{9,13},{6,2},{2,6},{1... | collective-permute-start | bytes 786440 | tf_op jit(solution)/shard_map/ppermute | solution.py:218
  22.6 7.0 %collective-permute-start.6 = (bf16[64,640]{1,0:T(8,128)(2,1)S(1)}, bf16[64,640]{1,0:T(8,128)(2,1)S(1)}, u32[]{:S(2)}, u32[]{:S(2)}) collective-permute-start(bf16[64,640]{1,0:T(8,128)(2,1)S(1)} %get-tuple-element.15.refs_1_), channel_id=1, source_target_pairs={{12,0},{8,4},{4,8},{0,12},{13,1},{9,5},{5,9},{1,13},{14,2},{10,6},... | collective-permute-start | bytes 245768 | tf_op jit(solution)/shard_map/ppermute | solution.py:218
  30.3 4.5 %collective-permute-start.7 = (bf16[64,640]{1,0:T(8,128)(2,1)S(1)}, bf16[64,640]{1,0:T(8,128)(2,1)S(1)}, u32[]{:S(2)}, u32[]{:S(2)}) collective-permute-start(bf16[64,640]{1,0:T(8,128)(2,1)S(1)} %get-tuple-element.17.refs_0_), channel_id=1, source_target_pairs={{4,0},{0,4},{12,8},{8,12},{5,1},{1,5},{13,9},{9,13},{6,2},{2,6},{1... | collective-permute-start | bytes 245768 | tf_op jit(solution)/shard_map/ppermute | solution.py:218

commit v15 on v14

--- a/solution.py
+++ b/solution.py
@@ -41,17 +41,22 @@
     )()
 
 
-def panel_kernel(pattern_ref, cross_ref, diag_ref, top_hbm, token_ref, panel_ref, top_ref, sem):
+def panel_kernel(pattern_hbm, cross_ref, diag_ref, top_hbm, token_ref, panel_ref, top_ref, pattern_ref, sems):
     del token_ref
     width = diag_ref.shape[1]
-    top_copy = pltpu.make_async_copy(top_hbm, top_ref, sem)
+    pattern_copy = pltpu.make_async_copy(pattern_hbm, pattern_ref, sems.at[0])
+    pattern_copy.start()
+    top_copy = pltpu.make_async_copy(top_hbm, top_ref, sems.at[1])
     top_copy.start()
     diag_high, diag_low = split(diag_ref[0])
-    for a in range(pattern_ref.shape[1]):
-        rows = pl.ds(a * width, width)
-        high, low = split(cross_ref[rows, :] * pattern_ref[:, a:a + 1].astype(jnp.float32))
-        solved = dot(high, diag_high) + (dot(high, diag_low) + dot(low, diag_high))
-        panel_ref[rows, :] = solved.astype(jnp.bfloat16)
+    solved = []
+    for a in range(pattern_hbm.shape[0]):
+        high, low = split(cross_ref[pl.ds(a * width, width), :])
+        solved.append(dot(high, diag_high) + (dot(high, diag_low) + dot(low, diag_high)))
+    pattern_copy.wait()
+    for a, block in enumerate(solved):
+        kept = jnp.where(pattern_ref[a] != 0, block, 0.0)
+        panel_ref[pl.ds(a * width, width), :] = kept.astype(jnp.bfloat16)
     top_copy.wait()
 
 
@@ -62,12 +67,18 @@
             pltpu.VMEM(cross_blocks.shape, jnp.bfloat16),
             pltpu.VMEM(inverse_top.shape, inverse_top.dtype),
         ),
-        in_specs=[VMEM, VMEM, VMEM, HBM, ANY],
+        in_specs=[HBM, VMEM, VMEM, HBM, ANY],
         out_specs=(VMEM, VMEM),
-        scratch_shapes=[pltpu.SemaphoreType.DMA],
+        scratch_shapes=[pltpu.SMEM((pattern.size,), jnp.int32), pltpu.SemaphoreType.DMA((2,))],
         compiler_params=PARAMS,
         name="panel",
-    )(pattern.T, cross_blocks, diag_inverse, pltpu.with_memory_space_constraint(inverse_top, pltpu.HBM), token())
+    )(
+        pltpu.with_memory_space_constraint(pattern.reshape(-1), pltpu.HBM),
+        cross_blocks,
+        diag_inverse,
+        pltpu.with_memory_space_constraint(inverse_top, pltpu.HBM),
+        token(),
+    )
 
 
 def relay_kernel(*refs):
@@ -225,8 +236,7 @@
     beside = mate(factor_panel, "prow")
     crossed = [from_pair(factor_panel, "prow", d, 1) for d in range(1, pairs)]
     near = [after(block, factor_panel) for block in near]
-    crossed = [after(block, near[0], cost=HOP_COST) for block in crossed]
-    beside = after(beside, *crossed, cost=2 * HOP_COST)
+    crossed = [after(block, near[0], beside, cost=HOP_COST) for block in crossed]
     swapped = [mate(block, "prow") for block in crossed]
 
     tops = [inverse_top, mate(inverse_top, "pcol")]

time: 35.8 us -> 35.9 us (level)
  waiting for transfers between devices: 15.5 us -> 19.4 us
  starting transfers between devices: 13.6 us -> 10.5 us
  local copies, waits for them, and re-layouts: 0.66 us -> 0.01 us
    ppermute x8, waiting for transfers between devices: 15.5 us -> 19.4 us  [from_pair(): return lax.ppermute(block, axis, moves)]
    ppermute x8, starting transfers between devices: 13.6 us -> 10.5 us  [from_pair(): return lax.ppermute(block, axis, moves)]
    unnamed x6 -> x4, local copies, waits for them, and re-layouts: 0.66 us -> 0.01 us
  transfers between devices with their start and end apart: 8 -> 8, of which waited for: 6 -> 5; matrix products, arithmetic and copies ran while one was open for 2% -> 2% of each run, Pallas kernels for 8% -> 8%
where the time goes in v15:
time: 35.9 us; the launch traced here: 35.7 us
  waiting for transfers between devices  19.4 us (54%)
  starting transfers between devices  10.5 us (29%)
  Pallas kernels  4.33 us (12%)
  other arithmetic  0.85 us (2%)
  between operations  0.69 us (2%)
    ppermute x8, waiting for transfers between devices, from_pair(): return lax.ppermute(block, axis, moves)  19.4 us
    ppermute x8, starting transfers between devices, from_pair(): return lax.ppermute(block, axis, moves)  10.5 us
    pallas_call x1, Pallas kernels, partial_product(): pl.pallas_call(functools.partial(partial_kernel, n), out_shape=(jax.Shape...  1.69 us
    pallas_call x1, Pallas kernels, build_panel(): pl.pallas_call(panel_kernel, out_shape=(pltpu.VMEM(cross_blocks.shape, jn...  1.08 us
    pallas_call x1, Pallas kernels, finish(): pl.pallas_call(finish_kernel, out_shape=jax.ShapeDtypeStruct(diag_inverse...  0.86 us
    neg x1, other arithmetic, on_device(): return (-selected, finish(diag_inverse, [update, mate(update, 'prow')]))  0.83 us
  transfers between devices with their start and end apart: 8, of which 5 were waited for; matrix products, arithmetic and copies ran while one was open for 2% of the time, Pallas kernels for 8%

profile of v15, /device:TPU:0, one launch (start us, length us, event | category | flops | bytes accessed | tf_op | source)
XLA Modules:
  0.0 35.7 jit_solution(13072522734246667239)
XLA Ops:
  0.6 0.0 copy-start
  0.6 0.0 copy-start.1
  0.6 3.0 %collective-permute-start.1 = (bf16[512,512]{1,0:T(8,128)(2,1)}, bf16[512,512]{1,0:T(8,128)(2,1)S(1)}, u32[]{:S(2)}, u32[]{:S(2)}) collective-permute-start(bf16[512,512]{1,0:T(8,128)(2,1)} %top_hbm.1), channel_id=1, source_target_pairs={{2,0},{3,1},{0,2},{1,3},{6,4},{7,5},{4,6},{5,7},{10,8},{11,9},{8,1... | collective-permute-start | bytes 1572872 | tf_op jit(solution)/shard_map/ppermute | solution.py:229
  3.7 0.0 copy-done
  3.7 0.0 copy-done.1
  3.7 1.1 %panel.1 = (bf16[512,256]{1,0:T(8,128)(2,1)S(1)}, bf16[512,512]{1,0:T(8,128)(2,1)S(1)}) custom-call(s32[2]{0:T(128)} %bitcast.1, f32[512,256]{1,0:T(8,128)S(1)} %copy-done.1, f32[1,256,256]{2,1,0:T(8,128)S(1)} %copy-done, bf16[512,512]{1,0:T(8,128)(2,1)} %top_hbm.1, f32[8,128]{1,0:T(8,128)S(1)} %token_.1.token_ref), custom_call_target="tpu_custom_call" | custom-call | tf_op jit(solution)/shard_map/panel/pallas_call | solution.py:64
  4.8 1.6 %collective-permute-start.3 = (bf16[512,256]{1,0:T(8,128)(2,1)S(1)}, bf16[512,256]{1,0:T(8,128)(2,1)S(1)}, u32[]{:S(2)}, u32[]{:S(2)}) collective-permute-start(bf16[512,256]{1,0:T(8,128)(2,1)S(1)} %get-tuple-element.11.refs_1_.refs_4_), channel_id=1, source_target_pairs={{4,0},{0,4},{12,8},{8,12},{5,1},{1,5},{13,9},{9,13},{6,2},{2,6},{1... | collective-permute-start | bytes 786440 | tf_op jit(solution)/shard_map/ppermute | solution.py:229
  6.4 2.5 %collective-permute-start.4 = (bf16[512,256]{1,0:T(8,128)(2,1)S(1)}, bf16[512,256]{1,0:T(8,128)(2,1)S(1)}, u32[]{:S(2)}, u32[]{:S(2)}) collective-permute-start(bf16[512,256]{1,0:T(8,128)(2,1)S(1)} %get-tuple-element.11.refs_1_.refs_4_), channel_id=1, source_target_pairs={{12,0},{8,4},{4,8},{0,12},{13,1},{9,5},{5,9},{1,13},{14,2},{10,6},... | collective-permute-start | bytes 786440 | tf_op jit(solution)/shard_map/ppermute | solution.py:229
  8.9 0.0 collective-permute-start
  8.9 6.9 %collective-permute-done.1.refs_0_ = bf16[512,512]{1,0:T(8,128)(2,1)S(1)} collective-permute-done((bf16[512,512]{1,0:T(8,128)(2,1)}, bf16[512,512]{1,0:T(8,128)(2,1)S(1)}, u32[]{:S(2)}, u32[]{:S(2)}) %collective-permute-start.1) | collective-permute-done | bytes 524320 | tf_op jit(solution)/shard_map/ppermute | solution.py:229
  15.8 0.0 collective-permute-start.2
  15.8 0.0 collective-permute-done.3.refs_2_.refs_5_
  15.8 4.5 %collective-permute-done.4.refs_0_ = bf16[512,256]{1,0:T(8,128)(2,1)S(1)} collective-permute-done((bf16[512,256]{1,0:T(8,128)(2,1)S(1)}, bf16[512,256]{1,0:T(8,128)(2,1)S(1)}, u32[]{:S(2)}, u32[]{:S(2)}) %collective-permute-start.4) | collective-permute-done | bytes 262176 | tf_op jit(solution)/shard_map/ppermute | solution.py:229
  20.3 0.6 %collective-permute-start.5 = (bf16[512,256]{1,0:T(8,128)(2,1)S(1)}, bf16[512,256]{1,0:T(8,128)(2,1)S(1)}, u32[]{:S(2)}, u32[]{:S(2)}) collective-permute-start(bf16[512,256]{1,0:T(8,128)(2,1)S(1)} %relay.4.refs_6_), channel_id=1, source_target_pairs={{4,0},{0,4},{12,8},{8,12},{5,1},{1,5},{13,9},{9,13},{6,2},{2,6},{1... | collective-permute-start | bytes 786440 | tf_op jit(solution)/shard_map/ppermute | solution.py:229
  20.9 0.0 collective-permute-done.refs_1_
  20.9 0.0 collective-permute-done.2.refs_3_
  20.9 1.7 %partial.1 = (f32[512,256]{1,0:T(8,128)S(1)}, bf16[1,512,512]{2,1,0:T(8,128)(2,1)S(1)}, bf16[256,512]{1,0:T(8,128)(2,1)S(1)}, bf16[64,640]{1,0:T(8,128)(2,1)S(1)}) custom-call(s32[4]{0:T(128)S(1)} %fusion.2.slots_ref, bf16[512,512]{1,0:T(8,128)(2,1)S(1)} %get-tuple-element.10.refs_0_, bf16[512,512]{1,0:T(8,128)(2,1)S(1)} %collective-permute-done.refs_1_, ...), custom_call_target="tpu_custom_call" | custom-call | flops 536870912 | bytes 3145728 | tf_op jit(solution)/shard_map/partial/pallas_call | solution.py:140
  22.6 2.7 %collective-permute-start.6 = (bf16[64,640]{1,0:T(8,128)(2,1)S(1)}, bf16[64,640]{1,0:T(8,128)(2,1)S(1)}, u32[]{:S(2)}, u32[]{:S(2)}) collective-permute-start(bf16[64,640]{1,0:T(8,128)(2,1)S(1)} %get-tuple-element.15.refs_1_), channel_id=1, source_target_pairs={{12,0},{8,4},{4,8},{0,12},{13,1},{9,5},{5,9},{1,13},{14,2},{10,6},... | collective-permute-start | bytes 245768 | tf_op jit(solution)/shard_map/ppermute | solution.py:229
  25.4 2.7 %collective-permute-done.5.refs_1_.refs_0_ = bf16[512,256]{1,0:T(8,128)(2,1)S(1)} collective-permute-done((bf16[512,256]{1,0:T(8,128)(2,1)S(1)}, bf16[512,256]{1,0:T(8,128)(2,1)S(1)}, u32[]{:S(2)}, u32[]{:S(2)}) %collective-permute-start.5) | collective-permute-done | bytes 262176 | tf_op jit(solution)/shard_map/ppermute | solution.py:229
  28.0 1.6 %collective-permute-done.6.refs_0_ = bf16[64,640]{1,0:T(8,128)(2,1)S(1)} collective-permute-done((bf16[64,640]{1,0:T(8,128)(2,1)S(1)}, bf16[64,640]{1,0:T(8,128)(2,1)S(1)}, u32[]{:S(2)}, u32[]{:S(2)}) %collective-permute-start.6) | collective-permute-done | bytes 81952 | tf_op jit(solution)/shard_map/ppermute | solution.py:229
  29.7 0.7 %products.1 = (f32[512,256]{1,0:T(8,128)S(1)}, bf16[64,640]{1,0:T(8,128)(2,1)S(1)}) custom-call(f32[512,256]{1,0:T(8,128)S(1)} %get-tuple-element.12.partial_ref, bf16[1,512,512]{2,1,0:T(8,128)(2,1)S(1)} %get-tuple-element.13.chosen_ref, bf16[256,512]{1,0:T(8,128)(2,1)S(1)} %get-tuple-element.14.turned_ref, ...), custom_call_target="tpu_custom_call" | custom-call | tf_op jit(solution)/shard_map/products/pallas_call | solution.py:174
  30.4 0.1 collective-permute-start.7
  30.4 0.8 %neg.3 = f32[512,256]{1,0:T(8,128)} negate(f32[512,256]{1,0:T(8,128)S(1)} %get-tuple-element.16) | non-fusion elementwise | flops 131072 | bytes 1048576 | tf_op jit(solution)/shard_map/neg | solution.py:259
  31.3 3.6 %collective-permute-done.7.refs_1_ = bf16[64,640]{1,0:T(8,128)(2,1)S(1)} collective-permute-done((bf16[64,640]{1,0:T(8,128)(2,1)S(1)}, bf16[64,640]{1,0:T(8,128)(2,1)S(1)}, u32[]{:S(2)}, u32[]{:S(2)}) %collective-permute-start.7) | collective-permute-done | bytes 81952 | tf_op jit(solution)/shard_map/ppermute | solution.py:229
  34.9 0.9 %finish.1 = f32[1,256,256]{2,1,0:T(8,128)} custom-call(f32[1,256,256]{2,1,0:T(8,128)S(1)} %copy-done, bf16[64,640]{1,0:T(8,128)(2,1)S(1)} %get-tuple-element.17.refs_0_, bf16[64,640]{1,0:T(8,128)(2,1)S(1)} %collective-permute-done.7.refs_1_), custom_call_target="tpu_custom_call" | custom-call | tf_op jit(solution)/shard_map/finish/pallas_call | solution.py:211
  (5 shorter events, 0.0 us)
Async XLA Ops:
  0.6 3.0 %copy-start = (f32[1,256,256]{2,1,0:T(8,128)S(1)}, f32[1,256,256]{2,1,0:T(8,128)}, u32[]{:S(2)}) copy-start(f32[1,256,256]{2,1,0:T(8,128)} %diag_ref.3) | copy-start | bytes 786436
  0.6 3.0 %copy-start.1 = (f32[512,256]{1,0:T(8,128)S(1)}, f32[512,256]{1,0:T(8,128)}, u32[]{:S(2)}) copy-start(f32[512,256]{1,0:T(8,128)} %cross_ref.1) | copy-start | bytes 1572868
  0.6 15.1 %collective-permute-start.1 = (bf16[512,512]{1,0:T(8,128)(2,1)}, bf16[512,512]{1,0:T(8,128)(2,1)S(1)}, u32[]{:S(2)}, u32[]{:S(2)}) collective-permute-start(bf16[512,512]{1,0:T(8,128)(2,1)} %top_hbm.1), channel_id=1, source_target_pairs={{2,0},{3,1},{0,2},{1,3},{6,4},{7,5},{4,6},{5,7},{10,8},{11,9},{8,1... | collective-permute-start | bytes 1572872 | tf_op jit(solution)/shard_map/ppermute | solution.py:229
  4.8 11.0 %collective-permute-start.3 = (bf16[512,256]{1,0:T(8,128)(2,1)S(1)}, bf16[512,256]{1,0:T(8,128)(2,1)S(1)}, u32[]{:S(2)}, u32[]{:S(2)}) collective-permute-start(bf16[512,256]{1,0:T(8,128)(2,1)S(1)} %get-tuple-element.11.refs_1_.refs_4_), channel_id=1, source_target_pairs={{4,0},{0,4},{12,8},{8,12},{5,1},{1,5},{13,9},{9,13},{6,2},{2,6},{1... | collective-permute-start | bytes 786440 | tf_op jit(solution)/shard_map/ppermute | solution.py:229
  6.4 13.9 %collective-permute-start.4 = (bf16[512,256]{1,0:T(8,128)(2,1)S(1)}, bf16[512,256]{1,0:T(8,128)(2,1)S(1)}, u32[]{:S(2)}, u32[]{:S(2)}) collective-permute-start(bf16[512,256]{1,0:T(8,128)(2,1)S(1)} %get-tuple-element.11.refs_1_.refs_4_), channel_id=1, source_target_pairs={{12,0},{8,4},{4,8},{0,12},{13,1},{9,5},{5,9},{1,13},{14,2},{10,6},... | collective-permute-start | bytes 786440 | tf_op jit(solution)/shard_map/ppermute | solution.py:229
  8.9 12.1 %collective-permute-start = (bf16[512,512]{1,0:T(8,128)(2,1)S(1)}, bf16[512,512]{1,0:T(8,128)(2,1)S(1)}, u32[]{:S(2)}, u32[]{:S(2)}) collective-permute-start(bf16[512,512]{1,0:T(8,128)(2,1)S(1)} %get-tuple-element.10.refs_0_), channel_id=1, source_target_pairs={{1,0},{0,1},{3,2},{2,3},{5,4},{4,5},{7,6},{6,7},{9,8},{8,9},{11,10... | collective-permute-start | bytes 1572872 | tf_op jit(solution)/shard_map/ppermute | solution.py:229
  15.8 5.2 %collective-permute-start.2 = (bf16[512,512]{1,0:T(8,128)(2,1)S(1)}, bf16[512,512]{1,0:T(8,128)(2,1)S(1)}, u32[]{:S(2)}, u32[]{:S(2)}) collective-permute-start(bf16[512,512]{1,0:T(8,128)(2,1)S(1)} %relay.3.refs_1_.refs_2_), channel_id=1, source_target_pairs={{1,0},{0,1},{3,2},{2,3},{5,4},{4,5},{7,6},{6,7},{9,8},{8,9},{11,10... | collective-permute-start | bytes 1572872 | tf_op jit(solution)/shard_map/ppermute | solution.py:229
  20.3 7.7 %collective-permute-start.5 = (bf16[512,256]{1,0:T(8,128)(2,1)S(1)}, bf16[512,256]{1,0:T(8,128)(2,1)S(1)}, u32[]{:S(2)}, u32[]{:S(2)}) collective-permute-start(bf16[512,256]{1,0:T(8,128)(2,1)S(1)} %relay.4.refs_6_), channel_id=1, source_target_pairs={{4,0},{0,4},{12,8},{8,12},{5,1},{1,5},{13,9},{9,13},{6,2},{2,6},{1... | collective-permute-start | bytes 786440 | tf_op jit(solution)/shard_map/ppermute | solution.py:229
  22.6 7.0 %collective-permute-start.6 = (bf16[64,640]{1,0:T(8,128)(2,1)S(1)}, bf16[64,640]{1,0:T(8,128)(2,1)S(1)}, u32[]{:S(2)}, u32[]{:S(2)}) collective-permute-start(bf16[64,640]{1,0:T(8,128)(2,1)S(1)} %get-tuple-element.15.refs_1_), channel_id=1, source_target_pairs={{12,0},{8,4},{4,8},{0,12},{13,1},{9,5},{5,9},{1,13},{14,2},{10,6},... | collective-permute-start | bytes 245768 | tf_op jit(solution)/shard_map/ppermute | solution.py:229
  30.4 4.5 %collective-permute-start.7 = (bf16[64,640]{1,0:T(8,128)(2,1)S(1)}, bf16[64,640]{1,0:T(8,128)(2,1)S(1)}, u32[]{:S(2)}, u32[]{:S(2)}) collective-permute-start(bf16[64,640]{1,0:T(8,128)(2,1)S(1)} %get-tuple-element.17.refs_0_), channel_id=1, source_target_pairs={{4,0},{0,4},{12,8},{8,12},{5,1},{1,5},{13,9},{9,13},{6,2},{2,6},{1... | collective-permute-start | bytes 245768 | tf_op jit(solution)/shard_map/ppermute | solution.py:229

commit v16 on v15

--- a/solution.py
+++ b/solution.py
@@ -41,8 +41,9 @@
     )()
 
 
-def panel_kernel(pattern_hbm, cross_ref, diag_ref, top_hbm, token_ref, panel_ref, top_ref, pattern_ref, sems):
+def panel_kernel(pattern_hbm, cross_ref, diag_ref, top_hbm, token_ref, panel_ref, top_ref, *refs):
     del token_ref
+    bands, (pattern_ref, sems) = refs[:-2], refs[-2:]
     width = diag_ref.shape[1]
     pattern_copy = pltpu.make_async_copy(pattern_hbm, pattern_ref, sems.at[0])
     pattern_copy.start()
@@ -55,20 +56,24 @@
         solved.append(dot(high, diag_high) + (dot(high, diag_low) + dot(low, diag_high)))
     pattern_copy.wait()
     for a, block in enumerate(solved):
-        kept = jnp.where(pattern_ref[a] != 0, block, 0.0)
-        panel_ref[pl.ds(a * width, width), :] = kept.astype(jnp.bfloat16)
+        kept = jnp.where(pattern_ref[a] != 0, block, 0.0).astype(jnp.bfloat16)
+        panel_ref[pl.ds(a * width, width), :] = kept
+        bands[a][...] = kept
     top_copy.wait()
 
 
 def build_panel(cross_blocks, diag_inverse, pattern, inverse_top):
+    blocks = pattern.size
+    band = (cross_blocks.shape[0] // blocks, cross_blocks.shape[1])
     return pl.pallas_call(
         panel_kernel,
         out_shape=(
             pltpu.VMEM(cross_blocks.shape, jnp.bfloat16),
             pltpu.VMEM(inverse_top.shape, inverse_top.dtype),
-        ),
+        )
+        + (pltpu.VMEM(band, jnp.bfloat16),) * blocks,
         in_specs=[HBM, VMEM, VMEM, HBM, ANY],
-        out_specs=(VMEM, VMEM),
+        out_specs=(VMEM,) * (2 + blocks),
         scratch_shapes=[pltpu.SMEM((pattern.size,), jnp.int32), pltpu.SemaphoreType.DMA((2,))],
         compiler_params=PARAMS,
         name="panel",
@@ -112,76 +117,119 @@
         out_ref[:, columns] = tile.astype(jnp.bfloat16)
 
 
-def partial_kernel(n, slots_ref, *refs):
-    tops, panels = refs[:n], refs[n:n + n // 2 + 1]
-    partial_ref, chosen_ref, turned_ref, update_ref, panel_buf = refs[n + n // 2 + 1:]
-    places = [0] + list(range(1, n, 2))
-    for place, panel in zip(places, panels):
-        panel_buf[slots_ref[place]] = panel[...]
-    for d, place in enumerate(range(2, n, 2)):
-        slot = slots_ref[place]
-        panel_buf[slot] = jnp.zeros(panel_buf.shape[1:], panel_buf.dtype)
-        for t in range(n):
-            @pl.when(slot == t)
-            def _():
-                chosen_ref[d] = tops[t][...]
-    total = dot(tops[0][...], panel_buf[0])
-    for t in range(1, n):
-        total += dot(tops[t][...], panel_buf[t])
-    partial_ref[...] = total
+def share(turned, product):
+    return dot(turned, product.astype(jnp.bfloat16))
+
+
+def choose(slot, tops, out_ref):
+    for t, top in enumerate(tops):
+        @pl.when(slot == t)
+        def _():
+            out_ref[...] = top[...]
+
+
+def near_kernel(n, slots_ref, *refs):
+    tops, panels = refs[:n], refs[n:n + PAIR]
+    partial_ref, turned_ref, update_ref, chosen_ref = refs[n + PAIR:]
+    for s in range(PAIR):
+        choose(slots_ref[s], tops, chosen_ref.at[s])
     turned = panels[0][...].astype(jnp.float32).T.astype(jnp.bfloat16)
     turned_ref[...] = turned
-    store_upper(update_ref, dot(turned, total.astype(jnp.bfloat16)))
-
-
-def partial_product(tops, panels, slots):
-    n = len(tops)
+    total = dot(chosen_ref[0], panels[0][...])
+    for s in range(1, PAIR):
+        total += dot(chosen_ref[s], panels[s][...])
+    partial_ref[...] = total
+    store_upper(update_ref, share(turned, total))
+
+
+def near_product(tops, panels, slots):
     rows, width = panels[0].shape
     return pl.pallas_call(
-        functools.partial(partial_kernel, n),
+        functools.partial(near_kernel, len(tops)),
         out_shape=(
             jax.ShapeDtypeStruct((rows, width), jnp.float32),
-            jax.ShapeDtypeStruct((n // 2 - 1,) + tops[0].shape, jnp.bfloat16),
             jax.ShapeDtypeStruct((width, rows), jnp.bfloat16),
             jax.ShapeDtypeStruct((width // 4, 5 * (width // 2)), jnp.bfloat16),
         ),
-        in_specs=[SMEM] + [VMEM] * (n + len(panels)),
-        out_specs=(VMEM, VMEM, VMEM, VMEM),
-        scratch_shapes=[pltpu.VMEM((n, rows, width), jnp.bfloat16)],
-        compiler_params=PARAMS,
-        cost_estimate=pl.CostEstimate(
-            flops=2 * n * rows * rows * width, bytes_accessed=2 * n * rows * (rows + width), transcendentals=0
+        in_specs=[SMEM] + [VMEM] * (len(tops) + len(panels)),
+        out_specs=(VMEM, VMEM, VMEM),
+        scratch_shapes=[pltpu.VMEM((PAIR,) + tops[0].shape, jnp.bfloat16)],
+        compiler_params=PARAMS,
+        name="near",
+    )(slots, *tops, *panels)
+
+
+def banded_dot(top, bands):
+    height = bands[0].shape[0]
+    total = dot(top[:, :height], bands[0][...])
+    for b, band in enumerate(bands[1:], 1):
+        total += dot(top[:, b * height:(b + 1) * height], band[...])
+    return total
+
+
+def far_kernel(n, blocks, slots_ref, partial_ref, turned_ref, *refs):
+    count = n // 2 - 1
+    tops, bands = refs[:n], refs[n:n + count * blocks]
+    out_ref, chosen_ref, update_ref, crossing_ref = refs[n + count * blocks:]
+    for d in range(count):
+        choose(slots_ref[2 * d + 3], tops, crossing_ref.at[d])
+        choose(slots_ref[2 * d + 2], tops, chosen_ref.at[d])
+    total = banded_dot(crossing_ref.at[0], bands[:blocks])
+    for d in range(1, count):
+        total += banded_dot(crossing_ref.at[d], bands[d * blocks:(d + 1) * blocks])
+    out_ref[...] = partial_ref[...] + total
+    update = share(turned_ref[...], total)
+    if count == 1:
+        update += update.T
+    store_upper(update_ref, update)
+
+
+def far_product(tops, partial, turned, crossed, slots):
+    n, blocks = len(tops), len(crossed[0])
+    rows, width = partial.shape
+    chosen = (n // 2 - 1,) + tops[0].shape
+    bands = [band for bands in crossed for band in bands]
+    return pl.pallas_call(
+        functools.partial(far_kernel, n, blocks),
+        out_shape=(
+            jax.ShapeDtypeStruct((rows, width), jnp.float32),
+            jax.ShapeDtypeStruct(chosen, jnp.bfloat16),
+            jax.ShapeDtypeStruct((width // 4, 5 * (width // 2)), jnp.bfloat16),
         ),
-        name="partial",
-    )(slots, *tops, *panels)
-
-
-def product_kernel(count, alone, partial_ref, chosen_ref, turned_ref, *refs):
-    panels, early, (selected_ref, update_ref) = refs[:count], refs[count:-2], refs[-2:]
-    rest = dot(chosen_ref[0], panels[0][...])
-    for d, panel in enumerate(panels[1:], 1):
-        rest += dot(chosen_ref[d], panel[...])
-    selected_ref[...] = partial_ref[...] + rest
-    update = dot(turned_ref[...], rest.astype(jnp.bfloat16))
-    if alone:
+        in_specs=[SMEM] + [VMEM] * (2 + n + len(bands)),
+        out_specs=(VMEM, VMEM, VMEM),
+        scratch_shapes=[pltpu.VMEM(chosen, jnp.bfloat16)],
+        compiler_params=PARAMS,
+        name="far",
+    )(slots, partial, turned, *tops, *bands)
+
+
+def last_kernel(count, blocks, partial_ref, chosen_ref, turned_ref, *refs):
+    bands, others, (selected_ref, update_ref) = refs[:count * blocks], refs[count * blocks:-2], refs[-2:]
+    total = banded_dot(chosen_ref.at[0], bands[:blocks])
+    for d in range(1, count):
+        total += banded_dot(chosen_ref.at[d], bands[d * blocks:(d + 1) * blocks])
+    selected_ref[...] = partial_ref[...] + total
+    update = share(turned_ref[...], total)
+    if count == 1:
         update += update.T
-    store_upper(update_ref, update, *early)
-
-
-def products(partial, chosen, turned, panels, early):
-    rows, width = panels[0].shape
-    alone = len(panels) == 1
-    return pl.pallas_call(
-        functools.partial(product_kernel, len(panels), alone),
+    store_upper(update_ref, update, *others)
+
+
+def last_product(partial, chosen, turned, swapped, others):
+    rows, width = partial.shape
+    bands = [band for bands in swapped for band in bands]
+    return pl.pallas_call(
+        functools.partial(last_kernel, len(swapped), len(swapped[0])),
         out_shape=(
             jax.ShapeDtypeStruct((rows, width), jnp.float32),
             jax.ShapeDtypeStruct((width // 4, 5 * (width // 2)), jnp.bfloat16),
         ),
-        in_specs=[VMEM] * (3 + len(panels) + len(early)),
+        in_specs=[VMEM] * (3 + len(bands) + len(others)),
         out_specs=(VMEM, VMEM),
         compiler_params=PARAMS,
-        name="products",
-    )(partial, chosen, turned, *panels, *early)
+        name="last",
+    )(partial, chosen, turned, *bands, *others)
 
 
 def finish_kernel(diag_ref, *refs):
@@ -232,12 +280,13 @@
         return from_pair(block, axis, 0, 1)
 
     near = [from_pair(inverse_top, "pcol", d, 0) for d in range(1, pairs)]
-    factor_panel, inverse_top = build_panel(cross_blocks, diag_inverse, pattern, inverse_top)
+    factor_panel, inverse_top, *bands = build_panel(cross_blocks, diag_inverse, pattern, inverse_top)
     beside = mate(factor_panel, "prow")
-    crossed = [from_pair(factor_panel, "prow", d, 1) for d in range(1, pairs)]
-    near = [after(block, factor_panel) for block in near]
-    crossed = [after(block, near[0], beside, cost=HOP_COST) for block in crossed]
-    swapped = [mate(block, "prow") for block in crossed]
+    crossed = [[from_pair(band, "prow", d, 1) for band in bands] for d in range(1, pairs)]
+    crossed = [[after(held[0], beside, cost=0)] + held[1:] for held in crossed]
+    near = [after(block, crossed[0][0], cost=0) for block in near]
+    crossed = [held[:1] + [after(band, near[0], cost=4 * HOP_COST) for band in held[1:]] for held in crossed]
+    swapped = [[mate(band, "prow") for band in held] for held in crossed]
 
     tops = [inverse_top, mate(inverse_top, "pcol")]
     for block in near:
@@ -248,14 +297,15 @@
     wanted_side = (row % PAIR) ^ (place % PAIR)
     slots = ((wanted_pair - col // PAIR) % pairs) * PAIR + (wanted_side ^ (col % PAIR))
 
-    partial, chosen, turned, early = partial_product(tops, [factor_panel, beside] + crossed, slots)
-    early = [early] + [after(from_pair(early, "prow", d, 1), swapped[-1]) for d in range(1, pairs)]
+    partial, turned, early = near_product(tops, [factor_panel, beside], slots)
+    partial, chosen, far = far_product(tops, partial, turned, crossed, slots)
     if pairs > 2:
-        selected, late = products(partial, chosen, turned, swapped, [])
-        parts = early + [late] + [from_pair(late, "prow", d, 0) for d in range(1, pairs)]
+        selected, update = last_product(partial, chosen, turned, swapped, [early, far])
+        parts = [update] + [from_pair(update, "prow", d, 0) for d in range(1, pairs)]
         update = functools.reduce(jnp.add, [part.astype(jnp.float32) for part in parts]).astype(jnp.bfloat16)
     else:
-        selected, update = products(partial, chosen, turned, swapped, early)
+        others = [early, after(from_pair(early, "prow", 1, 1), swapped[0][-1]), far]
+        selected, update = last_product(partial, chosen, turned, swapped, others)
     return -selected, finish(diag_inverse, [update, mate(update, "prow")])
 
 

time: 35.9 us -> 35.7 us (level)
  waiting for transfers between devices: 19.4 us -> 16.9 us
  starting transfers between devices: 10.5 us -> 11.7 us
  Pallas kernels: 4.33 us -> 5.37 us
    ppermute x8 -> x10, waiting for transfers between devices: 19.4 us -> 16.9 us  [from_pair(): return lax.ppermute(block, axis, moves)]
    ppermute x8 -> x10, starting transfers between devices: 10.5 us -> 11.7 us  [from_pair(): return lax.ppermute(block, axis, moves)]
    pallas_call x2 -> x3, Pallas kernels: 2.38 us -> 3.42 us  [the longest x1 1.4 us: near_product(): pl.pallas_call(functools.partial(near_kernel, len(tops)), out_shape=(jax....]
  transfers between devices with their start and end apart: 8 -> 10, of which waited for: 5 -> 5; matrix products, arithmetic and copies ran while one was open for 2% -> 2% of each run, Pallas kernels for 8% -> 11%
where the time goes in v16:
time: 35.7 us; the launch traced here: 35.6 us
  waiting for transfers between devices  16.9 us (47%)
  starting transfers between devices  11.7 us (33%)
  Pallas kernels  5.37 us (15%)
  other arithmetic  0.85 us (2%)
  between operations  0.71 us (2%)
    ppermute x10, waiting for transfers between devices, from_pair(): return lax.ppermute(block, axis, moves)  16.9 us
    ppermute x10, starting transfers between devices, from_pair(): return lax.ppermute(block, axis, moves)  11.7 us
    pallas_call x1, Pallas kernels, near_product(): pl.pallas_call(functools.partial(near_kernel, len(tops)), out_shape=(jax....  1.4 us
    pallas_call x1, Pallas kernels, far_product(): pl.pallas_call(functools.partial(far_kernel, n, blocks), out_shape=(jax.S...  1.33 us
    pallas_call x1, Pallas kernels, build_panel(): pl.pallas_call(panel_kernel, out_shape=(pltpu.VMEM(cross_blocks.shape, jn...  1.08 us
    pallas_call x1, Pallas kernels, finish(): pl.pallas_call(finish_kernel, out_shape=jax.ShapeDtypeStruct(diag_inverse...  0.86 us
    neg x1, other arithmetic, on_device(): return (-selected, finish(diag_inverse, [update, mate(update, 'prow')]))  0.83 us
  transfers between devices with their start and end apart: 10, of which 5 were waited for; matrix products, arithmetic and copies ran while one was open for 2% of the time, Pallas kernels for 11%

profile of v16, /device:TPU:0, one launch (start us, length us, event | category | flops | bytes accessed | tf_op | source)
XLA Modules:
  0.0 35.6 jit_solution(7782560813438684530)
XLA Ops:
  0.6 0.0 copy-start.1
  0.6 0.0 copy-start
  0.6 3.0 %collective-permute-start.1 = (bf16[512,512]{1,0:T(8,128)(2,1)}, bf16[512,512]{1,0:T(8,128)(2,1)S(1)}, u32[]{:S(2)}, u32[]{:S(2)}) collective-permute-start(bf16[512,512]{1,0:T(8,128)(2,1)} %top_hbm.1), channel_id=1, source_target_pairs={{2,0},{3,1},{0,2},{1,3},{6,4},{7,5},{4,6},{5,7},{10,8},{11,9},{8,1... | collective-permute-start | bytes 1572872 | tf_op jit(solution)/shard_map/ppermute | solution.py:277
  3.7 0.0 copy-done.1
  3.7 0.0 copy-done
  3.7 1.1 %panel.1 = (bf16[512,256]{1,0:T(8,128)(2,1)S(1)}, bf16[512,512]{1,0:T(8,128)(2,1)S(1)}, bf16[256,256]{1,0:T(8,128)(2,1)S(1)}, bf16[256,256]{1,0:T(8,128)(2,1)S(1)}) custom-call(s32[2]{0:T(128)} %bitcast.1, f32[512,256]{1,0:T(8,128)S(1)} %copy-done.1, f32[1,256,256]{2,1,0:T(8,128)S(1)} %copy-done, bf16[512,512]{1,0:T(8,128)(2,1)} %top_hbm.1, ...), custom_call_target="tpu_custom_call" | custom-call | tf_op jit(solution)/shard_map/panel/pallas_call | solution.py:68
  4.8 1.6 %collective-permute-start.3 = (bf16[512,256]{1,0:T(8,128)(2,1)S(1)}, bf16[512,256]{1,0:T(8,128)(2,1)S(1)}, u32[]{:S(2)}, u32[]{:S(2)}) collective-permute-start(bf16[512,256]{1,0:T(8,128)(2,1)S(1)} %get-tuple-element.16.refs_4_), channel_id=1, source_target_pairs={{4,0},{0,4},{12,8},{8,12},{5,1},{1,5},{13,9},{9,13},{6,2},{2,6},{1... | collective-permute-start | bytes 786440 | tf_op jit(solution)/shard_map/ppermute | solution.py:277
  6.4 2.5 %collective-permute-start.2 = (bf16[256,256]{1,0:T(8,128)(2,1)S(1)}, bf16[256,256]{1,0:T(8,128)(2,1)S(1)}, u32[]{:S(2)}, u32[]{:S(2)}) collective-permute-start(bf16[256,256]{1,0:T(8,128)(2,1)S(1)} %get-tuple-element.15), channel_id=1, source_target_pairs={{12,0},{8,4},{4,8},{0,12},{13,1},{9,5},{5,9},{1,13},{14,2},{10,6},... | collective-permute-start | bytes 393224 | tf_op jit(solution)/shard_map/ppermute | solution.py:277
  8.9 1.3 %collective-permute-start.5 = (bf16[256,256]{1,0:T(8,128)(2,1)S(1)}, bf16[256,256]{1,0:T(8,128)(2,1)S(1)}, u32[]{:S(2)}, u32[]{:S(2)}) collective-permute-start(bf16[256,256]{1,0:T(8,128)(2,1)S(1)} %get-tuple-element.19), channel_id=1, source_target_pairs={{12,0},{8,4},{4,8},{0,12},{13,1},{9,5},{5,9},{1,13},{14,2},{10,6},... | collective-permute-start | bytes 393224 | tf_op jit(solution)/shard_map/ppermute | solution.py:277
  10.2 0.0 collective-permute-start
  10.2 8.8 %collective-permute-done.2.refs_0_ = bf16[256,256]{1,0:T(8,128)(2,1)S(1)} collective-permute-done((bf16[256,256]{1,0:T(8,128)(2,1)S(1)}, bf16[256,256]{1,0:T(8,128)(2,1)S(1)}, u32[]{:S(2)}, u32[]{:S(2)}) %collective-permute-start.2) | collective-permute-done | bytes 131104 | tf_op jit(solution)/shard_map/ppermute | solution.py:277
  19.0 0.0 collective-permute-done.3.refs_1_.refs_5_
  19.0 0.0 collective-permute-start.6
  19.0 0.0 collective-permute-done.1.refs_0_
  19.0 0.1 collective-permute-start.4
  19.1 2.6 %collective-permute-done.5.refs_0_ = bf16[256,256]{1,0:T(8,128)(2,1)S(1)} collective-permute-done((bf16[256,256]{1,0:T(8,128)(2,1)S(1)}, bf16[256,256]{1,0:T(8,128)(2,1)S(1)}, u32[]{:S(2)}, u32[]{:S(2)}) %collective-permute-start.5) | collective-permute-done | bytes 131104 | tf_op jit(solution)/shard_map/ppermute | solution.py:277
  21.7 0.0 collective-permute-start.7
  21.7 0.0 collective-permute-done.refs_1_
  21.7 0.0 collective-permute-done.4.refs_3_
  21.7 1.4 %near.1 = (f32[512,256]{1,0:T(8,128)S(1)}, bf16[256,512]{1,0:T(8,128)(2,1)S(1)}, bf16[64,640]{1,0:T(8,128)(2,1)S(1)}) custom-call(s32[4]{0:T(128)S(1)} %fusion.2.slots_ref, bf16[512,512]{1,0:T(8,128)(2,1)S(1)} %get-tuple-element.14.refs_0_, bf16[512,512]{1,0:T(8,128)(2,1)S(1)} %collective-permute-done.refs_1_, bf16[512,512]{1,0:T(8,128)(2,1)S(1)} %relay.5.refs_2_.refs_1_, ...), custom_call_target="tpu_custom_call" | custom-call | tf_op jit(solution)/shard_map/near/pallas_call | solution.py:147
  23.1 1.9 %collective-permute-start.8 = (bf16[64,640]{1,0:T(8,128)(2,1)S(1)}, bf16[64,640]{1,0:T(8,128)(2,1)S(1)}, u32[]{:S(2)}, u32[]{:S(2)}) collective-permute-start(bf16[64,640]{1,0:T(8,128)(2,1)S(1)} %get-tuple-element.22.refs_2_), channel_id=1, source_target_pairs={{12,0},{8,4},{4,8},{0,12},{13,1},{9,5},{5,9},{1,13},{14,2},{10,6},... | collective-permute-start | bytes 245768 | tf_op jit(solution)/shard_map/ppermute | solution.py:277
  25.1 1.3 %far.1 = (f32[512,256]{1,0:T(8,128)S(1)}, bf16[1,512,512]{2,1,0:T(8,128)(2,1)S(1)}, bf16[64,640]{1,0:T(8,128)(2,1)S(1)}) custom-call(s32[4]{0:T(128)S(1)} %fusion.2.slots_ref, f32[512,256]{1,0:T(8,128)S(1)} %get-tuple-element.17.partial_ref, bf16[256,512]{1,0:T(8,128)(2,1)S(1)} %get-tuple-element.18.turned_ref, ...), custom_call_target="tpu_custom_call" | custom-call | tf_op jit(solution)/shard_map/far/pallas_call | solution.py:192
  26.4 0.3 collective-permute-done.7.refs_1_
  26.7 2.8 %collective-permute-done.8.refs_0_ = bf16[64,640]{1,0:T(8,128)(2,1)S(1)} collective-permute-done((bf16[64,640]{1,0:T(8,128)(2,1)S(1)}, bf16[64,640]{1,0:T(8,128)(2,1)S(1)}, u32[]{:S(2)}, u32[]{:S(2)}) %collective-permute-start.8) | collective-permute-done | bytes 81952 | tf_op jit(solution)/shard_map/ppermute | solution.py:277
  29.5 0.0 collective-permute-done.6.refs_0_
  29.5 0.7 %last.1 = (f32[512,256]{1,0:T(8,128)S(1)}, bf16[64,640]{1,0:T(8,128)(2,1)S(1)}) custom-call(f32[512,256]{1,0:T(8,128)S(1)} %get-tuple-element.20.partial_ref, bf16[1,512,512]{2,1,0:T(8,128)(2,1)S(1)} %get-tuple-element.21.chosen_ref, bf16[256,512]{1,0:T(8,128)(2,1)S(1)} %get-tuple-element.18.turned_ref, bf16[256,256]{1,0:T(8,128)(2,1)S(1)} %collective-permute-done.6.refs_0_, ...), custom_call_target="tpu_custom_call" | custom-call | tf_op jit(solution)/shard_map/last/pallas_call | solution.py:222
  30.2 1.2 %collective-permute-start.9 = (bf16[64,640]{1,0:T(8,128)(2,1)S(1)}, bf16[64,640]{1,0:T(8,128)(2,1)S(1)}, u32[]{:S(2)}, u32[]{:S(2)}) collective-permute-start(bf16[64,640]{1,0:T(8,128)(2,1)S(1)} %get-tuple-element.25.refs_0_), channel_id=1, source_target_pairs={{4,0},{0,4},{12,8},{8,12},{5,1},{1,5},{13,9},{9,13},{6,2},{2,6},{1... | collective-permute-start | bytes 245768 | tf_op jit(solution)/shard_map/ppermute | solution.py:277
  31.4 0.8 %neg.3 = f32[512,256]{1,0:T(8,128)} negate(f32[512,256]{1,0:T(8,128)S(1)} %get-tuple-element.24) | non-fusion elementwise | flops 131072 | bytes 1048576 | tf_op jit(solution)/shard_map/neg | solution.py:309
  32.2 2.5 %collective-permute-done.9.refs_1_ = bf16[64,640]{1,0:T(8,128)(2,1)S(1)} collective-permute-done((bf16[64,640]{1,0:T(8,128)(2,1)S(1)}, bf16[64,640]{1,0:T(8,128)(2,1)S(1)}, u32[]{:S(2)}, u32[]{:S(2)}) %collective-permute-start.9) | collective-permute-done | bytes 81952 | tf_op jit(solution)/shard_map/ppermute | solution.py:277
  34.7 0.9 %finish.1 = f32[1,256,256]{2,1,0:T(8,128)} custom-call(f32[1,256,256]{2,1,0:T(8,128)S(1)} %copy-done, bf16[64,640]{1,0:T(8,128)(2,1)S(1)} %get-tuple-element.25.refs_0_, bf16[64,640]{1,0:T(8,128)(2,1)S(1)} %collective-permute-done.9.refs_1_), custom_call_target="tpu_custom_call" | custom-call | tf_op jit(solution)/shard_map/finish/pallas_call | solution.py:259
  (6 shorter events, 0.0 us)
Async XLA Ops:
  0.6 3.0 %copy-start.1 = (f32[512,256]{1,0:T(8,128)S(1)}, f32[512,256]{1,0:T(8,128)}, u32[]{:S(2)}) copy-start(f32[512,256]{1,0:T(8,128)} %cross_ref.1) | copy-start | bytes 1572868
  0.6 3.0 %copy-start = (f32[1,256,256]{2,1,0:T(8,128)S(1)}, f32[1,256,256]{2,1,0:T(8,128)}, u32[]{:S(2)}) copy-start(f32[1,256,256]{2,1,0:T(8,128)} %diag_ref.3) | copy-start | bytes 786436
  0.6 18.3 %collective-permute-start.1 = (bf16[512,512]{1,0:T(8,128)(2,1)}, bf16[512,512]{1,0:T(8,128)(2,1)S(1)}, u32[]{:S(2)}, u32[]{:S(2)}) collective-permute-start(bf16[512,512]{1,0:T(8,128)(2,1)} %top_hbm.1), channel_id=1, source_target_pairs={{2,0},{3,1},{0,2},{1,3},{6,4},{7,5},{4,6},{5,7},{10,8},{11,9},{8,1... | collective-permute-start | bytes 1572872 | tf_op jit(solution)/shard_map/ppermute | solution.py:277
  4.8 14.2 %collective-permute-start.3 = (bf16[512,256]{1,0:T(8,128)(2,1)S(1)}, bf16[512,256]{1,0:T(8,128)(2,1)S(1)}, u32[]{:S(2)}, u32[]{:S(2)}) collective-permute-start(bf16[512,256]{1,0:T(8,128)(2,1)S(1)} %get-tuple-element.16.refs_4_), channel_id=1, source_target_pairs={{4,0},{0,4},{12,8},{8,12},{5,1},{1,5},{13,9},{9,13},{6,2},{2,6},{1... | collective-permute-start | bytes 786440 | tf_op jit(solution)/shard_map/ppermute | solution.py:277
  6.4 12.6 %collective-permute-start.2 = (bf16[256,256]{1,0:T(8,128)(2,1)S(1)}, bf16[256,256]{1,0:T(8,128)(2,1)S(1)}, u32[]{:S(2)}, u32[]{:S(2)}) collective-permute-start(bf16[256,256]{1,0:T(8,128)(2,1)S(1)} %get-tuple-element.15), channel_id=1, source_target_pairs={{12,0},{8,4},{4,8},{0,12},{13,1},{9,5},{5,9},{1,13},{14,2},{10,6},... | collective-permute-start | bytes 393224 | tf_op jit(solution)/shard_map/ppermute | solution.py:277
  8.9 12.8 %collective-permute-start.5 = (bf16[256,256]{1,0:T(8,128)(2,1)S(1)}, bf16[256,256]{1,0:T(8,128)(2,1)S(1)}, u32[]{:S(2)}, u32[]{:S(2)}) collective-permute-start(bf16[256,256]{1,0:T(8,128)(2,1)S(1)} %get-tuple-element.19), channel_id=1, source_target_pairs={{12,0},{8,4},{4,8},{0,12},{13,1},{9,5},{5,9},{1,13},{14,2},{10,6},... | collective-permute-start | bytes 393224 | tf_op jit(solution)/shard_map/ppermute | solution.py:277
  10.2 11.5 %collective-permute-start = (bf16[512,512]{1,0:T(8,128)(2,1)S(1)}, bf16[512,512]{1,0:T(8,128)(2,1)S(1)}, u32[]{:S(2)}, u32[]{:S(2)}) collective-permute-start(bf16[512,512]{1,0:T(8,128)(2,1)S(1)} %get-tuple-element.14.refs_0_), channel_id=1, source_target_pairs={{1,0},{0,1},{3,2},{2,3},{5,4},{4,5},{7,6},{6,7},{9,8},{8,9},{11,10... | collective-permute-start | bytes 1572872 | tf_op jit(solution)/shard_map/ppermute | solution.py:277
  19.0 10.5 %collective-permute-start.6 = (bf16[256,256]{1,0:T(8,128)(2,1)S(1)}, bf16[256,256]{1,0:T(8,128)(2,1)S(1)}, u32[]{:S(2)}, u32[]{:S(2)}) collective-permute-start(bf16[256,256]{1,0:T(8,128)(2,1)S(1)} %relay.4.refs_1_.refs_4_), channel_id=1, source_target_pairs={{4,0},{0,4},{12,8},{8,12},{5,1},{1,5},{13,9},{9,13},{6,2},{2,6},{1... | collective-permute-start | bytes 393224 | tf_op jit(solution)/shard_map/ppermute | solution.py:277
  19.0 2.7 %collective-permute-start.4 = (bf16[512,512]{1,0:T(8,128)(2,1)S(1)}, bf16[512,512]{1,0:T(8,128)(2,1)S(1)}, u32[]{:S(2)}, u32[]{:S(2)}) collective-permute-start(bf16[512,512]{1,0:T(8,128)(2,1)S(1)} %relay.5.refs_2_.refs_1_), channel_id=1, source_target_pairs={{1,0},{0,1},{3,2},{2,3},{5,4},{4,5},{7,6},{6,7},{9,8},{8,9},{11,10... | collective-permute-start | bytes 1572872 | tf_op jit(solution)/shard_map/ppermute | solution.py:277
  21.7 5.0 %collective-permute-start.7 = (bf16[256,256]{1,0:T(8,128)(2,1)S(1)}, bf16[256,256]{1,0:T(8,128)(2,1)S(1)}, u32[]{:S(2)}, u32[]{:S(2)}) collective-permute-start(bf16[256,256]{1,0:T(8,128)(2,1)S(1)} %relay.6.refs_5_), channel_id=1, source_target_pairs={{4,0},{0,4},{12,8},{8,12},{5,1},{1,5},{13,9},{9,13},{6,2},{2,6},{1... | collective-permute-start | bytes 393224 | tf_op jit(solution)/shard_map/ppermute | solution.py:277
  23.1 6.4 %collective-permute-start.8 = (bf16[64,640]{1,0:T(8,128)(2,1)S(1)}, bf16[64,640]{1,0:T(8,128)(2,1)S(1)}, u32[]{:S(2)}, u32[]{:S(2)}) collective-permute-start(bf16[64,640]{1,0:T(8,128)(2,1)S(1)} %get-tuple-element.22.refs_2_), channel_id=1, source_target_pairs={{12,0},{8,4},{4,8},{0,12},{13,1},{9,5},{5,9},{1,13},{14,2},{10,6},... | collective-permute-start | bytes 245768 | tf_op jit(solution)/shard_map/ppermute | solution.py:277
  30.2 4.5 %collective-permute-start.9 = (bf16[64,640]{1,0:T(8,128)(2,1)S(1)}, bf16[64,640]{1,0:T(8,128)(2,1)S(1)}, u32[]{:S(2)}, u32[]{:S(2)}) collective-permute-start(bf16[64,640]{1,0:T(8,128)(2,1)S(1)} %get-tuple-element.25.refs_0_), channel_id=1, source_target_pairs={{4,0},{0,4},{12,8},{8,12},{5,1},{1,5},{13,9},{9,13},{6,2},{2,6},{1... | collective-permute-start | bytes 245768 | tf_op jit(solution)/shard_map/ppermute | solution.py:277

commit v17 on v16

--- a/solution.py
+++ b/solution.py
@@ -129,21 +129,19 @@
 
 
 def near_kernel(n, slots_ref, *refs):
-    tops, panels = refs[:n], refs[n:n + PAIR]
-    partial_ref, turned_ref, update_ref, chosen_ref = refs[n + PAIR:]
+    tops, own, beside = refs[:n], refs[n], refs[n + 1:-4]
+    partial_ref, turned_ref, update_ref, chosen_ref = refs[-4:]
     for s in range(PAIR):
         choose(slots_ref[s], tops, chosen_ref.at[s])
-    turned = panels[0][...].astype(jnp.float32).T.astype(jnp.bfloat16)
+    turned = own[...].astype(jnp.float32).T.astype(jnp.bfloat16)
     turned_ref[...] = turned
-    total = dot(chosen_ref[0], panels[0][...])
-    for s in range(1, PAIR):
-        total += dot(chosen_ref[s], panels[s][...])
+    total = dot(chosen_ref[0], own[...]) + banded_dot(chosen_ref.at[1], beside)
     partial_ref[...] = total
     store_upper(update_ref, share(turned, total))
 
 
-def near_product(tops, panels, slots):
-    rows, width = panels[0].shape
+def near_product(tops, own, beside, slots):
+    rows, width = own.shape
     return pl.pallas_call(
         functools.partial(near_kernel, len(tops)),
         out_shape=(
@@ -151,12 +149,12 @@
             jax.ShapeDtypeStruct((width, rows), jnp.bfloat16),
             jax.ShapeDtypeStruct((width // 4, 5 * (width // 2)), jnp.bfloat16),
         ),
-        in_specs=[SMEM] + [VMEM] * (len(tops) + len(panels)),
+        in_specs=[SMEM] + [VMEM] * (len(tops) + 1 + len(beside)),
         out_specs=(VMEM, VMEM, VMEM),
         scratch_shapes=[pltpu.VMEM((PAIR,) + tops[0].shape, jnp.bfloat16)],
         compiler_params=PARAMS,
         name="near",
-    )(slots, *tops, *panels)
+    )(slots, *tops, own, *beside)
 
 
 def banded_dot(top, bands):
@@ -281,10 +279,10 @@
 
     near = [from_pair(inverse_top, "pcol", d, 0) for d in range(1, pairs)]
     factor_panel, inverse_top, *bands = build_panel(cross_blocks, diag_inverse, pattern, inverse_top)
-    beside = mate(factor_panel, "prow")
+    beside = [mate(band, "prow") for band in bands]
     crossed = [[from_pair(band, "prow", d, 1) for band in bands] for d in range(1, pairs)]
-    crossed = [[after(held[0], beside, cost=0)] + held[1:] for held in crossed]
-    near = [after(block, crossed[0][0], cost=0) for block in near]
+    crossed = [[after(held[0], factor_panel)] + held[1:] for held in crossed]
+    near = [after(block, crossed[0][0], *beside) for block in near]
     crossed = [held[:1] + [after(band, near[0], cost=4 * HOP_COST) for band in held[1:]] for held in crossed]
     swapped = [[mate(band, "prow") for band in held] for held in crossed]
 
@@ -297,7 +295,7 @@
     wanted_side = (row % PAIR) ^ (place % PAIR)
     slots = ((wanted_pair - col // PAIR) % pairs) * PAIR + (wanted_side ^ (col % PAIR))
 
-    partial, turned, early = near_product(tops, [factor_panel, beside], slots)
+    partial, turned, early = near_product(tops, factor_panel, beside, slots)
     partial, chosen, far = far_product(tops, partial, turned, crossed, slots)
     if pairs > 2:
         selected, update = last_product(partial, chosen, turned, swapped, [early, far])

time: 35.7 us -> 36.5 us (1.022)
  starting transfers between devices: 11.7 us -> 15.4 us
  waiting for transfers between devices: 16.9 us -> 14 us
    ppermute x10 -> x11, starting transfers between devices: 11.7 us -> 15.4 us  [from_pair(): return lax.ppermute(block, axis, moves)]
    ppermute x10 -> x11, waiting for transfers between devices: 16.9 us -> 14 us  [from_pair(): return lax.ppermute(block, axis, moves)]
  transfers between devices with their start and end apart: 10 -> 11, of which waited for: 5 -> 7; matrix products, arithmetic and copies ran while one was open for 2% -> 2% of each run, Pallas kernels for 11% -> 10%
where the time goes in v17:
time: 36.5 us; the launch traced here: 36.4 us
  starting transfers between devices  15.4 us (42%)
  waiting for transfers between devices  14 us (38%)
  Pallas kernels  5.37 us (15%)
  other arithmetic  0.85 us (2%)
  between operations  0.69 us (2%)
    ppermute x11, starting transfers between devices, from_pair(): return lax.ppermute(block, axis, moves)  15.4 us
    ppermute x11, waiting for transfers between devices, from_pair(): return lax.ppermute(block, axis, moves)  14 us
    pallas_call x1, Pallas kernels, near_product(): pl.pallas_call(functools.partial(near_kernel, len(tops)), out_shape=(jax....  1.4 us
    pallas_call x1, Pallas kernels, far_product(): pl.pallas_call(functools.partial(far_kernel, n, blocks), out_shape=(jax.S...  1.33 us
    pallas_call x1, Pallas kernels, build_panel(): pl.pallas_call(panel_kernel, out_shape=(pltpu.VMEM(cross_blocks.shape, jn...  1.08 us
    pallas_call x1, Pallas kernels, finish(): pl.pallas_call(finish_kernel, out_shape=jax.ShapeDtypeStruct(diag_inverse...  0.86 us
    neg x1, other arithmetic, on_device(): return (-selected, finish(diag_inverse, [update, mate(update, 'prow')]))  0.83 us
  transfers between devices with their start and end apart: 11, of which 7 were waited for; matrix products, arithmetic and copies ran while one was open for 2% of the time, Pallas kernels for 10%

profile of v17, /device:TPU:0, one launch (start us, length us, event | category | flops | bytes accessed | tf_op | source)
XLA Modules:
  0.0 36.4 jit_solution(3798275409712210248)
XLA Ops:
  0.6 0.0 copy-start.1
  0.6 0.0 copy-start
  0.6 3.0 %collective-permute-start.1 = (bf16[512,512]{1,0:T(8,128)(2,1)}, bf16[512,512]{1,0:T(8,128)(2,1)S(1)}, u32[]{:S(2)}, u32[]{:S(2)}) collective-permute-start(bf16[512,512]{1,0:T(8,128)(2,1)} %top_hbm.1), channel_id=1, source_target_pairs={{2,0},{3,1},{0,2},{1,3},{6,4},{7,5},{4,6},{5,7},{10,8},{11,9},{8,1... | collective-permute-start | bytes 1572872 | tf_op jit(solution)/shard_map/ppermute | solution.py:275
  3.7 0.0 copy-done.1
  3.7 0.0 copy-done
  3.7 1.1 %panel.1 = (bf16[512,256]{1,0:T(8,128)(2,1)S(1)}, bf16[512,512]{1,0:T(8,128)(2,1)S(1)}, bf16[256,256]{1,0:T(8,128)(2,1)S(1)}, bf16[256,256]{1,0:T(8,128)(2,1)S(1)}) custom-call(s32[2]{0:T(128)} %bitcast.1, f32[512,256]{1,0:T(8,128)S(1)} %copy-done.1, f32[1,256,256]{2,1,0:T(8,128)S(1)} %copy-done, bf16[512,512]{1,0:T(8,128)(2,1)} %top_hbm.1, ...), custom_call_target="tpu_custom_call" | custom-call | tf_op jit(solution)/shard_map/panel/pallas_call | solution.py:68
  4.8 3.7 %collective-permute-start.2 = (bf16[256,256]{1,0:T(8,128)(2,1)S(1)}, bf16[256,256]{1,0:T(8,128)(2,1)S(1)}, u32[]{:S(2)}, u32[]{:S(2)}) collective-permute-start(bf16[256,256]{1,0:T(8,128)(2,1)S(1)} %get-tuple-element.15), channel_id=1, source_target_pairs={{12,0},{8,4},{4,8},{0,12},{13,1},{9,5},{5,9},{1,13},{14,2},{10,6},... | collective-permute-start | bytes 393224 | tf_op jit(solution)/shard_map/ppermute | solution.py:275
  8.4 0.0 collective-permute-start.3
  8.4 2.0 %collective-permute-start.4 = (bf16[256,256]{1,0:T(8,128)(2,1)S(1)}, bf16[256,256]{1,0:T(8,128)(2,1)S(1)}, u32[]{:S(2)}, u32[]{:S(2)}) collective-permute-start(bf16[256,256]{1,0:T(8,128)(2,1)S(1)} %get-tuple-element.17), channel_id=1, source_target_pairs={{4,0},{0,4},{12,8},{8,12},{5,1},{1,5},{13,9},{9,13},{6,2},{2,6},{1... | collective-permute-start | bytes 393224 | tf_op jit(solution)/shard_map/ppermute | solution.py:275
  10.4 0.2 collective-permute-start.6
  10.7 2.4 %collective-permute-done.2.refs_0_ = bf16[256,256]{1,0:T(8,128)(2,1)S(1)} collective-permute-done((bf16[256,256]{1,0:T(8,128)(2,1)S(1)}, bf16[256,256]{1,0:T(8,128)(2,1)S(1)}, u32[]{:S(2)}, u32[]{:S(2)}) %collective-permute-start.2) | collective-permute-done | bytes 131104 | tf_op jit(solution)/shard_map/ppermute | solution.py:275
  13.0 0.0 collective-permute-start
  13.0 2.3 %collective-permute-done.3.refs_2_.refs_5_ = bf16[256,256]{1,0:T(8,128)(2,1)S(1)} collective-permute-done((bf16[256,256]{1,0:T(8,128)(2,1)S(1)}, bf16[256,256]{1,0:T(8,128)(2,1)S(1)}, u32[]{:S(2)}, u32[]{:S(2)}) %collective-permute-start.3) | collective-permute-done | bytes 131104 | tf_op jit(solution)/shard_map/ppermute | solution.py:275
  15.4 2.3 %collective-permute-start.7 = (bf16[256,256]{1,0:T(8,128)(2,1)S(1)}, bf16[256,256]{1,0:T(8,128)(2,1)S(1)}, u32[]{:S(2)}, u32[]{:S(2)}) collective-permute-start(bf16[256,256]{1,0:T(8,128)(2,1)S(1)} %relay.4.refs_1_.refs_4_), channel_id=1, source_target_pairs={{4,0},{0,4},{12,8},{8,12},{5,1},{1,5},{13,9},{9,13},{6,2},{2,6},{1... | collective-permute-start | bytes 393224 | tf_op jit(solution)/shard_map/ppermute | solution.py:275
  17.7 2.9 %collective-permute-done.4.refs_3_.refs_6_ = bf16[256,256]{1,0:T(8,128)(2,1)S(1)} collective-permute-done((bf16[256,256]{1,0:T(8,128)(2,1)S(1)}, bf16[256,256]{1,0:T(8,128)(2,1)S(1)}, u32[]{:S(2)}, u32[]{:S(2)}) %collective-permute-start.4) | collective-permute-done | bytes 131104 | tf_op jit(solution)/shard_map/ppermute | solution.py:275
  20.5 0.0 collective-permute-done.1.refs_0_
  20.5 0.0 collective-permute-start.5
  20.5 0.9 %collective-permute-done.6.refs_0_ = bf16[256,256]{1,0:T(8,128)(2,1)S(1)} collective-permute-done((bf16[256,256]{1,0:T(8,128)(2,1)S(1)}, bf16[256,256]{1,0:T(8,128)(2,1)S(1)}, u32[]{:S(2)}, u32[]{:S(2)}) %collective-permute-start.6) | collective-permute-done | bytes 131104 | tf_op jit(solution)/shard_map/ppermute | solution.py:275
  21.5 0.0 collective-permute-start.8
  21.5 0.0 collective-permute-done.refs_1_
  21.5 0.9 %collective-permute-done.5.refs_3_ = bf16[512,512]{1,0:T(8,128)(2,1)S(1)} collective-permute-done((bf16[512,512]{1,0:T(8,128)(2,1)S(1)}, bf16[512,512]{1,0:T(8,128)(2,1)S(1)}, u32[]{:S(2)}, u32[]{:S(2)}) %collective-permute-start.5) | collective-permute-done | bytes 524320 | tf_op jit(solution)/shard_map/ppermute | solution.py:275
  22.4 1.4 %near.1 = (f32[512,256]{1,0:T(8,128)S(1)}, bf16[256,512]{1,0:T(8,128)(2,1)S(1)}, bf16[64,640]{1,0:T(8,128)(2,1)S(1)}) custom-call(s32[4]{0:T(128)S(1)} %fusion.2.slots_ref, bf16[512,512]{1,0:T(8,128)(2,1)S(1)} %get-tuple-element.14.refs_0_, bf16[512,512]{1,0:T(8,128)(2,1)S(1)} %collective-permute-done.refs_1_, bf16[512,512]{1,0:T(8,128)(2,1)S(1)} %relay.5.refs_2_.refs_1_, ...), custom_call_target="tpu_custom_call" | custom-call | tf_op jit(solution)/shard_map/near/pallas_call | solution.py:145
  23.8 2.8 %collective-permute-start.9 = (bf16[64,640]{1,0:T(8,128)(2,1)S(1)}, bf16[64,640]{1,0:T(8,128)(2,1)S(1)}, u32[]{:S(2)}, u32[]{:S(2)}) collective-permute-start(bf16[64,640]{1,0:T(8,128)(2,1)S(1)} %get-tuple-element.22.refs_2_), channel_id=1, source_target_pairs={{12,0},{8,4},{4,8},{0,12},{13,1},{9,5},{5,9},{1,13},{14,2},{10,6},... | collective-permute-start | bytes 245768 | tf_op jit(solution)/shard_map/ppermute | solution.py:275
  26.7 1.3 %far.1 = (f32[512,256]{1,0:T(8,128)S(1)}, bf16[1,512,512]{2,1,0:T(8,128)(2,1)S(1)}, bf16[64,640]{1,0:T(8,128)(2,1)S(1)}) custom-call(s32[4]{0:T(128)S(1)} %fusion.2.slots_ref, f32[512,256]{1,0:T(8,128)S(1)} %get-tuple-element.18.partial_ref, bf16[256,512]{1,0:T(8,128)(2,1)S(1)} %get-tuple-element.19.turned_ref, ...), custom_call_target="tpu_custom_call" | custom-call | tf_op jit(solution)/shard_map/far/pallas_call | solution.py:190
  28.0 0.0 collective-permute-done.8.refs_1_
  28.0 2.3 %collective-permute-done.9.refs_0_ = bf16[64,640]{1,0:T(8,128)(2,1)S(1)} collective-permute-done((bf16[64,640]{1,0:T(8,128)(2,1)S(1)}, bf16[64,640]{1,0:T(8,128)(2,1)S(1)}, u32[]{:S(2)}, u32[]{:S(2)}) %collective-permute-start.9) | collective-permute-done | bytes 81952 | tf_op jit(solution)/shard_map/ppermute | solution.py:275
  30.3 0.0 collective-permute-done.7.refs_0_
  30.3 0.7 %last.1 = (f32[512,256]{1,0:T(8,128)S(1)}, bf16[64,640]{1,0:T(8,128)(2,1)S(1)}) custom-call(f32[512,256]{1,0:T(8,128)S(1)} %get-tuple-element.20.partial_ref, bf16[1,512,512]{2,1,0:T(8,128)(2,1)S(1)} %get-tuple-element.21.chosen_ref, bf16[256,512]{1,0:T(8,128)(2,1)S(1)} %get-tuple-element.19.turned_ref, bf16[256,256]{1,0:T(8,128)(2,1)S(1)} %collective-permute-done.7.refs_0_, ...), custom_call_target="tpu_custom_call" | custom-call | tf_op jit(solution)/shard_map/last/pallas_call | solution.py:220
  31.0 1.4 %collective-permute-start.10 = (bf16[64,640]{1,0:T(8,128)(2,1)S(1)}, bf16[64,640]{1,0:T(8,128)(2,1)S(1)}, u32[]{:S(2)}, u32[]{:S(2)}) collective-permute-start(bf16[64,640]{1,0:T(8,128)(2,1)S(1)} %get-tuple-element.25.refs_0_), channel_id=1, source_target_pairs={{4,0},{0,4},{12,8},{8,12},{5,1},{1,5},{13,9},{9,13},{6,2},{2,6},{1... | collective-permute-start | bytes 245768 | tf_op jit(solution)/shard_map/ppermute | solution.py:275
  32.4 0.8 %neg.3 = f32[512,256]{1,0:T(8,128)} negate(f32[512,256]{1,0:T(8,128)S(1)} %get-tuple-element.24) | non-fusion elementwise | flops 131072 | bytes 1048576 | tf_op jit(solution)/shard_map/neg | solution.py:307
  33.2 2.3 %collective-permute-done.10.refs_1_ = bf16[64,640]{1,0:T(8,128)(2,1)S(1)} collective-permute-done((bf16[64,640]{1,0:T(8,128)(2,1)S(1)}, bf16[64,640]{1,0:T(8,128)(2,1)S(1)}, u32[]{:S(2)}, u32[]{:S(2)}) %collective-permute-start.10) | collective-permute-done | bytes 81952 | tf_op jit(solution)/shard_map/ppermute | solution.py:275
  35.5 0.9 %finish.1 = f32[1,256,256]{2,1,0:T(8,128)} custom-call(f32[1,256,256]{2,1,0:T(8,128)S(1)} %copy-done, bf16[64,640]{1,0:T(8,128)(2,1)S(1)} %get-tuple-element.25.refs_0_, bf16[64,640]{1,0:T(8,128)(2,1)S(1)} %collective-permute-done.10.refs_1_), custom_call_target="tpu_custom_call" | custom-call | tf_op jit(solution)/shard_map/finish/pallas_call | solution.py:257
  (6 shorter events, 0.0 us)
Async XLA Ops:
  0.6 3.0 %copy-start.1 = (f32[512,256]{1,0:T(8,128)S(1)}, f32[512,256]{1,0:T(8,128)}, u32[]{:S(2)}) copy-start(f32[512,256]{1,0:T(8,128)} %cross_ref.1) | copy-start | bytes 1572868
  0.6 3.0 %copy-start = (f32[1,256,256]{2,1,0:T(8,128)S(1)}, f32[1,256,256]{2,1,0:T(8,128)}, u32[]{:S(2)}) copy-start(f32[1,256,256]{2,1,0:T(8,128)} %diag_ref.3) | copy-start | bytes 786436
  0.6 19.9 %collective-permute-start.1 = (bf16[512,512]{1,0:T(8,128)(2,1)}, bf16[512,512]{1,0:T(8,128)(2,1)S(1)}, u32[]{:S(2)}, u32[]{:S(2)}) collective-permute-start(bf16[512,512]{1,0:T(8,128)(2,1)} %top_hbm.1), channel_id=1, source_target_pairs={{2,0},{3,1},{0,2},{1,3},{6,4},{7,5},{4,6},{5,7},{10,8},{11,9},{8,1... | collective-permute-start | bytes 1572872 | tf_op jit(solution)/shard_map/ppermute | solution.py:275
  4.8 8.3 %collective-permute-start.2 = (bf16[256,256]{1,0:T(8,128)(2,1)S(1)}, bf16[256,256]{1,0:T(8,128)(2,1)S(1)}, u32[]{:S(2)}, u32[]{:S(2)}) collective-permute-start(bf16[256,256]{1,0:T(8,128)(2,1)S(1)} %get-tuple-element.15), channel_id=1, source_target_pairs={{12,0},{8,4},{4,8},{0,12},{13,1},{9,5},{5,9},{1,13},{14,2},{10,6},... | collective-permute-start | bytes 393224 | tf_op jit(solution)/shard_map/ppermute | solution.py:275
  8.4 7.0 %collective-permute-start.3 = (bf16[256,256]{1,0:T(8,128)(2,1)S(1)}, bf16[256,256]{1,0:T(8,128)(2,1)S(1)}, u32[]{:S(2)}, u32[]{:S(2)}) collective-permute-start(bf16[256,256]{1,0:T(8,128)(2,1)S(1)} %get-tuple-element.15), channel_id=1, source_target_pairs={{4,0},{0,4},{12,8},{8,12},{5,1},{1,5},{13,9},{9,13},{6,2},{2,6},{1... | collective-permute-start | bytes 393224 | tf_op jit(solution)/shard_map/ppermute | solution.py:275
  8.4 12.1 %collective-permute-start.4 = (bf16[256,256]{1,0:T(8,128)(2,1)S(1)}, bf16[256,256]{1,0:T(8,128)(2,1)S(1)}, u32[]{:S(2)}, u32[]{:S(2)}) collective-permute-start(bf16[256,256]{1,0:T(8,128)(2,1)S(1)} %get-tuple-element.17), channel_id=1, source_target_pairs={{4,0},{0,4},{12,8},{8,12},{5,1},{1,5},{13,9},{9,13},{6,2},{2,6},{1... | collective-permute-start | bytes 393224 | tf_op jit(solution)/shard_map/ppermute | solution.py:275
  10.4 11.0 %collective-permute-start.6 = (bf16[256,256]{1,0:T(8,128)(2,1)S(1)}, bf16[256,256]{1,0:T(8,128)(2,1)S(1)}, u32[]{:S(2)}, u32[]{:S(2)}) collective-permute-start(bf16[256,256]{1,0:T(8,128)(2,1)S(1)} %get-tuple-element.17), channel_id=1, source_target_pairs={{12,0},{8,4},{4,8},{0,12},{13,1},{9,5},{5,9},{1,13},{14,2},{10,6},... | collective-permute-start | bytes 393224 | tf_op jit(solution)/shard_map/ppermute | solution.py:275
  13.0 8.5 %collective-permute-start = (bf16[512,512]{1,0:T(8,128)(2,1)S(1)}, bf16[512,512]{1,0:T(8,128)(2,1)S(1)}, u32[]{:S(2)}, u32[]{:S(2)}) collective-permute-start(bf16[512,512]{1,0:T(8,128)(2,1)S(1)} %get-tuple-element.14.refs_0_), channel_id=1, source_target_pairs={{1,0},{0,1},{3,2},{2,3},{5,4},{4,5},{7,6},{6,7},{9,8},{8,9},{11,10... | collective-permute-start | bytes 1572872 | tf_op jit(solution)/shard_map/ppermute | solution.py:275
  15.4 14.9 %collective-permute-start.7 = (bf16[256,256]{1,0:T(8,128)(2,1)S(1)}, bf16[256,256]{1,0:T(8,128)(2,1)S(1)}, u32[]{:S(2)}, u32[]{:S(2)}) collective-permute-start(bf16[256,256]{1,0:T(8,128)(2,1)S(1)} %relay.4.refs_1_.refs_4_), channel_id=1, source_target_pairs={{4,0},{0,4},{12,8},{8,12},{5,1},{1,5},{13,9},{9,13},{6,2},{2,6},{1... | collective-permute-start | bytes 393224 | tf_op jit(solution)/shard_map/ppermute | solution.py:275
  20.5 1.9 %collective-permute-start.5 = (bf16[512,512]{1,0:T(8,128)(2,1)S(1)}, bf16[512,512]{1,0:T(8,128)(2,1)S(1)}, u32[]{:S(2)}, u32[]{:S(2)}) collective-permute-start(bf16[512,512]{1,0:T(8,128)(2,1)S(1)} %relay.5.refs_2_.refs_1_), channel_id=1, source_target_pairs={{1,0},{0,1},{3,2},{2,3},{5,4},{4,5},{7,6},{6,7},{9,8},{8,9},{11,10... | collective-permute-start | bytes 1572872 | tf_op jit(solution)/shard_map/ppermute | solution.py:275
  21.5 6.5 %collective-permute-start.8 = (bf16[256,256]{1,0:T(8,128)(2,1)S(1)}, bf16[256,256]{1,0:T(8,128)(2,1)S(1)}, u32[]{:S(2)}, u32[]{:S(2)}) collective-permute-start(bf16[256,256]{1,0:T(8,128)(2,1)S(1)} %relay.6.refs_5_), channel_id=1, source_target_pairs={{4,0},{0,4},{12,8},{8,12},{5,1},{1,5},{13,9},{9,13},{6,2},{2,6},{1... | collective-permute-start | bytes 393224 | tf_op jit(solution)/shard_map/ppermute | solution.py:275
  23.8 6.5 %collective-permute-start.9 = (bf16[64,640]{1,0:T(8,128)(2,1)S(1)}, bf16[64,640]{1,0:T(8,128)(2,1)S(1)}, u32[]{:S(2)}, u32[]{:S(2)}) collective-permute-start(bf16[64,640]{1,0:T(8,128)(2,1)S(1)} %get-tuple-element.22.refs_2_), channel_id=1, source_target_pairs={{12,0},{8,4},{4,8},{0,12},{13,1},{9,5},{5,9},{1,13},{14,2},{10,6},... | collective-permute-start | bytes 245768 | tf_op jit(solution)/shard_map/ppermute | solution.py:275
  31.0 4.5 %collective-permute-start.10 = (bf16[64,640]{1,0:T(8,128)(2,1)S(1)}, bf16[64,640]{1,0:T(8,128)(2,1)S(1)}, u32[]{:S(2)}, u32[]{:S(2)}) collective-permute-start(bf16[64,640]{1,0:T(8,128)(2,1)S(1)} %get-tuple-element.25.refs_0_), channel_id=1, source_target_pairs={{4,0},{0,4},{12,8},{8,12},{5,1},{1,5},{13,9},{9,13},{6,2},{2,6},{1... | collective-permute-start | bytes 245768 | tf_op jit(solution)/shard_map/ppermute | solution.py:275

commit v18 on v15

--- a/solution.py
+++ b/solution.py
@@ -249,14 +249,15 @@
     slots = ((wanted_pair - col // PAIR) % pairs) * PAIR + (wanted_side ^ (col % PAIR))
 
     partial, chosen, turned, early = partial_product(tops, [factor_panel, beside] + crossed, slots)
-    early = [early] + [after(from_pair(early, "prow", d, 1), swapped[-1]) for d in range(1, pairs)]
     if pairs > 2:
         selected, late = products(partial, chosen, turned, swapped, [])
-        parts = early + [late] + [from_pair(late, "prow", d, 0) for d in range(1, pairs)]
+        parts = [early, late] + [from_pair(part, "prow", d, 0) for part in (early, late) for d in range(1, pairs)]
         update = functools.reduce(jnp.add, [part.astype(jnp.float32) for part in parts]).astype(jnp.bfloat16)
+        others = []
     else:
-        selected, update = products(partial, chosen, turned, swapped, early)
-    return -selected, finish(diag_inverse, [update, mate(update, "prow")])
+        others = [from_pair(early, "prow", 1, flip) for flip in (1, 0)]
+        selected, update = products(partial, chosen, turned, swapped, [early])
+    return -selected, finish(diag_inverse, [update, mate(update, "prow")] + others)
 
 
 def solution(mesh):

time: 35.9 us -> 37.5 us (1.045)
  starting transfers between devices: 10.5 us -> 11.3 us
  waiting for transfers between devices: 19.4 us -> 20.2 us
    ppermute x8 -> x9, waiting for transfers between devices: 19.4 us -> 20.2 us  [from_pair(): return lax.ppermute(block, axis, moves)]
    ppermute x8 -> x9, starting transfers between devices: 10.5 us -> 11.3 us  [from_pair(): return lax.ppermute(block, axis, moves)]
  transfers between devices with their start and end apart: 8 -> 9, of which waited for: 5 -> 6; matrix products, arithmetic and copies ran while one was open for 2% -> 2% of each run, Pallas kernels for 8% -> 7%
where the time goes in v18:
time: 37.5 us; the launch traced here: 37.3 us
  waiting for transfers between devices  20.2 us (54%)
  starting transfers between devices  11.3 us (30%)
  Pallas kernels  4.33 us (12%)
  other arithmetic  0.85 us (2%)
  between operations  0.69 us (2%)
    ppermute x9, waiting for transfers between devices, from_pair(): return lax.ppermute(block, axis, moves)  20.2 us
    ppermute x9, starting transfers between devices, from_pair(): return lax.ppermute(block, axis, moves)  11.3 us
    pallas_call x1, Pallas kernels, partial_product(): pl.pallas_call(functools.partial(partial_kernel, n), out_shape=(jax.Shape...  1.69 us
    pallas_call x1, Pallas kernels, build_panel(): pl.pallas_call(panel_kernel, out_shape=(pltpu.VMEM(cross_blocks.shape, jn...  1.08 us
    pallas_call x1, Pallas kernels, finish(): pl.pallas_call(finish_kernel, out_shape=jax.ShapeDtypeStruct(diag_inverse...  0.86 us
    neg x1, other arithmetic, on_device(): -selected  0.83 us
  transfers between devices with their start and end apart: 9, of which 6 were waited for; matrix products, arithmetic and copies ran while one was open for 2% of the time, Pallas kernels for 7%

profile of v18, /device:TPU:0, one launch (start us, length us, event | category | flops | bytes accessed | tf_op | source)
XLA Modules:
  0.0 37.3 jit_solution(7889849986171811213)
XLA Ops:
  0.6 0.0 copy-start
  0.6 0.0 copy-start.1
  0.6 3.0 %collective-permute-start.1 = (bf16[512,512]{1,0:T(8,128)(2,1)}, bf16[512,512]{1,0:T(8,128)(2,1)S(1)}, u32[]{:S(2)}, u32[]{:S(2)}) collective-permute-start(bf16[512,512]{1,0:T(8,128)(2,1)} %top_hbm.1), channel_id=1, source_target_pairs={{2,0},{3,1},{0,2},{1,3},{6,4},{7,5},{4,6},{5,7},{10,8},{11,9},{8,1... | collective-permute-start | bytes 1572872 | tf_op jit(solution)/shard_map/ppermute | solution.py:229
  3.7 0.0 copy-done
  3.7 0.0 copy-done.1
  3.7 1.1 %panel.1 = (bf16[512,256]{1,0:T(8,128)(2,1)S(1)}, bf16[512,512]{1,0:T(8,128)(2,1)S(1)}) custom-call(s32[2]{0:T(128)} %bitcast.1, f32[512,256]{1,0:T(8,128)S(1)} %copy-done.1, f32[1,256,256]{2,1,0:T(8,128)S(1)} %copy-done, bf16[512,512]{1,0:T(8,128)(2,1)} %top_hbm.1, f32[8,128]{1,0:T(8,128)S(1)} %token_.1.token_ref), custom_call_target="tpu_custom_call" | custom-call | tf_op jit(solution)/shard_map/panel/pallas_call | solution.py:64
  4.8 1.6 %collective-permute-start.3 = (bf16[512,256]{1,0:T(8,128)(2,1)S(1)}, bf16[512,256]{1,0:T(8,128)(2,1)S(1)}, u32[]{:S(2)}, u32[]{:S(2)}) collective-permute-start(bf16[512,256]{1,0:T(8,128)(2,1)S(1)} %get-tuple-element.11.refs_1_.refs_4_), channel_id=1, source_target_pairs={{4,0},{0,4},{12,8},{8,12},{5,1},{1,5},{13,9},{9,13},{6,2},{2,6},{1... | collective-permute-start | bytes 786440 | tf_op jit(solution)/shard_map/ppermute | solution.py:229
  6.4 2.5 %collective-permute-start.4 = (bf16[512,256]{1,0:T(8,128)(2,1)S(1)}, bf16[512,256]{1,0:T(8,128)(2,1)S(1)}, u32[]{:S(2)}, u32[]{:S(2)}) collective-permute-start(bf16[512,256]{1,0:T(8,128)(2,1)S(1)} %get-tuple-element.11.refs_1_.refs_4_), channel_id=1, source_target_pairs={{12,0},{8,4},{4,8},{0,12},{13,1},{9,5},{5,9},{1,13},{14,2},{10,6},... | collective-permute-start | bytes 786440 | tf_op jit(solution)/shard_map/ppermute | solution.py:229
  8.9 0.0 collective-permute-start
  8.9 6.9 %collective-permute-done.1.refs_0_ = bf16[512,512]{1,0:T(8,128)(2,1)S(1)} collective-permute-done((bf16[512,512]{1,0:T(8,128)(2,1)}, bf16[512,512]{1,0:T(8,128)(2,1)S(1)}, u32[]{:S(2)}, u32[]{:S(2)}) %collective-permute-start.1) | collective-permute-done | bytes 524320 | tf_op jit(solution)/shard_map/ppermute | solution.py:229
  15.8 0.0 collective-permute-start.2
  15.8 0.0 collective-permute-done.3.refs_2_.refs_5_
  15.8 4.5 %collective-permute-done.4.refs_0_ = bf16[512,256]{1,0:T(8,128)(2,1)S(1)} collective-permute-done((bf16[512,256]{1,0:T(8,128)(2,1)S(1)}, bf16[512,256]{1,0:T(8,128)(2,1)S(1)}, u32[]{:S(2)}, u32[]{:S(2)}) %collective-permute-start.4) | collective-permute-done | bytes 262176 | tf_op jit(solution)/shard_map/ppermute | solution.py:229
  20.3 0.6 %collective-permute-start.5 = (bf16[512,256]{1,0:T(8,128)(2,1)S(1)}, bf16[512,256]{1,0:T(8,128)(2,1)S(1)}, u32[]{:S(2)}, u32[]{:S(2)}) collective-permute-start(bf16[512,256]{1,0:T(8,128)(2,1)S(1)} %relay.3.refs_6_), channel_id=1, source_target_pairs={{4,0},{0,4},{12,8},{8,12},{5,1},{1,5},{13,9},{9,13},{6,2},{2,6},{1... | collective-permute-start | bytes 786440 | tf_op jit(solution)/shard_map/ppermute | solution.py:229
  20.9 0.0 collective-permute-done.refs_1_
  20.9 0.0 collective-permute-done.2.refs_3_
  20.9 1.7 %partial.1 = (f32[512,256]{1,0:T(8,128)S(1)}, bf16[1,512,512]{2,1,0:T(8,128)(2,1)S(1)}, bf16[256,512]{1,0:T(8,128)(2,1)S(1)}, bf16[64,640]{1,0:T(8,128)(2,1)S(1)}) custom-call(s32[4]{0:T(128)S(1)} %fusion.2.slots_ref, bf16[512,512]{1,0:T(8,128)(2,1)S(1)} %get-tuple-element.10.refs_0_, bf16[512,512]{1,0:T(8,128)(2,1)S(1)} %collective-permute-done.refs_1_, ...), custom_call_target="tpu_custom_call" | custom-call | flops 536870912 | bytes 3145728 | tf_op jit(solution)/shard_map/partial/pallas_call | solution.py:140
  22.6 4.5 %collective-permute-done.5.refs_0_ = bf16[512,256]{1,0:T(8,128)(2,1)S(1)} collective-permute-done((bf16[512,256]{1,0:T(8,128)(2,1)S(1)}, bf16[512,256]{1,0:T(8,128)(2,1)S(1)}, u32[]{:S(2)}, u32[]{:S(2)}) %collective-permute-start.5) | collective-permute-done | bytes 262176 | tf_op jit(solution)/shard_map/ppermute | solution.py:229
  27.1 0.7 %products.1 = (f32[512,256]{1,0:T(8,128)S(1)}, bf16[64,640]{1,0:T(8,128)(2,1)S(1)}) custom-call(f32[512,256]{1,0:T(8,128)S(1)} %get-tuple-element.12.partial_ref, bf16[1,512,512]{2,1,0:T(8,128)(2,1)S(1)} %get-tuple-element.13.chosen_ref, bf16[256,512]{1,0:T(8,128)(2,1)S(1)} %get-tuple-element.14.turned_ref, ...), custom_call_target="tpu_custom_call" | custom-call | tf_op jit(solution)/shard_map/products/pallas_call | solution.py:174
  27.8 0.3 collective-permute-start.6
  28.2 2.7 %collective-permute-start.7 = (bf16[64,640]{1,0:T(8,128)(2,1)S(1)}, bf16[64,640]{1,0:T(8,128)(2,1)S(1)}, u32[]{:S(2)}, u32[]{:S(2)}) collective-permute-start(bf16[64,640]{1,0:T(8,128)(2,1)S(1)} %get-tuple-element.15.refs_1_), channel_id=1, source_target_pairs={{12,0},{8,4},{4,8},{0,12},{13,1},{9,5},{5,9},{1,13},{14,2},{10,6},... | collective-permute-start | bytes 245768 | tf_op jit(solution)/shard_map/ppermute | solution.py:229
  30.9 0.5 %collective-permute-start.8 = (bf16[64,640]{1,0:T(8,128)(2,1)S(1)}, bf16[64,640]{1,0:T(8,128)(2,1)S(1)}, u32[]{:S(2)}, u32[]{:S(2)}) collective-permute-start(bf16[64,640]{1,0:T(8,128)(2,1)S(1)} %get-tuple-element.15.refs_1_), channel_id=1, source_target_pairs={{8,0},{12,4},{0,8},{4,12},{9,1},{13,5},{1,9},{5,13},{10,2},{14,6},... | collective-permute-start | bytes 245768 | tf_op jit(solution)/shard_map/ppermute | solution.py:229
  31.4 0.8 %neg.3 = f32[512,256]{1,0:T(8,128)} negate(f32[512,256]{1,0:T(8,128)S(1)} %get-tuple-element.16) | non-fusion elementwise | flops 131072 | bytes 1048576 | tf_op jit(solution)/shard_map/neg | solution.py:260
  32.2 1.0 %collective-permute-done.6.refs_1_ = bf16[64,640]{1,0:T(8,128)(2,1)S(1)} collective-permute-done((bf16[64,640]{1,0:T(8,128)(2,1)S(1)}, bf16[64,640]{1,0:T(8,128)(2,1)S(1)}, u32[]{:S(2)}, u32[]{:S(2)}) %collective-permute-start.6) | collective-permute-done | bytes 81952 | tf_op jit(solution)/shard_map/ppermute | solution.py:229
  33.2 1.3 %collective-permute-done.7.refs_2_ = bf16[64,640]{1,0:T(8,128)(2,1)S(1)} collective-permute-done((bf16[64,640]{1,0:T(8,128)(2,1)S(1)}, bf16[64,640]{1,0:T(8,128)(2,1)S(1)}, u32[]{:S(2)}, u32[]{:S(2)}) %collective-permute-start.7) | collective-permute-done | bytes 81952 | tf_op jit(solution)/shard_map/ppermute | solution.py:229
  34.5 1.9 %collective-permute-done.8.refs_3_ = bf16[64,640]{1,0:T(8,128)(2,1)S(1)} collective-permute-done((bf16[64,640]{1,0:T(8,128)(2,1)S(1)}, bf16[64,640]{1,0:T(8,128)(2,1)S(1)}, u32[]{:S(2)}, u32[]{:S(2)}) %collective-permute-start.8) | collective-permute-done | bytes 81952 | tf_op jit(solution)/shard_map/ppermute | solution.py:229
  36.4 0.9 %finish.1 = f32[1,256,256]{2,1,0:T(8,128)} custom-call(f32[1,256,256]{2,1,0:T(8,128)S(1)} %copy-done, bf16[64,640]{1,0:T(8,128)(2,1)S(1)} %get-tuple-element.17.refs_0_, bf16[64,640]{1,0:T(8,128)(2,1)S(1)} %collective-permute-done.6.refs_1_, bf16[64,640]{1,0:T(8,128)(2,1)S(1)} %collective-permute-done.7.refs_2_, ...), custom_call_target="tpu_custom_call" | custom-call | tf_op jit(solution)/shard_map/finish/pallas_call | solution.py:211
  (4 shorter events, 0.0 us)
Async XLA Ops:
  0.6 3.0 %copy-start = (f32[1,256,256]{2,1,0:T(8,128)S(1)}, f32[1,256,256]{2,1,0:T(8,128)}, u32[]{:S(2)}) copy-start(f32[1,256,256]{2,1,0:T(8,128)} %diag_ref.3) | copy-start | bytes 786436
  0.6 3.0 %copy-start.1 = (f32[512,256]{1,0:T(8,128)S(1)}, f32[512,256]{1,0:T(8,128)}, u32[]{:S(2)}) copy-start(f32[512,256]{1,0:T(8,128)} %cross_ref.1) | copy-start | bytes 1572868
  0.6 15.1 %collective-permute-start.1 = (bf16[512,512]{1,0:T(8,128)(2,1)}, bf16[512,512]{1,0:T(8,128)(2,1)S(1)}, u32[]{:S(2)}, u32[]{:S(2)}) collective-permute-start(bf16[512,512]{1,0:T(8,128)(2,1)} %top_hbm.1), channel_id=1, source_target_pairs={{2,0},{3,1},{0,2},{1,3},{6,4},{7,5},{4,6},{5,7},{10,8},{11,9},{8,1... | collective-permute-start | bytes 1572872 | tf_op jit(solution)/shard_map/ppermute | solution.py:229
  4.8 11.0 %collective-permute-start.3 = (bf16[512,256]{1,0:T(8,128)(2,1)S(1)}, bf16[512,256]{1,0:T(8,128)(2,1)S(1)}, u32[]{:S(2)}, u32[]{:S(2)}) collective-permute-start(bf16[512,256]{1,0:T(8,128)(2,1)S(1)} %get-tuple-element.11.refs_1_.refs_4_), channel_id=1, source_target_pairs={{4,0},{0,4},{12,8},{8,12},{5,1},{1,5},{13,9},{9,13},{6,2},{2,6},{1... | collective-permute-start | bytes 786440 | tf_op jit(solution)/shard_map/ppermute | solution.py:229
  6.4 13.9 %collective-permute-start.4 = (bf16[512,256]{1,0:T(8,128)(2,1)S(1)}, bf16[512,256]{1,0:T(8,128)(2,1)S(1)}, u32[]{:S(2)}, u32[]{:S(2)}) collective-permute-start(bf16[512,256]{1,0:T(8,128)(2,1)S(1)} %get-tuple-element.11.refs_1_.refs_4_), channel_id=1, source_target_pairs={{12,0},{8,4},{4,8},{0,12},{13,1},{9,5},{5,9},{1,13},{14,2},{10,6},... | collective-permute-start | bytes 786440 | tf_op jit(solution)/shard_map/ppermute | solution.py:229
  8.9 12.1 %collective-permute-start = (bf16[512,512]{1,0:T(8,128)(2,1)S(1)}, bf16[512,512]{1,0:T(8,128)(2,1)S(1)}, u32[]{:S(2)}, u32[]{:S(2)}) collective-permute-start(bf16[512,512]{1,0:T(8,128)(2,1)S(1)} %get-tuple-element.10.refs_0_), channel_id=1, source_target_pairs={{1,0},{0,1},{3,2},{2,3},{5,4},{4,5},{7,6},{6,7},{9,8},{8,9},{11,10... | collective-permute-start | bytes 1572872 | tf_op jit(solution)/shard_map/ppermute | solution.py:229
  15.8 5.2 %collective-permute-start.2 = (bf16[512,512]{1,0:T(8,128)(2,1)S(1)}, bf16[512,512]{1,0:T(8,128)(2,1)S(1)}, u32[]{:S(2)}, u32[]{:S(2)}) collective-permute-start(bf16[512,512]{1,0:T(8,128)(2,1)S(1)} %relay.2.refs_1_.refs_2_), channel_id=1, source_target_pairs={{1,0},{0,1},{3,2},{2,3},{5,4},{4,5},{7,6},{6,7},{9,8},{8,9},{11,10... | collective-permute-start | bytes 1572872 | tf_op jit(solution)/shard_map/ppermute | solution.py:229
  20.3 6.8 %collective-permute-start.5 = (bf16[512,256]{1,0:T(8,128)(2,1)S(1)}, bf16[512,256]{1,0:T(8,128)(2,1)S(1)}, u32[]{:S(2)}, u32[]{:S(2)}) collective-permute-start(bf16[512,256]{1,0:T(8,128)(2,1)S(1)} %relay.3.refs_6_), channel_id=1, source_target_pairs={{4,0},{0,4},{12,8},{8,12},{5,1},{1,5},{13,9},{9,13},{6,2},{2,6},{1... | collective-permute-start | bytes 786440 | tf_op jit(solution)/shard_map/ppermute | solution.py:229
  27.8 5.4 %collective-permute-start.6 = (bf16[64,640]{1,0:T(8,128)(2,1)S(1)}, bf16[64,640]{1,0:T(8,128)(2,1)S(1)}, u32[]{:S(2)}, u32[]{:S(2)}) collective-permute-start(bf16[64,640]{1,0:T(8,128)(2,1)S(1)} %get-tuple-element.17.refs_0_), channel_id=1, source_target_pairs={{4,0},{0,4},{12,8},{8,12},{5,1},{1,5},{13,9},{9,13},{6,2},{2,6},{1... | collective-permute-start | bytes 245768 | tf_op jit(solution)/shard_map/ppermute | solution.py:229
  28.2 6.3 %collective-permute-start.7 = (bf16[64,640]{1,0:T(8,128)(2,1)S(1)}, bf16[64,640]{1,0:T(8,128)(2,1)S(1)}, u32[]{:S(2)}, u32[]{:S(2)}) collective-permute-start(bf16[64,640]{1,0:T(8,128)(2,1)S(1)} %get-tuple-element.15.refs_1_), channel_id=1, source_target_pairs={{12,0},{8,4},{4,8},{0,12},{13,1},{9,5},{5,9},{1,13},{14,2},{10,6},... | collective-permute-start | bytes 245768 | tf_op jit(solution)/shard_map/ppermute | solution.py:229
  30.9 5.5 %collective-permute-start.8 = (bf16[64,640]{1,0:T(8,128)(2,1)S(1)}, bf16[64,640]{1,0:T(8,128)(2,1)S(1)}, u32[]{:S(2)}, u32[]{:S(2)}) collective-permute-start(bf16[64,640]{1,0:T(8,128)(2,1)S(1)} %get-tuple-element.15.refs_1_), channel_id=1, source_target_pairs={{8,0},{12,4},{0,8},{4,12},{9,1},{13,5},{1,9},{5,13},{10,2},{14,6},... | collective-permute-start | bytes 245768 | tf_op jit(solution)/shard_map/ppermute | solution.py:229

commit v19 on v18

--- a/solution.py
+++ b/solution.py
@@ -255,7 +255,7 @@
         update = functools.reduce(jnp.add, [part.astype(jnp.float32) for part in parts]).astype(jnp.bfloat16)
         others = []
     else:
-        others = [from_pair(early, "prow", 1, flip) for flip in (1, 0)]
+        others = [after(from_pair(early, "prow", 1, flip), early, cost=0) for flip in (1, 0)]
         selected, update = products(partial, chosen, turned, swapped, [early])
     return -selected, finish(diag_inverse, [update, mate(update, "prow")] + others)
 

time: 37.5 us -> 36.5 us (0.973)
  waiting for transfers between devices: 20.2 us -> 18.9 us
    ppermute x9, waiting for transfers between devices: 20.2 us -> 18.9 us  [from_pair(): return lax.ppermute(block, axis, moves)]
    ppermute x9, starting transfers between devices: 11.3 us -> 11.6 us  [from_pair(): return lax.ppermute(block, axis, moves)]
  transfers between devices with their start and end apart: 9 -> 9, of which waited for: 6 -> 5; matrix products, arithmetic and copies ran while one was open for 2% -> 2% of each run, Pallas kernels for 7% -> 10%
where the time goes in v19:
time: 36.5 us; the launch traced here: 36.4 us
  waiting for transfers between devices  18.9 us (52%)
  starting transfers between devices  11.6 us (32%)
  Pallas kernels  4.33 us (12%)
  other arithmetic  0.85 us (2%)
  between operations  0.7 us (2%)
    ppermute x9, waiting for transfers between devices, from_pair(): return lax.ppermute(block, axis, moves)  18.9 us
    ppermute x9, starting transfers between devices, from_pair(): return lax.ppermute(block, axis, moves)  11.6 us
    pallas_call x1, Pallas kernels, partial_product(): pl.pallas_call(functools.partial(partial_kernel, n), out_shape=(jax.Shape...  1.69 us
    pallas_call x1, Pallas kernels, build_panel(): pl.pallas_call(panel_kernel, out_shape=(pltpu.VMEM(cross_blocks.shape, jn...  1.08 us
    pallas_call x1, Pallas kernels, finish(): pl.pallas_call(finish_kernel, out_shape=jax.ShapeDtypeStruct(diag_inverse...  0.86 us
    neg x1, other arithmetic, on_device(): -selected  0.83 us
  transfers between devices with their start and end apart: 9, of which 5 were waited for; matrix products, arithmetic and copies ran while one was open for 2% of the time, Pallas kernels for 10%

profile of v19, /device:TPU:0, one launch (start us, length us, event | category | flops | bytes accessed | tf_op | source)
XLA Modules:
  0.0 36.4 jit_solution(15247093488748301110)
XLA Ops:
  0.6 0.0 copy-start
  0.6 0.0 copy-start.1
  0.6 3.0 %collective-permute-start.1 = (bf16[512,512]{1,0:T(8,128)(2,1)}, bf16[512,512]{1,0:T(8,128)(2,1)S(1)}, u32[]{:S(2)}, u32[]{:S(2)}) collective-permute-start(bf16[512,512]{1,0:T(8,128)(2,1)} %top_hbm.1), channel_id=1, source_target_pairs={{2,0},{3,1},{0,2},{1,3},{6,4},{7,5},{4,6},{5,7},{10,8},{11,9},{8,1... | collective-permute-start | bytes 1572872 | tf_op jit(solution)/shard_map/ppermute | solution.py:229
  3.7 0.0 copy-done
  3.7 0.0 copy-done.1
  3.7 1.1 %panel.1 = (bf16[512,256]{1,0:T(8,128)(2,1)S(1)}, bf16[512,512]{1,0:T(8,128)(2,1)S(1)}) custom-call(s32[2]{0:T(128)} %bitcast.1, f32[512,256]{1,0:T(8,128)S(1)} %copy-done.1, f32[1,256,256]{2,1,0:T(8,128)S(1)} %copy-done, bf16[512,512]{1,0:T(8,128)(2,1)} %top_hbm.1, f32[8,128]{1,0:T(8,128)S(1)} %token_.1.token_ref), custom_call_target="tpu_custom_call" | custom-call | tf_op jit(solution)/shard_map/panel/pallas_call | solution.py:64
  4.8 1.6 %collective-permute-start.3 = (bf16[512,256]{1,0:T(8,128)(2,1)S(1)}, bf16[512,256]{1,0:T(8,128)(2,1)S(1)}, u32[]{:S(2)}, u32[]{:S(2)}) collective-permute-start(bf16[512,256]{1,0:T(8,128)(2,1)S(1)} %get-tuple-element.11.refs_1_.refs_4_), channel_id=1, source_target_pairs={{4,0},{0,4},{12,8},{8,12},{5,1},{1,5},{13,9},{9,13},{6,2},{2,6},{1... | collective-permute-start | bytes 786440 | tf_op jit(solution)/shard_map/ppermute | solution.py:229
  6.4 2.5 %collective-permute-start.4 = (bf16[512,256]{1,0:T(8,128)(2,1)S(1)}, bf16[512,256]{1,0:T(8,128)(2,1)S(1)}, u32[]{:S(2)}, u32[]{:S(2)}) collective-permute-start(bf16[512,256]{1,0:T(8,128)(2,1)S(1)} %get-tuple-element.11.refs_1_.refs_4_), channel_id=1, source_target_pairs={{12,0},{8,4},{4,8},{0,12},{13,1},{9,5},{5,9},{1,13},{14,2},{10,6},... | collective-permute-start | bytes 786440 | tf_op jit(solution)/shard_map/ppermute | solution.py:229
  8.9 0.0 collective-permute-start
  8.9 6.9 %collective-permute-done.1.refs_0_ = bf16[512,512]{1,0:T(8,128)(2,1)S(1)} collective-permute-done((bf16[512,512]{1,0:T(8,128)(2,1)}, bf16[512,512]{1,0:T(8,128)(2,1)S(1)}, u32[]{:S(2)}, u32[]{:S(2)}) %collective-permute-start.1) | collective-permute-done | bytes 524320 | tf_op jit(solution)/shard_map/ppermute | solution.py:229
  15.8 0.0 collective-permute-start.2
  15.8 0.0 collective-permute-done.3.refs_2_.refs_5_
  15.8 4.5 %collective-permute-done.4.refs_0_ = bf16[512,256]{1,0:T(8,128)(2,1)S(1)} collective-permute-done((bf16[512,256]{1,0:T(8,128)(2,1)S(1)}, bf16[512,256]{1,0:T(8,128)(2,1)S(1)}, u32[]{:S(2)}, u32[]{:S(2)}) %collective-permute-start.4) | collective-permute-done | bytes 262176 | tf_op jit(solution)/shard_map/ppermute | solution.py:229
  20.3 0.6 %collective-permute-start.5 = (bf16[512,256]{1,0:T(8,128)(2,1)S(1)}, bf16[512,256]{1,0:T(8,128)(2,1)S(1)}, u32[]{:S(2)}, u32[]{:S(2)}) collective-permute-start(bf16[512,256]{1,0:T(8,128)(2,1)S(1)} %relay.5.refs_6_), channel_id=1, source_target_pairs={{4,0},{0,4},{12,8},{8,12},{5,1},{1,5},{13,9},{9,13},{6,2},{2,6},{1... | collective-permute-start | bytes 786440 | tf_op jit(solution)/shard_map/ppermute | solution.py:229
  20.9 0.0 collective-permute-done.refs_1_
  20.9 0.0 collective-permute-done.2.refs_3_
  20.9 1.7 %partial.1 = (f32[512,256]{1,0:T(8,128)S(1)}, bf16[1,512,512]{2,1,0:T(8,128)(2,1)S(1)}, bf16[256,512]{1,0:T(8,128)(2,1)S(1)}, bf16[64,640]{1,0:T(8,128)(2,1)S(1)}) custom-call(s32[4]{0:T(128)S(1)} %fusion.2.slots_ref, bf16[512,512]{1,0:T(8,128)(2,1)S(1)} %get-tuple-element.10.refs_0_, bf16[512,512]{1,0:T(8,128)(2,1)S(1)} %collective-permute-done.refs_1_, ...), custom_call_target="tpu_custom_call" | custom-call | flops 536870912 | bytes 3145728 | tf_op jit(solution)/shard_map/partial/pallas_call | solution.py:140
  22.6 1.5 %collective-permute-start.8 = (bf16[64,640]{1,0:T(8,128)(2,1)S(1)}, bf16[64,640]{1,0:T(8,128)(2,1)S(1)}, u32[]{:S(2)}, u32[]{:S(2)}) collective-permute-start(bf16[64,640]{1,0:T(8,128)(2,1)S(1)} %get-tuple-element.15.refs_1_), channel_id=1, source_target_pairs={{8,0},{12,4},{0,8},{4,12},{9,1},{13,5},{1,9},{5,13},{10,2},{14,6},... | collective-permute-start | bytes 245768 | tf_op jit(solution)/shard_map/ppermute | solution.py:229
  24.2 2.3 %collective-permute-start.7 = (bf16[64,640]{1,0:T(8,128)(2,1)S(1)}, bf16[64,640]{1,0:T(8,128)(2,1)S(1)}, u32[]{:S(2)}, u32[]{:S(2)}) collective-permute-start(bf16[64,640]{1,0:T(8,128)(2,1)S(1)} %get-tuple-element.15.refs_1_), channel_id=1, source_target_pairs={{12,0},{8,4},{4,8},{0,12},{13,1},{9,5},{5,9},{1,13},{14,2},{10,6},... | collective-permute-start | bytes 245768 | tf_op jit(solution)/shard_map/ppermute | solution.py:229
  26.5 3.8 %collective-permute-done.5.refs_0_ = bf16[512,256]{1,0:T(8,128)(2,1)S(1)} collective-permute-done((bf16[512,256]{1,0:T(8,128)(2,1)S(1)}, bf16[512,256]{1,0:T(8,128)(2,1)S(1)}, u32[]{:S(2)}, u32[]{:S(2)}) %collective-permute-start.5) | collective-permute-done | bytes 262176 | tf_op jit(solution)/shard_map/ppermute | solution.py:229
  30.3 0.7 %products.1 = (f32[512,256]{1,0:T(8,128)S(1)}, bf16[64,640]{1,0:T(8,128)(2,1)S(1)}) custom-call(f32[512,256]{1,0:T(8,128)S(1)} %get-tuple-element.12.partial_ref, bf16[1,512,512]{2,1,0:T(8,128)(2,1)S(1)} %get-tuple-element.13.chosen_ref, bf16[256,512]{1,0:T(8,128)(2,1)S(1)} %get-tuple-element.14.turned_ref, ...), custom_call_target="tpu_custom_call" | custom-call | tf_op jit(solution)/shard_map/products/pallas_call | solution.py:174
  31.0 0.1 collective-permute-start.6
  31.1 0.8 %neg.3 = f32[512,256]{1,0:T(8,128)} negate(f32[512,256]{1,0:T(8,128)S(1)} %get-tuple-element.16) | non-fusion elementwise | flops 131072 | bytes 1048576 | tf_op jit(solution)/shard_map/neg | solution.py:260
  31.9 0.0 collective-permute-done.8.refs_0_
  31.9 0.4 collective-permute-done.7.refs_0_
  32.3 3.2 %collective-permute-done.6.refs_1_ = bf16[64,640]{1,0:T(8,128)(2,1)S(1)} collective-permute-done((bf16[64,640]{1,0:T(8,128)(2,1)S(1)}, bf16[64,640]{1,0:T(8,128)(2,1)S(1)}, u32[]{:S(2)}, u32[]{:S(2)}) %collective-permute-start.6) | collective-permute-done | bytes 81952 | tf_op jit(solution)/shard_map/ppermute | solution.py:229
  35.5 0.9 %finish.1 = f32[1,256,256]{2,1,0:T(8,128)} custom-call(f32[1,256,256]{2,1,0:T(8,128)S(1)} %copy-done, bf16[64,640]{1,0:T(8,128)(2,1)S(1)} %get-tuple-element.17.refs_0_, bf16[64,640]{1,0:T(8,128)(2,1)S(1)} %collective-permute-done.6.refs_1_, bf16[64,640]{1,0:T(8,128)(2,1)S(1)} %relay.6.refs_2_, bf16[64,640]{1,0:T(8,128)(2,1)S(1)} %relay.7.refs_3_), custom_call_target="tpu_custom_call" | custom-call | tf_op jit(solution)/shard_map/finish/pallas_call | solution.py:211
  (6 shorter events, 0.0 us)
Async XLA Ops:
  0.6 3.0 %copy-start = (f32[1,256,256]{2,1,0:T(8,128)S(1)}, f32[1,256,256]{2,1,0:T(8,128)}, u32[]{:S(2)}) copy-start(f32[1,256,256]{2,1,0:T(8,128)} %diag_ref.3) | copy-start | bytes 786436
  0.6 3.0 %copy-start.1 = (f32[512,256]{1,0:T(8,128)S(1)}, f32[512,256]{1,0:T(8,128)}, u32[]{:S(2)}) copy-start(f32[512,256]{1,0:T(8,128)} %cross_ref.1) | copy-start | bytes 1572868
  0.6 15.1 %collective-permute-start.1 = (bf16[512,512]{1,0:T(8,128)(2,1)}, bf16[512,512]{1,0:T(8,128)(2,1)S(1)}, u32[]{:S(2)}, u32[]{:S(2)}) collective-permute-start(bf16[512,512]{1,0:T(8,128)(2,1)} %top_hbm.1), channel_id=1, source_target_pairs={{2,0},{3,1},{0,2},{1,3},{6,4},{7,5},{4,6},{5,7},{10,8},{11,9},{8,1... | collective-permute-start | bytes 1572872 | tf_op jit(solution)/shard_map/ppermute | solution.py:229
  4.8 11.0 %collective-permute-start.3 = (bf16[512,256]{1,0:T(8,128)(2,1)S(1)}, bf16[512,256]{1,0:T(8,128)(2,1)S(1)}, u32[]{:S(2)}, u32[]{:S(2)}) collective-permute-start(bf16[512,256]{1,0:T(8,128)(2,1)S(1)} %get-tuple-element.11.refs_1_.refs_4_), channel_id=1, source_target_pairs={{4,0},{0,4},{12,8},{8,12},{5,1},{1,5},{13,9},{9,13},{6,2},{2,6},{1... | collective-permute-start | bytes 786440 | tf_op jit(solution)/shard_map/ppermute | solution.py:229
  6.4 13.9 %collective-permute-start.4 = (bf16[512,256]{1,0:T(8,128)(2,1)S(1)}, bf16[512,256]{1,0:T(8,128)(2,1)S(1)}, u32[]{:S(2)}, u32[]{:S(2)}) collective-permute-start(bf16[512,256]{1,0:T(8,128)(2,1)S(1)} %get-tuple-element.11.refs_1_.refs_4_), channel_id=1, source_target_pairs={{12,0},{8,4},{4,8},{0,12},{13,1},{9,5},{5,9},{1,13},{14,2},{10,6},... | collective-permute-start | bytes 786440 | tf_op jit(solution)/shard_map/ppermute | solution.py:229
  8.9 12.1 %collective-permute-start = (bf16[512,512]{1,0:T(8,128)(2,1)S(1)}, bf16[512,512]{1,0:T(8,128)(2,1)S(1)}, u32[]{:S(2)}, u32[]{:S(2)}) collective-permute-start(bf16[512,512]{1,0:T(8,128)(2,1)S(1)} %get-tuple-element.10.refs_0_), channel_id=1, source_target_pairs={{1,0},{0,1},{3,2},{2,3},{5,4},{4,5},{7,6},{6,7},{9,8},{8,9},{11,10... | collective-permute-start | bytes 1572872 | tf_op jit(solution)/shard_map/ppermute | solution.py:229
  15.8 5.2 %collective-permute-start.2 = (bf16[512,512]{1,0:T(8,128)(2,1)S(1)}, bf16[512,512]{1,0:T(8,128)(2,1)S(1)}, u32[]{:S(2)}, u32[]{:S(2)}) collective-permute-start(bf16[512,512]{1,0:T(8,128)(2,1)S(1)} %relay.4.refs_1_.refs_2_), channel_id=1, source_target_pairs={{1,0},{0,1},{3,2},{2,3},{5,4},{4,5},{7,6},{6,7},{9,8},{8,9},{11,10... | collective-permute-start | bytes 1572872 | tf_op jit(solution)/shard_map/ppermute | solution.py:229
  20.3 10.0 %collective-permute-start.5 = (bf16[512,256]{1,0:T(8,128)(2,1)S(1)}, bf16[512,256]{1,0:T(8,128)(2,1)S(1)}, u32[]{:S(2)}, u32[]{:S(2)}) collective-permute-start(bf16[512,256]{1,0:T(8,128)(2,1)S(1)} %relay.5.refs_6_), channel_id=1, source_target_pairs={{4,0},{0,4},{12,8},{8,12},{5,1},{1,5},{13,9},{9,13},{6,2},{2,6},{1... | collective-permute-start | bytes 786440 | tf_op jit(solution)/shard_map/ppermute | solution.py:229
  22.6 9.3 %collective-permute-start.8 = (bf16[64,640]{1,0:T(8,128)(2,1)S(1)}, bf16[64,640]{1,0:T(8,128)(2,1)S(1)}, u32[]{:S(2)}, u32[]{:S(2)}) collective-permute-start(bf16[64,640]{1,0:T(8,128)(2,1)S(1)} %get-tuple-element.15.refs_1_), channel_id=1, source_target_pairs={{8,0},{12,4},{0,8},{4,12},{9,1},{13,5},{1,9},{5,13},{10,2},{14,6},... | collective-permute-start | bytes 245768 | tf_op jit(solution)/shard_map/ppermute | solution.py:229
  24.2 8.1 %collective-permute-start.7 = (bf16[64,640]{1,0:T(8,128)(2,1)S(1)}, bf16[64,640]{1,0:T(8,128)(2,1)S(1)}, u32[]{:S(2)}, u32[]{:S(2)}) collective-permute-start(bf16[64,640]{1,0:T(8,128)(2,1)S(1)} %get-tuple-element.15.refs_1_), channel_id=1, source_target_pairs={{12,0},{8,4},{4,8},{0,12},{13,1},{9,5},{5,9},{1,13},{14,2},{10,6},... | collective-permute-start | bytes 245768 | tf_op jit(solution)/shard_map/ppermute | solution.py:229
  31.0 4.5 %collective-permute-start.6 = (bf16[64,640]{1,0:T(8,128)(2,1)S(1)}, bf16[64,640]{1,0:T(8,128)(2,1)S(1)}, u32[]{:S(2)}, u32[]{:S(2)}) collective-permute-start(bf16[64,640]{1,0:T(8,128)(2,1)S(1)} %get-tuple-element.17.refs_0_), channel_id=1, source_target_pairs={{4,0},{0,4},{12,8},{8,12},{5,1},{1,5},{13,9},{9,13},{6,2},{2,6},{1... | collective-permute-start | bytes 245768 | tf_op jit(solution)/shard_map/ppermute | solution.py:229

commit v20 on v15

--- a/solution.py
+++ b/solution.py
@@ -114,46 +114,73 @@
 
 def partial_kernel(n, slots_ref, *refs):
     tops, panels = refs[:n], refs[n:n + n // 2 + 1]
-    partial_ref, chosen_ref, turned_ref, update_ref, panel_buf = refs[n + n // 2 + 1:]
+    turned_ref, partial_ref, update_ref, panel_buf = refs[n + n // 2 + 1:]
     places = [0] + list(range(1, n, 2))
     for place, panel in zip(places, panels):
         panel_buf[slots_ref[place]] = panel[...]
-    for d, place in enumerate(range(2, n, 2)):
-        slot = slots_ref[place]
-        panel_buf[slot] = jnp.zeros(panel_buf.shape[1:], panel_buf.dtype)
-        for t in range(n):
-            @pl.when(slot == t)
-            def _():
-                chosen_ref[d] = tops[t][...]
+    for place in range(2, n, 2):
+        panel_buf[slots_ref[place]] = jnp.zeros(panel_buf.shape[1:], panel_buf.dtype)
     total = dot(tops[0][...], panel_buf[0])
     for t in range(1, n):
         total += dot(tops[t][...], panel_buf[t])
     partial_ref[...] = total
-    turned = panels[0][...].astype(jnp.float32).T.astype(jnp.bfloat16)
-    turned_ref[...] = turned
-    store_upper(update_ref, dot(turned, total.astype(jnp.bfloat16)))
-
-
-def partial_product(tops, panels, slots):
+    store_upper(update_ref, dot(turned_ref[...], total.astype(jnp.bfloat16)))
+
+
+def partial_product(tops, panels, turned, slots):
     n = len(tops)
     rows, width = panels[0].shape
     return pl.pallas_call(
         functools.partial(partial_kernel, n),
         out_shape=(
             jax.ShapeDtypeStruct((rows, width), jnp.float32),
-            jax.ShapeDtypeStruct((n // 2 - 1,) + tops[0].shape, jnp.bfloat16),
-            jax.ShapeDtypeStruct((width, rows), jnp.bfloat16),
             jax.ShapeDtypeStruct((width // 4, 5 * (width // 2)), jnp.bfloat16),
         ),
-        in_specs=[SMEM] + [VMEM] * (n + len(panels)),
-        out_specs=(VMEM, VMEM, VMEM, VMEM),
+        in_specs=[SMEM] + [VMEM] * (n + len(panels) + 1),
+        out_specs=(VMEM, VMEM),
         scratch_shapes=[pltpu.VMEM((n, rows, width), jnp.bfloat16)],
         compiler_params=PARAMS,
         cost_estimate=pl.CostEstimate(
             flops=2 * n * rows * rows * width, bytes_accessed=2 * n * rows * (rows + width), transcendentals=0
         ),
         name="partial",
-    )(slots, *tops, *panels)
+    )(slots, *tops, *panels, turned)
+
+
+def turn_kernel(panel_ref, turned_ref):
+    turned_ref[...] = panel_ref[...].astype(jnp.float32).T.astype(jnp.bfloat16)
+
+
+def turn(panel):
+    return pl.pallas_call(
+        turn_kernel,
+        out_shape=jax.ShapeDtypeStruct(panel.shape[::-1], panel.dtype),
+        in_specs=[VMEM],
+        out_specs=VMEM,
+        compiler_params=PARAMS,
+        name="turn",
+    )(panel)
+
+
+def choose_kernel(n, slots_ref, *refs):
+    tops, chosen_ref = refs[:n], refs[n]
+    for d, place in enumerate(range(2, n, 2)):
+        for t in range(n):
+            @pl.when(slots_ref[place] == t)
+            def _():
+                chosen_ref[d] = tops[t][...]
+
+
+def choose(tops, slots):
+    n = len(tops)
+    return pl.pallas_call(
+        functools.partial(choose_kernel, n),
+        out_shape=jax.ShapeDtypeStruct((n // 2 - 1,) + tops[0].shape, jnp.bfloat16),
+        in_specs=[SMEM] + [VMEM] * n,
+        out_specs=VMEM,
+        compiler_params=PARAMS,
+        name="choose",
+    )(slots, *tops)
 
 
 def product_kernel(count, alone, partial_ref, chosen_ref, turned_ref, *refs):
@@ -185,9 +212,9 @@
 
 
 def finish_kernel(diag_ref, *refs):
-    out_ref = refs[-1]
-    total = refs[0][...].astype(jnp.float32)
-    for ref in refs[1:-1]:
+    updates, (out_hbm, out_ref, sems) = refs[:-3], refs[-3:]
+    total = updates[0][...].astype(jnp.float32)
+    for ref in updates[1:]:
         total += ref[...].astype(jnp.float32)
     quarter = total.shape[0]
     half = 2 * quarter
@@ -195,24 +222,33 @@
     rows = lax.broadcasted_iota(jnp.int32, (half, half), 0)
     columns = lax.broadcasted_iota(jnp.int32, (half, half), 1)
     mirrored = (rows >= quarter) & (columns < quarter)
+    stores = [
+        pltpu.make_async_copy(out_ref.at[h], out_hbm.at[0, pl.ds(h * half, half)], sems.at[h]) for h in range(2)
+    ]
 
     def corner(top, bottom):
         block = jnp.concatenate([top, bottom], axis=0)
         return jnp.where(mirrored, block.T, block)
 
     side = jnp.concatenate([tiles[1], tiles[2]], axis=0)
-    out_ref[0, :half, :half] = diag_ref[0, :half, :half] + corner(tiles[0], tiles[4])
-    out_ref[0, :half, half:] = diag_ref[0, :half, half:] + side
-    out_ref[0, half:, :half] = diag_ref[0, half:, :half] + side.T
-    out_ref[0, half:, half:] = diag_ref[0, half:, half:] + corner(tiles[3], pltpu.roll(tiles[4], quarter, 1))
+    out_ref[0, :, :half] = diag_ref[0, :half, :half] + corner(tiles[0], tiles[4])
+    out_ref[0, :, half:] = diag_ref[0, :half, half:] + side
+    stores[0].start()
+    out_ref[1, :, :half] = diag_ref[0, half:, :half] + side.T
+    out_ref[1, :, half:] = diag_ref[0, half:, half:] + corner(tiles[3], pltpu.roll(tiles[4], quarter, 1))
+    stores[1].start()
+    for store in stores:
+        store.wait()
 
 
 def finish(diag_inverse, updates):
+    width = diag_inverse.shape[1]
     return pl.pallas_call(
         finish_kernel,
         out_shape=jax.ShapeDtypeStruct(diag_inverse.shape, jnp.float32),
         in_specs=[VMEM] * (1 + len(updates)),
-        out_specs=VMEM,
+        out_specs=ANY,
+        scratch_shapes=[pltpu.VMEM((2, width // 2, width), jnp.float32), pltpu.SemaphoreType.DMA((2,))],
         compiler_params=PARAMS,
         name="finish",
     )(diag_inverse, *updates)
@@ -235,8 +271,10 @@
     factor_panel, inverse_top = build_panel(cross_blocks, diag_inverse, pattern, inverse_top)
     beside = mate(factor_panel, "prow")
     crossed = [from_pair(factor_panel, "prow", d, 1) for d in range(1, pairs)]
-    near = [after(block, factor_panel) for block in near]
-    crossed = [after(block, near[0], beside, cost=HOP_COST) for block in crossed]
+    turned = turn(factor_panel)
+    near = [after(block, turned) for block in near]
+    crossed = [after(block, near[0], cost=HOP_COST) for block in crossed]
+    beside = after(beside, *crossed, cost=2 * HOP_COST)
     swapped = [mate(block, "prow") for block in crossed]
 
     tops = [inverse_top, mate(inverse_top, "pcol")]
@@ -248,7 +286,8 @@
     wanted_side = (row % PAIR) ^ (place % PAIR)
     slots = ((wanted_pair - col // PAIR) % pairs) * PAIR + (wanted_side ^ (col % PAIR))
 
-    partial, chosen, turned, early = partial_product(tops, [factor_panel, beside] + crossed, slots)
+    partial, early = partial_product(tops, [factor_panel, beside] + crossed, turned, slots)
+    chosen = choose(tops, slots)
     early = [early] + [after(from_pair(early, "prow", d, 1), swapped[-1]) for d in range(1, pairs)]
     if pairs > 2:
         selected, late = products(partial, chosen, turned, swapped, [])

time: 35.9 us -> 35.2 us (0.981)
  waiting for transfers between devices: 19.4 us -> 14.8 us
  starting transfers between devices: 10.5 us -> 13.6 us
  Pallas kernels: 4.33 us -> 4.99 us
    ppermute x8, waiting for transfers between devices: 19.4 us -> 14.8 us  [from_pair(): return lax.ppermute(block, axis, moves)]
    ppermute x8, starting transfers between devices: 10.5 us -> 13.6 us  [from_pair(): return lax.ppermute(block, axis, moves)]
    pallas_call x0 -> x2, Pallas kernels: none -> 0.73 us  [the longest x1 0.6 us: choose(): pl.pallas_call(functools.partial(choose_kernel, n), out_shape=jax.ShapeDt...]
  transfers between devices with their start and end apart: 8 -> 8, of which waited for: 5 -> 6; matrix products, arithmetic and copies ran while one was open for 2% -> 2% of each run, Pallas kernels for 8% -> 10%
where the time goes in v20:
time: 35.2 us; the launch traced here: 35 us
  waiting for transfers between devices  14.8 us (42%)
  starting transfers between devices  13.6 us (39%)
  Pallas kernels  4.99 us (14%)
  other arithmetic  0.85 us (2%)
  between operations  0.73 us (2%)
    ppermute x8, waiting for transfers between devices, from_pair(): return lax.ppermute(block, axis, moves)  14.8 us
    ppermute x8, starting transfers between devices, from_pair(): return lax.ppermute(block, axis, moves)  13.6 us
    pallas_call x1, Pallas kernels, partial_product(): pl.pallas_call(functools.partial(partial_kernel, n), out_shape=(jax.Shape...  1.64 us
    pallas_call x1, Pallas kernels, build_panel(): pl.pallas_call(panel_kernel, out_shape=(pltpu.VMEM(cross_blocks.shape, jn...  1.08 us
    pallas_call x1, Pallas kernels, finish(): pl.pallas_call(finish_kernel, out_shape=jax.ShapeDtypeStruct(diag_inverse...  0.84 us
    neg x1, other arithmetic, on_device(): return (-selected, finish(diag_inverse, [update, mate(update, 'prow')]))  0.83 us
  transfers between devices with their start and end apart: 8, of which 6 were waited for; matrix products, arithmetic and copies ran while one was open for 2% of the time, Pallas kernels for 10%

profile of v20, /device:TPU:0, one launch (start us, length us, event | category | flops | bytes accessed | tf_op | source)
XLA Modules:
  0.0 35.0 jit_solution(16448036333906329878)
XLA Ops:
  0.6 0.0 copy-start.1
  0.6 0.0 copy-start
  0.6 3.0 %collective-permute-start.1 = (bf16[512,512]{1,0:T(8,128)(2,1)}, bf16[512,512]{1,0:T(8,128)(2,1)S(1)}, u32[]{:S(2)}, u32[]{:S(2)}) collective-permute-start(bf16[512,512]{1,0:T(8,128)(2,1)} %top_hbm.1), channel_id=1, source_target_pairs={{2,0},{3,1},{0,2},{1,3},{6,4},{7,5},{4,6},{5,7},{10,8},{11,9},{8,1... | collective-permute-start | bytes 1572872 | tf_op jit(solution)/shard_map/ppermute | solution.py:265
  3.7 0.0 copy-done.1
  3.7 0.0 copy-done
  3.7 1.1 %panel.1 = (bf16[512,256]{1,0:T(8,128)(2,1)S(1)}, bf16[512,512]{1,0:T(8,128)(2,1)S(1)}) custom-call(s32[2]{0:T(128)} %bitcast.1, f32[512,256]{1,0:T(8,128)S(1)} %copy-done.1, f32[1,256,256]{2,1,0:T(8,128)S(1)} %copy-done, bf16[512,512]{1,0:T(8,128)(2,1)} %top_hbm.1, f32[8,128]{1,0:T(8,128)S(1)} %token_.1.token_ref), custom_call_target="tpu_custom_call" | custom-call | tf_op jit(solution)/shard_map/panel/pallas_call | solution.py:64
  4.8 3.7 %collective-permute-start.4 = (bf16[512,256]{1,0:T(8,128)(2,1)S(1)}, bf16[512,256]{1,0:T(8,128)(2,1)S(1)}, u32[]{:S(2)}, u32[]{:S(2)}) collective-permute-start(bf16[512,256]{1,0:T(8,128)(2,1)S(1)} %get-tuple-element.9.panel_ref.refs_4_), channel_id=1, source_target_pairs={{12,0},{8,4},{4,8},{0,12},{13,1},{9,5},{5,9},{1,13},{14,2},{10,6},... | collective-permute-start | bytes 786440 | tf_op jit(solution)/shard_map/ppermute | solution.py:265
  8.4 0.0 collective-permute-start.3
  8.4 0.0 collective-permute-start
  8.4 0.1 turn.1.refs_1_.refs_7_.turned_ref
  8.6 7.2 %collective-permute-done.1.refs_0_ = bf16[512,512]{1,0:T(8,128)(2,1)S(1)} collective-permute-done((bf16[512,512]{1,0:T(8,128)(2,1)}, bf16[512,512]{1,0:T(8,128)(2,1)S(1)}, u32[]{:S(2)}, u32[]{:S(2)}) %collective-permute-start.1) | collective-permute-done | bytes 524320 | tf_op jit(solution)/shard_map/ppermute | solution.py:265
  15.8 0.0 collective-permute-start.2
  15.8 0.1 collective-permute-done.4.refs_0_
  15.9 3.9 %collective-permute-start.5 = (bf16[512,256]{1,0:T(8,128)(2,1)S(1)}, bf16[512,256]{1,0:T(8,128)(2,1)S(1)}, u32[]{:S(2)}, u32[]{:S(2)}) collective-permute-start(bf16[512,256]{1,0:T(8,128)(2,1)S(1)} %relay.5.refs_1_.refs_6_), channel_id=1, source_target_pairs={{4,0},{0,4},{12,8},{8,12},{5,1},{1,5},{13,9},{9,13},{6,2},{2,6},{1... | collective-permute-start | bytes 786440 | tf_op jit(solution)/shard_map/ppermute | solution.py:265
  19.8 0.5 %collective-permute-done.3.refs_0_ = bf16[512,256]{1,0:T(8,128)(2,1)S(1)} collective-permute-done((bf16[512,256]{1,0:T(8,128)(2,1)S(1)}, bf16[512,256]{1,0:T(8,128)(2,1)S(1)}, u32[]{:S(2)}, u32[]{:S(2)}) %collective-permute-start.3) | collective-permute-done | bytes 262176 | tf_op jit(solution)/shard_map/ppermute | solution.py:265
  20.3 0.0 collective-permute-done.refs_1_
  20.3 0.0 collective-permute-done.2.refs_3_
  20.3 1.6 %partial.1 = (f32[512,256]{1,0:T(8,128)S(1)}, bf16[64,640]{1,0:T(8,128)(2,1)S(1)}) custom-call(s32[4]{0:T(128)S(1)} %fusion.2.slots_ref, bf16[512,512]{1,0:T(8,128)(2,1)S(1)} %get-tuple-element.8.refs_0_, bf16[512,512]{1,0:T(8,128)(2,1)S(1)} %collective-permute-done.refs_1_, bf16[512,512]{1,0:T(8,128)(2,1)S(1)} %relay.4.refs_1_.refs_2_, ...), custom_call_target="tpu_custom_call" | custom-call | flops 536870912 | bytes 3145728 | tf_op jit(solution)/shard_map/partial/pallas_call | solution.py:133
  21.9 2.1 %collective-permute-start.6 = (bf16[64,640]{1,0:T(8,128)(2,1)S(1)}, bf16[64,640]{1,0:T(8,128)(2,1)S(1)}, u32[]{:S(2)}, u32[]{:S(2)}) collective-permute-start(bf16[64,640]{1,0:T(8,128)(2,1)S(1)} %get-tuple-element.11.refs_1_), channel_id=1, source_target_pairs={{12,0},{8,4},{4,8},{0,12},{13,1},{9,5},{5,9},{1,13},{14,2},{10,6},... | collective-permute-start | bytes 245768 | tf_op jit(solution)/shard_map/ppermute | solution.py:265
  24.0 0.6 %choose.1.chosen_ref = bf16[1,512,512]{2,1,0:T(8,128)(2,1)S(1)} custom-call(s32[4]{0:T(128)S(1)} %fusion.2.slots_ref, bf16[512,512]{1,0:T(8,128)(2,1)S(1)} %get-tuple-element.8.refs_0_, bf16[512,512]{1,0:T(8,128)(2,1)S(1)} %collective-permute-done.refs_1_, bf16[512,512]{1,0:T(8,128)(2,1)S(1)} %relay.4.refs_1_.refs_2_, ...), custom_call_target="tpu_custom_call" | custom-call | tf_op jit(solution)/shard_map/choose/pallas_call | solution.py:176
  24.6 1.3 %collective-permute-done.5.refs_1_.refs_0_ = bf16[512,256]{1,0:T(8,128)(2,1)S(1)} collective-permute-done((bf16[512,256]{1,0:T(8,128)(2,1)S(1)}, bf16[512,256]{1,0:T(8,128)(2,1)S(1)}, u32[]{:S(2)}, u32[]{:S(2)}) %collective-permute-start.5) | collective-permute-done | bytes 262176 | tf_op jit(solution)/shard_map/ppermute | solution.py:265
  25.9 3.1 %collective-permute-done.6.refs_0_ = bf16[64,640]{1,0:T(8,128)(2,1)S(1)} collective-permute-done((bf16[64,640]{1,0:T(8,128)(2,1)S(1)}, bf16[64,640]{1,0:T(8,128)(2,1)S(1)}, u32[]{:S(2)}, u32[]{:S(2)}) %collective-permute-start.6) | collective-permute-done | bytes 81952 | tf_op jit(solution)/shard_map/ppermute | solution.py:265
  29.0 0.7 %products.1 = (f32[512,256]{1,0:T(8,128)S(1)}, bf16[64,640]{1,0:T(8,128)(2,1)S(1)}) custom-call(f32[512,256]{1,0:T(8,128)S(1)} %get-tuple-element.10.partial_ref, bf16[1,512,512]{2,1,0:T(8,128)(2,1)S(1)} %choose.1.chosen_ref, bf16[256,512]{1,0:T(8,128)(2,1)S(1)} %turn.1.refs_1_.refs_7_.turned_ref, ...), custom_call_target="tpu_custom_call" | custom-call | tf_op jit(solution)/shard_map/products/pallas_call | solution.py:201
  29.6 0.9 %collective-permute-start.7 = (bf16[64,640]{1,0:T(8,128)(2,1)S(1)}, bf16[64,640]{1,0:T(8,128)(2,1)S(1)}, u32[]{:S(2)}, u32[]{:S(2)}) collective-permute-start(bf16[64,640]{1,0:T(8,128)(2,1)S(1)} %get-tuple-element.13.refs_0_), channel_id=1, source_target_pairs={{4,0},{0,4},{12,8},{8,12},{5,1},{1,5},{13,9},{9,13},{6,2},{2,6},{1... | collective-permute-start | bytes 245768 | tf_op jit(solution)/shard_map/ppermute | solution.py:265
  30.6 0.8 %neg.3 = f32[512,256]{1,0:T(8,128)} negate(f32[512,256]{1,0:T(8,128)S(1)} %get-tuple-element.12) | non-fusion elementwise | flops 131072 | bytes 1048576 | tf_op jit(solution)/shard_map/neg | solution.py:298
  31.4 2.8 %collective-permute-done.7.refs_1_ = bf16[64,640]{1,0:T(8,128)(2,1)S(1)} collective-permute-done((bf16[64,640]{1,0:T(8,128)(2,1)S(1)}, bf16[64,640]{1,0:T(8,128)(2,1)S(1)}, u32[]{:S(2)}, u32[]{:S(2)}) %collective-permute-start.7) | collective-permute-done | bytes 81952 | tf_op jit(solution)/shard_map/ppermute | solution.py:265
  34.1 0.8 %finish.1 = f32[1,256,256]{2,1,0:T(8,128)} custom-call(f32[1,256,256]{2,1,0:T(8,128)S(1)} %copy-done, bf16[64,640]{1,0:T(8,128)(2,1)S(1)} %get-tuple-element.13.refs_0_, bf16[64,640]{1,0:T(8,128)(2,1)S(1)} %collective-permute-done.7.refs_1_), custom_call_target="tpu_custom_call" | custom-call | tf_op jit(solution)/shard_map/finish/pallas_call | solution.py:246
  (6 shorter events, 0.0 us)
Async XLA Ops:
  0.6 3.0 %copy-start.1 = (f32[512,256]{1,0:T(8,128)S(1)}, f32[512,256]{1,0:T(8,128)}, u32[]{:S(2)}) copy-start(f32[512,256]{1,0:T(8,128)} %cross_ref.1) | copy-start | bytes 1572868
  0.6 3.0 %copy-start = (f32[1,256,256]{2,1,0:T(8,128)S(1)}, f32[1,256,256]{2,1,0:T(8,128)}, u32[]{:S(2)}) copy-start(f32[1,256,256]{2,1,0:T(8,128)} %diag_ref.3) | copy-start | bytes 786436
  0.6 15.1 %collective-permute-start.1 = (bf16[512,512]{1,0:T(8,128)(2,1)}, bf16[512,512]{1,0:T(8,128)(2,1)S(1)}, u32[]{:S(2)}, u32[]{:S(2)}) collective-permute-start(bf16[512,512]{1,0:T(8,128)(2,1)} %top_hbm.1), channel_id=1, source_target_pairs={{2,0},{3,1},{0,2},{1,3},{6,4},{7,5},{4,6},{5,7},{10,8},{11,9},{8,1... | collective-permute-start | bytes 1572872 | tf_op jit(solution)/shard_map/ppermute | solution.py:265
  4.8 11.1 %collective-permute-start.4 = (bf16[512,256]{1,0:T(8,128)(2,1)S(1)}, bf16[512,256]{1,0:T(8,128)(2,1)S(1)}, u32[]{:S(2)}, u32[]{:S(2)}) collective-permute-start(bf16[512,256]{1,0:T(8,128)(2,1)S(1)} %get-tuple-element.9.panel_ref.refs_4_), channel_id=1, source_target_pairs={{12,0},{8,4},{4,8},{0,12},{13,1},{9,5},{5,9},{1,13},{14,2},{10,6},... | collective-permute-start | bytes 786440 | tf_op jit(solution)/shard_map/ppermute | solution.py:265
  8.4 11.8 %collective-permute-start.3 = (bf16[512,256]{1,0:T(8,128)(2,1)S(1)}, bf16[512,256]{1,0:T(8,128)(2,1)S(1)}, u32[]{:S(2)}, u32[]{:S(2)}) collective-permute-start(bf16[512,256]{1,0:T(8,128)(2,1)S(1)} %get-tuple-element.9.panel_ref.refs_4_), channel_id=1, source_target_pairs={{4,0},{0,4},{12,8},{8,12},{5,1},{1,5},{13,9},{9,13},{6,2},{2,6},{1... | collective-permute-start | bytes 786440 | tf_op jit(solution)/shard_map/ppermute | solution.py:265
  8.4 11.8 %collective-permute-start = (bf16[512,512]{1,0:T(8,128)(2,1)S(1)}, bf16[512,512]{1,0:T(8,128)(2,1)S(1)}, u32[]{:S(2)}, u32[]{:S(2)}) collective-permute-start(bf16[512,512]{1,0:T(8,128)(2,1)S(1)} %get-tuple-element.8.refs_0_), channel_id=1, source_target_pairs={{1,0},{0,1},{3,2},{2,3},{5,4},{4,5},{7,6},{6,7},{9,8},{8,9},{11,10... | collective-permute-start | bytes 1572872 | tf_op jit(solution)/shard_map/ppermute | solution.py:265
  15.8 4.5 %collective-permute-start.2 = (bf16[512,512]{1,0:T(8,128)(2,1)S(1)}, bf16[512,512]{1,0:T(8,128)(2,1)S(1)}, u32[]{:S(2)}, u32[]{:S(2)}) collective-permute-start(bf16[512,512]{1,0:T(8,128)(2,1)S(1)} %relay.4.refs_1_.refs_2_), channel_id=1, source_target_pairs={{1,0},{0,1},{3,2},{2,3},{5,4},{4,5},{7,6},{6,7},{9,8},{8,9},{11,10... | collective-permute-start | bytes 1572872 | tf_op jit(solution)/shard_map/ppermute | solution.py:265
  15.9 10.0 %collective-permute-start.5 = (bf16[512,256]{1,0:T(8,128)(2,1)S(1)}, bf16[512,256]{1,0:T(8,128)(2,1)S(1)}, u32[]{:S(2)}, u32[]{:S(2)}) collective-permute-start(bf16[512,256]{1,0:T(8,128)(2,1)S(1)} %relay.5.refs_1_.refs_6_), channel_id=1, source_target_pairs={{4,0},{0,4},{12,8},{8,12},{5,1},{1,5},{13,9},{9,13},{6,2},{2,6},{1... | collective-permute-start | bytes 786440 | tf_op jit(solution)/shard_map/ppermute | solution.py:265
  21.9 7.0 %collective-permute-start.6 = (bf16[64,640]{1,0:T(8,128)(2,1)S(1)}, bf16[64,640]{1,0:T(8,128)(2,1)S(1)}, u32[]{:S(2)}, u32[]{:S(2)}) collective-permute-start(bf16[64,640]{1,0:T(8,128)(2,1)S(1)} %get-tuple-element.11.refs_1_), channel_id=1, source_target_pairs={{12,0},{8,4},{4,8},{0,12},{13,1},{9,5},{5,9},{1,13},{14,2},{10,6},... | collective-permute-start | bytes 245768 | tf_op jit(solution)/shard_map/ppermute | solution.py:265
  29.6 4.5 %collective-permute-start.7 = (bf16[64,640]{1,0:T(8,128)(2,1)S(1)}, bf16[64,640]{1,0:T(8,128)(2,1)S(1)}, u32[]{:S(2)}, u32[]{:S(2)}) collective-permute-start(bf16[64,640]{1,0:T(8,128)(2,1)S(1)} %get-tuple-element.13.refs_0_), channel_id=1, source_target_pairs={{4,0},{0,4},{12,8},{8,12},{5,1},{1,5},{13,9},{9,13},{6,2},{2,6},{1... | collective-permute-start | bytes 245768 | tf_op jit(solution)/shard_map/ppermute | solution.py:265

commit v21 on v20

--- a/solution.py
+++ b/solution.py
@@ -109,22 +109,30 @@
         columns = pl.ds(t * half, half)
         for other in others:
             tile += other[:, columns].astype(jnp.float32)
-        out_ref[:, columns] = tile.astype(jnp.bfloat16)
+        out_ref[:, columns] = tile.astype(out_ref.dtype)
 
 
 def partial_kernel(n, slots_ref, *refs):
     tops, panels = refs[:n], refs[n:n + n // 2 + 1]
     turned_ref, partial_ref, update_ref, panel_buf = refs[n + n // 2 + 1:]
+
+    def run(pairs):
+        total = dot(*[ref[...] for ref in pairs[0]])
+        for top, panel in pairs[1:]:
+            total += dot(top[...], panel[...])
+        partial_ref[...] = total
+        store_upper(update_ref, dot(turned_ref[...], total.astype(jnp.bfloat16)))
+
+    if n == 2 * PAIR:
+        for own in range(n):
+            pl.when(slots_ref[0] == own)(functools.partial(run, list(zip([tops[own ^ s] for s in (0, 1, 3)], panels))))
+        return
     places = [0] + list(range(1, n, 2))
     for place, panel in zip(places, panels):
         panel_buf[slots_ref[place]] = panel[...]
     for place in range(2, n, 2):
         panel_buf[slots_ref[place]] = jnp.zeros(panel_buf.shape[1:], panel_buf.dtype)
-    total = dot(tops[0][...], panel_buf[0])
-    for t in range(1, n):
-        total += dot(tops[t][...], panel_buf[t])
-    partial_ref[...] = total
-    store_upper(update_ref, dot(turned_ref[...], total.astype(jnp.bfloat16)))
+    run([(tops[t], panel_buf.at[t]) for t in range(n)])
 
 
 def partial_product(tops, panels, turned, slots):
@@ -202,7 +210,7 @@
         functools.partial(product_kernel, len(panels), alone),
         out_shape=(
             jax.ShapeDtypeStruct((rows, width), jnp.float32),
-            jax.ShapeDtypeStruct((width // 4, 5 * (width // 2)), jnp.bfloat16),
+            jax.ShapeDtypeStruct((width // 4, 5 * (width // 2)), jnp.float32),
         ),
         in_specs=[VMEM] * (3 + len(panels) + len(early)),
         out_specs=(VMEM, VMEM),
@@ -288,13 +296,13 @@
 
     partial, early = partial_product(tops, [factor_panel, beside] + crossed, turned, slots)
     chosen = choose(tops, slots)
-    early = [early] + [after(from_pair(early, "prow", d, 1), swapped[-1]) for d in range(1, pairs)]
+    crossing = [after(from_pair(early, "prow", d, 1), swapped[-1]) for d in range(1, pairs)]
+    selected, late = products(partial, chosen, turned, swapped, [early])
+    parts = [late] + crossing
     if pairs > 2:
-        selected, late = products(partial, chosen, turned, swapped, [])
-        parts = early + [late] + [from_pair(late, "prow", d, 0) for d in range(1, pairs)]
-        update = functools.reduce(jnp.add, [part.astype(jnp.float32) for part in parts]).astype(jnp.bfloat16)
-    else:
-        selected, update = products(partial, chosen, turned, swapped, early)
+        rest = (late - early.astype(jnp.float32)).astype(jnp.bfloat16)
+        parts += [from_pair(rest, "prow", d, 0) for d in range(1, pairs)]
+    update = functools.reduce(jnp.add, [part.astype(jnp.float32) for part in parts]).astype(jnp.bfloat16)
     return -selected, finish(diag_inverse, [update, mate(update, "prow")])
 
 

time: 35.2 us -> 34.5 us (0.980)
  transfers between devices with their start and end apart: 8 -> 8, of which waited for: 6 -> 6; matrix products, arithmetic and copies ran while one was open for 2% -> 2% of each run, Pallas kernels for 10% -> 12%
where the time goes in v21:
time: 34.5 us; the launch traced here: 34.3 us
  waiting for transfers between devices  14.5 us (42%)
  starting transfers between devices  13.4 us (39%)
  Pallas kernels  4.81 us (14%)
  other arithmetic  0.87 us (3%)
  between operations  0.74 us (2%)
    ppermute x8, waiting for transfers between devices, from_pair(): return lax.ppermute(block, axis, moves)  14.5 us
    ppermute x8, starting transfers between devices, from_pair(): return lax.ppermute(block, axis, moves)  13.4 us
    pallas_call x1, Pallas kernels, partial_product(): pl.pallas_call(functools.partial(partial_kernel, n), out_shape=(jax.Shape...  1.46 us
    pallas_call x1, Pallas kernels, build_panel(): pl.pallas_call(panel_kernel, out_shape=(pltpu.VMEM(cross_blocks.shape, jn...  1.08 us
    pallas_call x1, Pallas kernels, finish(): pl.pallas_call(finish_kernel, out_shape=jax.ShapeDtypeStruct(diag_inverse...  0.84 us
    neg x1, other arithmetic, on_device(): return (-selected, finish(diag_inverse, [update, mate(update, 'prow')]))  0.83 us
  transfers between devices with their start and end apart: 8, of which 6 were waited for; matrix products, arithmetic and copies ran while one was open for 2% of the time, Pallas kernels for 12%

profile of v21, /device:TPU:0, one launch (start us, length us, event | category | flops | bytes accessed | tf_op | source)
XLA Modules:
  0.0 34.3 jit_solution(12623499949372872604)
XLA Ops:
  0.6 0.0 copy-start.1
  0.6 0.0 copy-start
  0.6 3.0 %collective-permute-start.1 = (bf16[512,512]{1,0:T(8,128)(2,1)}, bf16[512,512]{1,0:T(8,128)(2,1)S(1)}, u32[]{:S(2)}, u32[]{:S(2)}) collective-permute-start(bf16[512,512]{1,0:T(8,128)(2,1)} %top_hbm.1), channel_id=1, source_target_pairs={{2,0},{3,1},{0,2},{1,3},{6,4},{7,5},{4,6},{5,7},{10,8},{11,9},{8,1... | collective-permute-start | bytes 1572872 | tf_op jit(solution)/shard_map/ppermute | solution.py:273
  3.7 0.0 copy-done.1
  3.7 0.0 copy-done
  3.7 1.1 %panel.1 = (bf16[512,256]{1,0:T(8,128)(2,1)S(1)}, bf16[512,512]{1,0:T(8,128)(2,1)S(1)}) custom-call(s32[2]{0:T(128)} %bitcast.1, f32[512,256]{1,0:T(8,128)S(1)} %copy-done.1, f32[1,256,256]{2,1,0:T(8,128)S(1)} %copy-done, bf16[512,512]{1,0:T(8,128)(2,1)} %top_hbm.1, f32[8,128]{1,0:T(8,128)S(1)} %token_.1.token_ref), custom_call_target="tpu_custom_call" | custom-call | tf_op jit(solution)/shard_map/panel/pallas_call | solution.py:64
  4.8 3.7 %collective-permute-start.4 = (bf16[512,256]{1,0:T(8,128)(2,1)S(1)}, bf16[512,256]{1,0:T(8,128)(2,1)S(1)}, u32[]{:S(2)}, u32[]{:S(2)}) collective-permute-start(bf16[512,256]{1,0:T(8,128)(2,1)S(1)} %get-tuple-element.9.panel_ref.refs_4_), channel_id=1, source_target_pairs={{12,0},{8,4},{4,8},{0,12},{13,1},{9,5},{5,9},{1,13},{14,2},{10,6},... | collective-permute-start | bytes 786440 | tf_op jit(solution)/shard_map/ppermute | solution.py:273
  8.4 0.0 collective-permute-start.3
  8.4 0.0 collective-permute-start
  8.4 0.1 turn.1.refs_1_.refs_7_.turned_ref
  8.6 7.2 %collective-permute-done.1.refs_0_ = bf16[512,512]{1,0:T(8,128)(2,1)S(1)} collective-permute-done((bf16[512,512]{1,0:T(8,128)(2,1)}, bf16[512,512]{1,0:T(8,128)(2,1)S(1)}, u32[]{:S(2)}, u32[]{:S(2)}) %collective-permute-start.1) | collective-permute-done | bytes 524320 | tf_op jit(solution)/shard_map/ppermute | solution.py:273
  15.8 0.0 collective-permute-start.2
  15.8 0.1 collective-permute-done.4.refs_0_
  15.9 3.9 %collective-permute-start.5 = (bf16[512,256]{1,0:T(8,128)(2,1)S(1)}, bf16[512,256]{1,0:T(8,128)(2,1)S(1)}, u32[]{:S(2)}, u32[]{:S(2)}) collective-permute-start(bf16[512,256]{1,0:T(8,128)(2,1)S(1)} %relay.5.refs_1_.refs_6_), channel_id=1, source_target_pairs={{4,0},{0,4},{12,8},{8,12},{5,1},{1,5},{13,9},{9,13},{6,2},{2,6},{1... | collective-permute-start | bytes 786440 | tf_op jit(solution)/shard_map/ppermute | solution.py:273
  19.8 0.5 %collective-permute-done.3.refs_0_ = bf16[512,256]{1,0:T(8,128)(2,1)S(1)} collective-permute-done((bf16[512,256]{1,0:T(8,128)(2,1)S(1)}, bf16[512,256]{1,0:T(8,128)(2,1)S(1)}, u32[]{:S(2)}, u32[]{:S(2)}) %collective-permute-start.3) | collective-permute-done | bytes 262176 | tf_op jit(solution)/shard_map/ppermute | solution.py:273
  20.3 0.0 collective-permute-done.refs_1_
  20.3 0.0 collective-permute-done.2.refs_3_
  20.3 1.5 %partial.1 = (f32[512,256]{1,0:T(8,128)S(1)}, bf16[64,640]{1,0:T(8,128)(2,1)S(1)}) custom-call(s32[4]{0:T(128)S(1)} %fusion.2.slots_ref, bf16[512,512]{1,0:T(8,128)(2,1)S(1)} %get-tuple-element.8.refs_0_, bf16[512,512]{1,0:T(8,128)(2,1)S(1)} %collective-permute-done.refs_1_, bf16[512,512]{1,0:T(8,128)(2,1)S(1)} %relay.4.refs_1_.refs_2_, ...), custom_call_target="tpu_custom_call" | custom-call | flops 536870912 | bytes 3145728 | tf_op jit(solution)/shard_map/partial/pallas_call | solution.py:141
  21.7 2.1 %collective-permute-start.6 = (bf16[64,640]{1,0:T(8,128)(2,1)S(1)}, bf16[64,640]{1,0:T(8,128)(2,1)S(1)}, u32[]{:S(2)}, u32[]{:S(2)}) collective-permute-start(bf16[64,640]{1,0:T(8,128)(2,1)S(1)} %get-tuple-element.11.refs_1_), channel_id=1, source_target_pairs={{12,0},{8,4},{4,8},{0,12},{13,1},{9,5},{5,9},{1,13},{14,2},{10,6},... | collective-permute-start | bytes 245768 | tf_op jit(solution)/shard_map/ppermute | solution.py:273
  23.8 0.6 %choose.1.chosen_ref = bf16[1,512,512]{2,1,0:T(8,128)(2,1)S(1)} custom-call(s32[4]{0:T(128)S(1)} %fusion.2.slots_ref, bf16[512,512]{1,0:T(8,128)(2,1)S(1)} %get-tuple-element.8.refs_0_, bf16[512,512]{1,0:T(8,128)(2,1)S(1)} %collective-permute-done.refs_1_, bf16[512,512]{1,0:T(8,128)(2,1)S(1)} %relay.4.refs_1_.refs_2_, ...), custom_call_target="tpu_custom_call" | custom-call | tf_op jit(solution)/shard_map/choose/pallas_call | solution.py:184
  24.4 1.5 %collective-permute-done.5.refs_0_.refs_1_ = bf16[512,256]{1,0:T(8,128)(2,1)S(1)} collective-permute-done((bf16[512,256]{1,0:T(8,128)(2,1)S(1)}, bf16[512,256]{1,0:T(8,128)(2,1)S(1)}, u32[]{:S(2)}, u32[]{:S(2)}) %collective-permute-start.5) | collective-permute-done | bytes 262176 | tf_op jit(solution)/shard_map/ppermute | solution.py:273
  25.9 0.7 %products.1 = (f32[512,256]{1,0:T(8,128)S(1)}, f32[64,640]{1,0:T(8,128)S(1)}) custom-call(f32[512,256]{1,0:T(8,128)S(1)} %get-tuple-element.10.partial_ref, bf16[1,512,512]{2,1,0:T(8,128)(2,1)S(1)} %choose.1.chosen_ref, bf16[256,512]{1,0:T(8,128)(2,1)S(1)} %turn.1.refs_1_.refs_7_.turned_ref, bf16[512,256]{1,0:T(8,128)(2,1)S(1)} %collective-permute-done.5.refs_0_.refs_1_, ...), custom_call_target="tpu_custom_call" | custom-call | tf_op jit(solution)/shard_map/products/pallas_call | solution.py:209
  26.6 2.4 %collective-permute-done.6.refs_0_ = bf16[64,640]{1,0:T(8,128)(2,1)S(1)} collective-permute-done((bf16[64,640]{1,0:T(8,128)(2,1)S(1)}, bf16[64,640]{1,0:T(8,128)(2,1)S(1)}, u32[]{:S(2)}, u32[]{:S(2)}) %collective-permute-start.6) | collective-permute-done | bytes 81952 | tf_op jit(solution)/shard_map/ppermute | solution.py:273
  29.0 0.7 %collective-permute-start.7 = (bf16[64,640]{1,0:T(8,128)(2,1)S(1)}, bf16[64,640]{1,0:T(8,128)(2,1)S(1)}, u32[]{:S(2)}, u32[]{:S(2)}) collective-permute-start(bf16[64,640]{1,0:T(8,128)(2,1)S(1)} %add_convert_fusion.refs_0_), channel_id=1, source_target_pairs={{4,0},{0,4},{12,8},{8,12},{5,1},{1,5},{13,9},{9,13},{6,2},{2,6},{1... | collective-permute-start | bytes 245768 | tf_op jit(solution)/shard_map/ppermute | solution.py:273
  29.7 0.8 %neg.3 = f32[512,256]{1,0:T(8,128)} negate(f32[512,256]{1,0:T(8,128)S(1)} %get-tuple-element.12) | non-fusion elementwise | flops 131072 | bytes 1048576 | tf_op jit(solution)/shard_map/neg | solution.py:306
  30.5 2.9 %collective-permute-done.7.refs_1_ = bf16[64,640]{1,0:T(8,128)(2,1)S(1)} collective-permute-done((bf16[64,640]{1,0:T(8,128)(2,1)S(1)}, bf16[64,640]{1,0:T(8,128)(2,1)S(1)}, u32[]{:S(2)}, u32[]{:S(2)}) %collective-permute-start.7) | collective-permute-done | bytes 81952 | tf_op jit(solution)/shard_map/ppermute | solution.py:273
  33.5 0.8 %finish.1 = f32[1,256,256]{2,1,0:T(8,128)} custom-call(f32[1,256,256]{2,1,0:T(8,128)S(1)} %copy-done, bf16[64,640]{1,0:T(8,128)(2,1)S(1)} %add_convert_fusion.refs_0_, bf16[64,640]{1,0:T(8,128)(2,1)S(1)} %collective-permute-done.7.refs_1_), custom_call_target="tpu_custom_call" | custom-call | tf_op jit(solution)/shard_map/finish/pallas_call | solution.py:254
  (7 shorter events, 0.0 us)
Async XLA Ops:
  0.6 3.0 %copy-start.1 = (f32[512,256]{1,0:T(8,128)S(1)}, f32[512,256]{1,0:T(8,128)}, u32[]{:S(2)}) copy-start(f32[512,256]{1,0:T(8,128)} %cross_ref.1) | copy-start | bytes 1572868
  0.6 3.0 %copy-start = (f32[1,256,256]{2,1,0:T(8,128)S(1)}, f32[1,256,256]{2,1,0:T(8,128)}, u32[]{:S(2)}) copy-start(f32[1,256,256]{2,1,0:T(8,128)} %diag_ref.3) | copy-start | bytes 786436
  0.6 15.1 %collective-permute-start.1 = (bf16[512,512]{1,0:T(8,128)(2,1)}, bf16[512,512]{1,0:T(8,128)(2,1)S(1)}, u32[]{:S(2)}, u32[]{:S(2)}) collective-permute-start(bf16[512,512]{1,0:T(8,128)(2,1)} %top_hbm.1), channel_id=1, source_target_pairs={{2,0},{3,1},{0,2},{1,3},{6,4},{7,5},{4,6},{5,7},{10,8},{11,9},{8,1... | collective-permute-start | bytes 1572872 | tf_op jit(solution)/shard_map/ppermute | solution.py:273
  4.8 11.1 %collective-permute-start.4 = (bf16[512,256]{1,0:T(8,128)(2,1)S(1)}, bf16[512,256]{1,0:T(8,128)(2,1)S(1)}, u32[]{:S(2)}, u32[]{:S(2)}) collective-permute-start(bf16[512,256]{1,0:T(8,128)(2,1)S(1)} %get-tuple-element.9.panel_ref.refs_4_), channel_id=1, source_target_pairs={{12,0},{8,4},{4,8},{0,12},{13,1},{9,5},{5,9},{1,13},{14,2},{10,6},... | collective-permute-start | bytes 786440 | tf_op jit(solution)/shard_map/ppermute | solution.py:273
  8.4 11.8 %collective-permute-start.3 = (bf16[512,256]{1,0:T(8,128)(2,1)S(1)}, bf16[512,256]{1,0:T(8,128)(2,1)S(1)}, u32[]{:S(2)}, u32[]{:S(2)}) collective-permute-start(bf16[512,256]{1,0:T(8,128)(2,1)S(1)} %get-tuple-element.9.panel_ref.refs_4_), channel_id=1, source_target_pairs={{4,0},{0,4},{12,8},{8,12},{5,1},{1,5},{13,9},{9,13},{6,2},{2,6},{1... | collective-permute-start | bytes 786440 | tf_op jit(solution)/shard_map/ppermute | solution.py:273
  8.4 11.8 %collective-permute-start = (bf16[512,512]{1,0:T(8,128)(2,1)S(1)}, bf16[512,512]{1,0:T(8,128)(2,1)S(1)}, u32[]{:S(2)}, u32[]{:S(2)}) collective-permute-start(bf16[512,512]{1,0:T(8,128)(2,1)S(1)} %get-tuple-element.8.refs_0_), channel_id=1, source_target_pairs={{1,0},{0,1},{3,2},{2,3},{5,4},{4,5},{7,6},{6,7},{9,8},{8,9},{11,10... | collective-permute-start | bytes 1572872 | tf_op jit(solution)/shard_map/ppermute | solution.py:273
  15.8 4.5 %collective-permute-start.2 = (bf16[512,512]{1,0:T(8,128)(2,1)S(1)}, bf16[512,512]{1,0:T(8,128)(2,1)S(1)}, u32[]{:S(2)}, u32[]{:S(2)}) collective-permute-start(bf16[512,512]{1,0:T(8,128)(2,1)S(1)} %relay.4.refs_1_.refs_2_), channel_id=1, source_target_pairs={{1,0},{0,1},{3,2},{2,3},{5,4},{4,5},{7,6},{6,7},{9,8},{8,9},{11,10... | collective-permute-start | bytes 1572872 | tf_op jit(solution)/shard_map/ppermute | solution.py:273
  15.9 10.0 %collective-permute-start.5 = (bf16[512,256]{1,0:T(8,128)(2,1)S(1)}, bf16[512,256]{1,0:T(8,128)(2,1)S(1)}, u32[]{:S(2)}, u32[]{:S(2)}) collective-permute-start(bf16[512,256]{1,0:T(8,128)(2,1)S(1)} %relay.5.refs_1_.refs_6_), channel_id=1, source_target_pairs={{4,0},{0,4},{12,8},{8,12},{5,1},{1,5},{13,9},{9,13},{6,2},{2,6},{1... | collective-permute-start | bytes 786440 | tf_op jit(solution)/shard_map/ppermute | solution.py:273
  21.7 7.2 %collective-permute-start.6 = (bf16[64,640]{1,0:T(8,128)(2,1)S(1)}, bf16[64,640]{1,0:T(8,128)(2,1)S(1)}, u32[]{:S(2)}, u32[]{:S(2)}) collective-permute-start(bf16[64,640]{1,0:T(8,128)(2,1)S(1)} %get-tuple-element.11.refs_1_), channel_id=1, source_target_pairs={{12,0},{8,4},{4,8},{0,12},{13,1},{9,5},{5,9},{1,13},{14,2},{10,6},... | collective-permute-start | bytes 245768 | tf_op jit(solution)/shard_map/ppermute | solution.py:273
  29.0 4.5 %collective-permute-start.7 = (bf16[64,640]{1,0:T(8,128)(2,1)S(1)}, bf16[64,640]{1,0:T(8,128)(2,1)S(1)}, u32[]{:S(2)}, u32[]{:S(2)}) collective-permute-start(bf16[64,640]{1,0:T(8,128)(2,1)S(1)} %add_convert_fusion.refs_0_), channel_id=1, source_target_pairs={{4,0},{0,4},{12,8},{8,12},{5,1},{1,5},{13,9},{9,13},{6,2},{2,6},{1... | collective-permute-start | bytes 245768 | tf_op jit(solution)/shard_map/ppermute | solution.py:273

commit v22 on v21

--- a/solution.py
+++ b/solution.py
@@ -11,7 +11,6 @@
 VMEM_LIMIT = 40 * 1024 * 1024
 PARAMS = pltpu.CompilerParams(vmem_limit_bytes=VMEM_LIMIT)
 SMALL = pltpu.CompilerParams(vmem_limit_bytes=1024 * 1024)
-SMEM = pl.BlockSpec(memory_space=pltpu.SMEM)
 VMEM = pl.BlockSpec(memory_space=pltpu.VMEM)
 ANY = pl.BlockSpec(memory_space=pl.ANY)
 HBM = pl.BlockSpec(memory_space=pltpu.HBM)
@@ -41,13 +40,11 @@
     )()
 
 
-def panel_kernel(pattern_hbm, cross_ref, diag_ref, top_hbm, token_ref, panel_ref, top_ref, pattern_ref, sems):
+def panel_kernel(pattern_hbm, cross_ref, diag_ref, token_ref, panel_ref, pattern_ref, sem):
     del token_ref
     width = diag_ref.shape[1]
-    pattern_copy = pltpu.make_async_copy(pattern_hbm, pattern_ref, sems.at[0])
+    pattern_copy = pltpu.make_async_copy(pattern_hbm, pattern_ref, sem)
     pattern_copy.start()
-    top_copy = pltpu.make_async_copy(top_hbm, top_ref, sems.at[1])
-    top_copy.start()
     diag_high, diag_low = split(diag_ref[0])
     solved = []
     for a in range(pattern_hbm.shape[0]):
@@ -57,26 +54,21 @@
     for a, block in enumerate(solved):
         kept = jnp.where(pattern_ref[a] != 0, block, 0.0)
         panel_ref[pl.ds(a * width, width), :] = kept.astype(jnp.bfloat16)
-    top_copy.wait()
-
-
-def build_panel(cross_blocks, diag_inverse, pattern, inverse_top):
+
+
+def build_panel(cross_blocks, diag_inverse, pattern):
     return pl.pallas_call(
         panel_kernel,
-        out_shape=(
-            pltpu.VMEM(cross_blocks.shape, jnp.bfloat16),
-            pltpu.VMEM(inverse_top.shape, inverse_top.dtype),
-        ),
-        in_specs=[HBM, VMEM, VMEM, HBM, ANY],
-        out_specs=(VMEM, VMEM),
-        scratch_shapes=[pltpu.SMEM((pattern.size,), jnp.int32), pltpu.SemaphoreType.DMA((2,))],
+        out_shape=pltpu.VMEM(cross_blocks.shape, jnp.bfloat16),
+        in_specs=[HBM, VMEM, VMEM, ANY],
+        out_specs=VMEM,
+        scratch_shapes=[pltpu.SMEM((pattern.size,), jnp.int32), pltpu.SemaphoreType.DMA],
         compiler_params=PARAMS,
         name="panel",
     )(
         pltpu.with_memory_space_constraint(pattern.reshape(-1), pltpu.HBM),
         cross_blocks,
         diag_inverse,
-        pltpu.with_memory_space_constraint(inverse_top, pltpu.HBM),
         token(),
     )
 
@@ -112,7 +104,15 @@
         out_ref[:, columns] = tile.astype(out_ref.dtype)
 
 
-def partial_kernel(n, slots_ref, *refs):
+def place_of(n, d, f):
+    pairs = n // PAIR
+    row, col = lax.axis_index("prow"), lax.axis_index("pcol")
+    pair = (row // PAIR + d + pairs - col // PAIR) % pairs
+    side = (row + f + col) % PAIR
+    return pair * PAIR + side
+
+
+def partial_kernel(n, *refs):
     tops, panels = refs[:n], refs[n:n + n // 2 + 1]
     turned_ref, partial_ref, update_ref, panel_buf = refs[n + n // 2 + 1:]
 
@@ -124,18 +124,20 @@
         store_upper(update_ref, dot(turned_ref[...], total.astype(jnp.bfloat16)))
 
     if n == 2 * PAIR:
+        place = place_of(n, 0, 0)
         for own in range(n):
-            pl.when(slots_ref[0] == own)(functools.partial(run, list(zip([tops[own ^ s] for s in (0, 1, 3)], panels))))
+            pl.when(place == own)(functools.partial(run, list(zip([tops[own ^ s] for s in (0, 1, 3)], panels))))
         return
-    places = [0] + list(range(1, n, 2))
-    for place, panel in zip(places, panels):
-        panel_buf[slots_ref[place]] = panel[...]
-    for place in range(2, n, 2):
-        panel_buf[slots_ref[place]] = jnp.zeros(panel_buf.shape[1:], panel_buf.dtype)
+    pairs = n // PAIR
+    held = [(0, 0)] + [(d, 1) for d in range(pairs)]
+    for (d, f), panel in zip(held, panels):
+        panel_buf[place_of(n, d, f)] = panel[...]
+    for d in range(1, pairs):
+        panel_buf[place_of(n, d, 0)] = jnp.zeros(panel_buf.shape[1:], panel_buf.dtype)
     run([(tops[t], panel_buf.at[t]) for t in range(n)])
 
 
-def partial_product(tops, panels, turned, slots):
+def partial_product(tops, panels, turned):
     n = len(tops)
     rows, width = panels[0].shape
     return pl.pallas_call(
@@ -144,7 +146,7 @@
             jax.ShapeDtypeStruct((rows, width), jnp.float32),
             jax.ShapeDtypeStruct((width // 4, 5 * (width // 2)), jnp.bfloat16),
         ),
-        in_specs=[SMEM] + [VMEM] * (n + len(panels) + 1),
+        in_specs=[VMEM] * (n + len(panels) + 1),
         out_specs=(VMEM, VMEM),
         scratch_shapes=[pltpu.VMEM((n, rows, width), jnp.bfloat16)],
         compiler_params=PARAMS,
@@ -152,43 +154,48 @@
             flops=2 * n * rows * rows * width, bytes_accessed=2 * n * rows * (rows + width), transcendentals=0
         ),
         name="partial",
-    )(slots, *tops, *panels, turned)
-
-
-def turn_kernel(panel_ref, turned_ref):
+    )(*tops, *panels, turned)
+
+
+def stage_kernel(panel_ref, top_hbm, turned_ref, top_ref, sem):
+    copy = pltpu.make_async_copy(top_hbm, top_ref, sem)
+    copy.start()
     turned_ref[...] = panel_ref[...].astype(jnp.float32).T.astype(jnp.bfloat16)
-
-
-def turn(panel):
-    return pl.pallas_call(
-        turn_kernel,
-        out_shape=jax.ShapeDtypeStruct(panel.shape[::-1], panel.dtype),
-        in_specs=[VMEM],
-        out_specs=VMEM,
-        compiler_params=PARAMS,
-        name="turn",
-    )(panel)
-
-
-def choose_kernel(n, slots_ref, *refs):
+    copy.wait()
+
+
+def stage(panel, inverse_top):
+    return pl.pallas_call(
+        stage_kernel,
+        out_shape=(pltpu.VMEM(panel.shape[::-1], panel.dtype), pltpu.VMEM(inverse_top.shape, inverse_top.dtype)),
+        in_specs=[VMEM, HBM],
+        out_specs=(VMEM, VMEM),
+        scratch_shapes=[pltpu.SemaphoreType.DMA],
+        compiler_params=PARAMS,
+        name="stage",
+    )(panel, pltpu.with_memory_space_constraint(inverse_top, pltpu.HBM))
+
+
+def choose_kernel(n, *refs):
     tops, chosen_ref = refs[:n], refs[n]
-    for d, place in enumerate(range(2, n, 2)):
+    for d in range(1, n // PAIR):
+        place = place_of(n, d, 0)
         for t in range(n):
-            @pl.when(slots_ref[place] == t)
+            @pl.when(place == t)
             def _():
-                chosen_ref[d] = tops[t][...]
-
-
-def choose(tops, slots):
+                chosen_ref[d - 1] = tops[t][...]
+
+
+def choose(tops):
     n = len(tops)
     return pl.pallas_call(
         functools.partial(choose_kernel, n),
         out_shape=jax.ShapeDtypeStruct((n // 2 - 1,) + tops[0].shape, jnp.bfloat16),
-        in_specs=[SMEM] + [VMEM] * n,
+        in_specs=[VMEM] * n,
         out_specs=VMEM,
         compiler_params=PARAMS,
         name="choose",
-    )(slots, *tops)
+    )(*tops)
 
 
 def product_kernel(count, alone, partial_ref, chosen_ref, turned_ref, *refs):
@@ -264,7 +271,6 @@
 
 def on_device(n, inverse_top, diag_inverse, cross_blocks, pattern):
     pairs = n // PAIR
-    row, col = lax.axis_index("prow"), lax.axis_index("pcol")
 
     def from_pair(block, axis, shift, flip):
         moves = [
@@ -276,10 +282,10 @@
         return from_pair(block, axis, 0, 1)
 
     near = [from_pair(inverse_top, "pcol", d, 0) for d in range(1, pairs)]
-    factor_panel, inverse_top = build_panel(cross_blocks, diag_inverse, pattern, inverse_top)
+    factor_panel = build_panel(cross_blocks, diag_inverse, pattern)
     beside = mate(factor_panel, "prow")
     crossed = [from_pair(factor_panel, "prow", d, 1) for d in range(1, pairs)]
-    turned = turn(factor_panel)
+    turned, inverse_top = stage(factor_panel, inverse_top)
     near = [after(block, turned) for block in near]
     crossed = [after(block, near[0], cost=HOP_COST) for block in crossed]
     beside = after(beside, *crossed, cost=2 * HOP_COST)
@@ -289,13 +295,8 @@
     for block in near:
         tops += [block, mate(block, "pcol")]
 
-    place = jnp.arange(n, dtype=jnp.int32)
-    wanted_pair = (row // PAIR + place // PAIR) % pairs
-    wanted_side = (row % PAIR) ^ (place % PAIR)
-    slots = ((wanted_pair - col // PAIR) % pairs) * PAIR + (wanted_side ^ (col % PAIR))
-
-    partial, early = partial_product(tops, [factor_panel, beside] + crossed, turned, slots)
-    chosen = choose(tops, slots)
+    partial, early = partial_product(tops, [factor_panel, beside] + crossed, turned)
+    chosen = choose(tops)
     crossing = [after(from_pair(early, "prow", d, 1), swapped[-1]) for d in range(1, pairs)]
     selected, late = products(partial, chosen, turned, swapped, [early])
     parts = [late] + crossing

time: 34.5 us -> 34.1 us (0.988)
  waiting for transfers between devices: 14.5 us -> 15.2 us
  starting transfers between devices: 13.4 us -> 12.8 us
  Pallas kernels: 4.81 us -> 4.38 us
    pallas_call x2, Pallas kernels: 1.22 us -> 1.89 us  [the longest x1 1.07 us: stage(): pl.pallas_call(stage_kernel, out_shape=(pltpu.VMEM(panel.shape[::-1], pan...]
    ppermute x8, waiting for transfers between devices: 14.5 us -> 15.2 us  [from_pair(): return lax.ppermute(block, axis, moves)]
    ppermute x8, starting transfers between devices: 13.4 us -> 12.8 us  [from_pair(): return lax.ppermute(block, axis, moves)]
    pallas_call x1, Pallas kernels: 0.6 us -> 0.04 us  [choose(): pl.pallas_call(functools.partial(choose_kernel, n), out_shape=jax.ShapeDt...]
    pallas_call x1, Pallas kernels: 1.46 us -> 0.93 us  [partial_product(): pl.pallas_call(functools.partial(partial_kernel, n), out_shape=(jax.Shape...]
  transfers between devices with their start and end apart: 8 -> 8, of which waited for: 6 -> 5; matrix products, arithmetic and copies ran while one was open for 2% -> 2% of each run, Pallas kernels for 12% -> 10%
where the time goes in v22:
time: 34.1 us; the launch traced here: 33.9 us
  waiting for transfers between devices  15.2 us (45%)
  starting transfers between devices  12.8 us (38%)
  Pallas kernels  4.38 us (13%)
  other arithmetic  0.85 us (2%)
  between operations  0.71 us (2%)
    ppermute x8, waiting for transfers between devices, from_pair(): return lax.ppermute(block, axis, moves)  15.2 us
    ppermute x8, starting transfers between devices, from_pair(): return lax.ppermute(block, axis, moves)  12.8 us
    pallas_call x1, Pallas kernels, stage(): pl.pallas_call(stage_kernel, out_shape=(pltpu.VMEM(panel.shape[::-1], pan...  1.07 us
    pallas_call x1, Pallas kernels, partial_product(): pl.pallas_call(functools.partial(partial_kernel, n), out_shape=(jax.Shape...  0.93 us
    pallas_call x1, Pallas kernels, finish(): pl.pallas_call(finish_kernel, out_shape=jax.ShapeDtypeStruct(diag_inverse...  0.84 us
    neg x1, other arithmetic, on_device(): return (-selected, finish(diag_inverse, [update, mate(update, 'prow')]))  0.83 us
    pallas_call x1, Pallas kernels, build_panel(): pl.pallas_call(panel_kernel, out_shape=pltpu.VMEM(cross_blocks.shape, jnp...  0.82 us
    pallas_call x1, Pallas kernels, products(): pl.pallas_call(functools.partial(product_kernel, len(panels), alone), out...  0.69 us
  transfers between devices with their start and end apart: 8, of which 5 were waited for; matrix products, arithmetic and copies ran while one was open for 2% of the time, Pallas kernels for 10%

profile of v22, /device:TPU:0, one launch (start us, length us, event | category | flops | bytes accessed | tf_op | source)
XLA Modules:
  0.0 33.9 jit_solution(7376092816959095781)
XLA Ops:
  0.6 0.0 copy-start.1
  0.6 0.0 copy-start
  0.6 3.0 %collective-permute-start.1 = (bf16[512,512]{1,0:T(8,128)(2,1)}, bf16[512,512]{1,0:T(8,128)(2,1)S(1)}, u32[]{:S(2)}, u32[]{:S(2)}) collective-permute-start(bf16[512,512]{1,0:T(8,128)(2,1)} %top_hbm.1), channel_id=1, source_target_pairs={{2,0},{3,1},{0,2},{1,3},{6,4},{7,5},{4,6},{5,7},{10,8},{11,9},{8,1... | collective-permute-start | bytes 1572872 | tf_op jit(solution)/shard_map/ppermute | solution.py:279
  3.7 0.0 copy-done.1
  3.7 0.0 copy-done
  3.7 0.8 %panel.1.panel_ref.refs_4_ = bf16[512,256]{1,0:T(8,128)(2,1)S(1)} custom-call(s32[2]{0:T(128)} %bitcast.1, f32[512,256]{1,0:T(8,128)S(1)} %copy-done.1, f32[1,256,256]{2,1,0:T(8,128)S(1)} %copy-done, f32[8,128]{1,0:T(8,128)S(1)} %token_.1.token_ref), custom_call_target="tpu_custom_call" | custom-call | tf_op jit(solution)/shard_map/panel/pallas_call | solution.py:60
  4.5 3.7 %collective-permute-start.4 = (bf16[512,256]{1,0:T(8,128)(2,1)S(1)}, bf16[512,256]{1,0:T(8,128)(2,1)S(1)}, u32[]{:S(2)}, u32[]{:S(2)}) collective-permute-start(bf16[512,256]{1,0:T(8,128)(2,1)S(1)} %panel.1.panel_ref.refs_4_), channel_id=1, source_target_pairs={{12,0},{8,4},{4,8},{0,12},{13,1},{9,5},{5,9},{1,13},{14,2},{10,6},... | collective-permute-start | bytes 786440 | tf_op jit(solution)/shard_map/ppermute | solution.py:279
  8.2 0.0 collective-permute-start.3
  8.2 1.1 %stage.1 = (bf16[256,512]{1,0:T(8,128)(2,1)S(1)}, bf16[512,512]{1,0:T(8,128)(2,1)S(1)}) custom-call(bf16[512,256]{1,0:T(8,128)(2,1)S(1)} %panel.1.panel_ref.refs_4_, bf16[512,512]{1,0:T(8,128)(2,1)} %top_hbm.1), custom_call_target="tpu_custom_call" | custom-call | tf_op jit(solution)/shard_map/stage/pallas_call | solution.py:168
  9.2 0.1 collective-permute-start
  9.3 6.5 %collective-permute-done.1.refs_0_ = bf16[512,512]{1,0:T(8,128)(2,1)S(1)} collective-permute-done((bf16[512,512]{1,0:T(8,128)(2,1)}, bf16[512,512]{1,0:T(8,128)(2,1)S(1)}, u32[]{:S(2)}, u32[]{:S(2)}) %collective-permute-start.1) | collective-permute-done | bytes 524320 | tf_op jit(solution)/shard_map/ppermute | solution.py:279
  15.8 0.0 collective-permute-start.2
  15.8 0.0 collective-permute-done.4.refs_0_
  15.8 3.7 %collective-permute-start.5 = (bf16[512,256]{1,0:T(8,128)(2,1)S(1)}, bf16[512,256]{1,0:T(8,128)(2,1)S(1)}, u32[]{:S(2)}, u32[]{:S(2)}) collective-permute-start(bf16[512,256]{1,0:T(8,128)(2,1)S(1)} %relay.5.refs_1_.refs_6_), channel_id=1, source_target_pairs={{4,0},{0,4},{12,8},{8,12},{5,1},{1,5},{13,9},{9,13},{6,2},{2,6},{1... | collective-permute-start | bytes 786440 | tf_op jit(solution)/shard_map/ppermute | solution.py:279
  19.5 0.5 %collective-permute-done.3.refs_0_ = bf16[512,256]{1,0:T(8,128)(2,1)S(1)} collective-permute-done((bf16[512,256]{1,0:T(8,128)(2,1)S(1)}, bf16[512,256]{1,0:T(8,128)(2,1)S(1)}, u32[]{:S(2)}, u32[]{:S(2)}) %collective-permute-start.3) | collective-permute-done | bytes 262176 | tf_op jit(solution)/shard_map/ppermute | solution.py:279
  20.0 0.0 collective-permute-done.refs_1_
  20.0 0.0 collective-permute-done.2.refs_3_
  20.0 0.9 %partial.1 = (f32[512,256]{1,0:T(8,128)S(1)}, bf16[64,640]{1,0:T(8,128)(2,1)S(1)}) custom-call(bf16[512,512]{1,0:T(8,128)(2,1)S(1)} %get-tuple-element.8.refs_0_, bf16[512,512]{1,0:T(8,128)(2,1)S(1)} %collective-permute-done.refs_1_, bf16[512,512]{1,0:T(8,128)(2,1)S(1)} %relay.4.refs_1_.refs_2_, bf16[512,512]{1,0:T(8,128)(2,1)S(1)} %collective-permute-done.2.refs_3_, ...), custom_call_target="tpu_custom_call" | custom-call | flops 536870912 | bytes 3145728 | tf_op jit(solution)/shard_map/partial/pallas_call | solution.py:143
  20.9 2.1 %collective-permute-start.6 = (bf16[64,640]{1,0:T(8,128)(2,1)S(1)}, bf16[64,640]{1,0:T(8,128)(2,1)S(1)}, u32[]{:S(2)}, u32[]{:S(2)}) collective-permute-start(bf16[64,640]{1,0:T(8,128)(2,1)S(1)} %get-tuple-element.11.refs_1_), channel_id=1, source_target_pairs={{12,0},{8,4},{4,8},{0,12},{13,1},{9,5},{5,9},{1,13},{14,2},{10,6},... | collective-permute-start | bytes 245768 | tf_op jit(solution)/shard_map/ppermute | solution.py:279
  23.1 2.6 %collective-permute-done.5.refs_0_.refs_1_ = bf16[512,256]{1,0:T(8,128)(2,1)S(1)} collective-permute-done((bf16[512,256]{1,0:T(8,128)(2,1)S(1)}, bf16[512,256]{1,0:T(8,128)(2,1)S(1)}, u32[]{:S(2)}, u32[]{:S(2)}) %collective-permute-start.5) | collective-permute-done | bytes 262176 | tf_op jit(solution)/shard_map/ppermute | solution.py:279
  25.6 0.7 %products.1 = (f32[512,256]{1,0:T(8,128)S(1)}, f32[64,640]{1,0:T(8,128)S(1)}) custom-call(f32[512,256]{1,0:T(8,128)S(1)} %get-tuple-element.10.partial_ref, bf16[1,512,512]{2,1,0:T(8,128)(2,1)S(1)} %choose.1.chosen_ref, bf16[256,512]{1,0:T(8,128)(2,1)S(1)} %get-tuple-element.9.refs_1_.refs_7_.turned_ref, ...), custom_call_target="tpu_custom_call" | custom-call | tf_op jit(solution)/shard_map/products/pallas_call | solution.py:216
  26.3 2.2 %collective-permute-done.6.refs_0_ = bf16[64,640]{1,0:T(8,128)(2,1)S(1)} collective-permute-done((bf16[64,640]{1,0:T(8,128)(2,1)S(1)}, bf16[64,640]{1,0:T(8,128)(2,1)S(1)}, u32[]{:S(2)}, u32[]{:S(2)}) %collective-permute-start.6) | collective-permute-done | bytes 81952 | tf_op jit(solution)/shard_map/ppermute | solution.py:279
  28.6 0.3 collective-permute-start.7
  28.9 0.8 %neg.3 = f32[512,256]{1,0:T(8,128)} negate(f32[512,256]{1,0:T(8,128)S(1)} %get-tuple-element.12) | non-fusion elementwise | flops 131072 | bytes 1048576 | tf_op jit(solution)/shard_map/neg | solution.py:307
  29.7 3.4 %collective-permute-done.7.refs_1_ = bf16[64,640]{1,0:T(8,128)(2,1)S(1)} collective-permute-done((bf16[64,640]{1,0:T(8,128)(2,1)S(1)}, bf16[64,640]{1,0:T(8,128)(2,1)S(1)}, u32[]{:S(2)}, u32[]{:S(2)}) %collective-permute-start.7) | collective-permute-done | bytes 81952 | tf_op jit(solution)/shard_map/ppermute | solution.py:279
  33.1 0.8 %finish.1 = f32[1,256,256]{2,1,0:T(8,128)} custom-call(f32[1,256,256]{2,1,0:T(8,128)S(1)} %copy-done, bf16[64,640]{1,0:T(8,128)(2,1)S(1)} %add_convert_fusion.refs_0_, bf16[64,640]{1,0:T(8,128)(2,1)S(1)} %collective-permute-done.7.refs_1_), custom_call_target="tpu_custom_call" | custom-call | tf_op jit(solution)/shard_map/finish/pallas_call | solution.py:261
  (7 shorter events, 0.1 us)
Async XLA Ops:
  0.6 3.0 %copy-start.1 = (f32[512,256]{1,0:T(8,128)S(1)}, f32[512,256]{1,0:T(8,128)}, u32[]{:S(2)}) copy-start(f32[512,256]{1,0:T(8,128)} %cross_ref.1) | copy-start | bytes 1572868
  0.6 3.0 %copy-start = (f32[1,256,256]{2,1,0:T(8,128)S(1)}, f32[1,256,256]{2,1,0:T(8,128)}, u32[]{:S(2)}) copy-start(f32[1,256,256]{2,1,0:T(8,128)} %diag_ref.3) | copy-start | bytes 786436
  0.6 15.1 %collective-permute-start.1 = (bf16[512,512]{1,0:T(8,128)(2,1)}, bf16[512,512]{1,0:T(8,128)(2,1)S(1)}, u32[]{:S(2)}, u32[]{:S(2)}) collective-permute-start(bf16[512,512]{1,0:T(8,128)(2,1)} %top_hbm.1), channel_id=1, source_target_pairs={{2,0},{3,1},{0,2},{1,3},{6,4},{7,5},{4,6},{5,7},{10,8},{11,9},{8,1... | collective-permute-start | bytes 1572872 | tf_op jit(solution)/shard_map/ppermute | solution.py:279
  4.5 11.3 %collective-permute-start.4 = (bf16[512,256]{1,0:T(8,128)(2,1)S(1)}, bf16[512,256]{1,0:T(8,128)(2,1)S(1)}, u32[]{:S(2)}, u32[]{:S(2)}) collective-permute-start(bf16[512,256]{1,0:T(8,128)(2,1)S(1)} %panel.1.panel_ref.refs_4_), channel_id=1, source_target_pairs={{12,0},{8,4},{4,8},{0,12},{13,1},{9,5},{5,9},{1,13},{14,2},{10,6},... | collective-permute-start | bytes 786440 | tf_op jit(solution)/shard_map/ppermute | solution.py:279
  8.2 11.8 %collective-permute-start.3 = (bf16[512,256]{1,0:T(8,128)(2,1)S(1)}, bf16[512,256]{1,0:T(8,128)(2,1)S(1)}, u32[]{:S(2)}, u32[]{:S(2)}) collective-permute-start(bf16[512,256]{1,0:T(8,128)(2,1)S(1)} %panel.1.panel_ref.refs_4_), channel_id=1, source_target_pairs={{4,0},{0,4},{12,8},{8,12},{5,1},{1,5},{13,9},{9,13},{6,2},{2,6},{1... | collective-permute-start | bytes 786440 | tf_op jit(solution)/shard_map/ppermute | solution.py:279
  9.2 10.8 %collective-permute-start = (bf16[512,512]{1,0:T(8,128)(2,1)S(1)}, bf16[512,512]{1,0:T(8,128)(2,1)S(1)}, u32[]{:S(2)}, u32[]{:S(2)}) collective-permute-start(bf16[512,512]{1,0:T(8,128)(2,1)S(1)} %get-tuple-element.8.refs_0_), channel_id=1, source_target_pairs={{1,0},{0,1},{3,2},{2,3},{5,4},{4,5},{7,6},{6,7},{9,8},{8,9},{11,10... | collective-permute-start | bytes 1572872 | tf_op jit(solution)/shard_map/ppermute | solution.py:279
  15.8 4.2 %collective-permute-start.2 = (bf16[512,512]{1,0:T(8,128)(2,1)S(1)}, bf16[512,512]{1,0:T(8,128)(2,1)S(1)}, u32[]{:S(2)}, u32[]{:S(2)}) collective-permute-start(bf16[512,512]{1,0:T(8,128)(2,1)S(1)} %relay.4.refs_1_.refs_2_), channel_id=1, source_target_pairs={{1,0},{0,1},{3,2},{2,3},{5,4},{4,5},{7,6},{6,7},{9,8},{8,9},{11,10... | collective-permute-start | bytes 1572872 | tf_op jit(solution)/shard_map/ppermute | solution.py:279
  15.8 9.8 %collective-permute-start.5 = (bf16[512,256]{1,0:T(8,128)(2,1)S(1)}, bf16[512,256]{1,0:T(8,128)(2,1)S(1)}, u32[]{:S(2)}, u32[]{:S(2)}) collective-permute-start(bf16[512,256]{1,0:T(8,128)(2,1)S(1)} %relay.5.refs_1_.refs_6_), channel_id=1, source_target_pairs={{4,0},{0,4},{12,8},{8,12},{5,1},{1,5},{13,9},{9,13},{6,2},{2,6},{1... | collective-permute-start | bytes 786440 | tf_op jit(solution)/shard_map/ppermute | solution.py:279
  20.9 7.6 %collective-permute-start.6 = (bf16[64,640]{1,0:T(8,128)(2,1)S(1)}, bf16[64,640]{1,0:T(8,128)(2,1)S(1)}, u32[]{:S(2)}, u32[]{:S(2)}) collective-permute-start(bf16[64,640]{1,0:T(8,128)(2,1)S(1)} %get-tuple-element.11.refs_1_), channel_id=1, source_target_pairs={{12,0},{8,4},{4,8},{0,12},{13,1},{9,5},{5,9},{1,13},{14,2},{10,6},... | collective-permute-start | bytes 245768 | tf_op jit(solution)/shard_map/ppermute | solution.py:279
  28.6 4.5 %collective-permute-start.7 = (bf16[64,640]{1,0:T(8,128)(2,1)S(1)}, bf16[64,640]{1,0:T(8,128)(2,1)S(1)}, u32[]{:S(2)}, u32[]{:S(2)}) collective-permute-start(bf16[64,640]{1,0:T(8,128)(2,1)S(1)} %add_convert_fusion.refs_0_), channel_id=1, source_target_pairs={{4,0},{0,4},{12,8},{8,12},{5,1},{1,5},{13,9},{9,13},{6,2},{2,6},{1... | collective-permute-start | bytes 245768 | tf_op jit(solution)/shard_map/ppermute | solution.py:279

commit v23 on v22

--- a/solution.py
+++ b/solution.py
@@ -114,7 +114,7 @@
 
 def partial_kernel(n, *refs):
     tops, panels = refs[:n], refs[n:n + n // 2 + 1]
-    turned_ref, partial_ref, update_ref, panel_buf = refs[n + n // 2 + 1:]
+    turned_ref, partial_ref, update_ref, copy_ref, panel_buf = refs[n + n // 2 + 1:]
 
     def run(pairs):
         total = dot(*[ref[...] for ref in pairs[0]])
@@ -122,6 +122,7 @@
             total += dot(top[...], panel[...])
         partial_ref[...] = total
         store_upper(update_ref, dot(turned_ref[...], total.astype(jnp.bfloat16)))
+        copy_ref[...] = update_ref[...]
 
     if n == 2 * PAIR:
         place = place_of(n, 0, 0)
@@ -140,14 +141,16 @@
 def partial_product(tops, panels, turned):
     n = len(tops)
     rows, width = panels[0].shape
+    share = jax.ShapeDtypeStruct((width // 4, 5 * (width // 2)), jnp.bfloat16)
     return pl.pallas_call(
         functools.partial(partial_kernel, n),
         out_shape=(
             jax.ShapeDtypeStruct((rows, width), jnp.float32),
-            jax.ShapeDtypeStruct((width // 4, 5 * (width // 2)), jnp.bfloat16),
+            share,
+            share,
         ),
         in_specs=[VMEM] * (n + len(panels) + 1),
-        out_specs=(VMEM, VMEM),
+        out_specs=(VMEM, VMEM, VMEM),
         scratch_shapes=[pltpu.VMEM((n, rows, width), jnp.bfloat16)],
         compiler_params=PARAMS,
         cost_estimate=pl.CostEstimate(
@@ -278,6 +281,15 @@
         ]
         return lax.ppermute(block, axis, moves)
 
+    def across(block, shift, side):
+        moves = [
+            ((((m + shift) % pairs * PAIR + (b ^ 1)) * n + col), (m * PAIR + b) * n + col)
+            for m in range(pairs)
+            for b in range(PAIR)
+            for col in range(side, n, PAIR)
+        ]
+        return lax.ppermute(block, ("prow", "pcol"), moves)
+
     def mate(block, axis):
         return from_pair(block, axis, 0, 1)
 
@@ -295,9 +307,11 @@
     for block in near:
         tops += [block, mate(block, "pcol")]
 
-    partial, early = partial_product(tops, [factor_panel, beside] + crossed, turned)
+    partial, early, again = partial_product(tops, [factor_panel, beside] + crossed, turned)
     chosen = choose(tops)
-    crossing = [after(from_pair(early, "prow", d, 1), swapped[-1]) for d in range(1, pairs)]
+    again = after(again, swapped[-1], cost=HOP_COST)
+    crossing = [after(across(early, d, 0), again, cost=0) for d in range(1, pairs)]
+    crossing += [after(across(again, d, 1), crossing[0], cost=0) for d in range(1, pairs)]
     selected, late = products(partial, chosen, turned, swapped, [early])
     parts = [late] + crossing
     if pairs > 2:

time: 34.1 us -> 35.4 us (1.038)
  the two profiles are of different devices: /device:TPU:0 before, /device:TPU:1 now
where the time goes in v23:
time: 35.4 us; the launch traced here: 35.2 us
  starting transfers between devices  15.8 us (45%)
  waiting for transfers between devices  13.4 us (38%)
  Pallas kernels  4.44 us (13%)
  other arithmetic  0.86 us (2%)
  between operations  0.74 us (2%)
    ppermute x7, waiting for transfers between devices, from_pair(): return lax.ppermute(block, axis, moves)  12.1 us
    ppermute x7, starting transfers between devices, from_pair(): return lax.ppermute(block, axis, moves)  10.1 us
    ppermute x2, starting transfers between devices, across(): return lax.ppermute(block, ('prow', 'pcol'), moves)  5.63 us
    ppermute x2, waiting for transfers between devices, across(): return lax.ppermute(block, ('prow', 'pcol'), moves)  1.21 us
    pallas_call x1, Pallas kernels, stage(): pl.pallas_call(stage_kernel, out_shape=(pltpu.VMEM(panel.shape[::-1], pan...  1.07 us
    pallas_call x1, Pallas kernels, partial_product(): pl.pallas_call(functools.partial(partial_kernel, n), out_shape=(jax.Shape...  0.95 us
    pallas_call x1, Pallas kernels, finish(): pl.pallas_call(finish_kernel, out_shape=jax.ShapeDtypeStruct(diag_inverse...  0.84 us
    neg x1, other arithmetic, on_device(): return (-selected, finish(diag_inverse, [update, mate(update, 'prow')]))  0.83 us
  transfers between devices with their start and end apart: 9, of which 5 were waited for; matrix products, arithmetic and copies ran while one was open for 2% of the time, Pallas kernels for 10%

profile of v23, /device:TPU:1, one launch (start us, length us, event | category | flops | bytes accessed | tf_op | source)
XLA Modules:
  0.0 35.2 jit_solution(11943544237064423905)
XLA Ops:
  0.6 0.0 copy-start.1
  0.6 0.0 copy-start
  0.6 2.1 %collective-permute-start.1 = (bf16[512,512]{1,0:T(8,128)(2,1)}, bf16[512,512]{1,0:T(8,128)(2,1)S(1)}, u32[]{:S(2)}, u32[]{:S(2)}) collective-permute-start(bf16[512,512]{1,0:T(8,128)(2,1)} %top_hbm.1), channel_id=1, source_target_pairs={{2,0},{3,1},{0,2},{1,3},{6,4},{7,5},{4,6},{5,7},{10,8},{11,9},{8,1... | collective-permute-start | bytes 1572872 | tf_op jit(solution)/shard_map/ppermute | solution.py:282
  2.8 0.0 copy-done.1
  2.8 0.0 copy-done
  2.8 0.8 %panel.1.panel_ref.refs_4_ = bf16[512,256]{1,0:T(8,128)(2,1)S(1)} custom-call(s32[2]{0:T(128)} %bitcast.1, f32[512,256]{1,0:T(8,128)S(1)} %copy-done.1, f32[1,256,256]{2,1,0:T(8,128)S(1)} %copy-done, f32[8,128]{1,0:T(8,128)S(1)} %token_.1.token_ref), custom_call_target="tpu_custom_call" | custom-call | tf_op jit(solution)/shard_map/panel/pallas_call | solution.py:60
  3.6 3.4 %collective-permute-start.4 = (bf16[512,256]{1,0:T(8,128)(2,1)S(1)}, bf16[512,256]{1,0:T(8,128)(2,1)S(1)}, u32[]{:S(2)}, u32[]{:S(2)}) collective-permute-start(bf16[512,256]{1,0:T(8,128)(2,1)S(1)} %panel.1.panel_ref.refs_4_), channel_id=1, source_target_pairs={{12,0},{8,4},{4,8},{0,12},{13,1},{9,5},{5,9},{1,13},{14,2},{10,6},... | collective-permute-start | bytes 786440 | tf_op jit(solution)/shard_map/ppermute | solution.py:282
  7.0 0.0 collective-permute-start.3
  7.0 1.1 %stage.1 = (bf16[256,512]{1,0:T(8,128)(2,1)S(1)}, bf16[512,512]{1,0:T(8,128)(2,1)S(1)}) custom-call(bf16[512,256]{1,0:T(8,128)(2,1)S(1)} %panel.1.panel_ref.refs_4_, bf16[512,512]{1,0:T(8,128)(2,1)} %top_hbm.1), custom_call_target="tpu_custom_call" | custom-call | tf_op jit(solution)/shard_map/stage/pallas_call | solution.py:171
  8.0 1.3 %collective-permute-start = (bf16[512,512]{1,0:T(8,128)(2,1)S(1)}, bf16[512,512]{1,0:T(8,128)(2,1)S(1)}, u32[]{:S(2)}, u32[]{:S(2)}) collective-permute-start(bf16[512,512]{1,0:T(8,128)(2,1)S(1)} %get-tuple-element.9.refs_0_), channel_id=1, source_target_pairs={{1,0},{0,1},{3,2},{2,3},{5,4},{4,5},{7,6},{6,7},{9,8},{8,9},{11,10... | collective-permute-start | bytes 1572872 | tf_op jit(solution)/shard_map/ppermute | solution.py:282
  9.3 5.3 %collective-permute-done.1.refs_0_ = bf16[512,512]{1,0:T(8,128)(2,1)S(1)} collective-permute-done((bf16[512,512]{1,0:T(8,128)(2,1)}, bf16[512,512]{1,0:T(8,128)(2,1)S(1)}, u32[]{:S(2)}, u32[]{:S(2)}) %collective-permute-start.1) | collective-permute-done | bytes 524320 | tf_op jit(solution)/shard_map/ppermute | solution.py:282
  14.6 1.2 %collective-permute-start.2 = (bf16[512,512]{1,0:T(8,128)(2,1)S(1)}, bf16[512,512]{1,0:T(8,128)(2,1)S(1)}, u32[]{:S(2)}, u32[]{:S(2)}) collective-permute-start(bf16[512,512]{1,0:T(8,128)(2,1)S(1)} %relay.6.refs_1_.refs_2_), channel_id=1, source_target_pairs={{1,0},{0,1},{3,2},{2,3},{5,4},{4,5},{7,6},{6,7},{9,8},{8,9},{11,10... | collective-permute-start | bytes 1572872 | tf_op jit(solution)/shard_map/ppermute | solution.py:282
  15.8 0.0 collective-permute-done.4.refs_0_
  15.9 2.0 %collective-permute-start.5 = (bf16[512,256]{1,0:T(8,128)(2,1)S(1)}, bf16[512,256]{1,0:T(8,128)(2,1)S(1)}, u32[]{:S(2)}, u32[]{:S(2)}) collective-permute-start(bf16[512,256]{1,0:T(8,128)(2,1)S(1)} %relay.7.refs_1_.refs_6_), channel_id=1, source_target_pairs={{4,0},{0,4},{12,8},{8,12},{5,1},{1,5},{13,9},{9,13},{6,2},{2,6},{1... | collective-permute-start | bytes 786440 | tf_op jit(solution)/shard_map/ppermute | solution.py:282
  17.9 1.6 %collective-permute-done.3.refs_0_ = bf16[512,256]{1,0:T(8,128)(2,1)S(1)} collective-permute-done((bf16[512,256]{1,0:T(8,128)(2,1)S(1)}, bf16[512,256]{1,0:T(8,128)(2,1)S(1)}, u32[]{:S(2)}, u32[]{:S(2)}) %collective-permute-start.3) | collective-permute-done | bytes 262176 | tf_op jit(solution)/shard_map/ppermute | solution.py:282
  19.5 0.0 collective-permute-done.refs_1_
  19.5 0.0 collective-permute-done.2.refs_3_
  19.5 0.9 %partial.1 = (f32[512,256]{1,0:T(8,128)S(1)}, bf16[64,640]{1,0:T(8,128)(2,1)S(1)}, bf16[64,640]{1,0:T(8,128)(2,1)S(1)}) custom-call(bf16[512,512]{1,0:T(8,128)(2,1)S(1)} %get-tuple-element.9.refs_0_, bf16[512,512]{1,0:T(8,128)(2,1)S(1)} %collective-permute-done.refs_1_, bf16[512,512]{1,0:T(8,128)(2,1)S(1)} %relay.6.refs_1_.refs_2_, ...), custom_call_target="tpu_custom_call" | custom-call | flops 536870912 | bytes 3145728 | tf_op jit(solution)/shard_map/partial/pallas_call | solution.py:145
  20.4 0.7 %collective-permute-start.6 = (bf16[64,640]{1,0:T(8,128)(2,1)S(1)}, bf16[64,640]{1,0:T(8,128)(2,1)S(1)}, u32[]{:S(2)}, u32[]{:S(2)}) collective-permute-start(bf16[64,640]{1,0:T(8,128)(2,1)S(1)} %get-tuple-element.12.refs_1_), channel_id=1, source_target_pairs={{12,0},{14,2},{8,4},{10,6},{4,8},{6,10},{0,12},{2,14},{28,16},{30,... | collective-permute-start | bytes 245768 | tf_op jit(solution)/shard_map/ppermute | solution.py:291
  21.1 2.9 %collective-permute-done.5.refs_0_.refs_1_ = bf16[512,256]{1,0:T(8,128)(2,1)S(1)} collective-permute-done((bf16[512,256]{1,0:T(8,128)(2,1)S(1)}, bf16[512,256]{1,0:T(8,128)(2,1)S(1)}, u32[]{:S(2)}, u32[]{:S(2)}) %collective-permute-start.5) | collective-permute-done | bytes 262176 | tf_op jit(solution)/shard_map/ppermute | solution.py:282
  23.9 5.0 %collective-permute-start.7 = (bf16[64,640]{1,0:T(8,128)(2,1)S(1)}, bf16[64,640]{1,0:T(8,128)(2,1)S(1)}, u32[]{:S(2)}, u32[]{:S(2)}) collective-permute-start(bf16[64,640]{1,0:T(8,128)(2,1)S(1)} %relay.9.refs_1_), channel_id=1, source_target_pairs={{13,1},{15,3},{9,5},{11,7},{5,9},{7,11},{1,13},{3,15},{29,17},{31,... | collective-permute-start | bytes 245768 | tf_op jit(solution)/shard_map/ppermute | solution.py:291
  28.9 0.1 choose.1.chosen_ref
  29.0 0.7 %products.1 = (f32[512,256]{1,0:T(8,128)S(1)}, f32[64,640]{1,0:T(8,128)S(1)}) custom-call(f32[512,256]{1,0:T(8,128)S(1)} %get-tuple-element.11.partial_ref, bf16[1,512,512]{2,1,0:T(8,128)(2,1)S(1)} %choose.1.chosen_ref, bf16[256,512]{1,0:T(8,128)(2,1)S(1)} %get-tuple-element.10.refs_1_.refs_7_.turned_ref, ...), custom_call_target="tpu_custom_call" | custom-call | tf_op jit(solution)/shard_map/products/pallas_call | solution.py:219
  29.7 0.0 collective-permute-done.6.refs_0_
  29.7 1.2 %collective-permute-done.7.refs_0_ = bf16[64,640]{1,0:T(8,128)(2,1)S(1)} collective-permute-done((bf16[64,640]{1,0:T(8,128)(2,1)S(1)}, bf16[64,640]{1,0:T(8,128)(2,1)S(1)}, u32[]{:S(2)}, u32[]{:S(2)}) %collective-permute-start.7) | collective-permute-done | bytes 81952 | tf_op jit(solution)/shard_map/ppermute | solution.py:291
  31.0 0.1 collective-permute-start.8
  31.0 0.8 %neg.3 = f32[512,256]{1,0:T(8,128)} negate(f32[512,256]{1,0:T(8,128)S(1)} %get-tuple-element.13) | non-fusion elementwise | flops 131072 | bytes 1048576 | tf_op jit(solution)/shard_map/neg | solution.py:321
  31.9 2.4 %collective-permute-done.8.refs_1_ = bf16[64,640]{1,0:T(8,128)(2,1)S(1)} collective-permute-done((bf16[64,640]{1,0:T(8,128)(2,1)S(1)}, bf16[64,640]{1,0:T(8,128)(2,1)S(1)}, u32[]{:S(2)}, u32[]{:S(2)}) %collective-permute-start.8) | collective-permute-done | bytes 81952 | tf_op jit(solution)/shard_map/ppermute | solution.py:282
  34.3 0.8 %finish.1 = f32[1,256,256]{2,1,0:T(8,128)} custom-call(f32[1,256,256]{2,1,0:T(8,128)S(1)} %copy-done, bf16[64,640]{1,0:T(8,128)(2,1)S(1)} %add_convert_fusion.refs_0_, bf16[64,640]{1,0:T(8,128)(2,1)S(1)} %collective-permute-done.8.refs_1_), custom_call_target="tpu_custom_call" | custom-call | tf_op jit(solution)/shard_map/finish/pallas_call | solution.py:264
  (8 shorter events, 0.0 us)
Async XLA Ops:
  0.6 2.1 %copy-start.1 = (f32[512,256]{1,0:T(8,128)S(1)}, f32[512,256]{1,0:T(8,128)}, u32[]{:S(2)}) copy-start(f32[512,256]{1,0:T(8,128)} %cross_ref.1) | copy-start | bytes 1572868
  0.6 2.1 %copy-start = (f32[1,256,256]{2,1,0:T(8,128)S(1)}, f32[1,256,256]{2,1,0:T(8,128)}, u32[]{:S(2)}) copy-start(f32[1,256,256]{2,1,0:T(8,128)} %diag_ref.3) | copy-start | bytes 786436
  0.6 14.0 %collective-permute-start.1 = (bf16[512,512]{1,0:T(8,128)(2,1)}, bf16[512,512]{1,0:T(8,128)(2,1)S(1)}, u32[]{:S(2)}, u32[]{:S(2)}) collective-permute-start(bf16[512,512]{1,0:T(8,128)(2,1)} %top_hbm.1), channel_id=1, source_target_pairs={{2,0},{3,1},{0,2},{1,3},{6,4},{7,5},{4,6},{5,7},{10,8},{11,9},{8,1... | collective-permute-start | bytes 1572872 | tf_op jit(solution)/shard_map/ppermute | solution.py:282
  3.6 12.3 %collective-permute-start.4 = (bf16[512,256]{1,0:T(8,128)(2,1)S(1)}, bf16[512,256]{1,0:T(8,128)(2,1)S(1)}, u32[]{:S(2)}, u32[]{:S(2)}) collective-permute-start(bf16[512,256]{1,0:T(8,128)(2,1)S(1)} %panel.1.panel_ref.refs_4_), channel_id=1, source_target_pairs={{12,0},{8,4},{4,8},{0,12},{13,1},{9,5},{5,9},{1,13},{14,2},{10,6},... | collective-permute-start | bytes 786440 | tf_op jit(solution)/shard_map/ppermute | solution.py:282
  7.0 12.5 %collective-permute-start.3 = (bf16[512,256]{1,0:T(8,128)(2,1)S(1)}, bf16[512,256]{1,0:T(8,128)(2,1)S(1)}, u32[]{:S(2)}, u32[]{:S(2)}) collective-permute-start(bf16[512,256]{1,0:T(8,128)(2,1)S(1)} %panel.1.panel_ref.refs_4_), channel_id=1, source_target_pairs={{4,0},{0,4},{12,8},{8,12},{5,1},{1,5},{13,9},{9,13},{6,2},{2,6},{1... | collective-permute-start | bytes 786440 | tf_op jit(solution)/shard_map/ppermute | solution.py:282
  8.0 11.4 %collective-permute-start = (bf16[512,512]{1,0:T(8,128)(2,1)S(1)}, bf16[512,512]{1,0:T(8,128)(2,1)S(1)}, u32[]{:S(2)}, u32[]{:S(2)}) collective-permute-start(bf16[512,512]{1,0:T(8,128)(2,1)S(1)} %get-tuple-element.9.refs_0_), channel_id=1, source_target_pairs={{1,0},{0,1},{3,2},{2,3},{5,4},{4,5},{7,6},{6,7},{9,8},{8,9},{11,10... | collective-permute-start | bytes 1572872 | tf_op jit(solution)/shard_map/ppermute | solution.py:282
  14.6 4.8 %collective-permute-start.2 = (bf16[512,512]{1,0:T(8,128)(2,1)S(1)}, bf16[512,512]{1,0:T(8,128)(2,1)S(1)}, u32[]{:S(2)}, u32[]{:S(2)}) collective-permute-start(bf16[512,512]{1,0:T(8,128)(2,1)S(1)} %relay.6.refs_1_.refs_2_), channel_id=1, source_target_pairs={{1,0},{0,1},{3,2},{2,3},{5,4},{4,5},{7,6},{6,7},{9,8},{8,9},{11,10... | collective-permute-start | bytes 1572872 | tf_op jit(solution)/shard_map/ppermute | solution.py:282
  15.9 8.1 %collective-permute-start.5 = (bf16[512,256]{1,0:T(8,128)(2,1)S(1)}, bf16[512,256]{1,0:T(8,128)(2,1)S(1)}, u32[]{:S(2)}, u32[]{:S(2)}) collective-permute-start(bf16[512,256]{1,0:T(8,128)(2,1)S(1)} %relay.7.refs_1_.refs_6_), channel_id=1, source_target_pairs={{4,0},{0,4},{12,8},{8,12},{5,1},{1,5},{13,9},{9,13},{6,2},{2,6},{1... | collective-permute-start | bytes 786440 | tf_op jit(solution)/shard_map/ppermute | solution.py:282
  20.4 9.3 %collective-permute-start.6 = (bf16[64,640]{1,0:T(8,128)(2,1)S(1)}, bf16[64,640]{1,0:T(8,128)(2,1)S(1)}, u32[]{:S(2)}, u32[]{:S(2)}) collective-permute-start(bf16[64,640]{1,0:T(8,128)(2,1)S(1)} %get-tuple-element.12.refs_1_), channel_id=1, source_target_pairs={{12,0},{14,2},{8,4},{10,6},{4,8},{6,10},{0,12},{2,14},{28,16},{30,... | collective-permute-start | bytes 245768 | tf_op jit(solution)/shard_map/ppermute | solution.py:291
  23.9 7.0 %collective-permute-start.7 = (bf16[64,640]{1,0:T(8,128)(2,1)S(1)}, bf16[64,640]{1,0:T(8,128)(2,1)S(1)}, u32[]{:S(2)}, u32[]{:S(2)}) collective-permute-start(bf16[64,640]{1,0:T(8,128)(2,1)S(1)} %relay.9.refs_1_), channel_id=1, source_target_pairs={{13,1},{15,3},{9,5},{11,7},{5,9},{7,11},{1,13},{3,15},{29,17},{31,... | collective-permute-start | bytes 245768 | tf_op jit(solution)/shard_map/ppermute | solution.py:291
  31.0 3.4 %collective-permute-start.8 = (bf16[64,640]{1,0:T(8,128)(2,1)S(1)}, bf16[64,640]{1,0:T(8,128)(2,1)S(1)}, u32[]{:S(2)}, u32[]{:S(2)}) collective-permute-start(bf16[64,640]{1,0:T(8,128)(2,1)S(1)} %add_convert_fusion.refs_0_), channel_id=1, source_target_pairs={{4,0},{0,4},{12,8},{8,12},{5,1},{1,5},{13,9},{9,13},{6,2},{2,6},{1... | collective-permute-start | bytes 245768 | tf_op jit(solution)/shard_map/ppermute | solution.py:282

commit v24 on v22

--- a/solution.py
+++ b/solution.py
@@ -287,8 +287,7 @@
     crossed = [from_pair(factor_panel, "prow", d, 1) for d in range(1, pairs)]
     turned, inverse_top = stage(factor_panel, inverse_top)
     near = [after(block, turned) for block in near]
-    crossed = [after(block, near[0], cost=HOP_COST) for block in crossed]
-    beside = after(beside, *crossed, cost=2 * HOP_COST)
+    crossed = [after(block, near[0], beside, cost=HOP_COST) for block in crossed]
     swapped = [mate(block, "prow") for block in crossed]
 
     tops = [inverse_top, mate(inverse_top, "pcol")]

time: 34.1 us -> 34.2 us (level)
  starting transfers between devices: 12.8 us -> 10.6 us
  waiting for transfers between devices: 15.2 us -> 17.4 us
    ppermute x8, waiting for transfers between devices: 15.2 us -> 17.4 us  [from_pair(): return lax.ppermute(block, axis, moves)]
    ppermute x8, starting transfers between devices: 12.8 us -> 10.6 us  [from_pair(): return lax.ppermute(block, axis, moves)]
where the time goes in v24:
time: 34.2 us; the launch traced here: 34 us
  waiting for transfers between devices  17.4 us (51%)
  starting transfers between devices  10.6 us (31%)
  Pallas kernels  4.36 us (13%)
  other arithmetic  0.85 us (2%)
  between operations  0.71 us (2%)
    ppermute x8, waiting for transfers between devices, from_pair(): return lax.ppermute(block, axis, moves)  17.4 us
    ppermute x8, starting transfers between devices, from_pair(): return lax.ppermute(block, axis, moves)  10.6 us
    pallas_call x1, Pallas kernels, stage(): pl.pallas_call(stage_kernel, out_shape=(pltpu.VMEM(panel.shape[::-1], pan...  1.07 us
    pallas_call x1, Pallas kernels, partial_product(): pl.pallas_call(functools.partial(partial_kernel, n), out_shape=(jax.Shape...  0.91 us
    pallas_call x1, Pallas kernels, finish(): pl.pallas_call(finish_kernel, out_shape=jax.ShapeDtypeStruct(diag_inverse...  0.84 us
    neg x1, other arithmetic, on_device(): return (-selected, finish(diag_inverse, [update, mate(update, 'prow')]))  0.83 us
    pallas_call x1, Pallas kernels, build_panel(): pl.pallas_call(panel_kernel, out_shape=pltpu.VMEM(cross_blocks.shape, jnp...  0.82 us
    pallas_call x1, Pallas kernels, products(): pl.pallas_call(functools.partial(product_kernel, len(panels), alone), out...  0.69 us
  transfers between devices with their start and end apart: 8, of which 5 were waited for; matrix products, arithmetic and copies ran while one was open for 2% of the time, Pallas kernels for 10%

profile of v24, /device:TPU:0, one launch (start us, length us, event | category | flops | bytes accessed | tf_op | source)
XLA Modules:
  0.0 34.0 jit_solution(16594077734701116884)
XLA Ops:
  0.6 0.0 copy-start.1
  0.6 0.0 copy-start
  0.6 3.0 %collective-permute-start.1 = (bf16[512,512]{1,0:T(8,128)(2,1)}, bf16[512,512]{1,0:T(8,128)(2,1)S(1)}, u32[]{:S(2)}, u32[]{:S(2)}) collective-permute-start(bf16[512,512]{1,0:T(8,128)(2,1)} %top_hbm.1), channel_id=1, source_target_pairs={{2,0},{3,1},{0,2},{1,3},{6,4},{7,5},{4,6},{5,7},{10,8},{11,9},{8,1... | collective-permute-start | bytes 1572872 | tf_op jit(solution)/shard_map/ppermute | solution.py:279
  3.7 0.0 copy-done.1
  3.7 0.0 copy-done
  3.7 0.8 %panel.1.panel_ref.refs_4_ = bf16[512,256]{1,0:T(8,128)(2,1)S(1)} custom-call(s32[2]{0:T(128)} %bitcast.1, f32[512,256]{1,0:T(8,128)S(1)} %copy-done.1, f32[1,256,256]{2,1,0:T(8,128)S(1)} %copy-done, f32[8,128]{1,0:T(8,128)S(1)} %token_.1.token_ref), custom_call_target="tpu_custom_call" | custom-call | tf_op jit(solution)/shard_map/panel/pallas_call | solution.py:60
  4.5 1.6 %collective-permute-start.3 = (bf16[512,256]{1,0:T(8,128)(2,1)S(1)}, bf16[512,256]{1,0:T(8,128)(2,1)S(1)}, u32[]{:S(2)}, u32[]{:S(2)}) collective-permute-start(bf16[512,256]{1,0:T(8,128)(2,1)S(1)} %panel.1.panel_ref.refs_4_), channel_id=1, source_target_pairs={{4,0},{0,4},{12,8},{8,12},{5,1},{1,5},{13,9},{9,13},{6,2},{2,6},{1... | collective-permute-start | bytes 786440 | tf_op jit(solution)/shard_map/ppermute | solution.py:279
  6.1 2.5 %collective-permute-start.4 = (bf16[512,256]{1,0:T(8,128)(2,1)S(1)}, bf16[512,256]{1,0:T(8,128)(2,1)S(1)}, u32[]{:S(2)}, u32[]{:S(2)}) collective-permute-start(bf16[512,256]{1,0:T(8,128)(2,1)S(1)} %panel.1.panel_ref.refs_4_), channel_id=1, source_target_pairs={{12,0},{8,4},{4,8},{0,12},{13,1},{9,5},{5,9},{1,13},{14,2},{10,6},... | collective-permute-start | bytes 786440 | tf_op jit(solution)/shard_map/ppermute | solution.py:279
  8.6 1.1 %stage.1 = (bf16[256,512]{1,0:T(8,128)(2,1)S(1)}, bf16[512,512]{1,0:T(8,128)(2,1)S(1)}) custom-call(bf16[512,256]{1,0:T(8,128)(2,1)S(1)} %panel.1.panel_ref.refs_4_, bf16[512,512]{1,0:T(8,128)(2,1)} %top_hbm.1), custom_call_target="tpu_custom_call" | custom-call | tf_op jit(solution)/shard_map/stage/pallas_call | solution.py:168
  9.7 0.1 collective-permute-start
  9.8 6.0 %collective-permute-done.1.refs_0_ = bf16[512,512]{1,0:T(8,128)(2,1)S(1)} collective-permute-done((bf16[512,512]{1,0:T(8,128)(2,1)}, bf16[512,512]{1,0:T(8,128)(2,1)S(1)}, u32[]{:S(2)}, u32[]{:S(2)}) %collective-permute-start.1) | collective-permute-done | bytes 524320 | tf_op jit(solution)/shard_map/ppermute | solution.py:279
  15.8 0.0 collective-permute-start.2
  15.8 0.0 collective-permute-done.3.refs_2_.refs_5_
  15.8 4.3 %collective-permute-done.4.refs_0_ = bf16[512,256]{1,0:T(8,128)(2,1)S(1)} collective-permute-done((bf16[512,256]{1,0:T(8,128)(2,1)S(1)}, bf16[512,256]{1,0:T(8,128)(2,1)S(1)}, u32[]{:S(2)}, u32[]{:S(2)}) %collective-permute-start.4) | collective-permute-done | bytes 262176 | tf_op jit(solution)/shard_map/ppermute | solution.py:279
  20.1 0.6 %collective-permute-start.5 = (bf16[512,256]{1,0:T(8,128)(2,1)S(1)}, bf16[512,256]{1,0:T(8,128)(2,1)S(1)}, u32[]{:S(2)}, u32[]{:S(2)}) collective-permute-start(bf16[512,256]{1,0:T(8,128)(2,1)S(1)} %relay.4.refs_6_), channel_id=1, source_target_pairs={{4,0},{0,4},{12,8},{8,12},{5,1},{1,5},{13,9},{9,13},{6,2},{2,6},{1... | collective-permute-start | bytes 786440 | tf_op jit(solution)/shard_map/ppermute | solution.py:279
  20.6 0.0 collective-permute-done.refs_1_
  20.6 0.0 collective-permute-done.2.refs_3_
  20.6 0.9 %partial.1 = (f32[512,256]{1,0:T(8,128)S(1)}, bf16[64,640]{1,0:T(8,128)(2,1)S(1)}) custom-call(bf16[512,512]{1,0:T(8,128)(2,1)S(1)} %get-tuple-element.8.refs_0_, bf16[512,512]{1,0:T(8,128)(2,1)S(1)} %collective-permute-done.refs_1_, bf16[512,512]{1,0:T(8,128)(2,1)S(1)} %relay.3.refs_1_.refs_2_, bf16[512,512]{1,0:T(8,128)(2,1)S(1)} %collective-permute-done.2.refs_3_, ...), custom_call_target="tpu_custom_call" | custom-call | flops 536870912 | bytes 3145728 | tf_op jit(solution)/shard_map/partial/pallas_call | solution.py:143
  21.6 2.7 %collective-permute-start.6 = (bf16[64,640]{1,0:T(8,128)(2,1)S(1)}, bf16[64,640]{1,0:T(8,128)(2,1)S(1)}, u32[]{:S(2)}, u32[]{:S(2)}) collective-permute-start(bf16[64,640]{1,0:T(8,128)(2,1)S(1)} %get-tuple-element.11.refs_1_), channel_id=1, source_target_pairs={{12,0},{8,4},{4,8},{0,12},{13,1},{9,5},{5,9},{1,13},{14,2},{10,6},... | collective-permute-start | bytes 245768 | tf_op jit(solution)/shard_map/ppermute | solution.py:279
  24.3 3.4 %collective-permute-done.5.refs_0_.refs_1_ = bf16[512,256]{1,0:T(8,128)(2,1)S(1)} collective-permute-done((bf16[512,256]{1,0:T(8,128)(2,1)S(1)}, bf16[512,256]{1,0:T(8,128)(2,1)S(1)}, u32[]{:S(2)}, u32[]{:S(2)}) %collective-permute-start.5) | collective-permute-done | bytes 262176 | tf_op jit(solution)/shard_map/ppermute | solution.py:279
  27.7 0.7 %products.1 = (f32[512,256]{1,0:T(8,128)S(1)}, f32[64,640]{1,0:T(8,128)S(1)}) custom-call(f32[512,256]{1,0:T(8,128)S(1)} %get-tuple-element.10.partial_ref, bf16[1,512,512]{2,1,0:T(8,128)(2,1)S(1)} %choose.1.chosen_ref, bf16[256,512]{1,0:T(8,128)(2,1)S(1)} %get-tuple-element.9.refs_1_.refs_7_.turned_ref, ...), custom_call_target="tpu_custom_call" | custom-call | tf_op jit(solution)/shard_map/products/pallas_call | solution.py:216
  28.4 0.2 collective-permute-done.6.refs_0_
  28.6 0.2 collective-permute-start.7
  28.8 0.8 %neg.3 = f32[512,256]{1,0:T(8,128)} negate(f32[512,256]{1,0:T(8,128)S(1)} %get-tuple-element.12) | non-fusion elementwise | flops 131072 | bytes 1048576 | tf_op jit(solution)/shard_map/neg | solution.py:306
  29.6 3.5 %collective-permute-done.7.refs_1_ = bf16[64,640]{1,0:T(8,128)(2,1)S(1)} collective-permute-done((bf16[64,640]{1,0:T(8,128)(2,1)S(1)}, bf16[64,640]{1,0:T(8,128)(2,1)S(1)}, u32[]{:S(2)}, u32[]{:S(2)}) %collective-permute-start.7) | collective-permute-done | bytes 81952 | tf_op jit(solution)/shard_map/ppermute | solution.py:279
  33.1 0.8 %finish.1 = f32[1,256,256]{2,1,0:T(8,128)} custom-call(f32[1,256,256]{2,1,0:T(8,128)S(1)} %copy-done, bf16[64,640]{1,0:T(8,128)(2,1)S(1)} %add_convert_fusion.refs_0_, bf16[64,640]{1,0:T(8,128)(2,1)S(1)} %collective-permute-done.7.refs_1_), custom_call_target="tpu_custom_call" | custom-call | tf_op jit(solution)/shard_map/finish/pallas_call | solution.py:261
  (6 shorter events, 0.1 us)
Async XLA Ops:
  0.6 3.0 %copy-start.1 = (f32[512,256]{1,0:T(8,128)S(1)}, f32[512,256]{1,0:T(8,128)}, u32[]{:S(2)}) copy-start(f32[512,256]{1,0:T(8,128)} %cross_ref.1) | copy-start | bytes 1572868
  0.6 3.0 %copy-start = (f32[1,256,256]{2,1,0:T(8,128)S(1)}, f32[1,256,256]{2,1,0:T(8,128)}, u32[]{:S(2)}) copy-start(f32[1,256,256]{2,1,0:T(8,128)} %diag_ref.3) | copy-start | bytes 786436
  0.6 15.1 %collective-permute-start.1 = (bf16[512,512]{1,0:T(8,128)(2,1)}, bf16[512,512]{1,0:T(8,128)(2,1)S(1)}, u32[]{:S(2)}, u32[]{:S(2)}) collective-permute-start(bf16[512,512]{1,0:T(8,128)(2,1)} %top_hbm.1), channel_id=1, source_target_pairs={{2,0},{3,1},{0,2},{1,3},{6,4},{7,5},{4,6},{5,7},{10,8},{11,9},{8,1... | collective-permute-start | bytes 1572872 | tf_op jit(solution)/shard_map/ppermute | solution.py:279
  4.5 11.3 %collective-permute-start.3 = (bf16[512,256]{1,0:T(8,128)(2,1)S(1)}, bf16[512,256]{1,0:T(8,128)(2,1)S(1)}, u32[]{:S(2)}, u32[]{:S(2)}) collective-permute-start(bf16[512,256]{1,0:T(8,128)(2,1)S(1)} %panel.1.panel_ref.refs_4_), channel_id=1, source_target_pairs={{4,0},{0,4},{12,8},{8,12},{5,1},{1,5},{13,9},{9,13},{6,2},{2,6},{1... | collective-permute-start | bytes 786440 | tf_op jit(solution)/shard_map/ppermute | solution.py:279
  6.1 13.9 %collective-permute-start.4 = (bf16[512,256]{1,0:T(8,128)(2,1)S(1)}, bf16[512,256]{1,0:T(8,128)(2,1)S(1)}, u32[]{:S(2)}, u32[]{:S(2)}) collective-permute-start(bf16[512,256]{1,0:T(8,128)(2,1)S(1)} %panel.1.panel_ref.refs_4_), channel_id=1, source_target_pairs={{12,0},{8,4},{4,8},{0,12},{13,1},{9,5},{5,9},{1,13},{14,2},{10,6},... | collective-permute-start | bytes 786440 | tf_op jit(solution)/shard_map/ppermute | solution.py:279
  9.7 11.0 %collective-permute-start = (bf16[512,512]{1,0:T(8,128)(2,1)S(1)}, bf16[512,512]{1,0:T(8,128)(2,1)S(1)}, u32[]{:S(2)}, u32[]{:S(2)}) collective-permute-start(bf16[512,512]{1,0:T(8,128)(2,1)S(1)} %get-tuple-element.8.refs_0_), channel_id=1, source_target_pairs={{1,0},{0,1},{3,2},{2,3},{5,4},{4,5},{7,6},{6,7},{9,8},{8,9},{11,10... | collective-permute-start | bytes 1572872 | tf_op jit(solution)/shard_map/ppermute | solution.py:279
  15.8 4.9 %collective-permute-start.2 = (bf16[512,512]{1,0:T(8,128)(2,1)S(1)}, bf16[512,512]{1,0:T(8,128)(2,1)S(1)}, u32[]{:S(2)}, u32[]{:S(2)}) collective-permute-start(bf16[512,512]{1,0:T(8,128)(2,1)S(1)} %relay.3.refs_1_.refs_2_), channel_id=1, source_target_pairs={{1,0},{0,1},{3,2},{2,3},{5,4},{4,5},{7,6},{6,7},{9,8},{8,9},{11,10... | collective-permute-start | bytes 1572872 | tf_op jit(solution)/shard_map/ppermute | solution.py:279
  20.1 7.7 %collective-permute-start.5 = (bf16[512,256]{1,0:T(8,128)(2,1)S(1)}, bf16[512,256]{1,0:T(8,128)(2,1)S(1)}, u32[]{:S(2)}, u32[]{:S(2)}) collective-permute-start(bf16[512,256]{1,0:T(8,128)(2,1)S(1)} %relay.4.refs_6_), channel_id=1, source_target_pairs={{4,0},{0,4},{12,8},{8,12},{5,1},{1,5},{13,9},{9,13},{6,2},{2,6},{1... | collective-permute-start | bytes 786440 | tf_op jit(solution)/shard_map/ppermute | solution.py:279
  21.6 7.1 %collective-permute-start.6 = (bf16[64,640]{1,0:T(8,128)(2,1)S(1)}, bf16[64,640]{1,0:T(8,128)(2,1)S(1)}, u32[]{:S(2)}, u32[]{:S(2)}) collective-permute-start(bf16[64,640]{1,0:T(8,128)(2,1)S(1)} %get-tuple-element.11.refs_1_), channel_id=1, source_target_pairs={{12,0},{8,4},{4,8},{0,12},{13,1},{9,5},{5,9},{1,13},{14,2},{10,6},... | collective-permute-start | bytes 245768 | tf_op jit(solution)/shard_map/ppermute | solution.py:279
  28.6 4.5 %collective-permute-start.7 = (bf16[64,640]{1,0:T(8,128)(2,1)S(1)}, bf16[64,640]{1,0:T(8,128)(2,1)S(1)}, u32[]{:S(2)}, u32[]{:S(2)}) collective-permute-start(bf16[64,640]{1,0:T(8,128)(2,1)S(1)} %add_convert_fusion.refs_0_), channel_id=1, source_target_pairs={{4,0},{0,4},{12,8},{8,12},{5,1},{1,5},{13,9},{9,13},{6,2},{2,6},{1... | collective-permute-start | bytes 245768 | tf_op jit(solution)/shard_map/ppermute | solution.py:279

commit v25 on v24

--- a/solution.py
+++ b/solution.py
@@ -40,7 +40,41 @@
     )()
 
 
-def panel_kernel(pattern_hbm, cross_ref, diag_ref, token_ref, panel_ref, pattern_ref, sem):
+def stage_work(panel_ref, top_hbm, turned_ref, top_ref, sem):
+    copy = pltpu.make_async_copy(top_hbm, top_ref, sem)
+    copy.start()
+    turned_ref[...] = panel_ref[...].astype(jnp.float32).T.astype(jnp.bfloat16)
+    copy.wait()
+
+
+def on_side(side):
+    return pl.when(lax.axis_index("pcol") % PAIR == side)
+
+
+def stage_kernel(panel_ref, top_hbm, turned_in, top_in, turned_ref, top_ref, sem):
+    del turned_in, top_in
+
+    @on_side(0)
+    def _():
+        stage_work(panel_ref, top_hbm, turned_ref, top_ref, sem)
+
+
+def stage(panel, inverse_top, turned, top):
+    return pl.pallas_call(
+        stage_kernel,
+        out_shape=(pltpu.VMEM(turned.shape, turned.dtype), pltpu.VMEM(top.shape, top.dtype)),
+        in_specs=[VMEM, HBM, VMEM, VMEM],
+        out_specs=(VMEM, VMEM),
+        input_output_aliases={2: 0, 3: 1},
+        scratch_shapes=[pltpu.SemaphoreType.DMA],
+        compiler_params=PARAMS,
+        name="stage",
+    )(panel, pltpu.with_memory_space_constraint(inverse_top, pltpu.HBM), turned, top)
+
+
+def panel_kernel(
+    pattern_hbm, cross_ref, diag_ref, top_hbm, token_ref, panel_ref, turned_ref, top_ref, pattern_ref, sem, top_sem
+):
     del token_ref
     width = diag_ref.shape[1]
     pattern_copy = pltpu.make_async_copy(pattern_hbm, pattern_ref, sem)
@@ -55,20 +89,34 @@
         kept = jnp.where(pattern_ref[a] != 0, block, 0.0)
         panel_ref[pl.ds(a * width, width), :] = kept.astype(jnp.bfloat16)
 
-
-def build_panel(cross_blocks, diag_inverse, pattern):
+    @on_side(1)
+    def _():
+        stage_work(panel_ref, top_hbm, turned_ref, top_ref, top_sem)
+
+
+def build_panel(cross_blocks, diag_inverse, pattern, inverse_top):
+    shape = cross_blocks.shape
     return pl.pallas_call(
         panel_kernel,
-        out_shape=pltpu.VMEM(cross_blocks.shape, jnp.bfloat16),
-        in_specs=[HBM, VMEM, VMEM, ANY],
-        out_specs=VMEM,
-        scratch_shapes=[pltpu.SMEM((pattern.size,), jnp.int32), pltpu.SemaphoreType.DMA],
+        out_shape=(
+            pltpu.VMEM(shape, jnp.bfloat16),
+            pltpu.VMEM(shape[::-1], jnp.bfloat16),
+            pltpu.VMEM(inverse_top.shape, inverse_top.dtype),
+        ),
+        in_specs=[HBM, VMEM, VMEM, HBM, ANY],
+        out_specs=(VMEM, VMEM, VMEM),
+        scratch_shapes=[
+            pltpu.SMEM((pattern.size,), jnp.int32),
+            pltpu.SemaphoreType.DMA,
+            pltpu.SemaphoreType.DMA,
+        ],
         compiler_params=PARAMS,
         name="panel",
     )(
         pltpu.with_memory_space_constraint(pattern.reshape(-1), pltpu.HBM),
         cross_blocks,
         diag_inverse,
+        pltpu.with_memory_space_constraint(inverse_top, pltpu.HBM),
         token(),
     )
 
@@ -155,25 +203,6 @@
         ),
         name="partial",
     )(*tops, *panels, turned)
-
-
-def stage_kernel(panel_ref, top_hbm, turned_ref, top_ref, sem):
-    copy = pltpu.make_async_copy(top_hbm, top_ref, sem)
-    copy.start()
-    turned_ref[...] = panel_ref[...].astype(jnp.float32).T.astype(jnp.bfloat16)
-    copy.wait()
-
-
-def stage(panel, inverse_top):
-    return pl.pallas_call(
-        stage_kernel,
-        out_shape=(pltpu.VMEM(panel.shape[::-1], panel.dtype), pltpu.VMEM(inverse_top.shape, inverse_top.dtype)),
-        in_specs=[VMEM, HBM],
-        out_specs=(VMEM, VMEM),
-        scratch_shapes=[pltpu.SemaphoreType.DMA],
-        compiler_params=PARAMS,
-        name="stage",
-    )(panel, pltpu.with_memory_space_constraint(inverse_top, pltpu.HBM))
 
 
 def choose_kernel(n, *refs):
@@ -282,10 +311,10 @@
         return from_pair(block, axis, 0, 1)
 
     near = [from_pair(inverse_top, "pcol", d, 0) for d in range(1, pairs)]
-    factor_panel = build_panel(cross_blocks, diag_inverse, pattern)
+    factor_panel, turned, top = build_panel(cross_blocks, diag_inverse, pattern, inverse_top)
     beside = mate(factor_panel, "prow")
     crossed = [from_pair(factor_panel, "prow", d, 1) for d in range(1, pairs)]
-    turned, inverse_top = stage(factor_panel, inverse_top)
+    turned, inverse_top = stage(factor_panel, inverse_top, turned, top)
     near = [after(block, turned) for block in near]
     crossed = [after(block, near[0], beside, cost=HOP_COST) for block in crossed]
     swapped = [mate(block, "prow") for block in crossed]

time: 34.2 us -> 37.4 us (1.094)
  waiting for transfers between devices: 17.4 us -> 20.7 us
    ppermute x8, waiting for transfers between devices: 17.4 us -> 20.7 us  [from_pair(): return lax.ppermute(block, axis, moves)]
  transfers between devices with their start and end apart: 8 -> 8, of which waited for: 5 -> 5; matrix products, arithmetic and copies ran while one was open for 2% -> 2% of each run, Pallas kernels for 10% -> 9%
where the time goes in v25:
time: 37.4 us; the launch traced here: 37.2 us
  waiting for transfers between devices  20.7 us (55%)
  starting transfers between devices  10.5 us (28%)
  Pallas kernels  4.36 us (12%)
  other arithmetic  0.85 us (2%)
  between operations  0.71 us (2%)
    ppermute x8, waiting for transfers between devices, from_pair(): return lax.ppermute(block, axis, moves)  20.7 us
    ppermute x8, starting transfers between devices, from_pair(): return lax.ppermute(block, axis, moves)  10.5 us
    pallas_call x1, Pallas kernels, stage(): pl.pallas_call(stage_kernel, out_shape=(pltpu.VMEM(turned.shape, turned.d...  1.07 us
    pallas_call x1, Pallas kernels, partial_product(): pl.pallas_call(functools.partial(partial_kernel, n), out_shape=(jax.Shape...  0.91 us
    pallas_call x1, Pallas kernels, finish(): pl.pallas_call(finish_kernel, out_shape=jax.ShapeDtypeStruct(diag_inverse...  0.84 us
    neg x1, other arithmetic, on_device(): return (-selected, finish(diag_inverse, [update, mate(update, 'prow')]))  0.83 us
    pallas_call x1, Pallas kernels, build_panel(): pl.pallas_call(panel_kernel, out_shape=(pltpu.VMEM(shape, jnp.bfloat16),...  0.82 us
  transfers between devices with their start and end apart: 8, of which 5 were waited for; matrix products, arithmetic and copies ran while one was open for 2% of the time, Pallas kernels for 9%

profile of v25, /device:TPU:0, one launch (start us, length us, event | category | flops | bytes accessed | tf_op | source)
XLA Modules:
  0.0 37.2 jit_solution(6723584283411796458)
XLA Ops:
  0.6 0.0 copy-start.1
  0.6 0.0 copy-start
  0.6 3.0 %collective-permute-start.1 = (bf16[512,512]{1,0:T(8,128)(2,1)}, bf16[512,512]{1,0:T(8,128)(2,1)S(1)}, u32[]{:S(2)}, u32[]{:S(2)}) collective-permute-start(bf16[512,512]{1,0:T(8,128)(2,1)} %top_hbm.3), channel_id=1, source_target_pairs={{2,0},{3,1},{0,2},{1,3},{6,4},{7,5},{4,6},{5,7},{10,8},{11,9},{8,1... | collective-permute-start | bytes 1572872 | tf_op jit(solution)/shard_map/ppermute | solution.py:308
  3.7 0.0 copy-done.1
  3.7 0.0 copy-done
  3.7 0.8 %panel.1 = (bf16[512,256]{1,0:T(8,128)(2,1)S(1)}, bf16[256,512]{1,0:T(8,128)(2,1)S(1)}, bf16[512,512]{1,0:T(8,128)(2,1)S(1)}) custom-call(s32[2]{0:T(128)} %bitcast.1, f32[512,256]{1,0:T(8,128)S(1)} %copy-done.1, f32[1,256,256]{2,1,0:T(8,128)S(1)} %copy-done, bf16[512,512]{1,0:T(8,128)(2,1)} %top_hbm.3, f32[8,128]{1,0:T(8,128)S(1)} %token_.1.token_ref), custom_call_target="tpu_custom_call" | custom-call | tf_op jit(solution)/shard_map/panel/pallas_call | solution.py:99
  4.5 1.6 %collective-permute-start.3 = (bf16[512,256]{1,0:T(8,128)(2,1)S(1)}, bf16[512,256]{1,0:T(8,128)(2,1)S(1)}, u32[]{:S(2)}, u32[]{:S(2)}) collective-permute-start(bf16[512,256]{1,0:T(8,128)(2,1)S(1)} %get-tuple-element.11.panel_ref.refs_4_), channel_id=1, source_target_pairs={{4,0},{0,4},{12,8},{8,12},{5,1},{1,5},{13,9},{9,13},{6,2},{2,6},{1... | collective-permute-start | bytes 786440 | tf_op jit(solution)/shard_map/ppermute | solution.py:308
  6.1 2.5 %collective-permute-start.4 = (bf16[512,256]{1,0:T(8,128)(2,1)S(1)}, bf16[512,256]{1,0:T(8,128)(2,1)S(1)}, u32[]{:S(2)}, u32[]{:S(2)}) collective-permute-start(bf16[512,256]{1,0:T(8,128)(2,1)S(1)} %get-tuple-element.11.panel_ref.refs_4_), channel_id=1, source_target_pairs={{12,0},{8,4},{4,8},{0,12},{13,1},{9,5},{5,9},{1,13},{14,2},{10,6},... | collective-permute-start | bytes 786440 | tf_op jit(solution)/shard_map/ppermute | solution.py:308
  8.6 1.1 %stage.1 = (bf16[256,512]{1,0:T(8,128)(2,1)S(1)}, bf16[512,512]{1,0:T(8,128)(2,1)S(1)}) custom-call(bf16[512,256]{1,0:T(8,128)(2,1)S(1)} %get-tuple-element.11.panel_ref.refs_4_, bf16[512,512]{1,0:T(8,128)(2,1)} %top_hbm.3, bf16[256,512]{1,0:T(8,128)(2,1)S(1)} %get-tuple-element.12.turned_in, ...), custom_call_target="tpu_custom_call", output_to_operand_aliasing={{0}: (2, {}), {1}: (3, {})} | custom-call | tf_op jit(solution)/shard_map/stage/pallas_call | solution.py:63
  9.7 0.1 collective-permute-start
  9.8 6.0 %collective-permute-done.1.refs_0_ = bf16[512,512]{1,0:T(8,128)(2,1)S(1)} collective-permute-done((bf16[512,512]{1,0:T(8,128)(2,1)}, bf16[512,512]{1,0:T(8,128)(2,1)S(1)}, u32[]{:S(2)}, u32[]{:S(2)}) %collective-permute-start.1) | collective-permute-done | bytes 524320 | tf_op jit(solution)/shard_map/ppermute | solution.py:308
  15.8 0.0 collective-permute-start.2
  15.8 0.0 collective-permute-done.3.refs_2_.refs_5_
  15.8 5.3 %collective-permute-done.4.refs_0_ = bf16[512,256]{1,0:T(8,128)(2,1)S(1)} collective-permute-done((bf16[512,256]{1,0:T(8,128)(2,1)S(1)}, bf16[512,256]{1,0:T(8,128)(2,1)S(1)}, u32[]{:S(2)}, u32[]{:S(2)}) %collective-permute-start.4) | collective-permute-done | bytes 262176 | tf_op jit(solution)/shard_map/ppermute | solution.py:308
  21.1 0.6 %collective-permute-start.5 = (bf16[512,256]{1,0:T(8,128)(2,1)S(1)}, bf16[512,256]{1,0:T(8,128)(2,1)S(1)}, u32[]{:S(2)}, u32[]{:S(2)}) collective-permute-start(bf16[512,256]{1,0:T(8,128)(2,1)S(1)} %relay.4.refs_6_), channel_id=1, source_target_pairs={{4,0},{0,4},{12,8},{8,12},{5,1},{1,5},{13,9},{9,13},{6,2},{2,6},{1... | collective-permute-start | bytes 786440 | tf_op jit(solution)/shard_map/ppermute | solution.py:308
  21.7 0.0 collective-permute-done.refs_1_
  21.7 0.0 collective-permute-done.2.refs_3_
  21.7 0.9 %partial.1 = (f32[512,256]{1,0:T(8,128)S(1)}, bf16[64,640]{1,0:T(8,128)(2,1)S(1)}) custom-call(bf16[512,512]{1,0:T(8,128)(2,1)S(1)} %get-tuple-element.14.refs_0_, bf16[512,512]{1,0:T(8,128)(2,1)S(1)} %collective-permute-done.refs_1_, bf16[512,512]{1,0:T(8,128)(2,1)S(1)} %relay.3.refs_1_.refs_2_, bf16[512,512]{1,0:T(8,128)(2,1)S(1)} %collective-permute-done.2.refs_3_, ...), custom_call_target="tpu_custom_call" | custom-call | flops 536870912 | bytes 3145728 | tf_op jit(solution)/shard_map/partial/pallas_call | solution.py:191
  22.6 2.7 %collective-permute-start.6 = (bf16[64,640]{1,0:T(8,128)(2,1)S(1)}, bf16[64,640]{1,0:T(8,128)(2,1)S(1)}, u32[]{:S(2)}, u32[]{:S(2)}) collective-permute-start(bf16[64,640]{1,0:T(8,128)(2,1)S(1)} %get-tuple-element.17.refs_1_), channel_id=1, source_target_pairs={{12,0},{8,4},{4,8},{0,12},{13,1},{9,5},{5,9},{1,13},{14,2},{10,6},... | collective-permute-start | bytes 245768 | tf_op jit(solution)/shard_map/ppermute | solution.py:308
  25.4 4.3 %collective-permute-done.5.refs_0_.refs_1_ = bf16[512,256]{1,0:T(8,128)(2,1)S(1)} collective-permute-done((bf16[512,256]{1,0:T(8,128)(2,1)S(1)}, bf16[512,256]{1,0:T(8,128)(2,1)S(1)}, u32[]{:S(2)}, u32[]{:S(2)}) %collective-permute-start.5) | collective-permute-done | bytes 262176 | tf_op jit(solution)/shard_map/ppermute | solution.py:308
  29.7 0.7 %products.1 = (f32[512,256]{1,0:T(8,128)S(1)}, f32[64,640]{1,0:T(8,128)S(1)}) custom-call(f32[512,256]{1,0:T(8,128)S(1)} %get-tuple-element.16.partial_ref, bf16[1,512,512]{2,1,0:T(8,128)(2,1)S(1)} %choose.1.chosen_ref, bf16[256,512]{1,0:T(8,128)(2,1)S(1)} %get-tuple-element.15.refs_1_.refs_7_.turned_ref, ...), custom_call_target="tpu_custom_call" | custom-call | tf_op jit(solution)/shard_map/products/pallas_call | solution.py:245
  30.4 1.4 %collective-permute-done.6.refs_0_ = bf16[64,640]{1,0:T(8,128)(2,1)S(1)} collective-permute-done((bf16[64,640]{1,0:T(8,128)(2,1)S(1)}, bf16[64,640]{1,0:T(8,128)(2,1)S(1)}, u32[]{:S(2)}, u32[]{:S(2)}) %collective-permute-start.6) | collective-permute-done | bytes 81952 | tf_op jit(solution)/shard_map/ppermute | solution.py:308
  31.8 0.1 collective-permute-start.7
  31.9 0.8 %neg.3 = f32[512,256]{1,0:T(8,128)} negate(f32[512,256]{1,0:T(8,128)S(1)} %get-tuple-element.18) | non-fusion elementwise | flops 131072 | bytes 1048576 | tf_op jit(solution)/shard_map/neg | solution.py:335
  32.7 3.6 %collective-permute-done.7.refs_1_ = bf16[64,640]{1,0:T(8,128)(2,1)S(1)} collective-permute-done((bf16[64,640]{1,0:T(8,128)(2,1)S(1)}, bf16[64,640]{1,0:T(8,128)(2,1)S(1)}, u32[]{:S(2)}, u32[]{:S(2)}) %collective-permute-start.7) | collective-permute-done | bytes 81952 | tf_op jit(solution)/shard_map/ppermute | solution.py:308
  36.3 0.8 %finish.1 = f32[1,256,256]{2,1,0:T(8,128)} custom-call(f32[1,256,256]{2,1,0:T(8,128)S(1)} %copy-done, bf16[64,640]{1,0:T(8,128)(2,1)S(1)} %add_convert_fusion.refs_0_, bf16[64,640]{1,0:T(8,128)(2,1)S(1)} %collective-permute-done.7.refs_1_), custom_call_target="tpu_custom_call" | custom-call | tf_op jit(solution)/shard_map/finish/pallas_call | solution.py:290
  (6 shorter events, 0.1 us)
Async XLA Ops:
  0.6 3.0 %copy-start.1 = (f32[512,256]{1,0:T(8,128)S(1)}, f32[512,256]{1,0:T(8,128)}, u32[]{:S(2)}) copy-start(f32[512,256]{1,0:T(8,128)} %cross_ref.1) | copy-start | bytes 1572868
  0.6 3.0 %copy-start = (f32[1,256,256]{2,1,0:T(8,128)S(1)}, f32[1,256,256]{2,1,0:T(8,128)}, u32[]{:S(2)}) copy-start(f32[1,256,256]{2,1,0:T(8,128)} %diag_ref.3) | copy-start | bytes 786436
  0.6 15.1 %collective-permute-start.1 = (bf16[512,512]{1,0:T(8,128)(2,1)}, bf16[512,512]{1,0:T(8,128)(2,1)S(1)}, u32[]{:S(2)}, u32[]{:S(2)}) collective-permute-start(bf16[512,512]{1,0:T(8,128)(2,1)} %top_hbm.3), channel_id=1, source_target_pairs={{2,0},{3,1},{0,2},{1,3},{6,4},{7,5},{4,6},{5,7},{10,8},{11,9},{8,1... | collective-permute-start | bytes 1572872 | tf_op jit(solution)/shard_map/ppermute | solution.py:308
  4.5 11.3 %collective-permute-start.3 = (bf16[512,256]{1,0:T(8,128)(2,1)S(1)}, bf16[512,256]{1,0:T(8,128)(2,1)S(1)}, u32[]{:S(2)}, u32[]{:S(2)}) collective-permute-start(bf16[512,256]{1,0:T(8,128)(2,1)S(1)} %get-tuple-element.11.panel_ref.refs_4_), channel_id=1, source_target_pairs={{4,0},{0,4},{12,8},{8,12},{5,1},{1,5},{13,9},{9,13},{6,2},{2,6},{1... | collective-permute-start | bytes 786440 | tf_op jit(solution)/shard_map/ppermute | solution.py:308
  6.1 15.0 %collective-permute-start.4 = (bf16[512,256]{1,0:T(8,128)(2,1)S(1)}, bf16[512,256]{1,0:T(8,128)(2,1)S(1)}, u32[]{:S(2)}, u32[]{:S(2)}) collective-permute-start(bf16[512,256]{1,0:T(8,128)(2,1)S(1)} %get-tuple-element.11.panel_ref.refs_4_), channel_id=1, source_target_pairs={{12,0},{8,4},{4,8},{0,12},{13,1},{9,5},{5,9},{1,13},{14,2},{10,6},... | collective-permute-start | bytes 786440 | tf_op jit(solution)/shard_map/ppermute | solution.py:308
  9.7 12.0 %collective-permute-start = (bf16[512,512]{1,0:T(8,128)(2,1)S(1)}, bf16[512,512]{1,0:T(8,128)(2,1)S(1)}, u32[]{:S(2)}, u32[]{:S(2)}) collective-permute-start(bf16[512,512]{1,0:T(8,128)(2,1)S(1)} %get-tuple-element.14.refs_0_), channel_id=1, source_target_pairs={{1,0},{0,1},{3,2},{2,3},{5,4},{4,5},{7,6},{6,7},{9,8},{8,9},{11,10... | collective-permute-start | bytes 1572872 | tf_op jit(solution)/shard_map/ppermute | solution.py:308
  15.8 5.9 %collective-permute-start.2 = (bf16[512,512]{1,0:T(8,128)(2,1)S(1)}, bf16[512,512]{1,0:T(8,128)(2,1)S(1)}, u32[]{:S(2)}, u32[]{:S(2)}) collective-permute-start(bf16[512,512]{1,0:T(8,128)(2,1)S(1)} %relay.3.refs_1_.refs_2_), channel_id=1, source_target_pairs={{1,0},{0,1},{3,2},{2,3},{5,4},{4,5},{7,6},{6,7},{9,8},{8,9},{11,10... | collective-permute-start | bytes 1572872 | tf_op jit(solution)/shard_map/ppermute | solution.py:308
  21.1 8.6 %collective-permute-start.5 = (bf16[512,256]{1,0:T(8,128)(2,1)S(1)}, bf16[512,256]{1,0:T(8,128)(2,1)S(1)}, u32[]{:S(2)}, u32[]{:S(2)}) collective-permute-start(bf16[512,256]{1,0:T(8,128)(2,1)S(1)} %relay.4.refs_6_), channel_id=1, source_target_pairs={{4,0},{0,4},{12,8},{8,12},{5,1},{1,5},{13,9},{9,13},{6,2},{2,6},{1... | collective-permute-start | bytes 786440 | tf_op jit(solution)/shard_map/ppermute | solution.py:308
  22.6 9.2 %collective-permute-start.6 = (bf16[64,640]{1,0:T(8,128)(2,1)S(1)}, bf16[64,640]{1,0:T(8,128)(2,1)S(1)}, u32[]{:S(2)}, u32[]{:S(2)}) collective-permute-start(bf16[64,640]{1,0:T(8,128)(2,1)S(1)} %get-tuple-element.17.refs_1_), channel_id=1, source_target_pairs={{12,0},{8,4},{4,8},{0,12},{13,1},{9,5},{5,9},{1,13},{14,2},{10,6},... | collective-permute-start | bytes 245768 | tf_op jit(solution)/shard_map/ppermute | solution.py:308
  31.8 4.5 %collective-permute-start.7 = (bf16[64,640]{1,0:T(8,128)(2,1)S(1)}, bf16[64,640]{1,0:T(8,128)(2,1)S(1)}, u32[]{:S(2)}, u32[]{:S(2)}) collective-permute-start(bf16[64,640]{1,0:T(8,128)(2,1)S(1)} %add_convert_fusion.refs_0_), channel_id=1, source_target_pairs={{4,0},{0,4},{12,8},{8,12},{5,1},{1,5},{13,9},{9,13},{6,2},{2,6},{1... | collective-permute-start | bytes 245768 | tf_op jit(solution)/shard_map/ppermute | solution.py:308

commit v26 on v24

--- a/solution.py
+++ b/solution.py
@@ -198,19 +198,19 @@
     )(*tops)
 
 
-def product_kernel(count, alone, partial_ref, chosen_ref, turned_ref, *refs):
-    panels, early, (selected_ref, update_ref) = refs[:count], refs[count:-2], refs[-2:]
+def product_kernel(count, alone, chosen_ref, turned_ref, *refs):
+    panels, early, (rest_ref, update_ref) = refs[:count], refs[count:-2], refs[-2:]
     rest = dot(chosen_ref[0], panels[0][...])
     for d, panel in enumerate(panels[1:], 1):
         rest += dot(chosen_ref[d], panel[...])
-    selected_ref[...] = partial_ref[...] + rest
+    rest_ref[...] = rest
     update = dot(turned_ref[...], rest.astype(jnp.bfloat16))
     if alone:
         update += update.T
     store_upper(update_ref, update, *early)
 
 
-def products(partial, chosen, turned, panels, early):
+def products(chosen, turned, panels, early):
     rows, width = panels[0].shape
     alone = len(panels) == 1
     return pl.pallas_call(
@@ -219,11 +219,11 @@
             jax.ShapeDtypeStruct((rows, width), jnp.float32),
             jax.ShapeDtypeStruct((width // 4, 5 * (width // 2)), jnp.float32),
         ),
-        in_specs=[VMEM] * (3 + len(panels) + len(early)),
+        in_specs=[VMEM] * (2 + len(panels) + len(early)),
         out_specs=(VMEM, VMEM),
         compiler_params=PARAMS,
         name="products",
-    )(partial, chosen, turned, *panels, *early)
+    )(chosen, turned, *panels, *early)
 
 
 def finish_kernel(diag_ref, *refs):
@@ -296,14 +296,14 @@
 
     partial, early = partial_product(tops, [factor_panel, beside] + crossed, turned)
     chosen = choose(tops)
-    crossing = [after(from_pair(early, "prow", d, 1), swapped[-1]) for d in range(1, pairs)]
-    selected, late = products(partial, chosen, turned, swapped, [early])
+    crossing = [after(from_pair(early, "prow", d, 0), swapped[-1]) for d in range(1, pairs)]
+    rest, late = products(chosen, turned, swapped, [early])
     parts = [late] + crossing
     if pairs > 2:
-        rest = (late - early.astype(jnp.float32)).astype(jnp.bfloat16)
-        parts += [from_pair(rest, "prow", d, 0) for d in range(1, pairs)]
+        share = (late - early.astype(jnp.float32)).astype(jnp.bfloat16)
+        parts += [from_pair(share, "prow", d, 0) for d in range(1, pairs)]
     update = functools.reduce(jnp.add, [part.astype(jnp.float32) for part in parts]).astype(jnp.bfloat16)
-    return -selected, finish(diag_inverse, [update, mate(update, "prow")])
+    return -(partial + rest), finish(diag_inverse, [update, mate(update, "prow")])
 
 
 def solution(mesh):

time: 34.2 us -> 34.9 us (1.020)
  waiting for transfers between devices: 17.4 us -> 19.3 us
  starting transfers between devices: 10.6 us -> 9.46 us
    ppermute x8, waiting for transfers between devices: 17.4 us -> 19.3 us  [from_pair(): return lax.ppermute(block, axis, moves)]
    ppermute x8, starting transfers between devices: 10.6 us -> 9.46 us  [from_pair(): return lax.ppermute(block, axis, moves)]
  transfers between devices with their start and end apart: 8 -> 8, of which waited for: 5 -> 4; matrix products, arithmetic and copies ran while one was open for 2% -> 2% of each run, Pallas kernels for 10% -> 10%
where the time goes in v26:
time: 34.9 us; the launch traced here: 34.7 us
  waiting for transfers between devices  19.3 us (55%)
  starting transfers between devices  9.46 us (27%)
  Pallas kernels  4.35 us (12%)
  other arithmetic  0.88 us (3%)
  between operations  0.72 us (2%)
    ppermute x8, waiting for transfers between devices, from_pair(): return lax.ppermute(block, axis, moves)  19.3 us
    ppermute x8, starting transfers between devices, from_pair(): return lax.ppermute(block, axis, moves)  9.46 us
    pallas_call x1, Pallas kernels, stage(): pl.pallas_call(stage_kernel, out_shape=(pltpu.VMEM(panel.shape[::-1], pan...  1.07 us
    pallas_call x1, Pallas kernels, partial_product(): pl.pallas_call(functools.partial(partial_kernel, n), out_shape=(jax.Shape...  0.91 us
    neg x1, other arithmetic, on_device(): -(partial + rest)  0.86 us
    pallas_call x1, Pallas kernels, finish(): pl.pallas_call(finish_kernel, out_shape=jax.ShapeDtypeStruct(diag_inverse...  0.84 us
    pallas_call x1, Pallas kernels, build_panel(): pl.pallas_call(panel_kernel, out_shape=pltpu.VMEM(cross_blocks.shape, jnp...  0.81 us
  transfers between devices with their start and end apart: 8, of which 4 were waited for; matrix products, arithmetic and copies ran while one was open for 2% of the time, Pallas kernels for 10%

profile of v26, /device:TPU:0, one launch (start us, length us, event | category | flops | bytes accessed | tf_op | source)
XLA Modules:
  0.0 34.7 jit_solution(3476702438313338459)
XLA Ops:
  0.6 0.0 copy-start.1
  0.6 0.0 copy-start
  0.6 3.0 %collective-permute-start.1 = (bf16[512,512]{1,0:T(8,128)(2,1)}, bf16[512,512]{1,0:T(8,128)(2,1)S(1)}, u32[]{:S(2)}, u32[]{:S(2)}) collective-permute-start(bf16[512,512]{1,0:T(8,128)(2,1)} %top_hbm.1), channel_id=1, source_target_pairs={{2,0},{3,1},{0,2},{1,3},{6,4},{7,5},{4,6},{5,7},{10,8},{11,9},{8,1... | collective-permute-start | bytes 1572872 | tf_op jit(solution)/shard_map/ppermute | solution.py:279
  3.7 0.0 copy-done.1
  3.7 0.0 copy-done
  3.7 0.8 %panel.1.panel_ref.refs_4_ = bf16[512,256]{1,0:T(8,128)(2,1)S(1)} custom-call(s32[2]{0:T(128)} %bitcast.1, f32[512,256]{1,0:T(8,128)S(1)} %copy-done.1, f32[1,256,256]{2,1,0:T(8,128)S(1)} %copy-done, f32[8,128]{1,0:T(8,128)S(1)} %token_.1.token_ref), custom_call_target="tpu_custom_call" | custom-call | tf_op jit(solution)/shard_map/panel/pallas_call | solution.py:60
  4.5 1.6 %collective-permute-start.3 = (bf16[512,256]{1,0:T(8,128)(2,1)S(1)}, bf16[512,256]{1,0:T(8,128)(2,1)S(1)}, u32[]{:S(2)}, u32[]{:S(2)}) collective-permute-start(bf16[512,256]{1,0:T(8,128)(2,1)S(1)} %panel.1.panel_ref.refs_4_), channel_id=1, source_target_pairs={{4,0},{0,4},{12,8},{8,12},{5,1},{1,5},{13,9},{9,13},{6,2},{2,6},{1... | collective-permute-start | bytes 786440 | tf_op jit(solution)/shard_map/ppermute | solution.py:279
  6.1 2.5 %collective-permute-start.4 = (bf16[512,256]{1,0:T(8,128)(2,1)S(1)}, bf16[512,256]{1,0:T(8,128)(2,1)S(1)}, u32[]{:S(2)}, u32[]{:S(2)}) collective-permute-start(bf16[512,256]{1,0:T(8,128)(2,1)S(1)} %panel.1.panel_ref.refs_4_), channel_id=1, source_target_pairs={{12,0},{8,4},{4,8},{0,12},{13,1},{9,5},{5,9},{1,13},{14,2},{10,6},... | collective-permute-start | bytes 786440 | tf_op jit(solution)/shard_map/ppermute | solution.py:279
  8.6 1.1 %stage.1 = (bf16[256,512]{1,0:T(8,128)(2,1)S(1)}, bf16[512,512]{1,0:T(8,128)(2,1)S(1)}) custom-call(bf16[512,256]{1,0:T(8,128)(2,1)S(1)} %panel.1.panel_ref.refs_4_, bf16[512,512]{1,0:T(8,128)(2,1)} %top_hbm.1), custom_call_target="tpu_custom_call" | custom-call | tf_op jit(solution)/shard_map/stage/pallas_call | solution.py:168
  9.7 0.1 collective-permute-start
  9.7 6.0 %collective-permute-done.1.refs_0_ = bf16[512,512]{1,0:T(8,128)(2,1)S(1)} collective-permute-done((bf16[512,512]{1,0:T(8,128)(2,1)}, bf16[512,512]{1,0:T(8,128)(2,1)S(1)}, u32[]{:S(2)}, u32[]{:S(2)}) %collective-permute-start.1) | collective-permute-done | bytes 524320 | tf_op jit(solution)/shard_map/ppermute | solution.py:279
  15.8 0.0 collective-permute-start.2
  15.8 0.0 collective-permute-done.3.refs_2_.refs_5_
  15.8 4.3 %collective-permute-done.4.refs_0_ = bf16[512,256]{1,0:T(8,128)(2,1)S(1)} collective-permute-done((bf16[512,256]{1,0:T(8,128)(2,1)S(1)}, bf16[512,256]{1,0:T(8,128)(2,1)S(1)}, u32[]{:S(2)}, u32[]{:S(2)}) %collective-permute-start.4) | collective-permute-done | bytes 262176 | tf_op jit(solution)/shard_map/ppermute | solution.py:279
  20.1 0.6 %collective-permute-start.5 = (bf16[512,256]{1,0:T(8,128)(2,1)S(1)}, bf16[512,256]{1,0:T(8,128)(2,1)S(1)}, u32[]{:S(2)}, u32[]{:S(2)}) collective-permute-start(bf16[512,256]{1,0:T(8,128)(2,1)S(1)} %relay.4.refs_6_), channel_id=1, source_target_pairs={{4,0},{0,4},{12,8},{8,12},{5,1},{1,5},{13,9},{9,13},{6,2},{2,6},{1... | collective-permute-start | bytes 786440 | tf_op jit(solution)/shard_map/ppermute | solution.py:279
  20.6 0.0 collective-permute-done.refs_1_
  20.6 0.0 collective-permute-done.2.refs_3_
  20.6 0.9 %partial.1 = (f32[512,256]{1,0:T(8,128)S(1)}, bf16[64,640]{1,0:T(8,128)(2,1)S(1)}) custom-call(bf16[512,512]{1,0:T(8,128)(2,1)S(1)} %get-tuple-element.8.refs_0_, bf16[512,512]{1,0:T(8,128)(2,1)S(1)} %collective-permute-done.refs_1_, bf16[512,512]{1,0:T(8,128)(2,1)S(1)} %relay.3.refs_1_.refs_2_, bf16[512,512]{1,0:T(8,128)(2,1)S(1)} %collective-permute-done.2.refs_3_, ...), custom_call_target="tpu_custom_call" | custom-call | flops 536870912 | bytes 3145728 | tf_op jit(solution)/shard_map/partial/pallas_call | solution.py:143
  21.6 1.5 %collective-permute-start.6 = (bf16[64,640]{1,0:T(8,128)(2,1)S(1)}, bf16[64,640]{1,0:T(8,128)(2,1)S(1)}, u32[]{:S(2)}, u32[]{:S(2)}) collective-permute-start(bf16[64,640]{1,0:T(8,128)(2,1)S(1)} %get-tuple-element.11.refs_1_), channel_id=1, source_target_pairs={{8,0},{12,4},{0,8},{4,12},{9,1},{13,5},{1,9},{5,13},{10,2},{14,6},... | collective-permute-start | bytes 245768 | tf_op jit(solution)/shard_map/ppermute | solution.py:279
  23.1 5.5 %collective-permute-done.5.refs_0_.refs_1_ = bf16[512,256]{1,0:T(8,128)(2,1)S(1)} collective-permute-done((bf16[512,256]{1,0:T(8,128)(2,1)S(1)}, bf16[512,256]{1,0:T(8,128)(2,1)S(1)}, u32[]{:S(2)}, u32[]{:S(2)}) %collective-permute-start.5) | collective-permute-done | bytes 262176 | tf_op jit(solution)/shard_map/ppermute | solution.py:279
  28.6 0.7 %products.1 = (f32[512,256]{1,0:T(8,128)S(1)}, f32[64,640]{1,0:T(8,128)S(1)}) custom-call(bf16[1,512,512]{2,1,0:T(8,128)(2,1)S(1)} %choose.1.chosen_ref, bf16[256,512]{1,0:T(8,128)(2,1)S(1)} %get-tuple-element.9.refs_1_.refs_7_.turned_ref, bf16[512,256]{1,0:T(8,128)(2,1)S(1)} %collective-permute-done.5.refs_0_.refs_1_, ...), custom_call_target="tpu_custom_call" | custom-call | tf_op jit(solution)/shard_map/products/pallas_call | solution.py:216
  29.3 0.0 collective-permute-done.6.refs_0_
  29.4 0.2 collective-permute-start.7
  29.5 0.9 %add_negate_fusion = f32[512,256]{1,0:T(8,128)} fusion(f32[512,256]{1,0:T(8,128)S(1)} %get-tuple-element.10, f32[512,256]{1,0:T(8,128)S(1)} %get-tuple-element.12), kind=kLoop, calls=%fused_computation | loop fusion | flops 262144 | bytes 1572864 | tf_op jit(solution)/shard_map/neg | solution.py:306
  30.4 3.5 %collective-permute-done.7.refs_1_ = bf16[64,640]{1,0:T(8,128)(2,1)S(1)} collective-permute-done((bf16[64,640]{1,0:T(8,128)(2,1)S(1)}, bf16[64,640]{1,0:T(8,128)(2,1)S(1)}, u32[]{:S(2)}, u32[]{:S(2)}) %collective-permute-start.7) | collective-permute-done | bytes 81952 | tf_op jit(solution)/shard_map/ppermute | solution.py:279
  33.9 0.8 %finish.1 = f32[1,256,256]{2,1,0:T(8,128)} custom-call(f32[1,256,256]{2,1,0:T(8,128)S(1)} %copy-done, bf16[64,640]{1,0:T(8,128)(2,1)S(1)} %add_convert_fusion.refs_0_, bf16[64,640]{1,0:T(8,128)(2,1)S(1)} %collective-permute-done.7.refs_1_), custom_call_target="tpu_custom_call" | custom-call | tf_op jit(solution)/shard_map/finish/pallas_call | solution.py:261
  (6 shorter events, 0.1 us)
Async XLA Ops:
  0.6 3.0 %copy-start.1 = (f32[512,256]{1,0:T(8,128)S(1)}, f32[512,256]{1,0:T(8,128)}, u32[]{:S(2)}) copy-start(f32[512,256]{1,0:T(8,128)} %cross_ref.1) | copy-start | bytes 1572868
  0.6 3.0 %copy-start = (f32[1,256,256]{2,1,0:T(8,128)S(1)}, f32[1,256,256]{2,1,0:T(8,128)}, u32[]{:S(2)}) copy-start(f32[1,256,256]{2,1,0:T(8,128)} %diag_ref.3) | copy-start | bytes 786436
  0.6 15.1 %collective-permute-start.1 = (bf16[512,512]{1,0:T(8,128)(2,1)}, bf16[512,512]{1,0:T(8,128)(2,1)S(1)}, u32[]{:S(2)}, u32[]{:S(2)}) collective-permute-start(bf16[512,512]{1,0:T(8,128)(2,1)} %top_hbm.1), channel_id=1, source_target_pairs={{2,0},{3,1},{0,2},{1,3},{6,4},{7,5},{4,6},{5,7},{10,8},{11,9},{8,1... | collective-permute-start | bytes 1572872 | tf_op jit(solution)/shard_map/ppermute | solution.py:279
  4.5 11.3 %collective-permute-start.3 = (bf16[512,256]{1,0:T(8,128)(2,1)S(1)}, bf16[512,256]{1,0:T(8,128)(2,1)S(1)}, u32[]{:S(2)}, u32[]{:S(2)}) collective-permute-start(bf16[512,256]{1,0:T(8,128)(2,1)S(1)} %panel.1.panel_ref.refs_4_), channel_id=1, source_target_pairs={{4,0},{0,4},{12,8},{8,12},{5,1},{1,5},{13,9},{9,13},{6,2},{2,6},{1... | collective-permute-start | bytes 786440 | tf_op jit(solution)/shard_map/ppermute | solution.py:279
  6.1 13.9 %collective-permute-start.4 = (bf16[512,256]{1,0:T(8,128)(2,1)S(1)}, bf16[512,256]{1,0:T(8,128)(2,1)S(1)}, u32[]{:S(2)}, u32[]{:S(2)}) collective-permute-start(bf16[512,256]{1,0:T(8,128)(2,1)S(1)} %panel.1.panel_ref.refs_4_), channel_id=1, source_target_pairs={{12,0},{8,4},{4,8},{0,12},{13,1},{9,5},{5,9},{1,13},{14,2},{10,6},... | collective-permute-start | bytes 786440 | tf_op jit(solution)/shard_map/ppermute | solution.py:279
  9.7 11.0 %collective-permute-start = (bf16[512,512]{1,0:T(8,128)(2,1)S(1)}, bf16[512,512]{1,0:T(8,128)(2,1)S(1)}, u32[]{:S(2)}, u32[]{:S(2)}) collective-permute-start(bf16[512,512]{1,0:T(8,128)(2,1)S(1)} %get-tuple-element.8.refs_0_), channel_id=1, source_target_pairs={{1,0},{0,1},{3,2},{2,3},{5,4},{4,5},{7,6},{6,7},{9,8},{8,9},{11,10... | collective-permute-start | bytes 1572872 | tf_op jit(solution)/shard_map/ppermute | solution.py:279
  15.8 4.9 %collective-permute-start.2 = (bf16[512,512]{1,0:T(8,128)(2,1)S(1)}, bf16[512,512]{1,0:T(8,128)(2,1)S(1)}, u32[]{:S(2)}, u32[]{:S(2)}) collective-permute-start(bf16[512,512]{1,0:T(8,128)(2,1)S(1)} %relay.3.refs_1_.refs_2_), channel_id=1, source_target_pairs={{1,0},{0,1},{3,2},{2,3},{5,4},{4,5},{7,6},{6,7},{9,8},{8,9},{11,10... | collective-permute-start | bytes 1572872 | tf_op jit(solution)/shard_map/ppermute | solution.py:279
  20.1 8.6 %collective-permute-start.5 = (bf16[512,256]{1,0:T(8,128)(2,1)S(1)}, bf16[512,256]{1,0:T(8,128)(2,1)S(1)}, u32[]{:S(2)}, u32[]{:S(2)}) collective-permute-start(bf16[512,256]{1,0:T(8,128)(2,1)S(1)} %relay.4.refs_6_), channel_id=1, source_target_pairs={{4,0},{0,4},{12,8},{8,12},{5,1},{1,5},{13,9},{9,13},{6,2},{2,6},{1... | collective-permute-start | bytes 786440 | tf_op jit(solution)/shard_map/ppermute | solution.py:279
  21.6 7.8 %collective-permute-start.6 = (bf16[64,640]{1,0:T(8,128)(2,1)S(1)}, bf16[64,640]{1,0:T(8,128)(2,1)S(1)}, u32[]{:S(2)}, u32[]{:S(2)}) collective-permute-start(bf16[64,640]{1,0:T(8,128)(2,1)S(1)} %get-tuple-element.11.refs_1_), channel_id=1, source_target_pairs={{8,0},{12,4},{0,8},{4,12},{9,1},{13,5},{1,9},{5,13},{10,2},{14,6},... | collective-permute-start | bytes 245768 | tf_op jit(solution)/shard_map/ppermute | solution.py:279
  29.4 4.5 %collective-permute-start.7 = (bf16[64,640]{1,0:T(8,128)(2,1)S(1)}, bf16[64,640]{1,0:T(8,128)(2,1)S(1)}, u32[]{:S(2)}, u32[]{:S(2)}) collective-permute-start(bf16[64,640]{1,0:T(8,128)(2,1)S(1)} %add_convert_fusion.refs_0_), channel_id=1, source_target_pairs={{4,0},{0,4},{12,8},{8,12},{5,1},{1,5},{13,9},{9,13},{6,2},{2,6},{1... | collective-permute-start | bytes 245768 | tf_op jit(solution)/shard_map/ppermute | solution.py:279

commit v27 on v24

--- a/solution.py
+++ b/solution.py
@@ -198,32 +198,49 @@
     )(*tops)
 
 
-def product_kernel(count, alone, partial_ref, chosen_ref, turned_ref, *refs):
-    panels, early, (selected_ref, update_ref) = refs[:count], refs[count:-2], refs[-2:]
-    rest = dot(chosen_ref[0], panels[0][...])
+def last_terms(chosen_ref, panels):
+    total = dot(chosen_ref[0], panels[0][...])
     for d, panel in enumerate(panels[1:], 1):
-        rest += dot(chosen_ref[d], panel[...])
-    selected_ref[...] = partial_ref[...] + rest
-    update = dot(turned_ref[...], rest.astype(jnp.bfloat16))
-    if alone:
+        total += dot(chosen_ref[d], panel[...])
+    return total
+
+
+def late_kernel(chosen_ref, turned_ref, early_ref, *refs):
+    panels, update_ref = refs[:-1], refs[-1]
+    update = dot(turned_ref[...], last_terms(chosen_ref, panels).astype(jnp.bfloat16))
+    if len(panels) == 1:
         update += update.T
-    store_upper(update_ref, update, *early)
-
-
-def products(partial, chosen, turned, panels, early):
-    rows, width = panels[0].shape
-    alone = len(panels) == 1
-    return pl.pallas_call(
-        functools.partial(product_kernel, len(panels), alone),
-        out_shape=(
-            jax.ShapeDtypeStruct((rows, width), jnp.float32),
-            jax.ShapeDtypeStruct((width // 4, 5 * (width // 2)), jnp.float32),
+    store_upper(update_ref, update, early_ref)
+
+
+def late_share(chosen, turned, panels, early):
+    return pl.pallas_call(
+        late_kernel,
+        out_shape=jax.ShapeDtypeStruct(early.shape, jnp.float32),
+        in_specs=[VMEM] * (3 + len(panels)),
+        out_specs=VMEM,
+        compiler_params=PARAMS,
+        name="late",
+    )(chosen, turned, early, *panels)
+
+
+def cross_kernel(partial_ref, chosen_ref, *refs):
+    refs[-1][...] = -(partial_ref[...] + last_terms(chosen_ref, refs[:-1]))
+
+
+def cross_result(partial, chosen, panels):
+    rows, width = partial.shape
+    return pl.pallas_call(
+        cross_kernel,
+        out_shape=jax.ShapeDtypeStruct(partial.shape, jnp.float32),
+        in_specs=[VMEM] * (2 + len(panels)),
+        out_specs=VMEM,
+        compiler_params=PARAMS,
+        cost_estimate=pl.CostEstimate(
+            flops=2 * len(panels) * rows * rows * width, bytes_accessed=8 * rows * width, transcendentals=0
         ),
-        in_specs=[VMEM] * (3 + len(panels) + len(early)),
-        out_specs=(VMEM, VMEM),
-        compiler_params=PARAMS,
-        name="products",
-    )(partial, chosen, turned, *panels, *early)
+        name="cross",
+    )(partial, chosen, *panels)
 
 
 def finish_kernel(diag_ref, *refs):
@@ -297,13 +314,13 @@
     partial, early = partial_product(tops, [factor_panel, beside] + crossed, turned)
     chosen = choose(tops)
     crossing = [after(from_pair(early, "prow", d, 1), swapped[-1]) for d in range(1, pairs)]
-    selected, late = products(partial, chosen, turned, swapped, [early])
+    late = late_share(chosen, turned, swapped, early)
     parts = [late] + crossing
     if pairs > 2:
         rest = (late - early.astype(jnp.float32)).astype(jnp.bfloat16)
         parts += [from_pair(rest, "prow", d, 0) for d in range(1, pairs)]
     update = functools.reduce(jnp.add, [part.astype(jnp.float32) for part in parts]).astype(jnp.bfloat16)
-    return -selected, finish(diag_inverse, [update, mate(update, "prow")])
+    return cross_result(partial, chosen, swapped), finish(diag_inverse, [update, mate(update, "prow")])
 
 
 def solution(mesh):

time: 34.2 us -> 34.2 us (level)
  Pallas kernels: 4.36 us -> 5.45 us
  other arithmetic: 0.85 us -> 0.02 us
    pallas_call x1 -> x2, Pallas kernels: 0.69 us -> 1.78 us  [the longest x1 1.09 us: cross_result(): pl.pallas_call(cross_kernel, out_shape=jax.ShapeDtypeStruct(partial.shape...]
    neg x1 -> x0, other arithmetic: 0.83 us -> none  [on_device(): return (-selected, finish(diag_inverse, [update, mate(update, 'prow')]))]
  transfers between devices with their start and end apart: 8 -> 8, of which waited for: 5 -> 5; matrix products, arithmetic and copies ran while one was open for 2% -> 0% of each run, Pallas kernels for 10% -> 14%
where the time goes in v27:
time: 34.2 us; the launch traced here: 34 us
  waiting for transfers between devices  17.2 us (50%)
  starting transfers between devices  10.6 us (31%)
  Pallas kernels  5.45 us (16%)
  between operations  0.71 us (2%)
    ppermute x8, waiting for transfers between devices, from_pair(): return lax.ppermute(block, axis, moves)  17.2 us
    ppermute x8, starting transfers between devices, from_pair(): return lax.ppermute(block, axis, moves)  10.6 us
    pallas_call x1, Pallas kernels, cross_result(): pl.pallas_call(cross_kernel, out_shape=jax.ShapeDtypeStruct(partial.shape...  1.09 us
    pallas_call x1, Pallas kernels, stage(): pl.pallas_call(stage_kernel, out_shape=(pltpu.VMEM(panel.shape[::-1], pan...  1.07 us
    pallas_call x1, Pallas kernels, partial_product(): pl.pallas_call(functools.partial(partial_kernel, n), out_shape=(jax.Shape...  0.91 us
    pallas_call x1, Pallas kernels, finish(): pl.pallas_call(finish_kernel, out_shape=jax.ShapeDtypeStruct(diag_inverse...  0.84 us
    pallas_call x1, Pallas kernels, build_panel(): pl.pallas_call(panel_kernel, out_shape=pltpu.VMEM(cross_blocks.shape, jnp...  0.82 us
    pallas_call x1, Pallas kernels, late_share(): pl.pallas_call(late_kernel, out_shape=jax.ShapeDtypeStruct(early.shape, j...  0.69 us
  transfers between devices with their start and end apart: 8, of which 5 were waited for; matrix products, arithmetic and copies ran while one was open for 0% of the time, Pallas kernels for 14%

profile of v27, /device:TPU:0, one launch (start us, length us, event | category | flops | bytes accessed | tf_op | source)
XLA Modules:
  0.0 34.0 jit_solution(13077701324714514627)
XLA Ops:
  0.6 0.0 copy-start.1
  0.6 0.0 copy-start
  0.6 3.0 %collective-permute-start.1 = (bf16[512,512]{1,0:T(8,128)(2,1)}, bf16[512,512]{1,0:T(8,128)(2,1)S(1)}, u32[]{:S(2)}, u32[]{:S(2)}) collective-permute-start(bf16[512,512]{1,0:T(8,128)(2,1)} %top_hbm.1), channel_id=1, source_target_pairs={{2,0},{3,1},{0,2},{1,3},{6,4},{7,5},{4,6},{5,7},{10,8},{11,9},{8,1... | collective-permute-start | bytes 1572872 | tf_op jit(solution)/shard_map/ppermute | solution.py:296
  3.7 0.0 copy-done.1
  3.7 0.0 copy-done
  3.7 0.8 %panel.1.panel_ref.refs_4_ = bf16[512,256]{1,0:T(8,128)(2,1)S(1)} custom-call(s32[2]{0:T(128)} %bitcast.1, f32[512,256]{1,0:T(8,128)S(1)} %copy-done.1, f32[1,256,256]{2,1,0:T(8,128)S(1)} %copy-done, f32[8,128]{1,0:T(8,128)S(1)} %token_.1.token_ref), custom_call_target="tpu_custom_call" | custom-call | tf_op jit(solution)/shard_map/panel/pallas_call | solution.py:60
  4.5 1.6 %collective-permute-start.3 = (bf16[512,256]{1,0:T(8,128)(2,1)S(1)}, bf16[512,256]{1,0:T(8,128)(2,1)S(1)}, u32[]{:S(2)}, u32[]{:S(2)}) collective-permute-start(bf16[512,256]{1,0:T(8,128)(2,1)S(1)} %panel.1.panel_ref.refs_4_), channel_id=1, source_target_pairs={{4,0},{0,4},{12,8},{8,12},{5,1},{1,5},{13,9},{9,13},{6,2},{2,6},{1... | collective-permute-start | bytes 786440 | tf_op jit(solution)/shard_map/ppermute | solution.py:296
  6.1 2.5 %collective-permute-start.4 = (bf16[512,256]{1,0:T(8,128)(2,1)S(1)}, bf16[512,256]{1,0:T(8,128)(2,1)S(1)}, u32[]{:S(2)}, u32[]{:S(2)}) collective-permute-start(bf16[512,256]{1,0:T(8,128)(2,1)S(1)} %panel.1.panel_ref.refs_4_), channel_id=1, source_target_pairs={{12,0},{8,4},{4,8},{0,12},{13,1},{9,5},{5,9},{1,13},{14,2},{10,6},... | collective-permute-start | bytes 786440 | tf_op jit(solution)/shard_map/ppermute | solution.py:296
  8.6 1.1 %stage.1 = (bf16[256,512]{1,0:T(8,128)(2,1)S(1)}, bf16[512,512]{1,0:T(8,128)(2,1)S(1)}) custom-call(bf16[512,256]{1,0:T(8,128)(2,1)S(1)} %panel.1.panel_ref.refs_4_, bf16[512,512]{1,0:T(8,128)(2,1)} %top_hbm.1), custom_call_target="tpu_custom_call" | custom-call | tf_op jit(solution)/shard_map/stage/pallas_call | solution.py:168
  9.7 0.1 collective-permute-start
  9.8 6.0 %collective-permute-done.1.refs_0_ = bf16[512,512]{1,0:T(8,128)(2,1)S(1)} collective-permute-done((bf16[512,512]{1,0:T(8,128)(2,1)}, bf16[512,512]{1,0:T(8,128)(2,1)S(1)}, u32[]{:S(2)}, u32[]{:S(2)}) %collective-permute-start.1) | collective-permute-done | bytes 524320 | tf_op jit(solution)/shard_map/ppermute | solution.py:296
  15.8 0.0 collective-permute-start.2
  15.8 0.0 collective-permute-done.3.refs_2_.refs_5_
  15.8 4.3 %collective-permute-done.4.refs_0_ = bf16[512,256]{1,0:T(8,128)(2,1)S(1)} collective-permute-done((bf16[512,256]{1,0:T(8,128)(2,1)S(1)}, bf16[512,256]{1,0:T(8,128)(2,1)S(1)}, u32[]{:S(2)}, u32[]{:S(2)}) %collective-permute-start.4) | collective-permute-done | bytes 262176 | tf_op jit(solution)/shard_map/ppermute | solution.py:296
  20.1 0.6 %collective-permute-start.5 = (bf16[512,256]{1,0:T(8,128)(2,1)S(1)}, bf16[512,256]{1,0:T(8,128)(2,1)S(1)}, u32[]{:S(2)}, u32[]{:S(2)}) collective-permute-start(bf16[512,256]{1,0:T(8,128)(2,1)S(1)} %relay.4.refs_6_), channel_id=1, source_target_pairs={{4,0},{0,4},{12,8},{8,12},{5,1},{1,5},{13,9},{9,13},{6,2},{2,6},{1... | collective-permute-start | bytes 786440 | tf_op jit(solution)/shard_map/ppermute | solution.py:296
  20.6 0.0 collective-permute-done.refs_1_
  20.6 0.0 collective-permute-done.2.refs_3_
  20.6 0.9 %partial.1 = (f32[512,256]{1,0:T(8,128)S(1)}, bf16[64,640]{1,0:T(8,128)(2,1)S(1)}) custom-call(bf16[512,512]{1,0:T(8,128)(2,1)S(1)} %get-tuple-element.6.refs_0_, bf16[512,512]{1,0:T(8,128)(2,1)S(1)} %collective-permute-done.refs_1_, bf16[512,512]{1,0:T(8,128)(2,1)S(1)} %relay.3.refs_1_.refs_2_, bf16[512,512]{1,0:T(8,128)(2,1)S(1)} %collective-permute-done.2.refs_3_, ...), custom_call_target="tpu_custom_call" | custom-call | flops 536870912 | bytes 3145728 | tf_op jit(solution)/shard_map/partial/pallas_call | solution.py:143
  21.6 2.7 %collective-permute-start.6 = (bf16[64,640]{1,0:T(8,128)(2,1)S(1)}, bf16[64,640]{1,0:T(8,128)(2,1)S(1)}, u32[]{:S(2)}, u32[]{:S(2)}) collective-permute-start(bf16[64,640]{1,0:T(8,128)(2,1)S(1)} %get-tuple-element.9.early_ref), channel_id=1, source_target_pairs={{12,0},{8,4},{4,8},{0,12},{13,1},{9,5},{5,9},{1,13},{14,2},{10,6},... | collective-permute-start | bytes 245768 | tf_op jit(solution)/shard_map/ppermute | solution.py:296
  24.3 3.4 %collective-permute-done.5.refs_0_.refs_1_ = bf16[512,256]{1,0:T(8,128)(2,1)S(1)} collective-permute-done((bf16[512,256]{1,0:T(8,128)(2,1)S(1)}, bf16[512,256]{1,0:T(8,128)(2,1)S(1)}, u32[]{:S(2)}, u32[]{:S(2)}) %collective-permute-start.5) | collective-permute-done | bytes 262176 | tf_op jit(solution)/shard_map/ppermute | solution.py:296
  27.7 0.7 %late.1 = f32[64,640]{1,0:T(8,128)S(1)} custom-call(bf16[1,512,512]{2,1,0:T(8,128)(2,1)S(1)} %choose.1.chosen_ref, bf16[256,512]{1,0:T(8,128)(2,1)S(1)} %get-tuple-element.7.refs_1_.refs_7_.turned_ref, bf16[64,640]{1,0:T(8,128)(2,1)S(1)} %get-tuple-element.9.early_ref, bf16[512,256]{1,0:T(8,128)(2,1)S(1)} %collective-permute-done.5.refs_0_.refs_1_), custom_call_target="tpu_custom_call" | custom-call | tf_op jit(solution)/shard_map/late/pallas_call | solution.py:217
  28.4 0.2 collective-permute-done.6.refs_0_
  28.6 0.2 collective-permute-start.7
  28.8 1.1 %cross.1 = f32[512,256]{1,0:T(8,128)} custom-call(f32[512,256]{1,0:T(8,128)S(1)} %get-tuple-element.8.partial_ref, bf16[1,512,512]{2,1,0:T(8,128)(2,1)S(1)} %choose.1.chosen_ref, bf16[512,256]{1,0:T(8,128)(2,1)S(1)} %collective-permute-done.5.refs_0_.refs_1_), custom_call_target="tpu_custom_call" | custom-call | flops 134217728 | bytes 1048576 | tf_op jit(solution)/shard_map/cross/pallas_call | solution.py:233
  29.9 3.2 %collective-permute-done.7.refs_1_ = bf16[64,640]{1,0:T(8,128)(2,1)S(1)} collective-permute-done((bf16[64,640]{1,0:T(8,128)(2,1)S(1)}, bf16[64,640]{1,0:T(8,128)(2,1)S(1)}, u32[]{:S(2)}, u32[]{:S(2)}) %collective-permute-start.7) | collective-permute-done | bytes 81952 | tf_op jit(solution)/shard_map/ppermute | solution.py:296
  33.1 0.8 %finish.1 = f32[1,256,256]{2,1,0:T(8,128)} custom-call(f32[1,256,256]{2,1,0:T(8,128)S(1)} %copy-done, bf16[64,640]{1,0:T(8,128)(2,1)S(1)} %add_convert_fusion.refs_0_, bf16[64,640]{1,0:T(8,128)(2,1)S(1)} %collective-permute-done.7.refs_1_), custom_call_target="tpu_custom_call" | custom-call | tf_op jit(solution)/shard_map/finish/pallas_call | solution.py:278
  (6 shorter events, 0.1 us)
Async XLA Ops:
  0.6 3.0 %copy-start.1 = (f32[512,256]{1,0:T(8,128)S(1)}, f32[512,256]{1,0:T(8,128)}, u32[]{:S(2)}) copy-start(f32[512,256]{1,0:T(8,128)} %cross_ref.1) | copy-start | bytes 1572868
  0.6 3.0 %copy-start = (f32[1,256,256]{2,1,0:T(8,128)S(1)}, f32[1,256,256]{2,1,0:T(8,128)}, u32[]{:S(2)}) copy-start(f32[1,256,256]{2,1,0:T(8,128)} %diag_ref.3) | copy-start | bytes 786436
  0.6 15.1 %collective-permute-start.1 = (bf16[512,512]{1,0:T(8,128)(2,1)}, bf16[512,512]{1,0:T(8,128)(2,1)S(1)}, u32[]{:S(2)}, u32[]{:S(2)}) collective-permute-start(bf16[512,512]{1,0:T(8,128)(2,1)} %top_hbm.1), channel_id=1, source_target_pairs={{2,0},{3,1},{0,2},{1,3},{6,4},{7,5},{4,6},{5,7},{10,8},{11,9},{8,1... | collective-permute-start | bytes 1572872 | tf_op jit(solution)/shard_map/ppermute | solution.py:296
  4.5 11.3 %collective-permute-start.3 = (bf16[512,256]{1,0:T(8,128)(2,1)S(1)}, bf16[512,256]{1,0:T(8,128)(2,1)S(1)}, u32[]{:S(2)}, u32[]{:S(2)}) collective-permute-start(bf16[512,256]{1,0:T(8,128)(2,1)S(1)} %panel.1.panel_ref.refs_4_), channel_id=1, source_target_pairs={{4,0},{0,4},{12,8},{8,12},{5,1},{1,5},{13,9},{9,13},{6,2},{2,6},{1... | collective-permute-start | bytes 786440 | tf_op jit(solution)/shard_map/ppermute | solution.py:296
  6.1 13.9 %collective-permute-start.4 = (bf16[512,256]{1,0:T(8,128)(2,1)S(1)}, bf16[512,256]{1,0:T(8,128)(2,1)S(1)}, u32[]{:S(2)}, u32[]{:S(2)}) collective-permute-start(bf16[512,256]{1,0:T(8,128)(2,1)S(1)} %panel.1.panel_ref.refs_4_), channel_id=1, source_target_pairs={{12,0},{8,4},{4,8},{0,12},{13,1},{9,5},{5,9},{1,13},{14,2},{10,6},... | collective-permute-start | bytes 786440 | tf_op jit(solution)/shard_map/ppermute | solution.py:296
  9.7 11.0 %collective-permute-start = (bf16[512,512]{1,0:T(8,128)(2,1)S(1)}, bf16[512,512]{1,0:T(8,128)(2,1)S(1)}, u32[]{:S(2)}, u32[]{:S(2)}) collective-permute-start(bf16[512,512]{1,0:T(8,128)(2,1)S(1)} %get-tuple-element.6.refs_0_), channel_id=1, source_target_pairs={{1,0},{0,1},{3,2},{2,3},{5,4},{4,5},{7,6},{6,7},{9,8},{8,9},{11,10... | collective-permute-start | bytes 1572872 | tf_op jit(solution)/shard_map/ppermute | solution.py:296
  15.8 4.9 %collective-permute-start.2 = (bf16[512,512]{1,0:T(8,128)(2,1)S(1)}, bf16[512,512]{1,0:T(8,128)(2,1)S(1)}, u32[]{:S(2)}, u32[]{:S(2)}) collective-permute-start(bf16[512,512]{1,0:T(8,128)(2,1)S(1)} %relay.3.refs_1_.refs_2_), channel_id=1, source_target_pairs={{1,0},{0,1},{3,2},{2,3},{5,4},{4,5},{7,6},{6,7},{9,8},{8,9},{11,10... | collective-permute-start | bytes 1572872 | tf_op jit(solution)/shard_map/ppermute | solution.py:296
  20.1 7.7 %collective-permute-start.5 = (bf16[512,256]{1,0:T(8,128)(2,1)S(1)}, bf16[512,256]{1,0:T(8,128)(2,1)S(1)}, u32[]{:S(2)}, u32[]{:S(2)}) collective-permute-start(bf16[512,256]{1,0:T(8,128)(2,1)S(1)} %relay.4.refs_6_), channel_id=1, source_target_pairs={{4,0},{0,4},{12,8},{8,12},{5,1},{1,5},{13,9},{9,13},{6,2},{2,6},{1... | collective-permute-start | bytes 786440 | tf_op jit(solution)/shard_map/ppermute | solution.py:296
  21.6 7.1 %collective-permute-start.6 = (bf16[64,640]{1,0:T(8,128)(2,1)S(1)}, bf16[64,640]{1,0:T(8,128)(2,1)S(1)}, u32[]{:S(2)}, u32[]{:S(2)}) collective-permute-start(bf16[64,640]{1,0:T(8,128)(2,1)S(1)} %get-tuple-element.9.early_ref), channel_id=1, source_target_pairs={{12,0},{8,4},{4,8},{0,12},{13,1},{9,5},{5,9},{1,13},{14,2},{10,6},... | collective-permute-start | bytes 245768 | tf_op jit(solution)/shard_map/ppermute | solution.py:296
  28.6 4.5 %collective-permute-start.7 = (bf16[64,640]{1,0:T(8,128)(2,1)S(1)}, bf16[64,640]{1,0:T(8,128)(2,1)S(1)}, u32[]{:S(2)}, u32[]{:S(2)}) collective-permute-start(bf16[64,640]{1,0:T(8,128)(2,1)S(1)} %add_convert_fusion.refs_0_), channel_id=1, source_target_pairs={{4,0},{0,4},{12,8},{8,12},{5,1},{1,5},{13,9},{9,13},{6,2},{2,6},{1... | collective-permute-start | bytes 245768 | tf_op jit(solution)/shard_map/ppermute | solution.py:296

commit v28 on v27

--- a/solution.py
+++ b/solution.py
@@ -112,17 +112,7 @@
     return pair * PAIR + side
 
 
-def partial_kernel(n, *refs):
-    tops, panels = refs[:n], refs[n:n + n // 2 + 1]
-    turned_ref, partial_ref, update_ref, panel_buf = refs[n + n // 2 + 1:]
-
-    def run(pairs):
-        total = dot(*[ref[...] for ref in pairs[0]])
-        for top, panel in pairs[1:]:
-            total += dot(top[...], panel[...])
-        partial_ref[...] = total
-        store_upper(update_ref, dot(turned_ref[...], total.astype(jnp.bfloat16)))
-
+def matched(n, tops, panels, panel_buf, run):
     if n == 2 * PAIR:
         place = place_of(n, 0, 0)
         for own in range(n):
@@ -137,23 +127,37 @@
     run([(tops[t], panel_buf.at[t]) for t in range(n)])
 
 
-def partial_product(tops, panels, turned):
+def product(pairs):
+    total = dot(*[ref[...] for ref in pairs[0]])
+    for top, panel in pairs[1:]:
+        total += dot(top[...], panel[...])
+    return total
+
+
+def early_kernel(n, *refs):
+    tops, panels = refs[:n], refs[n:n + n // 2 + 1]
+    turned_ref, update_ref, panel_buf = refs[n + n // 2 + 1:]
+
+    def run(pairs):
+        store_upper(update_ref, dot(turned_ref[...], product(pairs).astype(jnp.bfloat16)))
+
+    matched(n, tops, panels, panel_buf, run)
+
+
+def early_share(tops, panels, turned):
     n = len(tops)
     rows, width = panels[0].shape
     return pl.pallas_call(
-        functools.partial(partial_kernel, n),
-        out_shape=(
-            jax.ShapeDtypeStruct((rows, width), jnp.float32),
-            jax.ShapeDtypeStruct((width // 4, 5 * (width // 2)), jnp.bfloat16),
-        ),
+        functools.partial(early_kernel, n),
+        out_shape=jax.ShapeDtypeStruct((width // 4, 5 * (width // 2)), jnp.bfloat16),
         in_specs=[VMEM] * (n + len(panels) + 1),
-        out_specs=(VMEM, VMEM),
+        out_specs=VMEM,
         scratch_shapes=[pltpu.VMEM((n, rows, width), jnp.bfloat16)],
         compiler_params=PARAMS,
         cost_estimate=pl.CostEstimate(
             flops=2 * n * rows * rows * width, bytes_accessed=2 * n * rows * (rows + width), transcendentals=0
         ),
-        name="partial",
+        name="early",
     )(*tops, *panels, turned)
 
 
@@ -224,23 +228,31 @@
     )(chosen, turned, early, *panels)
 
 
-def cross_kernel(partial_ref, chosen_ref, *refs):
-    refs[-1][...] = -(partial_ref[...] + last_terms(chosen_ref, refs[:-1]))
-
-
-def cross_result(partial, chosen, panels):
-    rows, width = partial.shape
-    return pl.pallas_call(
-        cross_kernel,
-        out_shape=jax.ShapeDtypeStruct(partial.shape, jnp.float32),
-        in_specs=[VMEM] * (2 + len(panels)),
-        out_specs=VMEM,
+def cross_kernel(n, *refs):
+    tops, panels = refs[:n], refs[n:n + n // 2 + 1]
+    chosen_ref, *swapped, out_ref, panel_buf = refs[n + n // 2 + 1:]
+
+    def run(pairs):
+        out_ref[...] = -(product(pairs) + last_terms(chosen_ref, swapped))
+
+    matched(n, tops, panels, panel_buf, run)
+
+
+def cross_result(tops, panels, chosen, swapped):
+    n = len(tops)
+    rows, width = panels[0].shape
+    return pl.pallas_call(
+        functools.partial(cross_kernel, n),
+        out_shape=jax.ShapeDtypeStruct((rows, width), jnp.float32),
+        in_specs=[VMEM] * (n + len(panels) + 1 + len(swapped)),
+        out_specs=VMEM,
+        scratch_shapes=[pltpu.VMEM((n, rows, width), jnp.bfloat16)],
         compiler_params=PARAMS,
         cost_estimate=pl.CostEstimate(
-            flops=2 * len(panels) * rows * rows * width, bytes_accessed=8 * rows * width, transcendentals=0
+            flops=2 * n * rows * rows * width, bytes_accessed=4 * rows * width, transcendentals=0
         ),
         name="cross",
-    )(partial, chosen, *panels)
+    )(*tops, *panels, chosen, *swapped)
 
 
 def finish_kernel(diag_ref, *refs):
@@ -311,7 +323,8 @@
     for block in near:
         tops += [block, mate(block, "pcol")]
 
-    partial, early = partial_product(tops, [factor_panel, beside] + crossed, turned)
+    panels = [factor_panel, beside] + crossed
+    early = early_share(tops, panels, turned)
     chosen = choose(tops)
     crossing = [after(from_pair(early, "prow", d, 1), swapped[-1]) for d in range(1, pairs)]
     late = late_share(chosen, turned, swapped, early)
@@ -320,7 +333,7 @@
         rest = (late - early.astype(jnp.float32)).astype(jnp.bfloat16)
         parts += [from_pair(rest, "prow", d, 0) for d in range(1, pairs)]
     update = functools.reduce(jnp.add, [part.astype(jnp.float32) for part in parts]).astype(jnp.bfloat16)
-    return cross_result(partial, chosen, swapped), finish(diag_inverse, [update, mate(update, "prow")])
+    return cross_result(tops, panels, chosen, swapped), finish(diag_inverse, [update, mate(update, "prow")])
 
 
 def solution(mesh):

time: 34.2 us -> 34.2 us (level)
  Pallas kernels: 5.45 us -> 5.86 us
  waiting for transfers between devices: 17.2 us -> 16.8 us
    pallas_call x2, Pallas kernels: 2 us -> 2.42 us  [the longest x1 1.51 us: cross_result(): pl.pallas_call(functools.partial(cross_kernel, n), out_shape=jax.ShapeDty...]
    ppermute x8, waiting for transfers between devices: 17.2 us -> 16.8 us  [from_pair(): return lax.ppermute(block, axis, moves)]
  transfers between devices with their start and end apart: 8 -> 8, of which waited for: 5 -> 5; matrix products, arithmetic and copies ran while one was open for 0% -> 0% of each run, Pallas kernels for 14% -> 15%
where the time goes in v28:
time: 34.2 us; the launch traced here: 34 us
  waiting for transfers between devices  16.8 us (49%)
  starting transfers between devices  10.6 us (31%)
  Pallas kernels  5.86 us (17%)
  between operations  0.71 us (2%)
    ppermute x8, waiting for transfers between devices, from_pair(): return lax.ppermute(block, axis, moves)  16.8 us
    ppermute x8, starting transfers between devices, from_pair(): return lax.ppermute(block, axis, moves)  10.6 us
    pallas_call x1, Pallas kernels, cross_result(): pl.pallas_call(functools.partial(cross_kernel, n), out_shape=jax.ShapeDty...  1.51 us
    pallas_call x1, Pallas kernels, stage(): pl.pallas_call(stage_kernel, out_shape=(pltpu.VMEM(panel.shape[::-1], pan...  1.07 us
    pallas_call x1, Pallas kernels, early_share(): pl.pallas_call(functools.partial(early_kernel, n), out_shape=jax.ShapeDty...  0.91 us
    pallas_call x1, Pallas kernels, finish(): pl.pallas_call(finish_kernel, out_shape=jax.ShapeDtypeStruct(diag_inverse...  0.84 us
    pallas_call x1, Pallas kernels, build_panel(): pl.pallas_call(panel_kernel, out_shape=pltpu.VMEM(cross_blocks.shape, jnp...  0.81 us
  transfers between devices with their start and end apart: 8, of which 5 were waited for; matrix products, arithmetic and copies ran while one was open for 0% of the time, Pallas kernels for 15%

profile of v28, /device:TPU:0, one launch (start us, length us, event | category | flops | bytes accessed | tf_op | source)
XLA Modules:
  0.0 34.0 jit_solution(13339410994154072151)
XLA Ops:
  0.6 0.0 copy-start
  0.6 0.0 copy-start.1
  0.6 3.0 %collective-permute-start.1 = (bf16[512,512]{1,0:T(8,128)(2,1)}, bf16[512,512]{1,0:T(8,128)(2,1)S(1)}, u32[]{:S(2)}, u32[]{:S(2)}) collective-permute-start(bf16[512,512]{1,0:T(8,128)(2,1)} %top_hbm.1), channel_id=1, source_target_pairs={{2,0},{3,1},{0,2},{1,3},{6,4},{7,5},{4,6},{5,7},{10,8},{11,9},{8,1... | collective-permute-start | bytes 1572872 | tf_op jit(solution)/shard_map/ppermute | solution.py:308
  3.7 0.0 copy-done
  3.7 0.0 copy-done.1
  3.7 0.8 %panel.1.panel_ref.refs_4_ = bf16[512,256]{1,0:T(8,128)(2,1)S(1)} custom-call(s32[2]{0:T(128)} %bitcast.1, f32[512,256]{1,0:T(8,128)S(1)} %copy-done.1, f32[1,256,256]{2,1,0:T(8,128)S(1)} %copy-done, f32[8,128]{1,0:T(8,128)S(1)} %token_.1.token_ref), custom_call_target="tpu_custom_call" | custom-call | tf_op jit(solution)/shard_map/panel/pallas_call | solution.py:60
  4.5 1.6 %collective-permute-start.3 = (bf16[512,256]{1,0:T(8,128)(2,1)S(1)}, bf16[512,256]{1,0:T(8,128)(2,1)S(1)}, u32[]{:S(2)}, u32[]{:S(2)}) collective-permute-start(bf16[512,256]{1,0:T(8,128)(2,1)S(1)} %panel.1.panel_ref.refs_4_), channel_id=1, source_target_pairs={{4,0},{0,4},{12,8},{8,12},{5,1},{1,5},{13,9},{9,13},{6,2},{2,6},{1... | collective-permute-start | bytes 786440 | tf_op jit(solution)/shard_map/ppermute | solution.py:308
  6.1 2.5 %collective-permute-start.4 = (bf16[512,256]{1,0:T(8,128)(2,1)S(1)}, bf16[512,256]{1,0:T(8,128)(2,1)S(1)}, u32[]{:S(2)}, u32[]{:S(2)}) collective-permute-start(bf16[512,256]{1,0:T(8,128)(2,1)S(1)} %panel.1.panel_ref.refs_4_), channel_id=1, source_target_pairs={{12,0},{8,4},{4,8},{0,12},{13,1},{9,5},{5,9},{1,13},{14,2},{10,6},... | collective-permute-start | bytes 786440 | tf_op jit(solution)/shard_map/ppermute | solution.py:308
  8.6 1.1 %stage.1 = (bf16[256,512]{1,0:T(8,128)(2,1)S(1)}, bf16[512,512]{1,0:T(8,128)(2,1)S(1)}) custom-call(bf16[512,256]{1,0:T(8,128)(2,1)S(1)} %panel.1.panel_ref.refs_4_, bf16[512,512]{1,0:T(8,128)(2,1)} %top_hbm.1), custom_call_target="tpu_custom_call" | custom-call | tf_op jit(solution)/shard_map/stage/pallas_call | solution.py:172
  9.7 0.1 collective-permute-start
  9.7 6.0 %collective-permute-done.1.refs_0_ = bf16[512,512]{1,0:T(8,128)(2,1)S(1)} collective-permute-done((bf16[512,512]{1,0:T(8,128)(2,1)}, bf16[512,512]{1,0:T(8,128)(2,1)S(1)}, u32[]{:S(2)}, u32[]{:S(2)}) %collective-permute-start.1) | collective-permute-done | bytes 524320 | tf_op jit(solution)/shard_map/ppermute | solution.py:308
  15.8 0.0 collective-permute-start.2
  15.8 0.0 collective-permute-done.3.refs_2_.refs_5_
  15.8 4.3 %collective-permute-done.4.refs_0_ = bf16[512,256]{1,0:T(8,128)(2,1)S(1)} collective-permute-done((bf16[512,256]{1,0:T(8,128)(2,1)S(1)}, bf16[512,256]{1,0:T(8,128)(2,1)S(1)}, u32[]{:S(2)}, u32[]{:S(2)}) %collective-permute-start.4) | collective-permute-done | bytes 262176 | tf_op jit(solution)/shard_map/ppermute | solution.py:308
  20.1 0.6 %collective-permute-start.5 = (bf16[512,256]{1,0:T(8,128)(2,1)S(1)}, bf16[512,256]{1,0:T(8,128)(2,1)S(1)}, u32[]{:S(2)}, u32[]{:S(2)}) collective-permute-start(bf16[512,256]{1,0:T(8,128)(2,1)S(1)} %relay.4.refs_6_), channel_id=1, source_target_pairs={{4,0},{0,4},{12,8},{8,12},{5,1},{1,5},{13,9},{9,13},{6,2},{2,6},{1... | collective-permute-start | bytes 786440 | tf_op jit(solution)/shard_map/ppermute | solution.py:308
  20.6 0.0 collective-permute-done.refs_1_
  20.6 0.0 collective-permute-done.2.refs_3_
  20.6 0.9 %early.1.early_ref = bf16[64,640]{1,0:T(8,128)(2,1)S(1)} custom-call(bf16[512,512]{1,0:T(8,128)(2,1)S(1)} %get-tuple-element.4.refs_0_, bf16[512,512]{1,0:T(8,128)(2,1)S(1)} %collective-permute-done.refs_1_, bf16[512,512]{1,0:T(8,128)(2,1)S(1)} %relay.3.refs_1_.refs_2_, bf16[512,512]{1,0:T(8,128)(2,1)S(1)} %collective-permute-done.2.refs_3_, ...), custom_call_target="tpu_custom_call" | custom-call | flops 536870912 | bytes 3145728 | tf_op jit(solution)/shard_map/early/pallas_call | solution.py:150
  21.6 2.7 %collective-permute-start.6 = (bf16[64,640]{1,0:T(8,128)(2,1)S(1)}, bf16[64,640]{1,0:T(8,128)(2,1)S(1)}, u32[]{:S(2)}, u32[]{:S(2)}) collective-permute-start(bf16[64,640]{1,0:T(8,128)(2,1)S(1)} %early.1.early_ref), channel_id=1, source_target_pairs={{12,0},{8,4},{4,8},{0,12},{13,1},{9,5},{5,9},{1,13},{14,2},{10,6},... | collective-permute-start | bytes 245768 | tf_op jit(solution)/shard_map/ppermute | solution.py:308
  24.3 3.4 %collective-permute-done.5.refs_8_.refs_0_.refs_1_ = bf16[512,256]{1,0:T(8,128)(2,1)S(1)} collective-permute-done((bf16[512,256]{1,0:T(8,128)(2,1)S(1)}, bf16[512,256]{1,0:T(8,128)(2,1)S(1)}, u32[]{:S(2)}, u32[]{:S(2)}) %collective-permute-start.5) | collective-permute-done | bytes 262176 | tf_op jit(solution)/shard_map/ppermute | solution.py:308
  27.7 0.7 %late.1 = f32[64,640]{1,0:T(8,128)S(1)} custom-call(bf16[1,512,512]{2,1,0:T(8,128)(2,1)S(1)} %choose.1.refs_7_.chosen_ref, bf16[256,512]{1,0:T(8,128)(2,1)S(1)} %get-tuple-element.5.refs_1_.refs_7_.turned_ref, bf16[64,640]{1,0:T(8,128)(2,1)S(1)} %early.1.early_ref, bf16[512,256]{1,0:T(8,128)(2,1)S(1)} %collective-permute-done.5.refs_8_.refs_0_.refs_1_), custom_call_target="tpu_custom_call" | custom-call | tf_op jit(solution)/shard_map/late/pallas_call | solution.py:221
  28.4 0.2 collective-permute-done.6.refs_0_
  28.6 0.2 collective-permute-start.7
  28.8 1.5 %cross.1 = f32[512,256]{1,0:T(8,128)} custom-call(bf16[512,512]{1,0:T(8,128)(2,1)S(1)} %get-tuple-element.4.refs_0_, bf16[512,512]{1,0:T(8,128)(2,1)S(1)} %collective-permute-done.refs_1_, bf16[512,512]{1,0:T(8,128)(2,1)S(1)} %relay.3.refs_1_.refs_2_, bf16[512,512]{1,0:T(8,128)(2,1)S(1)} %collective-permute-done.2.refs_3_, ...), custom_call_target="tpu_custom_call" | custom-call | flops 536870912 | bytes 524288 | tf_op jit(solution)/shard_map/cross/pallas_call | solution.py:244
  30.3 2.8 %collective-permute-done.7.refs_1_ = bf16[64,640]{1,0:T(8,128)(2,1)S(1)} collective-permute-done((bf16[64,640]{1,0:T(8,128)(2,1)S(1)}, bf16[64,640]{1,0:T(8,128)(2,1)S(1)}, u32[]{:S(2)}, u32[]{:S(2)}) %collective-permute-start.7) | collective-permute-done | bytes 81952 | tf_op jit(solution)/shard_map/ppermute | solution.py:308
  33.1 0.8 %finish.1 = f32[1,256,256]{2,1,0:T(8,128)} custom-call(f32[1,256,256]{2,1,0:T(8,128)S(1)} %copy-done, bf16[64,640]{1,0:T(8,128)(2,1)S(1)} %add_convert_fusion.refs_0_, bf16[64,640]{1,0:T(8,128)(2,1)S(1)} %collective-permute-done.7.refs_1_), custom_call_target="tpu_custom_call" | custom-call | tf_op jit(solution)/shard_map/finish/pallas_call | solution.py:290
  (6 shorter events, 0.1 us)
Async XLA Ops:
  0.6 3.0 %copy-start = (f32[1,256,256]{2,1,0:T(8,128)S(1)}, f32[1,256,256]{2,1,0:T(8,128)}, u32[]{:S(2)}) copy-start(f32[1,256,256]{2,1,0:T(8,128)} %diag_ref.3) | copy-start | bytes 786436
  0.6 3.0 %copy-start.1 = (f32[512,256]{1,0:T(8,128)S(1)}, f32[512,256]{1,0:T(8,128)}, u32[]{:S(2)}) copy-start(f32[512,256]{1,0:T(8,128)} %cross_ref.1) | copy-start | bytes 1572868
  0.6 15.1 %collective-permute-start.1 = (bf16[512,512]{1,0:T(8,128)(2,1)}, bf16[512,512]{1,0:T(8,128)(2,1)S(1)}, u32[]{:S(2)}, u32[]{:S(2)}) collective-permute-start(bf16[512,512]{1,0:T(8,128)(2,1)} %top_hbm.1), channel_id=1, source_target_pairs={{2,0},{3,1},{0,2},{1,3},{6,4},{7,5},{4,6},{5,7},{10,8},{11,9},{8,1... | collective-permute-start | bytes 1572872 | tf_op jit(solution)/shard_map/ppermute | solution.py:308
  4.5 11.3 %collective-permute-start.3 = (bf16[512,256]{1,0:T(8,128)(2,1)S(1)}, bf16[512,256]{1,0:T(8,128)(2,1)S(1)}, u32[]{:S(2)}, u32[]{:S(2)}) collective-permute-start(bf16[512,256]{1,0:T(8,128)(2,1)S(1)} %panel.1.panel_ref.refs_4_), channel_id=1, source_target_pairs={{4,0},{0,4},{12,8},{8,12},{5,1},{1,5},{13,9},{9,13},{6,2},{2,6},{1... | collective-permute-start | bytes 786440 | tf_op jit(solution)/shard_map/ppermute | solution.py:308
  6.1 13.9 %collective-permute-start.4 = (bf16[512,256]{1,0:T(8,128)(2,1)S(1)}, bf16[512,256]{1,0:T(8,128)(2,1)S(1)}, u32[]{:S(2)}, u32[]{:S(2)}) collective-permute-start(bf16[512,256]{1,0:T(8,128)(2,1)S(1)} %panel.1.panel_ref.refs_4_), channel_id=1, source_target_pairs={{12,0},{8,4},{4,8},{0,12},{13,1},{9,5},{5,9},{1,13},{14,2},{10,6},... | collective-permute-start | bytes 786440 | tf_op jit(solution)/shard_map/ppermute | solution.py:308
  9.7 11.0 %collective-permute-start = (bf16[512,512]{1,0:T(8,128)(2,1)S(1)}, bf16[512,512]{1,0:T(8,128)(2,1)S(1)}, u32[]{:S(2)}, u32[]{:S(2)}) collective-permute-start(bf16[512,512]{1,0:T(8,128)(2,1)S(1)} %get-tuple-element.4.refs_0_), channel_id=1, source_target_pairs={{1,0},{0,1},{3,2},{2,3},{5,4},{4,5},{7,6},{6,7},{9,8},{8,9},{11,10... | collective-permute-start | bytes 1572872 | tf_op jit(solution)/shard_map/ppermute | solution.py:308
  15.8 4.9 %collective-permute-start.2 = (bf16[512,512]{1,0:T(8,128)(2,1)S(1)}, bf16[512,512]{1,0:T(8,128)(2,1)S(1)}, u32[]{:S(2)}, u32[]{:S(2)}) collective-permute-start(bf16[512,512]{1,0:T(8,128)(2,1)S(1)} %relay.3.refs_1_.refs_2_), channel_id=1, source_target_pairs={{1,0},{0,1},{3,2},{2,3},{5,4},{4,5},{7,6},{6,7},{9,8},{8,9},{11,10... | collective-permute-start | bytes 1572872 | tf_op jit(solution)/shard_map/ppermute | solution.py:308
  20.1 7.7 %collective-permute-start.5 = (bf16[512,256]{1,0:T(8,128)(2,1)S(1)}, bf16[512,256]{1,0:T(8,128)(2,1)S(1)}, u32[]{:S(2)}, u32[]{:S(2)}) collective-permute-start(bf16[512,256]{1,0:T(8,128)(2,1)S(1)} %relay.4.refs_6_), channel_id=1, source_target_pairs={{4,0},{0,4},{12,8},{8,12},{5,1},{1,5},{13,9},{9,13},{6,2},{2,6},{1... | collective-permute-start | bytes 786440 | tf_op jit(solution)/shard_map/ppermute | solution.py:308
  21.6 7.1 %collective-permute-start.6 = (bf16[64,640]{1,0:T(8,128)(2,1)S(1)}, bf16[64,640]{1,0:T(8,128)(2,1)S(1)}, u32[]{:S(2)}, u32[]{:S(2)}) collective-permute-start(bf16[64,640]{1,0:T(8,128)(2,1)S(1)} %early.1.early_ref), channel_id=1, source_target_pairs={{12,0},{8,4},{4,8},{0,12},{13,1},{9,5},{5,9},{1,13},{14,2},{10,6},... | collective-permute-start | bytes 245768 | tf_op jit(solution)/shard_map/ppermute | solution.py:308
  28.6 4.5 %collective-permute-start.7 = (bf16[64,640]{1,0:T(8,128)(2,1)S(1)}, bf16[64,640]{1,0:T(8,128)(2,1)S(1)}, u32[]{:S(2)}, u32[]{:S(2)}) collective-permute-start(bf16[64,640]{1,0:T(8,128)(2,1)S(1)} %add_convert_fusion.refs_0_), channel_id=1, source_target_pairs={{4,0},{0,4},{12,8},{8,12},{5,1},{1,5},{13,9},{9,13},{6,2},{2,6},{1... | collective-permute-start | bytes 245768 | tf_op jit(solution)/shard_map/ppermute | solution.py:308

commit v29 on v27

--- a/solution.py
+++ b/solution.py
@@ -304,6 +304,7 @@
     crossed = [from_pair(factor_panel, "prow", d, 1) for d in range(1, pairs)]
     turned, inverse_top = stage(factor_panel, inverse_top)
     near = [after(block, turned) for block in near]
+    beside = after(beside, factor_panel, cost=HOP_COST // 2)
     crossed = [after(block, near[0], beside, cost=HOP_COST) for block in crossed]
     swapped = [mate(block, "prow") for block in crossed]
 

time: 34.2 us -> 37.3 us (1.091)
  starting transfers between devices: 10.6 us -> 11.7 us
  local copies, waits for them, and re-layouts: 0.01 us -> 1.09 us
  waiting for transfers between devices: 17.2 us -> 18 us
    unnamed x4 -> x6, local copies, waits for them, and re-layouts: 0.01 us -> 1.09 us
    ppermute x8, starting transfers between devices: 10.6 us -> 11.7 us  [from_pair(): return lax.ppermute(block, axis, moves)]
    ppermute x8, waiting for transfers between devices: 17.2 us -> 18 us  [from_pair(): return lax.ppermute(block, axis, moves)]
  transfers between devices with their start and end apart: 8 -> 8, of which waited for: 5 -> 6; matrix products, arithmetic and copies ran while one was open for 0% -> 0% of each run, Pallas kernels for 14% -> 10%
where the time goes in v29:
time: 37.3 us; the launch traced here: 37.1 us
  waiting for transfers between devices  18 us (48%)
  starting transfers between devices  11.7 us (31%)
  Pallas kernels  5.58 us (15%)
  local copies, waits for them, and re-layouts  1.09 us (3%)
  between operations  0.72 us (2%)
    ppermute x8, waiting for transfers between devices, from_pair(): return lax.ppermute(block, axis, moves)  18 us
    ppermute x8, starting transfers between devices, from_pair(): return lax.ppermute(block, axis, moves)  11.7 us
    pallas_call x1, Pallas kernels, cross_result(): pl.pallas_call(cross_kernel, out_shape=jax.ShapeDtypeStruct(partial.shape...  1.09 us
    unnamed x6, local copies, waits for them, and re-layouts  1.09 us
    pallas_call x1, Pallas kernels, stage(): pl.pallas_call(stage_kernel, out_shape=(pltpu.VMEM(panel.shape[::-1], pan...  1.07 us
    pallas_call x1, Pallas kernels, build_panel(): pl.pallas_call(panel_kernel, out_shape=pltpu.VMEM(cross_blocks.shape, jnp...  0.95 us
    pallas_call x1, Pallas kernels, partial_product(): pl.pallas_call(functools.partial(partial_kernel, n), out_shape=(jax.Shape...  0.91 us
    pallas_call x1, Pallas kernels, finish(): pl.pallas_call(finish_kernel, out_shape=jax.ShapeDtypeStruct(diag_inverse...  0.84 us
  transfers between devices with their start and end apart: 8, of which 6 were waited for; matrix products, arithmetic and copies ran while one was open for 0% of the time, Pallas kernels for 10%

profile of v29, /device:TPU:0, one launch (start us, length us, event | category | flops | bytes accessed | tf_op | source)
XLA Modules:
  0.0 37.1 jit_solution(17459255593392460816)
XLA Ops:
  0.6 0.0 copy-start.1
  0.6 0.0 copy-start
  0.7 1.0 %copy-done.1 = f32[512,256]{1,0:T(8,128)S(1)} copy-done((f32[512,256]{1,0:T(8,128)S(1)}, f32[512,256]{1,0:T(8,128)}, u32[]{:S(2)}) %copy-start.1) | copy-done | bytes 524312
  1.7 0.1 copy-done
  1.7 0.0 copy-start.2
  1.7 0.9 %panel.1.panel_ref.refs_1_.refs_4_ = bf16[512,256]{1,0:T(8,128)(2,1)S(1)} custom-call(s32[2]{0:T(128)} %bitcast.1, f32[512,256]{1,0:T(8,128)S(1)} %copy-done.1, f32[1,256,256]{2,1,0:T(8,128)S(1)} %copy-done, f32[8,128]{1,0:T(8,128)S(1)} %token_.1.token_ref), custom_call_target="tpu_custom_call" | custom-call | tf_op jit(solution)/shard_map/panel/pallas_call | solution.py:60
  2.7 3.1 %collective-permute-start.3 = (bf16[512,256]{1,0:T(8,128)(2,1)S(1)}, bf16[512,256]{1,0:T(8,128)(2,1)S(1)}, u32[]{:S(2)}, u32[]{:S(2)}) collective-permute-start(bf16[512,256]{1,0:T(8,128)(2,1)S(1)} %panel.1.panel_ref.refs_1_.refs_4_), channel_id=1, source_target_pairs={{4,0},{0,4},{12,8},{8,12},{5,1},{1,5},{13,9},{9,13},{6,2},{2,6},{1... | collective-permute-start | bytes 786440 | tf_op jit(solution)/shard_map/ppermute | solution.py:296
  5.8 0.0 copy-done.2
  5.8 1.5 %collective-permute-start.1 = (bf16[512,512]{1,0:T(8,128)(2,1)S(1)}, bf16[512,512]{1,0:T(8,128)(2,1)S(1)}, u32[]{:S(2)}, u32[]{:S(2)}) collective-permute-start(bf16[512,512]{1,0:T(8,128)(2,1)S(1)} %copy-done.2), channel_id=1, source_target_pairs={{2,0},{3,1},{0,2},{1,3},{6,4},{7,5},{4,6},{5,7},{10,8},{11,9},{8,1... | collective-permute-start | bytes 1572872 | tf_op jit(solution)/shard_map/ppermute | solution.py:296
  7.3 2.5 %collective-permute-start.4 = (bf16[512,256]{1,0:T(8,128)(2,1)S(1)}, bf16[512,256]{1,0:T(8,128)(2,1)S(1)}, u32[]{:S(2)}, u32[]{:S(2)}) collective-permute-start(bf16[512,256]{1,0:T(8,128)(2,1)S(1)} %panel.1.panel_ref.refs_1_.refs_4_), channel_id=1, source_target_pairs={{12,0},{8,4},{4,8},{0,12},{13,1},{9,5},{5,9},{1,13},{14,2},{10,6},... | collective-permute-start | bytes 786440 | tf_op jit(solution)/shard_map/ppermute | solution.py:296
  9.8 1.1 %stage.1 = (bf16[256,512]{1,0:T(8,128)(2,1)S(1)}, bf16[512,512]{1,0:T(8,128)(2,1)S(1)}) custom-call(bf16[512,256]{1,0:T(8,128)(2,1)S(1)} %panel.1.panel_ref.refs_1_.refs_4_, bf16[512,512]{1,0:T(8,128)(2,1)} %top_hbm.1), custom_call_target="tpu_custom_call" | custom-call | tf_op jit(solution)/shard_map/stage/pallas_call | solution.py:168
  10.8 0.1 collective-permute-start
  10.9 1.6 %collective-permute-done.3.refs_0_ = bf16[512,256]{1,0:T(8,128)(2,1)S(1)} collective-permute-done((bf16[512,256]{1,0:T(8,128)(2,1)S(1)}, bf16[512,256]{1,0:T(8,128)(2,1)S(1)}, u32[]{:S(2)}, u32[]{:S(2)}) %collective-permute-start.3) | collective-permute-done | bytes 262176 | tf_op jit(solution)/shard_map/ppermute | solution.py:296
  12.5 6.7 %collective-permute-done.1.refs_0_ = bf16[512,512]{1,0:T(8,128)(2,1)S(1)} collective-permute-done((bf16[512,512]{1,0:T(8,128)(2,1)S(1)}, bf16[512,512]{1,0:T(8,128)(2,1)S(1)}, u32[]{:S(2)}, u32[]{:S(2)}) %collective-permute-start.1) | collective-permute-done | bytes 524320 | tf_op jit(solution)/shard_map/ppermute | solution.py:296
  19.2 0.0 collective-permute-start.2
  19.2 0.8 %collective-permute-done.4.refs_0_ = bf16[512,256]{1,0:T(8,128)(2,1)S(1)} collective-permute-done((bf16[512,256]{1,0:T(8,128)(2,1)S(1)}, bf16[512,256]{1,0:T(8,128)(2,1)S(1)}, u32[]{:S(2)}, u32[]{:S(2)}) %collective-permute-start.4) | collective-permute-done | bytes 262176 | tf_op jit(solution)/shard_map/ppermute | solution.py:296
  20.0 1.8 %collective-permute-start.5 = (bf16[512,256]{1,0:T(8,128)(2,1)S(1)}, bf16[512,256]{1,0:T(8,128)(2,1)S(1)}, u32[]{:S(2)}, u32[]{:S(2)}) collective-permute-start(bf16[512,256]{1,0:T(8,128)(2,1)S(1)} %relay.6.refs_6_), channel_id=1, source_target_pairs={{4,0},{0,4},{12,8},{8,12},{5,1},{1,5},{13,9},{9,13},{6,2},{2,6},{1... | collective-permute-start | bytes 786440 | tf_op jit(solution)/shard_map/ppermute | solution.py:296
  21.8 0.0 collective-permute-done.refs_1_
  21.8 0.0 collective-permute-done.2.refs_3_
  21.8 0.9 %partial.1 = (f32[512,256]{1,0:T(8,128)S(1)}, bf16[64,640]{1,0:T(8,128)(2,1)S(1)}) custom-call(bf16[512,512]{1,0:T(8,128)(2,1)S(1)} %get-tuple-element.6.refs_0_, bf16[512,512]{1,0:T(8,128)(2,1)S(1)} %collective-permute-done.refs_1_, bf16[512,512]{1,0:T(8,128)(2,1)S(1)} %relay.4.refs_1_.refs_2_, bf16[512,512]{1,0:T(8,128)(2,1)S(1)} %collective-permute-done.2.refs_3_, ...), custom_call_target="tpu_custom_call" | custom-call | flops 536870912 | bytes 3145728 | tf_op jit(solution)/shard_map/partial/pallas_call | solution.py:143
  22.7 2.7 %collective-permute-start.6 = (bf16[64,640]{1,0:T(8,128)(2,1)S(1)}, bf16[64,640]{1,0:T(8,128)(2,1)S(1)}, u32[]{:S(2)}, u32[]{:S(2)}) collective-permute-start(bf16[64,640]{1,0:T(8,128)(2,1)S(1)} %get-tuple-element.9.early_ref), channel_id=1, source_target_pairs={{12,0},{8,4},{4,8},{0,12},{13,1},{9,5},{5,9},{1,13},{14,2},{10,6},... | collective-permute-start | bytes 245768 | tf_op jit(solution)/shard_map/ppermute | solution.py:296
  25.5 2.4 %collective-permute-done.5.refs_0_.refs_1_ = bf16[512,256]{1,0:T(8,128)(2,1)S(1)} collective-permute-done((bf16[512,256]{1,0:T(8,128)(2,1)S(1)}, bf16[512,256]{1,0:T(8,128)(2,1)S(1)}, u32[]{:S(2)}, u32[]{:S(2)}) %collective-permute-start.5) | collective-permute-done | bytes 262176 | tf_op jit(solution)/shard_map/ppermute | solution.py:296
  27.9 0.7 %late.1 = f32[64,640]{1,0:T(8,128)S(1)} custom-call(bf16[1,512,512]{2,1,0:T(8,128)(2,1)S(1)} %choose.1.chosen_ref, bf16[256,512]{1,0:T(8,128)(2,1)S(1)} %get-tuple-element.7.refs_1_.refs_7_.turned_ref, bf16[64,640]{1,0:T(8,128)(2,1)S(1)} %get-tuple-element.9.early_ref, bf16[512,256]{1,0:T(8,128)(2,1)S(1)} %collective-permute-done.5.refs_0_.refs_1_), custom_call_target="tpu_custom_call" | custom-call | tf_op jit(solution)/shard_map/late/pallas_call | solution.py:217
  28.6 3.1 %collective-permute-done.6.refs_0_ = bf16[64,640]{1,0:T(8,128)(2,1)S(1)} collective-permute-done((bf16[64,640]{1,0:T(8,128)(2,1)S(1)}, bf16[64,640]{1,0:T(8,128)(2,1)S(1)}, u32[]{:S(2)}, u32[]{:S(2)}) %collective-permute-start.6) | collective-permute-done | bytes 81952 | tf_op jit(solution)/shard_map/ppermute | solution.py:296
  31.7 0.1 collective-permute-start.7
  31.8 1.1 %cross.1 = f32[512,256]{1,0:T(8,128)} custom-call(f32[512,256]{1,0:T(8,128)S(1)} %get-tuple-element.8.partial_ref, bf16[1,512,512]{2,1,0:T(8,128)(2,1)S(1)} %choose.1.chosen_ref, bf16[512,256]{1,0:T(8,128)(2,1)S(1)} %collective-permute-done.5.refs_0_.refs_1_), custom_call_target="tpu_custom_call" | custom-call | flops 134217728 | bytes 1048576 | tf_op jit(solution)/shard_map/cross/pallas_call | solution.py:233
  32.9 3.3 %collective-permute-done.7.refs_1_ = bf16[64,640]{1,0:T(8,128)(2,1)S(1)} collective-permute-done((bf16[64,640]{1,0:T(8,128)(2,1)S(1)}, bf16[64,640]{1,0:T(8,128)(2,1)S(1)}, u32[]{:S(2)}, u32[]{:S(2)}) %collective-permute-start.7) | collective-permute-done | bytes 81952 | tf_op jit(solution)/shard_map/ppermute | solution.py:296
  36.2 0.8 %finish.1 = f32[1,256,256]{2,1,0:T(8,128)} custom-call(f32[1,256,256]{2,1,0:T(8,128)S(1)} %copy-done, bf16[64,640]{1,0:T(8,128)(2,1)S(1)} %add_convert_fusion.refs_0_, bf16[64,640]{1,0:T(8,128)(2,1)S(1)} %collective-permute-done.7.refs_1_), custom_call_target="tpu_custom_call" | custom-call | tf_op jit(solution)/shard_map/finish/pallas_call | solution.py:278
  (7 shorter events, 0.1 us)
Async XLA Ops:
  0.6 1.0 %copy-start.1 = (f32[512,256]{1,0:T(8,128)S(1)}, f32[512,256]{1,0:T(8,128)}, u32[]{:S(2)}) copy-start(f32[512,256]{1,0:T(8,128)} %cross_ref.1) | copy-start | bytes 1572868
  0.6 1.1 %copy-start = (f32[1,256,256]{2,1,0:T(8,128)S(1)}, f32[1,256,256]{2,1,0:T(8,128)}, u32[]{:S(2)}) copy-start(f32[1,256,256]{2,1,0:T(8,128)} %diag_ref.3) | copy-start | bytes 786436
  1.7 4.0 %copy-start.2 = (bf16[512,512]{1,0:T(8,128)(2,1)S(1)}, bf16[512,512]{1,0:T(8,128)(2,1)}, u32[]{:S(2)}) copy-start(bf16[512,512]{1,0:T(8,128)(2,1)} %top_hbm.1) | copy-start | bytes 1572868
  2.7 9.8 %collective-permute-start.3 = (bf16[512,256]{1,0:T(8,128)(2,1)S(1)}, bf16[512,256]{1,0:T(8,128)(2,1)S(1)}, u32[]{:S(2)}, u32[]{:S(2)}) collective-permute-start(bf16[512,256]{1,0:T(8,128)(2,1)S(1)} %panel.1.panel_ref.refs_1_.refs_4_), channel_id=1, source_target_pairs={{4,0},{0,4},{12,8},{8,12},{5,1},{1,5},{13,9},{9,13},{6,2},{2,6},{1... | collective-permute-start | bytes 786440 | tf_op jit(solution)/shard_map/ppermute | solution.py:296
  5.8 13.4 %collective-permute-start.1 = (bf16[512,512]{1,0:T(8,128)(2,1)S(1)}, bf16[512,512]{1,0:T(8,128)(2,1)S(1)}, u32[]{:S(2)}, u32[]{:S(2)}) collective-permute-start(bf16[512,512]{1,0:T(8,128)(2,1)S(1)} %copy-done.2), channel_id=1, source_target_pairs={{2,0},{3,1},{0,2},{1,3},{6,4},{7,5},{4,6},{5,7},{10,8},{11,9},{8,1... | collective-permute-start | bytes 1572872 | tf_op jit(solution)/shard_map/ppermute | solution.py:296
  7.3 12.7 %collective-permute-start.4 = (bf16[512,256]{1,0:T(8,128)(2,1)S(1)}, bf16[512,256]{1,0:T(8,128)(2,1)S(1)}, u32[]{:S(2)}, u32[]{:S(2)}) collective-permute-start(bf16[512,256]{1,0:T(8,128)(2,1)S(1)} %panel.1.panel_ref.refs_1_.refs_4_), channel_id=1, source_target_pairs={{12,0},{8,4},{4,8},{0,12},{13,1},{9,5},{5,9},{1,13},{14,2},{10,6},... | collective-permute-start | bytes 786440 | tf_op jit(solution)/shard_map/ppermute | solution.py:296
  10.8 11.0 %collective-permute-start = (bf16[512,512]{1,0:T(8,128)(2,1)S(1)}, bf16[512,512]{1,0:T(8,128)(2,1)S(1)}, u32[]{:S(2)}, u32[]{:S(2)}) collective-permute-start(bf16[512,512]{1,0:T(8,128)(2,1)S(1)} %get-tuple-element.6.refs_0_), channel_id=1, source_target_pairs={{1,0},{0,1},{3,2},{2,3},{5,4},{4,5},{7,6},{6,7},{9,8},{8,9},{11,10... | collective-permute-start | bytes 1572872 | tf_op jit(solution)/shard_map/ppermute | solution.py:296
  19.2 2.6 %collective-permute-start.2 = (bf16[512,512]{1,0:T(8,128)(2,1)S(1)}, bf16[512,512]{1,0:T(8,128)(2,1)S(1)}, u32[]{:S(2)}, u32[]{:S(2)}) collective-permute-start(bf16[512,512]{1,0:T(8,128)(2,1)S(1)} %relay.4.refs_1_.refs_2_), channel_id=1, source_target_pairs={{1,0},{0,1},{3,2},{2,3},{5,4},{4,5},{7,6},{6,7},{9,8},{8,9},{11,10... | collective-permute-start | bytes 1572872 | tf_op jit(solution)/shard_map/ppermute | solution.py:296
  20.0 7.9 %collective-permute-start.5 = (bf16[512,256]{1,0:T(8,128)(2,1)S(1)}, bf16[512,256]{1,0:T(8,128)(2,1)S(1)}, u32[]{:S(2)}, u32[]{:S(2)}) collective-permute-start(bf16[512,256]{1,0:T(8,128)(2,1)S(1)} %relay.6.refs_6_), channel_id=1, source_target_pairs={{4,0},{0,4},{12,8},{8,12},{5,1},{1,5},{13,9},{9,13},{6,2},{2,6},{1... | collective-permute-start | bytes 786440 | tf_op jit(solution)/shard_map/ppermute | solution.py:296
  22.7 9.0 %collective-permute-start.6 = (bf16[64,640]{1,0:T(8,128)(2,1)S(1)}, bf16[64,640]{1,0:T(8,128)(2,1)S(1)}, u32[]{:S(2)}, u32[]{:S(2)}) collective-permute-start(bf16[64,640]{1,0:T(8,128)(2,1)S(1)} %get-tuple-element.9.early_ref), channel_id=1, source_target_pairs={{12,0},{8,4},{4,8},{0,12},{13,1},{9,5},{5,9},{1,13},{14,2},{10,6},... | collective-permute-start | bytes 245768 | tf_op jit(solution)/shard_map/ppermute | solution.py:296
  31.7 4.5 %collective-permute-start.7 = (bf16[64,640]{1,0:T(8,128)(2,1)S(1)}, bf16[64,640]{1,0:T(8,128)(2,1)S(1)}, u32[]{:S(2)}, u32[]{:S(2)}) collective-permute-start(bf16[64,640]{1,0:T(8,128)(2,1)S(1)} %add_convert_fusion.refs_0_), channel_id=1, source_target_pairs={{4,0},{0,4},{12,8},{8,12},{5,1},{1,5},{13,9},{9,13},{6,2},{2,6},{1... | collective-permute-start | bytes 245768 | tf_op jit(solution)/shard_map/ppermute | solution.py:296

commit v30 on v27

--- a/solution.py
+++ b/solution.py
@@ -304,7 +304,8 @@
     crossed = [from_pair(factor_panel, "prow", d, 1) for d in range(1, pairs)]
     turned, inverse_top = stage(factor_panel, inverse_top)
     near = [after(block, turned) for block in near]
-    crossed = [after(block, near[0], beside, cost=HOP_COST) for block in crossed]
+    crossed = [after(block, near[0], cost=HOP_COST) for block in crossed]
+    beside = after(beside, *crossed, cost=2 * HOP_COST)
     swapped = [mate(block, "prow") for block in crossed]
 
     tops = [inverse_top, mate(inverse_top, "pcol")]
@@ -313,7 +314,7 @@
 
     partial, early = partial_product(tops, [factor_panel, beside] + crossed, turned)
     chosen = choose(tops)
-    crossing = [after(from_pair(early, "prow", d, 1), swapped[-1]) for d in range(1, pairs)]
+    crossing = [after(from_pair(early, "prow", d, 0), swapped[-1]) for d in range(1, pairs)]
     late = late_share(chosen, turned, swapped, early)
     parts = [late] + crossing
     if pairs > 2:

time: 34.2 us -> 33.5 us (0.980)
  waiting for transfers between devices: 17.2 us -> 14.8 us
  starting transfers between devices: 10.6 us -> 12.3 us
    ppermute x8, waiting for transfers between devices: 17.2 us -> 14.8 us  [from_pair(): return lax.ppermute(block, axis, moves)]
    ppermute x8, starting transfers between devices: 10.6 us -> 12.3 us  [from_pair(): return lax.ppermute(block, axis, moves)]
  transfers between devices with their start and end apart: 8 -> 8, of which waited for: 5 -> 4; matrix products, arithmetic and copies ran while one was open for 0% -> 0% of each run, Pallas kernels for 14% -> 14%
where the time goes in v30:
time: 33.5 us; the launch traced here: 33.4 us
  waiting for transfers between devices  14.8 us (44%)
  starting transfers between devices  12.3 us (37%)
  Pallas kernels  5.47 us (16%)
  between operations  0.73 us (2%)
    ppermute x8, waiting for transfers between devices, from_pair(): return lax.ppermute(block, axis, moves)  14.8 us
    ppermute x8, starting transfers between devices, from_pair(): return lax.ppermute(block, axis, moves)  12.3 us
    pallas_call x1, Pallas kernels, cross_result(): pl.pallas_call(cross_kernel, out_shape=jax.ShapeDtypeStruct(partial.shape...  1.09 us
    pallas_call x1, Pallas kernels, stage(): pl.pallas_call(stage_kernel, out_shape=(pltpu.VMEM(panel.shape[::-1], pan...  1.07 us
    pallas_call x1, Pallas kernels, partial_product(): pl.pallas_call(functools.partial(partial_kernel, n), out_shape=(jax.Shape...  0.93 us
    pallas_call x1, Pallas kernels, finish(): pl.pallas_call(finish_kernel, out_shape=jax.ShapeDtypeStruct(diag_inverse...  0.84 us
    pallas_call x1, Pallas kernels, build_panel(): pl.pallas_call(panel_kernel, out_shape=pltpu.VMEM(cross_blocks.shape, jnp...  0.82 us
    pallas_call x1, Pallas kernels, late_share(): pl.pallas_call(late_kernel, out_shape=jax.ShapeDtypeStruct(early.shape, j...  0.68 us
  transfers between devices with their start and end apart: 8, of which 4 were waited for; matrix products, arithmetic and copies ran while one was open for 0% of the time, Pallas kernels for 14%

profile of v30, /device:TPU:0, one launch (start us, length us, event | category | flops | bytes accessed | tf_op | source)
XLA Modules:
  0.0 33.4 jit_solution(8447695278542617717)
XLA Ops:
  0.6 0.0 copy-start.1
  0.6 0.0 copy-start
  0.6 3.0 %collective-permute-start.1 = (bf16[512,512]{1,0:T(8,128)(2,1)}, bf16[512,512]{1,0:T(8,128)(2,1)S(1)}, u32[]{:S(2)}, u32[]{:S(2)}) collective-permute-start(bf16[512,512]{1,0:T(8,128)(2,1)} %top_hbm.1), channel_id=1, source_target_pairs={{2,0},{3,1},{0,2},{1,3},{6,4},{7,5},{4,6},{5,7},{10,8},{11,9},{8,1... | collective-permute-start | bytes 1572872 | tf_op jit(solution)/shard_map/ppermute | solution.py:296
  3.7 0.0 copy-done.1
  3.7 0.0 copy-done
  3.7 0.8 %panel.1.panel_ref.refs_4_ = bf16[512,256]{1,0:T(8,128)(2,1)S(1)} custom-call(s32[2]{0:T(128)} %bitcast.1, f32[512,256]{1,0:T(8,128)S(1)} %copy-done.1, f32[1,256,256]{2,1,0:T(8,128)S(1)} %copy-done, f32[8,128]{1,0:T(8,128)S(1)} %token_.1.token_ref), custom_call_target="tpu_custom_call" | custom-call | tf_op jit(solution)/shard_map/panel/pallas_call | solution.py:60
  4.5 3.7 %collective-permute-start.4 = (bf16[512,256]{1,0:T(8,128)(2,1)S(1)}, bf16[512,256]{1,0:T(8,128)(2,1)S(1)}, u32[]{:S(2)}, u32[]{:S(2)}) collective-permute-start(bf16[512,256]{1,0:T(8,128)(2,1)S(1)} %panel.1.panel_ref.refs_4_), channel_id=1, source_target_pairs={{12,0},{8,4},{4,8},{0,12},{13,1},{9,5},{5,9},{1,13},{14,2},{10,6},... | collective-permute-start | bytes 786440 | tf_op jit(solution)/shard_map/ppermute | solution.py:296
  8.2 0.0 collective-permute-start.3
  8.2 1.1 %stage.1 = (bf16[256,512]{1,0:T(8,128)(2,1)S(1)}, bf16[512,512]{1,0:T(8,128)(2,1)S(1)}) custom-call(bf16[512,256]{1,0:T(8,128)(2,1)S(1)} %panel.1.panel_ref.refs_4_, bf16[512,512]{1,0:T(8,128)(2,1)} %top_hbm.1), custom_call_target="tpu_custom_call" | custom-call | tf_op jit(solution)/shard_map/stage/pallas_call | solution.py:168
  9.2 0.1 collective-permute-start
  9.3 6.5 %collective-permute-done.1.refs_0_ = bf16[512,512]{1,0:T(8,128)(2,1)S(1)} collective-permute-done((bf16[512,512]{1,0:T(8,128)(2,1)}, bf16[512,512]{1,0:T(8,128)(2,1)S(1)}, u32[]{:S(2)}, u32[]{:S(2)}) %collective-permute-start.1) | collective-permute-done | bytes 524320 | tf_op jit(solution)/shard_map/ppermute | solution.py:296
  15.8 0.0 collective-permute-start.2
  15.8 0.0 collective-permute-done.4.refs_0_
  15.8 3.7 %collective-permute-start.5 = (bf16[512,256]{1,0:T(8,128)(2,1)S(1)}, bf16[512,256]{1,0:T(8,128)(2,1)S(1)}, u32[]{:S(2)}, u32[]{:S(2)}) collective-permute-start(bf16[512,256]{1,0:T(8,128)(2,1)S(1)} %relay.5.refs_1_.refs_6_), channel_id=1, source_target_pairs={{4,0},{0,4},{12,8},{8,12},{5,1},{1,5},{13,9},{9,13},{6,2},{2,6},{1... | collective-permute-start | bytes 786440 | tf_op jit(solution)/shard_map/ppermute | solution.py:296
  19.5 0.5 %collective-permute-done.3.refs_0_ = bf16[512,256]{1,0:T(8,128)(2,1)S(1)} collective-permute-done((bf16[512,256]{1,0:T(8,128)(2,1)S(1)}, bf16[512,256]{1,0:T(8,128)(2,1)S(1)}, u32[]{:S(2)}, u32[]{:S(2)}) %collective-permute-start.3) | collective-permute-done | bytes 262176 | tf_op jit(solution)/shard_map/ppermute | solution.py:296
  20.0 0.0 collective-permute-done.refs_1_
  20.0 0.0 collective-permute-done.2.refs_3_
  20.0 0.9 %partial.1 = (f32[512,256]{1,0:T(8,128)S(1)}, bf16[64,640]{1,0:T(8,128)(2,1)S(1)}) custom-call(bf16[512,512]{1,0:T(8,128)(2,1)S(1)} %get-tuple-element.6.refs_0_, bf16[512,512]{1,0:T(8,128)(2,1)S(1)} %collective-permute-done.refs_1_, bf16[512,512]{1,0:T(8,128)(2,1)S(1)} %relay.4.refs_1_.refs_2_, bf16[512,512]{1,0:T(8,128)(2,1)S(1)} %collective-permute-done.2.refs_3_, ...), custom_call_target="tpu_custom_call" | custom-call | flops 536870912 | bytes 3145728 | tf_op jit(solution)/shard_map/partial/pallas_call | solution.py:143
  20.9 0.6 %collective-permute-start.6 = (bf16[64,640]{1,0:T(8,128)(2,1)S(1)}, bf16[64,640]{1,0:T(8,128)(2,1)S(1)}, u32[]{:S(2)}, u32[]{:S(2)}) collective-permute-start(bf16[64,640]{1,0:T(8,128)(2,1)S(1)} %get-tuple-element.9.early_ref), channel_id=1, source_target_pairs={{8,0},{12,4},{0,8},{4,12},{9,1},{13,5},{1,9},{5,13},{10,2},{14,6},... | collective-permute-start | bytes 245768 | tf_op jit(solution)/shard_map/ppermute | solution.py:296
  21.6 5.7 %collective-permute-done.5.refs_0_.refs_1_ = bf16[512,256]{1,0:T(8,128)(2,1)S(1)} collective-permute-done((bf16[512,256]{1,0:T(8,128)(2,1)S(1)}, bf16[512,256]{1,0:T(8,128)(2,1)S(1)}, u32[]{:S(2)}, u32[]{:S(2)}) %collective-permute-start.5) | collective-permute-done | bytes 262176 | tf_op jit(solution)/shard_map/ppermute | solution.py:296
  27.3 0.7 %late.1 = f32[64,640]{1,0:T(8,128)S(1)} custom-call(bf16[1,512,512]{2,1,0:T(8,128)(2,1)S(1)} %choose.1.chosen_ref, bf16[256,512]{1,0:T(8,128)(2,1)S(1)} %get-tuple-element.7.refs_1_.refs_7_.turned_ref, bf16[64,640]{1,0:T(8,128)(2,1)S(1)} %get-tuple-element.9.early_ref, bf16[512,256]{1,0:T(8,128)(2,1)S(1)} %collective-permute-done.5.refs_0_.refs_1_), custom_call_target="tpu_custom_call" | custom-call | tf_op jit(solution)/shard_map/late/pallas_call | solution.py:217
  28.0 0.0 collective-permute-done.6.refs_0_
  28.0 1.2 %collective-permute-start.7 = (bf16[64,640]{1,0:T(8,128)(2,1)S(1)}, bf16[64,640]{1,0:T(8,128)(2,1)S(1)}, u32[]{:S(2)}, u32[]{:S(2)}) collective-permute-start(bf16[64,640]{1,0:T(8,128)(2,1)S(1)} %add_convert_fusion.refs_0_), channel_id=1, source_target_pairs={{4,0},{0,4},{12,8},{8,12},{5,1},{1,5},{13,9},{9,13},{6,2},{2,6},{1... | collective-permute-start | bytes 245768 | tf_op jit(solution)/shard_map/ppermute | solution.py:296
  29.2 1.1 %cross.1 = f32[512,256]{1,0:T(8,128)} custom-call(f32[512,256]{1,0:T(8,128)S(1)} %get-tuple-element.8.partial_ref, bf16[1,512,512]{2,1,0:T(8,128)(2,1)S(1)} %choose.1.chosen_ref, bf16[512,256]{1,0:T(8,128)(2,1)S(1)} %collective-permute-done.5.refs_0_.refs_1_), custom_call_target="tpu_custom_call" | custom-call | flops 134217728 | bytes 1048576 | tf_op jit(solution)/shard_map/cross/pallas_call | solution.py:233
  30.3 2.2 %collective-permute-done.7.refs_1_ = bf16[64,640]{1,0:T(8,128)(2,1)S(1)} collective-permute-done((bf16[64,640]{1,0:T(8,128)(2,1)S(1)}, bf16[64,640]{1,0:T(8,128)(2,1)S(1)}, u32[]{:S(2)}, u32[]{:S(2)}) %collective-permute-start.7) | collective-permute-done | bytes 81952 | tf_op jit(solution)/shard_map/ppermute | solution.py:296
  32.5 0.8 %finish.1 = f32[1,256,256]{2,1,0:T(8,128)} custom-call(f32[1,256,256]{2,1,0:T(8,128)S(1)} %copy-done, bf16[64,640]{1,0:T(8,128)(2,1)S(1)} %add_convert_fusion.refs_0_, bf16[64,640]{1,0:T(8,128)(2,1)S(1)} %collective-permute-done.7.refs_1_), custom_call_target="tpu_custom_call" | custom-call | tf_op jit(solution)/shard_map/finish/pallas_call | solution.py:278
  (7 shorter events, 0.1 us)
Async XLA Ops:
  0.6 3.0 %copy-start.1 = (f32[512,256]{1,0:T(8,128)S(1)}, f32[512,256]{1,0:T(8,128)}, u32[]{:S(2)}) copy-start(f32[512,256]{1,0:T(8,128)} %cross_ref.1) | copy-start | bytes 1572868
  0.6 3.0 %copy-start = (f32[1,256,256]{2,1,0:T(8,128)S(1)}, f32[1,256,256]{2,1,0:T(8,128)}, u32[]{:S(2)}) copy-start(f32[1,256,256]{2,1,0:T(8,128)} %diag_ref.3) | copy-start | bytes 786436
  0.6 15.1 %collective-permute-start.1 = (bf16[512,512]{1,0:T(8,128)(2,1)}, bf16[512,512]{1,0:T(8,128)(2,1)S(1)}, u32[]{:S(2)}, u32[]{:S(2)}) collective-permute-start(bf16[512,512]{1,0:T(8,128)(2,1)} %top_hbm.1), channel_id=1, source_target_pairs={{2,0},{3,1},{0,2},{1,3},{6,4},{7,5},{4,6},{5,7},{10,8},{11,9},{8,1... | collective-permute-start | bytes 1572872 | tf_op jit(solution)/shard_map/ppermute | solution.py:296
  4.5 11.3 %collective-permute-start.4 = (bf16[512,256]{1,0:T(8,128)(2,1)S(1)}, bf16[512,256]{1,0:T(8,128)(2,1)S(1)}, u32[]{:S(2)}, u32[]{:S(2)}) collective-permute-start(bf16[512,256]{1,0:T(8,128)(2,1)S(1)} %panel.1.panel_ref.refs_4_), channel_id=1, source_target_pairs={{12,0},{8,4},{4,8},{0,12},{13,1},{9,5},{5,9},{1,13},{14,2},{10,6},... | collective-permute-start | bytes 786440 | tf_op jit(solution)/shard_map/ppermute | solution.py:296
  8.2 11.8 %collective-permute-start.3 = (bf16[512,256]{1,0:T(8,128)(2,1)S(1)}, bf16[512,256]{1,0:T(8,128)(2,1)S(1)}, u32[]{:S(2)}, u32[]{:S(2)}) collective-permute-start(bf16[512,256]{1,0:T(8,128)(2,1)S(1)} %panel.1.panel_ref.refs_4_), channel_id=1, source_target_pairs={{4,0},{0,4},{12,8},{8,12},{5,1},{1,5},{13,9},{9,13},{6,2},{2,6},{1... | collective-permute-start | bytes 786440 | tf_op jit(solution)/shard_map/ppermute | solution.py:296
  9.2 10.8 %collective-permute-start = (bf16[512,512]{1,0:T(8,128)(2,1)S(1)}, bf16[512,512]{1,0:T(8,128)(2,1)S(1)}, u32[]{:S(2)}, u32[]{:S(2)}) collective-permute-start(bf16[512,512]{1,0:T(8,128)(2,1)S(1)} %get-tuple-element.6.refs_0_), channel_id=1, source_target_pairs={{1,0},{0,1},{3,2},{2,3},{5,4},{4,5},{7,6},{6,7},{9,8},{8,9},{11,10... | collective-permute-start | bytes 1572872 | tf_op jit(solution)/shard_map/ppermute | solution.py:296
  15.8 4.2 %collective-permute-start.2 = (bf16[512,512]{1,0:T(8,128)(2,1)S(1)}, bf16[512,512]{1,0:T(8,128)(2,1)S(1)}, u32[]{:S(2)}, u32[]{:S(2)}) collective-permute-start(bf16[512,512]{1,0:T(8,128)(2,1)S(1)} %relay.4.refs_1_.refs_2_), channel_id=1, source_target_pairs={{1,0},{0,1},{3,2},{2,3},{5,4},{4,5},{7,6},{6,7},{9,8},{8,9},{11,10... | collective-permute-start | bytes 1572872 | tf_op jit(solution)/shard_map/ppermute | solution.py:296
  15.8 11.5 %collective-permute-start.5 = (bf16[512,256]{1,0:T(8,128)(2,1)S(1)}, bf16[512,256]{1,0:T(8,128)(2,1)S(1)}, u32[]{:S(2)}, u32[]{:S(2)}) collective-permute-start(bf16[512,256]{1,0:T(8,128)(2,1)S(1)} %relay.5.refs_1_.refs_6_), channel_id=1, source_target_pairs={{4,0},{0,4},{12,8},{8,12},{5,1},{1,5},{13,9},{9,13},{6,2},{2,6},{1... | collective-permute-start | bytes 786440 | tf_op jit(solution)/shard_map/ppermute | solution.py:296
  20.9 7.0 %collective-permute-start.6 = (bf16[64,640]{1,0:T(8,128)(2,1)S(1)}, bf16[64,640]{1,0:T(8,128)(2,1)S(1)}, u32[]{:S(2)}, u32[]{:S(2)}) collective-permute-start(bf16[64,640]{1,0:T(8,128)(2,1)S(1)} %get-tuple-element.9.early_ref), channel_id=1, source_target_pairs={{8,0},{12,4},{0,8},{4,12},{9,1},{13,5},{1,9},{5,13},{10,2},{14,6},... | collective-permute-start | bytes 245768 | tf_op jit(solution)/shard_map/ppermute | solution.py:296
  28.0 4.5 %collective-permute-start.7 = (bf16[64,640]{1,0:T(8,128)(2,1)S(1)}, bf16[64,640]{1,0:T(8,128)(2,1)S(1)}, u32[]{:S(2)}, u32[]{:S(2)}) collective-permute-start(bf16[64,640]{1,0:T(8,128)(2,1)S(1)} %add_convert_fusion.refs_0_), channel_id=1, source_target_pairs={{4,0},{0,4},{12,8},{8,12},{5,1},{1,5},{13,9},{9,13},{6,2},{2,6},{1... | collective-permute-start | bytes 245768 | tf_op jit(solution)/shard_map/ppermute | solution.py:296

commit v31 on v30

--- a/solution.py
+++ b/solution.py
@@ -177,51 +177,55 @@
 
 
 def choose_kernel(n, *refs):
-    tops, chosen_ref = refs[:n], refs[n]
+    tops, (turned_ref, chosen_ref, left_ref) = refs[:n], refs[n:]
     for d in range(1, n // PAIR):
         place = place_of(n, d, 0)
         for t in range(n):
             @pl.when(place == t)
             def _():
                 chosen_ref[d - 1] = tops[t][...]
-
-
-def choose(tops):
+        left_ref[d - 1] = dot(turned_ref[...], chosen_ref[d - 1]).astype(jnp.bfloat16)
+
+
+def choose(tops, turned):
     n = len(tops)
     return pl.pallas_call(
         functools.partial(choose_kernel, n),
-        out_shape=jax.ShapeDtypeStruct((n // 2 - 1,) + tops[0].shape, jnp.bfloat16),
-        in_specs=[VMEM] * n,
-        out_specs=VMEM,
+        out_shape=(
+            jax.ShapeDtypeStruct((n // 2 - 1,) + tops[0].shape, jnp.bfloat16),
+            jax.ShapeDtypeStruct((n // 2 - 1,) + turned.shape, jnp.bfloat16),
+        ),
+        in_specs=[VMEM] * (n + 1),
+        out_specs=(VMEM, VMEM),
         compiler_params=PARAMS,
         name="choose",
-    )(*tops)
-
-
-def last_terms(chosen_ref, panels):
-    total = dot(chosen_ref[0], panels[0][...])
+    )(*tops, turned)
+
+
+def last_terms(left_ref, panels):
+    total = dot(left_ref[0], panels[0][...])
     for d, panel in enumerate(panels[1:], 1):
-        total += dot(chosen_ref[d], panel[...])
+        total += dot(left_ref[d], panel[...])
     return total
 
 
-def late_kernel(chosen_ref, turned_ref, early_ref, *refs):
+def late_kernel(left_ref, early_ref, *refs):
     panels, update_ref = refs[:-1], refs[-1]
-    update = dot(turned_ref[...], last_terms(chosen_ref, panels).astype(jnp.bfloat16))
+    update = last_terms(left_ref, panels)
     if len(panels) == 1:
         update += update.T
     store_upper(update_ref, update, early_ref)
 
 
-def late_share(chosen, turned, panels, early):
+def late_share(left, panels, early):
     return pl.pallas_call(
         late_kernel,
         out_shape=jax.ShapeDtypeStruct(early.shape, jnp.float32),
-        in_specs=[VMEM] * (3 + len(panels)),
+        in_specs=[VMEM] * (2 + len(panels)),
         out_specs=VMEM,
         compiler_params=PARAMS,
         name="late",
-    )(chosen, turned, early, *panels)
+    )(left, early, *panels)
 
 
 def cross_kernel(partial_ref, chosen_ref, *refs):
@@ -313,9 +317,9 @@
         tops += [block, mate(block, "pcol")]
 
     partial, early = partial_product(tops, [factor_panel, beside] + crossed, turned)
-    chosen = choose(tops)
+    chosen, left = choose(tops, turned)
     crossing = [after(from_pair(early, "prow", d, 0), swapped[-1]) for d in range(1, pairs)]
-    late = late_share(chosen, turned, swapped, early)
+    late = late_share(left, swapped, early)
     parts = [late] + crossing
     if pairs > 2:
         rest = (late - early.astype(jnp.float32)).astype(jnp.bfloat16)

time: 33.5 us -> 33.2 us (level)
  waiting for transfers between devices: 14.8 us -> 14.2 us
    ppermute x8, waiting for transfers between devices: 14.8 us -> 14.2 us  [from_pair(): return lax.ppermute(block, axis, moves)]
where the time goes in v31:
time: 33.2 us; the launch traced here: 33 us
  waiting for transfers between devices  14.2 us (43%)
  starting transfers between devices  12.6 us (38%)
  Pallas kernels  5.44 us (16%)
  between operations  0.73 us (2%)
    ppermute x8, waiting for transfers between devices, from_pair(): return lax.ppermute(block, axis, moves)  14.2 us
    ppermute x8, starting transfers between devices, from_pair(): return lax.ppermute(block, axis, moves)  12.6 us
    pallas_call x1, Pallas kernels, cross_result(): pl.pallas_call(cross_kernel, out_shape=jax.ShapeDtypeStruct(partial.shape...  1.09 us
    pallas_call x1, Pallas kernels, stage(): pl.pallas_call(stage_kernel, out_shape=(pltpu.VMEM(panel.shape[::-1], pan...  1.07 us
    pallas_call x1, Pallas kernels, partial_product(): pl.pallas_call(functools.partial(partial_kernel, n), out_shape=(jax.Shape...  0.93 us
    pallas_call x1, Pallas kernels, finish(): pl.pallas_call(finish_kernel, out_shape=jax.ShapeDtypeStruct(diag_inverse...  0.84 us
    pallas_call x1, Pallas kernels, build_panel(): pl.pallas_call(panel_kernel, out_shape=pltpu.VMEM(cross_blocks.shape, jnp...  0.81 us
  transfers between devices with their start and end apart: 8, of which 4 were waited for; matrix products, arithmetic and copies ran while one was open for 0% of the time, Pallas kernels for 14%

profile of v31, /device:TPU:0, one launch (start us, length us, event | category | flops | bytes accessed | tf_op | source)
XLA Modules:
  0.0 33.0 jit_solution(2367258425378645082)
XLA Ops:
  0.6 0.0 copy-start
  0.6 0.0 copy-start.1
  0.6 3.0 %collective-permute-start.1 = (bf16[512,512]{1,0:T(8,128)(2,1)}, bf16[512,512]{1,0:T(8,128)(2,1)S(1)}, u32[]{:S(2)}, u32[]{:S(2)}) collective-permute-start(bf16[512,512]{1,0:T(8,128)(2,1)} %top_hbm.1), channel_id=1, source_target_pairs={{2,0},{3,1},{0,2},{1,3},{6,4},{7,5},{4,6},{5,7},{10,8},{11,9},{8,1... | collective-permute-start | bytes 1572872 | tf_op jit(solution)/shard_map/ppermute | solution.py:300
  3.7 0.0 copy-done
  3.7 0.0 copy-done.1
  3.7 0.8 %panel.1.panel_ref.refs_4_ = bf16[512,256]{1,0:T(8,128)(2,1)S(1)} custom-call(s32[2]{0:T(128)} %bitcast.1, f32[512,256]{1,0:T(8,128)S(1)} %copy-done.1, f32[1,256,256]{2,1,0:T(8,128)S(1)} %copy-done, f32[8,128]{1,0:T(8,128)S(1)} %token_.1.token_ref), custom_call_target="tpu_custom_call" | custom-call | tf_op jit(solution)/shard_map/panel/pallas_call | solution.py:60
  4.5 3.7 %collective-permute-start.4 = (bf16[512,256]{1,0:T(8,128)(2,1)S(1)}, bf16[512,256]{1,0:T(8,128)(2,1)S(1)}, u32[]{:S(2)}, u32[]{:S(2)}) collective-permute-start(bf16[512,256]{1,0:T(8,128)(2,1)S(1)} %panel.1.panel_ref.refs_4_), channel_id=1, source_target_pairs={{12,0},{8,4},{4,8},{0,12},{13,1},{9,5},{5,9},{1,13},{14,2},{10,6},... | collective-permute-start | bytes 786440 | tf_op jit(solution)/shard_map/ppermute | solution.py:300
  8.1 0.0 collective-permute-start.3
  8.1 1.1 %stage.1 = (bf16[256,512]{1,0:T(8,128)(2,1)S(1)}, bf16[512,512]{1,0:T(8,128)(2,1)S(1)}) custom-call(bf16[512,256]{1,0:T(8,128)(2,1)S(1)} %panel.1.panel_ref.refs_4_, bf16[512,512]{1,0:T(8,128)(2,1)} %top_hbm.1), custom_call_target="tpu_custom_call" | custom-call | tf_op jit(solution)/shard_map/stage/pallas_call | solution.py:168
  9.2 0.1 collective-permute-start
  9.3 6.5 %collective-permute-done.1.refs_0_ = bf16[512,512]{1,0:T(8,128)(2,1)S(1)} collective-permute-done((bf16[512,512]{1,0:T(8,128)(2,1)}, bf16[512,512]{1,0:T(8,128)(2,1)S(1)}, u32[]{:S(2)}, u32[]{:S(2)}) %collective-permute-start.1) | collective-permute-done | bytes 524320 | tf_op jit(solution)/shard_map/ppermute | solution.py:300
  15.8 0.0 collective-permute-start.2
  15.8 0.0 collective-permute-done.4.refs_0_
  15.8 3.7 %collective-permute-start.5 = (bf16[512,256]{1,0:T(8,128)(2,1)S(1)}, bf16[512,256]{1,0:T(8,128)(2,1)S(1)}, u32[]{:S(2)}, u32[]{:S(2)}) collective-permute-start(bf16[512,256]{1,0:T(8,128)(2,1)S(1)} %relay.5.refs_1_.refs_6_), channel_id=1, source_target_pairs={{4,0},{0,4},{12,8},{8,12},{5,1},{1,5},{13,9},{9,13},{6,2},{2,6},{1... | collective-permute-start | bytes 786440 | tf_op jit(solution)/shard_map/ppermute | solution.py:300
  19.5 0.5 %collective-permute-done.3.refs_0_ = bf16[512,256]{1,0:T(8,128)(2,1)S(1)} collective-permute-done((bf16[512,256]{1,0:T(8,128)(2,1)S(1)}, bf16[512,256]{1,0:T(8,128)(2,1)S(1)}, u32[]{:S(2)}, u32[]{:S(2)}) %collective-permute-start.3) | collective-permute-done | bytes 262176 | tf_op jit(solution)/shard_map/ppermute | solution.py:300
  20.0 0.0 collective-permute-done.refs_1_
  20.0 0.0 collective-permute-done.2.refs_3_
  20.0 0.9 %partial.1 = (f32[512,256]{1,0:T(8,128)S(1)}, bf16[64,640]{1,0:T(8,128)(2,1)S(1)}) custom-call(bf16[512,512]{1,0:T(8,128)(2,1)S(1)} %get-tuple-element.8.refs_0_, bf16[512,512]{1,0:T(8,128)(2,1)S(1)} %collective-permute-done.refs_1_, bf16[512,512]{1,0:T(8,128)(2,1)S(1)} %relay.4.refs_1_.refs_2_, bf16[512,512]{1,0:T(8,128)(2,1)S(1)} %collective-permute-done.2.refs_3_, ...), custom_call_target="tpu_custom_call" | custom-call | flops 536870912 | bytes 3145728 | tf_op jit(solution)/shard_map/partial/pallas_call | solution.py:143
  20.9 0.6 %collective-permute-start.6 = (bf16[64,640]{1,0:T(8,128)(2,1)S(1)}, bf16[64,640]{1,0:T(8,128)(2,1)S(1)}, u32[]{:S(2)}, u32[]{:S(2)}) collective-permute-start(bf16[64,640]{1,0:T(8,128)(2,1)S(1)} %get-tuple-element.13.early_ref), channel_id=1, source_target_pairs={{8,0},{12,4},{0,8},{4,12},{9,1},{13,5},{1,9},{5,13},{10,2},{14,6},... | collective-permute-start | bytes 245768 | tf_op jit(solution)/shard_map/ppermute | solution.py:300
  21.6 0.3 choose.1
  21.9 5.4 %collective-permute-done.5.refs_0_.refs_1_ = bf16[512,256]{1,0:T(8,128)(2,1)S(1)} collective-permute-done((bf16[512,256]{1,0:T(8,128)(2,1)S(1)}, bf16[512,256]{1,0:T(8,128)(2,1)S(1)}, u32[]{:S(2)}, u32[]{:S(2)}) %collective-permute-start.5) | collective-permute-done | bytes 262176 | tf_op jit(solution)/shard_map/ppermute | solution.py:300
  27.3 0.4 %late.1 = f32[64,640]{1,0:T(8,128)S(1)} custom-call(bf16[1,256,512]{2,1,0:T(8,128)(2,1)S(1)} %get-tuple-element.12.left_ref, bf16[64,640]{1,0:T(8,128)(2,1)S(1)} %get-tuple-element.13.early_ref, bf16[512,256]{1,0:T(8,128)(2,1)S(1)} %collective-permute-done.5.refs_0_.refs_1_), custom_call_target="tpu_custom_call" | custom-call | tf_op jit(solution)/shard_map/late/pallas_call | solution.py:221
  27.6 0.0 collective-permute-done.6.refs_0_
  27.7 1.5 %collective-permute-start.7 = (bf16[64,640]{1,0:T(8,128)(2,1)S(1)}, bf16[64,640]{1,0:T(8,128)(2,1)S(1)}, u32[]{:S(2)}, u32[]{:S(2)}) collective-permute-start(bf16[64,640]{1,0:T(8,128)(2,1)S(1)} %add_convert_fusion.refs_0_), channel_id=1, source_target_pairs={{4,0},{0,4},{12,8},{8,12},{5,1},{1,5},{13,9},{9,13},{6,2},{2,6},{1... | collective-permute-start | bytes 245768 | tf_op jit(solution)/shard_map/ppermute | solution.py:300
  29.2 1.1 %cross.1 = f32[512,256]{1,0:T(8,128)} custom-call(f32[512,256]{1,0:T(8,128)S(1)} %get-tuple-element.10.partial_ref, bf16[1,512,512]{2,1,0:T(8,128)(2,1)S(1)} %get-tuple-element.11.chosen_ref, bf16[512,256]{1,0:T(8,128)(2,1)S(1)} %collective-permute-done.5.refs_0_.refs_1_), custom_call_target="tpu_custom_call" | custom-call | flops 134217728 | bytes 1048576 | tf_op jit(solution)/shard_map/cross/pallas_call | solution.py:237
  30.3 1.9 %collective-permute-done.7.refs_1_ = bf16[64,640]{1,0:T(8,128)(2,1)S(1)} collective-permute-done((bf16[64,640]{1,0:T(8,128)(2,1)S(1)}, bf16[64,640]{1,0:T(8,128)(2,1)S(1)}, u32[]{:S(2)}, u32[]{:S(2)}) %collective-permute-start.7) | collective-permute-done | bytes 81952 | tf_op jit(solution)/shard_map/ppermute | solution.py:300
  32.2 0.8 %finish.1 = f32[1,256,256]{2,1,0:T(8,128)} custom-call(f32[1,256,256]{2,1,0:T(8,128)S(1)} %copy-done, bf16[64,640]{1,0:T(8,128)(2,1)S(1)} %add_convert_fusion.refs_0_, bf16[64,640]{1,0:T(8,128)(2,1)S(1)} %collective-permute-done.7.refs_1_), custom_call_target="tpu_custom_call" | custom-call | tf_op jit(solution)/shard_map/finish/pallas_call | solution.py:282
  (6 shorter events, 0.0 us)
Async XLA Ops:
  0.6 3.0 %copy-start = (f32[1,256,256]{2,1,0:T(8,128)S(1)}, f32[1,256,256]{2,1,0:T(8,128)}, u32[]{:S(2)}) copy-start(f32[1,256,256]{2,1,0:T(8,128)} %diag_ref.3) | copy-start | bytes 786436
  0.6 3.0 %copy-start.1 = (f32[512,256]{1,0:T(8,128)S(1)}, f32[512,256]{1,0:T(8,128)}, u32[]{:S(2)}) copy-start(f32[512,256]{1,0:T(8,128)} %cross_ref.1) | copy-start | bytes 1572868
  0.6 15.1 %collective-permute-start.1 = (bf16[512,512]{1,0:T(8,128)(2,1)}, bf16[512,512]{1,0:T(8,128)(2,1)S(1)}, u32[]{:S(2)}, u32[]{:S(2)}) collective-permute-start(bf16[512,512]{1,0:T(8,128)(2,1)} %top_hbm.1), channel_id=1, source_target_pairs={{2,0},{3,1},{0,2},{1,3},{6,4},{7,5},{4,6},{5,7},{10,8},{11,9},{8,1... | collective-permute-start | bytes 1572872 | tf_op jit(solution)/shard_map/ppermute | solution.py:300
  4.5 11.3 %collective-permute-start.4 = (bf16[512,256]{1,0:T(8,128)(2,1)S(1)}, bf16[512,256]{1,0:T(8,128)(2,1)S(1)}, u32[]{:S(2)}, u32[]{:S(2)}) collective-permute-start(bf16[512,256]{1,0:T(8,128)(2,1)S(1)} %panel.1.panel_ref.refs_4_), channel_id=1, source_target_pairs={{12,0},{8,4},{4,8},{0,12},{13,1},{9,5},{5,9},{1,13},{14,2},{10,6},... | collective-permute-start | bytes 786440 | tf_op jit(solution)/shard_map/ppermute | solution.py:300
  8.1 11.8 %collective-permute-start.3 = (bf16[512,256]{1,0:T(8,128)(2,1)S(1)}, bf16[512,256]{1,0:T(8,128)(2,1)S(1)}, u32[]{:S(2)}, u32[]{:S(2)}) collective-permute-start(bf16[512,256]{1,0:T(8,128)(2,1)S(1)} %panel.1.panel_ref.refs_4_), channel_id=1, source_target_pairs={{4,0},{0,4},{12,8},{8,12},{5,1},{1,5},{13,9},{9,13},{6,2},{2,6},{1... | collective-permute-start | bytes 786440 | tf_op jit(solution)/shard_map/ppermute | solution.py:300
  9.2 10.8 %collective-permute-start = (bf16[512,512]{1,0:T(8,128)(2,1)S(1)}, bf16[512,512]{1,0:T(8,128)(2,1)S(1)}, u32[]{:S(2)}, u32[]{:S(2)}) collective-permute-start(bf16[512,512]{1,0:T(8,128)(2,1)S(1)} %get-tuple-element.8.refs_0_), channel_id=1, source_target_pairs={{1,0},{0,1},{3,2},{2,3},{5,4},{4,5},{7,6},{6,7},{9,8},{8,9},{11,10... | collective-permute-start | bytes 1572872 | tf_op jit(solution)/shard_map/ppermute | solution.py:300
  15.8 4.2 %collective-permute-start.2 = (bf16[512,512]{1,0:T(8,128)(2,1)S(1)}, bf16[512,512]{1,0:T(8,128)(2,1)S(1)}, u32[]{:S(2)}, u32[]{:S(2)}) collective-permute-start(bf16[512,512]{1,0:T(8,128)(2,1)S(1)} %relay.4.refs_1_.refs_2_), channel_id=1, source_target_pairs={{1,0},{0,1},{3,2},{2,3},{5,4},{4,5},{7,6},{6,7},{9,8},{8,9},{11,10... | collective-permute-start | bytes 1572872 | tf_op jit(solution)/shard_map/ppermute | solution.py:300
  15.8 11.5 %collective-permute-start.5 = (bf16[512,256]{1,0:T(8,128)(2,1)S(1)}, bf16[512,256]{1,0:T(8,128)(2,1)S(1)}, u32[]{:S(2)}, u32[]{:S(2)}) collective-permute-start(bf16[512,256]{1,0:T(8,128)(2,1)S(1)} %relay.5.refs_1_.refs_6_), channel_id=1, source_target_pairs={{4,0},{0,4},{12,8},{8,12},{5,1},{1,5},{13,9},{9,13},{6,2},{2,6},{1... | collective-permute-start | bytes 786440 | tf_op jit(solution)/shard_map/ppermute | solution.py:300
  20.9 6.7 %collective-permute-start.6 = (bf16[64,640]{1,0:T(8,128)(2,1)S(1)}, bf16[64,640]{1,0:T(8,128)(2,1)S(1)}, u32[]{:S(2)}, u32[]{:S(2)}) collective-permute-start(bf16[64,640]{1,0:T(8,128)(2,1)S(1)} %get-tuple-element.13.early_ref), channel_id=1, source_target_pairs={{8,0},{12,4},{0,8},{4,12},{9,1},{13,5},{1,9},{5,13},{10,2},{14,6},... | collective-permute-start | bytes 245768 | tf_op jit(solution)/shard_map/ppermute | solution.py:300
  27.7 4.5 %collective-permute-start.7 = (bf16[64,640]{1,0:T(8,128)(2,1)S(1)}, bf16[64,640]{1,0:T(8,128)(2,1)S(1)}, u32[]{:S(2)}, u32[]{:S(2)}) collective-permute-start(bf16[64,640]{1,0:T(8,128)(2,1)S(1)} %add_convert_fusion.refs_0_), channel_id=1, source_target_pairs={{4,0},{0,4},{12,8},{8,12},{5,1},{1,5},{13,9},{9,13},{6,2},{2,6},{1... | collective-permute-start | bytes 245768 | tf_op jit(solution)/shard_map/ppermute | solution.py:300

commit v32 on v28

--- a/solution.py
+++ b/solution.py
@@ -134,31 +134,43 @@
     return total
 
 
-def early_kernel(n, *refs):
-    tops, panels = refs[:n], refs[n:n + n // 2 + 1]
-    turned_ref, update_ref, panel_buf = refs[n + n // 2 + 1:]
-
-    def run(pairs):
-        store_upper(update_ref, dot(turned_ref[...], product(pairs).astype(jnp.bfloat16)))
-
-    matched(n, tops, panels, panel_buf, run)
-
-
-def early_share(tops, panels, turned):
+def lefts_kernel(n, *refs):
+    tops, (turned_ref, lefts_ref) = refs[:n], refs[n:]
+    held = [(0, 0)] + [(d, 1) for d in range(n // PAIR)]
+    for p, (d, f) in enumerate(held):
+        place = place_of(n, d, f)
+        for t in range(n):
+            @pl.when(place == t)
+            def _():
+                lefts_ref[p] = dot(turned_ref[...], tops[t][...]).astype(jnp.bfloat16)
+
+
+def early_lefts(tops, turned):
     n = len(tops)
-    rows, width = panels[0].shape
-    return pl.pallas_call(
-        functools.partial(early_kernel, n),
+    return pl.pallas_call(
+        functools.partial(lefts_kernel, n),
+        out_shape=jax.ShapeDtypeStruct((n // 2 + 1,) + turned.shape, jnp.bfloat16),
+        in_specs=[VMEM] * (n + 1),
+        out_specs=VMEM,
+        compiler_params=PARAMS,
+        name="lefts",
+    )(*tops, turned)
+
+
+def early_kernel(lefts_ref, *refs):
+    store_upper(refs[-1], last_terms(lefts_ref, refs[:-1]))
+
+
+def early_share(lefts, panels):
+    width = panels[0].shape[1]
+    return pl.pallas_call(
+        early_kernel,
         out_shape=jax.ShapeDtypeStruct((width // 4, 5 * (width // 2)), jnp.bfloat16),
-        in_specs=[VMEM] * (n + len(panels) + 1),
-        out_specs=VMEM,
-        scratch_shapes=[pltpu.VMEM((n, rows, width), jnp.bfloat16)],
-        compiler_params=PARAMS,
-        cost_estimate=pl.CostEstimate(
-            flops=2 * n * rows * rows * width, bytes_accessed=2 * n * rows * (rows + width), transcendentals=0
-        ),
+        in_specs=[VMEM] * (1 + len(panels)),
+        out_specs=VMEM,
+        compiler_params=PARAMS,
         name="early",
-    )(*tops, *panels, turned)
+    )(lefts, *panels)
 
 
 def stage_kernel(panel_ref, top_hbm, turned_ref, top_ref, sem):
@@ -181,51 +193,55 @@
 
 
 def choose_kernel(n, *refs):
-    tops, chosen_ref = refs[:n], refs[n]
+    tops, (turned_ref, chosen_ref, left_ref) = refs[:n], refs[n:]
     for d in range(1, n // PAIR):
         place = place_of(n, d, 0)
         for t in range(n):
             @pl.when(place == t)
             def _():
                 chosen_ref[d - 1] = tops[t][...]
-
-
-def choose(tops):
+        left_ref[d - 1] = dot(turned_ref[...], chosen_ref[d - 1]).astype(jnp.bfloat16)
+
+
+def choose(tops, turned):
     n = len(tops)
     return pl.pallas_call(
         functools.partial(choose_kernel, n),
-        out_shape=jax.ShapeDtypeStruct((n // 2 - 1,) + tops[0].shape, jnp.bfloat16),
-        in_specs=[VMEM] * n,
-        out_specs=VMEM,
+        out_shape=(
+            jax.ShapeDtypeStruct((n // 2 - 1,) + tops[0].shape, jnp.bfloat16),
+            jax.ShapeDtypeStruct((n // 2 - 1,) + turned.shape, jnp.bfloat16),
+        ),
+        in_specs=[VMEM] * (n + 1),
+        out_specs=(VMEM, VMEM),
         compiler_params=PARAMS,
         name="choose",
-    )(*tops)
-
-
-def last_terms(chosen_ref, panels):
-    total = dot(chosen_ref[0], panels[0][...])
+    )(*tops, turned)
+
+
+def last_terms(left_ref, panels):
+    total = dot(left_ref[0], panels[0][...])
     for d, panel in enumerate(panels[1:], 1):
-        total += dot(chosen_ref[d], panel[...])
+        total += dot(left_ref[d], panel[...])
     return total
 
 
-def late_kernel(chosen_ref, turned_ref, early_ref, *refs):
+def late_kernel(left_ref, early_ref, *refs):
     panels, update_ref = refs[:-1], refs[-1]
-    update = dot(turned_ref[...], last_terms(chosen_ref, panels).astype(jnp.bfloat16))
+    update = last_terms(left_ref, panels)
     if len(panels) == 1:
         update += update.T
     store_upper(update_ref, update, early_ref)
 
 
-def late_share(chosen, turned, panels, early):
+def late_share(left, panels, early):
     return pl.pallas_call(
         late_kernel,
         out_shape=jax.ShapeDtypeStruct(early.shape, jnp.float32),
-        in_specs=[VMEM] * (3 + len(panels)),
+        in_specs=[VMEM] * (2 + len(panels)),
         out_specs=VMEM,
         compiler_params=PARAMS,
         name="late",
-    )(chosen, turned, early, *panels)
+    )(left, early, *panels)
 
 
 def cross_kernel(n, *refs):
@@ -316,18 +332,20 @@
     crossed = [from_pair(factor_panel, "prow", d, 1) for d in range(1, pairs)]
     turned, inverse_top = stage(factor_panel, inverse_top)
     near = [after(block, turned) for block in near]
-    crossed = [after(block, near[0], beside, cost=HOP_COST) for block in crossed]
+    crossed = [after(block, near[0], cost=HOP_COST) for block in crossed]
     swapped = [mate(block, "prow") for block in crossed]
 
     tops = [inverse_top, mate(inverse_top, "pcol")]
     for block in near:
         tops += [block, mate(block, "pcol")]
 
+    lefts = early_lefts(tops, turned)
+    beside = after(beside, lefts, *crossed, cost=2 * HOP_COST)
     panels = [factor_panel, beside] + crossed
-    early = early_share(tops, panels, turned)
-    chosen = choose(tops)
-    crossing = [after(from_pair(early, "prow", d, 1), swapped[-1]) for d in range(1, pairs)]
-    late = late_share(chosen, turned, swapped, early)
+    early = early_share(lefts, panels)
+    chosen, left = choose(tops, turned)
+    crossing = [after(from_pair(early, "prow", d, 0), swapped[-1]) for d in range(1, pairs)]
+    late = late_share(left, swapped, early)
     parts = [late] + crossing
     if pairs > 2:
         rest = (late - early.astype(jnp.float32)).astype(jnp.bfloat16)

time: 34.2 us -> 33.2 us (0.971)
  waiting for transfers between devices: 16.8 us -> 12.8 us
  starting transfers between devices: 10.6 us -> 13.1 us
  Pallas kernels: 5.86 us -> 6.32 us
    ppermute x8, waiting for transfers between devices: 16.8 us -> 12.8 us  [from_pair(): return lax.ppermute(block, axis, moves)]
    ppermute x8, starting transfers between devices: 10.6 us -> 13.1 us  [from_pair(): return lax.ppermute(block, axis, moves)]
    pallas_call x2 -> x3, Pallas kernels: 0.94 us -> 1.71 us  [the longest x1 0.94 us: early_lefts(): pl.pallas_call(functools.partial(lefts_kernel, n), out_shape=jax.ShapeDty...]
  transfers between devices with their start and end apart: 8 -> 8, of which waited for: 5 -> 3; matrix products, arithmetic and copies ran while one was open for 0% -> 0% of each run, Pallas kernels for 15% -> 17%
where the time goes in v32:
time: 33.2 us; the launch traced here: 33 us
  starting transfers between devices  13.1 us (39%)
  waiting for transfers between devices  12.8 us (39%)
  Pallas kernels  6.32 us (19%)
  between operations  0.75 us (2%)
    ppermute x8, starting transfers between devices, from_pair(): return lax.ppermute(block, axis, moves)  13.1 us
    ppermute x8, waiting for transfers between devices, from_pair(): return lax.ppermute(block, axis, moves)  12.8 us
    pallas_call x1, Pallas kernels, cross_result(): pl.pallas_call(functools.partial(cross_kernel, n), out_shape=jax.ShapeDty...  1.51 us
    pallas_call x1, Pallas kernels, stage(): pl.pallas_call(stage_kernel, out_shape=(pltpu.VMEM(panel.shape[::-1], pan...  1.07 us
    pallas_call x1, Pallas kernels, early_lefts(): pl.pallas_call(functools.partial(lefts_kernel, n), out_shape=jax.ShapeDty...  0.94 us
    pallas_call x1, Pallas kernels, finish(): pl.pallas_call(finish_kernel, out_shape=jax.ShapeDtypeStruct(diag_inverse...  0.84 us
    pallas_call x1, Pallas kernels, build_panel(): pl.pallas_call(panel_kernel, out_shape=pltpu.VMEM(cross_blocks.shape, jnp...  0.81 us
  transfers between devices with their start and end apart: 8, of which 3 were waited for; matrix products, arithmetic and copies ran while one was open for 0% of the time, Pallas kernels for 17%

profile of v32, /device:TPU:0, one launch (start us, length us, event | category | flops | bytes accessed | tf_op | source)
XLA Modules:
  0.0 33.0 jit_solution(15524488122393523580)
XLA Ops:
  0.6 0.0 copy-start
  0.6 0.0 copy-start.1
  0.6 3.0 %collective-permute-start.1 = (bf16[512,512]{1,0:T(8,128)(2,1)}, bf16[512,512]{1,0:T(8,128)(2,1)S(1)}, u32[]{:S(2)}, u32[]{:S(2)}) collective-permute-start(bf16[512,512]{1,0:T(8,128)(2,1)} %top_hbm.1), channel_id=1, source_target_pairs={{2,0},{3,1},{0,2},{1,3},{6,4},{7,5},{4,6},{5,7},{10,8},{11,9},{8,1... | collective-permute-start | bytes 1572872 | tf_op jit(solution)/shard_map/ppermute | solution.py:324
  3.7 0.0 copy-done
  3.7 0.0 copy-done.1
  3.7 0.8 %panel.1.panel_ref.refs_4_.refs_0_ = bf16[512,256]{1,0:T(8,128)(2,1)S(1)} custom-call(s32[2]{0:T(128)} %bitcast.1, f32[512,256]{1,0:T(8,128)S(1)} %copy-done.1, f32[1,256,256]{2,1,0:T(8,128)S(1)} %copy-done, f32[8,128]{1,0:T(8,128)S(1)} %token_.1.token_ref), custom_call_target="tpu_custom_call" | custom-call | tf_op jit(solution)/shard_map/panel/pallas_call | solution.py:60
  4.5 3.7 %collective-permute-start.4 = (bf16[512,256]{1,0:T(8,128)(2,1)S(1)}, bf16[512,256]{1,0:T(8,128)(2,1)S(1)}, u32[]{:S(2)}, u32[]{:S(2)}) collective-permute-start(bf16[512,256]{1,0:T(8,128)(2,1)S(1)} %panel.1.panel_ref.refs_4_.refs_0_), channel_id=1, source_target_pairs={{12,0},{8,4},{4,8},{0,12},{13,1},{9,5},{5,9},{1,13},{14,2},{10,6},... | collective-permute-start | bytes 786440 | tf_op jit(solution)/shard_map/ppermute | solution.py:324
  8.1 0.0 collective-permute-start.3
  8.1 1.1 %stage.1 = (bf16[256,512]{1,0:T(8,128)(2,1)S(1)}, bf16[512,512]{1,0:T(8,128)(2,1)S(1)}) custom-call(bf16[512,256]{1,0:T(8,128)(2,1)S(1)} %panel.1.panel_ref.refs_4_.refs_0_, bf16[512,512]{1,0:T(8,128)(2,1)} %top_hbm.1), custom_call_target="tpu_custom_call" | custom-call | tf_op jit(solution)/shard_map/stage/pallas_call | solution.py:184
  9.2 0.1 collective-permute-start
  9.3 6.5 %collective-permute-done.1.refs_0_ = bf16[512,512]{1,0:T(8,128)(2,1)S(1)} collective-permute-done((bf16[512,512]{1,0:T(8,128)(2,1)}, bf16[512,512]{1,0:T(8,128)(2,1)S(1)}, u32[]{:S(2)}, u32[]{:S(2)}) %collective-permute-start.1) | collective-permute-done | bytes 524320 | tf_op jit(solution)/shard_map/ppermute | solution.py:324
  15.8 0.0 collective-permute-start.2
  15.8 0.0 collective-permute-done.4.refs_0_
  15.8 3.7 %collective-permute-start.5 = (bf16[512,256]{1,0:T(8,128)(2,1)S(1)}, bf16[512,256]{1,0:T(8,128)(2,1)S(1)}, u32[]{:S(2)}, u32[]{:S(2)}) collective-permute-start(bf16[512,256]{1,0:T(8,128)(2,1)S(1)} %relay.5.refs_2_.refs_6_), channel_id=1, source_target_pairs={{4,0},{0,4},{12,8},{8,12},{5,1},{1,5},{13,9},{9,13},{6,2},{2,6},{1... | collective-permute-start | bytes 786440 | tf_op jit(solution)/shard_map/ppermute | solution.py:324
  19.5 0.0 collective-permute-done.refs_1_
  19.5 0.0 collective-permute-done.2.refs_3_
  19.5 0.9 %lefts.1.refs_1_.lefts_ref = bf16[3,256,512]{2,1,0:T(8,128)(2,1)S(1)} custom-call(bf16[512,512]{1,0:T(8,128)(2,1)S(1)} %get-tuple-element.6.refs_0_, bf16[512,512]{1,0:T(8,128)(2,1)S(1)} %collective-permute-done.refs_1_, bf16[512,512]{1,0:T(8,128)(2,1)S(1)} %relay.4.refs_2_.refs_1_, bf16[512,512]{1,0:T(8,128)(2,1)S(1)} %collective-permute-done.2.refs_3_, ...), custom_call_target="tpu_custom_call" | custom-call | tf_op jit(solution)/shard_map/lefts/pallas_call | solution.py:150
  20.5 0.0 collective-permute-done.3.refs_0_
  20.5 0.4 %early.1.early_ref = bf16[64,640]{1,0:T(8,128)(2,1)S(1)} custom-call(bf16[3,256,512]{2,1,0:T(8,128)(2,1)S(1)} %lefts.1.refs_1_.lefts_ref, bf16[512,256]{1,0:T(8,128)(2,1)S(1)} %panel.1.panel_ref.refs_4_.refs_0_, bf16[512,256]{1,0:T(8,128)(2,1)S(1)} %relay.6.refs_5_.refs_1_, bf16[512,256]{1,0:T(8,128)(2,1)S(1)} %relay.5.refs_2_.refs_6_), custom_call_target="tpu_custom_call" | custom-call | tf_op jit(solution)/shard_map/early/pallas_call | solution.py:166
  20.9 1.1 %collective-permute-start.6 = (bf16[64,640]{1,0:T(8,128)(2,1)S(1)}, bf16[64,640]{1,0:T(8,128)(2,1)S(1)}, u32[]{:S(2)}, u32[]{:S(2)}) collective-permute-start(bf16[64,640]{1,0:T(8,128)(2,1)S(1)} %early.1.early_ref), channel_id=1, source_target_pairs={{8,0},{12,4},{0,8},{4,12},{9,1},{13,5},{1,9},{5,13},{10,2},{14,6},... | collective-permute-start | bytes 245768 | tf_op jit(solution)/shard_map/ppermute | solution.py:324
  22.0 0.3 choose.1
  22.4 4.9 %collective-permute-done.5.refs_8_.refs_0_.refs_1_ = bf16[512,256]{1,0:T(8,128)(2,1)S(1)} collective-permute-done((bf16[512,256]{1,0:T(8,128)(2,1)S(1)}, bf16[512,256]{1,0:T(8,128)(2,1)S(1)}, u32[]{:S(2)}, u32[]{:S(2)}) %collective-permute-start.5) | collective-permute-done | bytes 262176 | tf_op jit(solution)/shard_map/ppermute | solution.py:324
  27.3 0.4 %late.1 = f32[64,640]{1,0:T(8,128)S(1)} custom-call(bf16[1,256,512]{2,1,0:T(8,128)(2,1)S(1)} %get-tuple-element.9.left_ref, bf16[64,640]{1,0:T(8,128)(2,1)S(1)} %early.1.early_ref, bf16[512,256]{1,0:T(8,128)(2,1)S(1)} %collective-permute-done.5.refs_8_.refs_0_.refs_1_), custom_call_target="tpu_custom_call" | custom-call | tf_op jit(solution)/shard_map/late/pallas_call | solution.py:237
  27.6 0.0 collective-permute-done.6.refs_0_
  27.7 1.5 %collective-permute-start.7 = (bf16[64,640]{1,0:T(8,128)(2,1)S(1)}, bf16[64,640]{1,0:T(8,128)(2,1)S(1)}, u32[]{:S(2)}, u32[]{:S(2)}) collective-permute-start(bf16[64,640]{1,0:T(8,128)(2,1)S(1)} %add_convert_fusion.refs_0_), channel_id=1, source_target_pairs={{4,0},{0,4},{12,8},{8,12},{5,1},{1,5},{13,9},{9,13},{6,2},{2,6},{1... | collective-permute-start | bytes 245768 | tf_op jit(solution)/shard_map/ppermute | solution.py:324
  29.2 1.5 %cross.1 = f32[512,256]{1,0:T(8,128)} custom-call(bf16[512,512]{1,0:T(8,128)(2,1)S(1)} %get-tuple-element.6.refs_0_, bf16[512,512]{1,0:T(8,128)(2,1)S(1)} %collective-permute-done.refs_1_, bf16[512,512]{1,0:T(8,128)(2,1)S(1)} %relay.4.refs_2_.refs_1_, bf16[512,512]{1,0:T(8,128)(2,1)S(1)} %collective-permute-done.2.refs_3_, ...), custom_call_target="tpu_custom_call" | custom-call | flops 536870912 | bytes 524288 | tf_op jit(solution)/shard_map/cross/pallas_call | solution.py:260
  30.7 1.5 %collective-permute-done.7.refs_1_ = bf16[64,640]{1,0:T(8,128)(2,1)S(1)} collective-permute-done((bf16[64,640]{1,0:T(8,128)(2,1)S(1)}, bf16[64,640]{1,0:T(8,128)(2,1)S(1)}, u32[]{:S(2)}, u32[]{:S(2)}) %collective-permute-start.7) | collective-permute-done | bytes 81952 | tf_op jit(solution)/shard_map/ppermute | solution.py:324
  32.2 0.8 %finish.1 = f32[1,256,256]{2,1,0:T(8,128)} custom-call(f32[1,256,256]{2,1,0:T(8,128)S(1)} %copy-done, bf16[64,640]{1,0:T(8,128)(2,1)S(1)} %add_convert_fusion.refs_0_, bf16[64,640]{1,0:T(8,128)(2,1)S(1)} %collective-permute-done.7.refs_1_), custom_call_target="tpu_custom_call" | custom-call | tf_op jit(solution)/shard_map/finish/pallas_call | solution.py:306
  (6 shorter events, 0.0 us)
Async XLA Ops:
  0.6 3.0 %copy-start = (f32[1,256,256]{2,1,0:T(8,128)S(1)}, f32[1,256,256]{2,1,0:T(8,128)}, u32[]{:S(2)}) copy-start(f32[1,256,256]{2,1,0:T(8,128)} %diag_ref.3) | copy-start | bytes 786436
  0.6 3.0 %copy-start.1 = (f32[512,256]{1,0:T(8,128)S(1)}, f32[512,256]{1,0:T(8,128)}, u32[]{:S(2)}) copy-start(f32[512,256]{1,0:T(8,128)} %cross_ref.1) | copy-start | bytes 1572868
  0.6 15.1 %collective-permute-start.1 = (bf16[512,512]{1,0:T(8,128)(2,1)}, bf16[512,512]{1,0:T(8,128)(2,1)S(1)}, u32[]{:S(2)}, u32[]{:S(2)}) collective-permute-start(bf16[512,512]{1,0:T(8,128)(2,1)} %top_hbm.1), channel_id=1, source_target_pairs={{2,0},{3,1},{0,2},{1,3},{6,4},{7,5},{4,6},{5,7},{10,8},{11,9},{8,1... | collective-permute-start | bytes 1572872 | tf_op jit(solution)/shard_map/ppermute | solution.py:324
  4.5 11.3 %collective-permute-start.4 = (bf16[512,256]{1,0:T(8,128)(2,1)S(1)}, bf16[512,256]{1,0:T(8,128)(2,1)S(1)}, u32[]{:S(2)}, u32[]{:S(2)}) collective-permute-start(bf16[512,256]{1,0:T(8,128)(2,1)S(1)} %panel.1.panel_ref.refs_4_.refs_0_), channel_id=1, source_target_pairs={{12,0},{8,4},{4,8},{0,12},{13,1},{9,5},{5,9},{1,13},{14,2},{10,6},... | collective-permute-start | bytes 786440 | tf_op jit(solution)/shard_map/ppermute | solution.py:324
  8.1 12.3 %collective-permute-start.3 = (bf16[512,256]{1,0:T(8,128)(2,1)S(1)}, bf16[512,256]{1,0:T(8,128)(2,1)S(1)}, u32[]{:S(2)}, u32[]{:S(2)}) collective-permute-start(bf16[512,256]{1,0:T(8,128)(2,1)S(1)} %panel.1.panel_ref.refs_4_.refs_0_), channel_id=1, source_target_pairs={{4,0},{0,4},{12,8},{8,12},{5,1},{1,5},{13,9},{9,13},{6,2},{2,6},{1... | collective-permute-start | bytes 786440 | tf_op jit(solution)/shard_map/ppermute | solution.py:324
  9.2 10.3 %collective-permute-start = (bf16[512,512]{1,0:T(8,128)(2,1)S(1)}, bf16[512,512]{1,0:T(8,128)(2,1)S(1)}, u32[]{:S(2)}, u32[]{:S(2)}) collective-permute-start(bf16[512,512]{1,0:T(8,128)(2,1)S(1)} %get-tuple-element.6.refs_0_), channel_id=1, source_target_pairs={{1,0},{0,1},{3,2},{2,3},{5,4},{4,5},{7,6},{6,7},{9,8},{8,9},{11,10... | collective-permute-start | bytes 1572872 | tf_op jit(solution)/shard_map/ppermute | solution.py:324
  15.8 3.7 %collective-permute-start.2 = (bf16[512,512]{1,0:T(8,128)(2,1)S(1)}, bf16[512,512]{1,0:T(8,128)(2,1)S(1)}, u32[]{:S(2)}, u32[]{:S(2)}) collective-permute-start(bf16[512,512]{1,0:T(8,128)(2,1)S(1)} %relay.4.refs_2_.refs_1_), channel_id=1, source_target_pairs={{1,0},{0,1},{3,2},{2,3},{5,4},{4,5},{7,6},{6,7},{9,8},{8,9},{11,10... | collective-permute-start | bytes 1572872 | tf_op jit(solution)/shard_map/ppermute | solution.py:324
  15.8 11.5 %collective-permute-start.5 = (bf16[512,256]{1,0:T(8,128)(2,1)S(1)}, bf16[512,256]{1,0:T(8,128)(2,1)S(1)}, u32[]{:S(2)}, u32[]{:S(2)}) collective-permute-start(bf16[512,256]{1,0:T(8,128)(2,1)S(1)} %relay.5.refs_2_.refs_6_), channel_id=1, source_target_pairs={{4,0},{0,4},{12,8},{8,12},{5,1},{1,5},{13,9},{9,13},{6,2},{2,6},{1... | collective-permute-start | bytes 786440 | tf_op jit(solution)/shard_map/ppermute | solution.py:324
  20.9 6.7 %collective-permute-start.6 = (bf16[64,640]{1,0:T(8,128)(2,1)S(1)}, bf16[64,640]{1,0:T(8,128)(2,1)S(1)}, u32[]{:S(2)}, u32[]{:S(2)}) collective-permute-start(bf16[64,640]{1,0:T(8,128)(2,1)S(1)} %early.1.early_ref), channel_id=1, source_target_pairs={{8,0},{12,4},{0,8},{4,12},{9,1},{13,5},{1,9},{5,13},{10,2},{14,6},... | collective-permute-start | bytes 245768 | tf_op jit(solution)/shard_map/ppermute | solution.py:324
  27.7 4.5 %collective-permute-start.7 = (bf16[64,640]{1,0:T(8,128)(2,1)S(1)}, bf16[64,640]{1,0:T(8,128)(2,1)S(1)}, u32[]{:S(2)}, u32[]{:S(2)}) collective-permute-start(bf16[64,640]{1,0:T(8,128)(2,1)S(1)} %add_convert_fusion.refs_0_), channel_id=1, source_target_pairs={{4,0},{0,4},{12,8},{8,12},{5,1},{1,5},{13,9},{9,13},{6,2},{2,6},{1... | collective-permute-start | bytes 245768 | tf_op jit(solution)/shard_map/ppermute | solution.py:324

commit v33 on v32

--- a/solution.py
+++ b/solution.py
@@ -229,7 +229,7 @@
     panels, update_ref = refs[:-1], refs[-1]
     update = last_terms(left_ref, panels)
     if len(panels) == 1:
-        update += update.T
+        update += update.astype(jnp.bfloat16).T.astype(jnp.float32)
     store_upper(update_ref, update, early_ref)
 
 

time: 33.2 us -> 33.2 us (level)
  no operation moved by 1% of the time
where the time goes in v33:
time: 33.2 us; the launch traced here: 33 us
  starting transfers between devices  13.1 us (39%)
  waiting for transfers between devices  12.9 us (39%)
  Pallas kernels  6.33 us (19%)
  between operations  0.75 us (2%)
    ppermute x8, starting transfers between devices, from_pair(): return lax.ppermute(block, axis, moves)  13.1 us
    ppermute x8, waiting for transfers between devices, from_pair(): return lax.ppermute(block, axis, moves)  12.9 us
    pallas_call x1, Pallas kernels, cross_result(): pl.pallas_call(functools.partial(cross_kernel, n), out_shape=jax.ShapeDty...  1.51 us
    pallas_call x1, Pallas kernels, stage(): pl.pallas_call(stage_kernel, out_shape=(pltpu.VMEM(panel.shape[::-1], pan...  1.07 us
    pallas_call x1, Pallas kernels, early_lefts(): pl.pallas_call(functools.partial(lefts_kernel, n), out_shape=jax.ShapeDty...  0.94 us
    pallas_call x1, Pallas kernels, finish(): pl.pallas_call(finish_kernel, out_shape=jax.ShapeDtypeStruct(diag_inverse...  0.84 us
    pallas_call x1, Pallas kernels, build_panel(): pl.pallas_call(panel_kernel, out_shape=pltpu.VMEM(cross_blocks.shape, jnp...  0.81 us
  transfers between devices with their start and end apart: 8, of which 3 were waited for; matrix products, arithmetic and copies ran while one was open for 0% of the time, Pallas kernels for 17%

profile of v33, /device:TPU:0, one launch (start us, length us, event | category | flops | bytes accessed | tf_op | source)
XLA Modules:
  0.0 33.0 jit_solution(8717072621383803383)
XLA Ops:
  0.6 0.0 copy-start
  0.6 0.0 copy-start.1
  0.6 3.0 %collective-permute-start.1 = (bf16[512,512]{1,0:T(8,128)(2,1)}, bf16[512,512]{1,0:T(8,128)(2,1)S(1)}, u32[]{:S(2)}, u32[]{:S(2)}) collective-permute-start(bf16[512,512]{1,0:T(8,128)(2,1)} %top_hbm.1), channel_id=1, source_target_pairs={{2,0},{3,1},{0,2},{1,3},{6,4},{7,5},{4,6},{5,7},{10,8},{11,9},{8,1... | collective-permute-start | bytes 1572872 | tf_op jit(solution)/shard_map/ppermute | solution.py:324
  3.7 0.0 copy-done
  3.7 0.0 copy-done.1
  3.7 0.8 %panel.1.panel_ref.refs_4_.refs_0_ = bf16[512,256]{1,0:T(8,128)(2,1)S(1)} custom-call(s32[2]{0:T(128)} %bitcast.1, f32[512,256]{1,0:T(8,128)S(1)} %copy-done.1, f32[1,256,256]{2,1,0:T(8,128)S(1)} %copy-done, f32[8,128]{1,0:T(8,128)S(1)} %token_.1.token_ref), custom_call_target="tpu_custom_call" | custom-call | tf_op jit(solution)/shard_map/panel/pallas_call | solution.py:60
  4.5 3.7 %collective-permute-start.4 = (bf16[512,256]{1,0:T(8,128)(2,1)S(1)}, bf16[512,256]{1,0:T(8,128)(2,1)S(1)}, u32[]{:S(2)}, u32[]{:S(2)}) collective-permute-start(bf16[512,256]{1,0:T(8,128)(2,1)S(1)} %panel.1.panel_ref.refs_4_.refs_0_), channel_id=1, source_target_pairs={{12,0},{8,4},{4,8},{0,12},{13,1},{9,5},{5,9},{1,13},{14,2},{10,6},... | collective-permute-start | bytes 786440 | tf_op jit(solution)/shard_map/ppermute | solution.py:324
  8.1 0.0 collective-permute-start.3
  8.1 1.1 %stage.1 = (bf16[256,512]{1,0:T(8,128)(2,1)S(1)}, bf16[512,512]{1,0:T(8,128)(2,1)S(1)}) custom-call(bf16[512,256]{1,0:T(8,128)(2,1)S(1)} %panel.1.panel_ref.refs_4_.refs_0_, bf16[512,512]{1,0:T(8,128)(2,1)} %top_hbm.1), custom_call_target="tpu_custom_call" | custom-call | tf_op jit(solution)/shard_map/stage/pallas_call | solution.py:184
  9.2 0.1 collective-permute-start
  9.3 6.5 %collective-permute-done.1.refs_0_ = bf16[512,512]{1,0:T(8,128)(2,1)S(1)} collective-permute-done((bf16[512,512]{1,0:T(8,128)(2,1)}, bf16[512,512]{1,0:T(8,128)(2,1)S(1)}, u32[]{:S(2)}, u32[]{:S(2)}) %collective-permute-start.1) | collective-permute-done | bytes 524320 | tf_op jit(solution)/shard_map/ppermute | solution.py:324
  15.8 0.0 collective-permute-start.2
  15.8 0.0 collective-permute-done.4.refs_0_
  15.8 3.7 %collective-permute-start.5 = (bf16[512,256]{1,0:T(8,128)(2,1)S(1)}, bf16[512,256]{1,0:T(8,128)(2,1)S(1)}, u32[]{:S(2)}, u32[]{:S(2)}) collective-permute-start(bf16[512,256]{1,0:T(8,128)(2,1)S(1)} %relay.5.refs_2_.refs_6_), channel_id=1, source_target_pairs={{4,0},{0,4},{12,8},{8,12},{5,1},{1,5},{13,9},{9,13},{6,2},{2,6},{1... | collective-permute-start | bytes 786440 | tf_op jit(solution)/shard_map/ppermute | solution.py:324
  19.5 0.0 collective-permute-done.refs_1_
  19.5 0.0 collective-permute-done.2.refs_3_
  19.5 0.9 %lefts.1.refs_1_.lefts_ref = bf16[3,256,512]{2,1,0:T(8,128)(2,1)S(1)} custom-call(bf16[512,512]{1,0:T(8,128)(2,1)S(1)} %get-tuple-element.6.refs_0_, bf16[512,512]{1,0:T(8,128)(2,1)S(1)} %collective-permute-done.refs_1_, bf16[512,512]{1,0:T(8,128)(2,1)S(1)} %relay.4.refs_2_.refs_1_, bf16[512,512]{1,0:T(8,128)(2,1)S(1)} %collective-permute-done.2.refs_3_, ...), custom_call_target="tpu_custom_call" | custom-call | tf_op jit(solution)/shard_map/lefts/pallas_call | solution.py:150
  20.5 0.0 collective-permute-done.3.refs_0_
  20.5 0.4 %early.1.early_ref = bf16[64,640]{1,0:T(8,128)(2,1)S(1)} custom-call(bf16[3,256,512]{2,1,0:T(8,128)(2,1)S(1)} %lefts.1.refs_1_.lefts_ref, bf16[512,256]{1,0:T(8,128)(2,1)S(1)} %panel.1.panel_ref.refs_4_.refs_0_, bf16[512,256]{1,0:T(8,128)(2,1)S(1)} %relay.6.refs_5_.refs_1_, bf16[512,256]{1,0:T(8,128)(2,1)S(1)} %relay.5.refs_2_.refs_6_), custom_call_target="tpu_custom_call" | custom-call | tf_op jit(solution)/shard_map/early/pallas_call | solution.py:166
  20.9 1.1 %collective-permute-start.6 = (bf16[64,640]{1,0:T(8,128)(2,1)S(1)}, bf16[64,640]{1,0:T(8,128)(2,1)S(1)}, u32[]{:S(2)}, u32[]{:S(2)}) collective-permute-start(bf16[64,640]{1,0:T(8,128)(2,1)S(1)} %early.1.early_ref), channel_id=1, source_target_pairs={{8,0},{12,4},{0,8},{4,12},{9,1},{13,5},{1,9},{5,13},{10,2},{14,6},... | collective-permute-start | bytes 245768 | tf_op jit(solution)/shard_map/ppermute | solution.py:324
  22.0 0.3 choose.1
  22.4 4.9 %collective-permute-done.5.refs_8_.refs_0_.refs_1_ = bf16[512,256]{1,0:T(8,128)(2,1)S(1)} collective-permute-done((bf16[512,256]{1,0:T(8,128)(2,1)S(1)}, bf16[512,256]{1,0:T(8,128)(2,1)S(1)}, u32[]{:S(2)}, u32[]{:S(2)}) %collective-permute-start.5) | collective-permute-done | bytes 262176 | tf_op jit(solution)/shard_map/ppermute | solution.py:324
  27.3 0.4 %late.1 = f32[64,640]{1,0:T(8,128)S(1)} custom-call(bf16[1,256,512]{2,1,0:T(8,128)(2,1)S(1)} %get-tuple-element.9.left_ref, bf16[64,640]{1,0:T(8,128)(2,1)S(1)} %early.1.early_ref, bf16[512,256]{1,0:T(8,128)(2,1)S(1)} %collective-permute-done.5.refs_8_.refs_0_.refs_1_), custom_call_target="tpu_custom_call" | custom-call | tf_op jit(solution)/shard_map/late/pallas_call | solution.py:237
  27.6 0.0 collective-permute-done.6.refs_0_
  27.7 1.5 %collective-permute-start.7 = (bf16[64,640]{1,0:T(8,128)(2,1)S(1)}, bf16[64,640]{1,0:T(8,128)(2,1)S(1)}, u32[]{:S(2)}, u32[]{:S(2)}) collective-permute-start(bf16[64,640]{1,0:T(8,128)(2,1)S(1)} %add_convert_fusion.refs_0_), channel_id=1, source_target_pairs={{4,0},{0,4},{12,8},{8,12},{5,1},{1,5},{13,9},{9,13},{6,2},{2,6},{1... | collective-permute-start | bytes 245768 | tf_op jit(solution)/shard_map/ppermute | solution.py:324
  29.2 1.5 %cross.1 = f32[512,256]{1,0:T(8,128)} custom-call(bf16[512,512]{1,0:T(8,128)(2,1)S(1)} %get-tuple-element.6.refs_0_, bf16[512,512]{1,0:T(8,128)(2,1)S(1)} %collective-permute-done.refs_1_, bf16[512,512]{1,0:T(8,128)(2,1)S(1)} %relay.4.refs_2_.refs_1_, bf16[512,512]{1,0:T(8,128)(2,1)S(1)} %collective-permute-done.2.refs_3_, ...), custom_call_target="tpu_custom_call" | custom-call | flops 536870912 | bytes 524288 | tf_op jit(solution)/shard_map/cross/pallas_call | solution.py:260
  30.7 1.5 %collective-permute-done.7.refs_1_ = bf16[64,640]{1,0:T(8,128)(2,1)S(1)} collective-permute-done((bf16[64,640]{1,0:T(8,128)(2,1)S(1)}, bf16[64,640]{1,0:T(8,128)(2,1)S(1)}, u32[]{:S(2)}, u32[]{:S(2)}) %collective-permute-start.7) | collective-permute-done | bytes 81952 | tf_op jit(solution)/shard_map/ppermute | solution.py:324
  32.2 0.8 %finish.1 = f32[1,256,256]{2,1,0:T(8,128)} custom-call(f32[1,256,256]{2,1,0:T(8,128)S(1)} %copy-done, bf16[64,640]{1,0:T(8,128)(2,1)S(1)} %add_convert_fusion.refs_0_, bf16[64,640]{1,0:T(8,128)(2,1)S(1)} %collective-permute-done.7.refs_1_), custom_call_target="tpu_custom_call" | custom-call | tf_op jit(solution)/shard_map/finish/pallas_call | solution.py:306
  (6 shorter events, 0.0 us)
Async XLA Ops:
  0.6 3.0 %copy-start = (f32[1,256,256]{2,1,0:T(8,128)S(1)}, f32[1,256,256]{2,1,0:T(8,128)}, u32[]{:S(2)}) copy-start(f32[1,256,256]{2,1,0:T(8,128)} %diag_ref.3) | copy-start | bytes 786436
  0.6 3.0 %copy-start.1 = (f32[512,256]{1,0:T(8,128)S(1)}, f32[512,256]{1,0:T(8,128)}, u32[]{:S(2)}) copy-start(f32[512,256]{1,0:T(8,128)} %cross_ref.1) | copy-start | bytes 1572868
  0.6 15.1 %collective-permute-start.1 = (bf16[512,512]{1,0:T(8,128)(2,1)}, bf16[512,512]{1,0:T(8,128)(2,1)S(1)}, u32[]{:S(2)}, u32[]{:S(2)}) collective-permute-start(bf16[512,512]{1,0:T(8,128)(2,1)} %top_hbm.1), channel_id=1, source_target_pairs={{2,0},{3,1},{0,2},{1,3},{6,4},{7,5},{4,6},{5,7},{10,8},{11,9},{8,1... | collective-permute-start | bytes 1572872 | tf_op jit(solution)/shard_map/ppermute | solution.py:324
  4.5 11.3 %collective-permute-start.4 = (bf16[512,256]{1,0:T(8,128)(2,1)S(1)}, bf16[512,256]{1,0:T(8,128)(2,1)S(1)}, u32[]{:S(2)}, u32[]{:S(2)}) collective-permute-start(bf16[512,256]{1,0:T(8,128)(2,1)S(1)} %panel.1.panel_ref.refs_4_.refs_0_), channel_id=1, source_target_pairs={{12,0},{8,4},{4,8},{0,12},{13,1},{9,5},{5,9},{1,13},{14,2},{10,6},... | collective-permute-start | bytes 786440 | tf_op jit(solution)/shard_map/ppermute | solution.py:324
  8.1 12.3 %collective-permute-start.3 = (bf16[512,256]{1,0:T(8,128)(2,1)S(1)}, bf16[512,256]{1,0:T(8,128)(2,1)S(1)}, u32[]{:S(2)}, u32[]{:S(2)}) collective-permute-start(bf16[512,256]{1,0:T(8,128)(2,1)S(1)} %panel.1.panel_ref.refs_4_.refs_0_), channel_id=1, source_target_pairs={{4,0},{0,4},{12,8},{8,12},{5,1},{1,5},{13,9},{9,13},{6,2},{2,6},{1... | collective-permute-start | bytes 786440 | tf_op jit(solution)/shard_map/ppermute | solution.py:324
  9.2 10.3 %collective-permute-start = (bf16[512,512]{1,0:T(8,128)(2,1)S(1)}, bf16[512,512]{1,0:T(8,128)(2,1)S(1)}, u32[]{:S(2)}, u32[]{:S(2)}) collective-permute-start(bf16[512,512]{1,0:T(8,128)(2,1)S(1)} %get-tuple-element.6.refs_0_), channel_id=1, source_target_pairs={{1,0},{0,1},{3,2},{2,3},{5,4},{4,5},{7,6},{6,7},{9,8},{8,9},{11,10... | collective-permute-start | bytes 1572872 | tf_op jit(solution)/shard_map/ppermute | solution.py:324
  15.8 3.7 %collective-permute-start.2 = (bf16[512,512]{1,0:T(8,128)(2,1)S(1)}, bf16[512,512]{1,0:T(8,128)(2,1)S(1)}, u32[]{:S(2)}, u32[]{:S(2)}) collective-permute-start(bf16[512,512]{1,0:T(8,128)(2,1)S(1)} %relay.4.refs_2_.refs_1_), channel_id=1, source_target_pairs={{1,0},{0,1},{3,2},{2,3},{5,4},{4,5},{7,6},{6,7},{9,8},{8,9},{11,10... | collective-permute-start | bytes 1572872 | tf_op jit(solution)/shard_map/ppermute | solution.py:324
  15.8 11.5 %collective-permute-start.5 = (bf16[512,256]{1,0:T(8,128)(2,1)S(1)}, bf16[512,256]{1,0:T(8,128)(2,1)S(1)}, u32[]{:S(2)}, u32[]{:S(2)}) collective-permute-start(bf16[512,256]{1,0:T(8,128)(2,1)S(1)} %relay.5.refs_2_.refs_6_), channel_id=1, source_target_pairs={{4,0},{0,4},{12,8},{8,12},{5,1},{1,5},{13,9},{9,13},{6,2},{2,6},{1... | collective-permute-start | bytes 786440 | tf_op jit(solution)/shard_map/ppermute | solution.py:324
  20.9 6.7 %collective-permute-start.6 = (bf16[64,640]{1,0:T(8,128)(2,1)S(1)}, bf16[64,640]{1,0:T(8,128)(2,1)S(1)}, u32[]{:S(2)}, u32[]{:S(2)}) collective-permute-start(bf16[64,640]{1,0:T(8,128)(2,1)S(1)} %early.1.early_ref), channel_id=1, source_target_pairs={{8,0},{12,4},{0,8},{4,12},{9,1},{13,5},{1,9},{5,13},{10,2},{14,6},... | collective-permute-start | bytes 245768 | tf_op jit(solution)/shard_map/ppermute | solution.py:324
  27.7 4.5 %collective-permute-start.7 = (bf16[64,640]{1,0:T(8,128)(2,1)S(1)}, bf16[64,640]{1,0:T(8,128)(2,1)S(1)}, u32[]{:S(2)}, u32[]{:S(2)}) collective-permute-start(bf16[64,640]{1,0:T(8,128)(2,1)S(1)} %add_convert_fusion.refs_0_), channel_id=1, source_target_pairs={{4,0},{0,4},{12,8},{8,12},{5,1},{1,5},{13,9},{9,13},{6,2},{2,6},{1... | collective-permute-start | bytes 245768 | tf_op jit(solution)/shard_map/ppermute | solution.py:324
